TPU v7x, 256 devices: a whole 4x4x8 slice. The times are simulated.
256 devices in a mesh: dp: 4 (over y_lo, core), shard: 64 (over z, x, y_hi).
Axes of the slice: x: 4, y: 4 (y_hi: 2, y_lo: 2; y = y_hi * 2 + y_lo), z: 8, core: 2. Of those that a mesh axis runs over, the one named last changes fastest.
Arguments:
- grad_parts: bfloat16 [4, 14336, 2048], P('dp', 'shard'), may hold values from -6 to 6
- coarse_weight: float32 [14336, 2048], P('shard', 'dp'), may hold values from -6 to 6
- first_moment: float32 [14336, 2048], P('shard', 'dp'), may hold values from -6 to 6
- second_moment: float32 [14336, 2048], P('shard', 'dp'), may hold values from 0.05 to 4
- partner_device: int32 [28672, 1], P('shard'), may hold values from 0 to 63; in each aligned block of 448 rows (0 to 447, 448 to 895, ...) at most 14 rows name the same one
- partner_column: int32 [28672], P('shard'), may hold values from 0 to 223
Outputs:
- fine_weight: float32 [28672, 4096], P('shard', 'dp')
- fine_first: float32 [28672, 4096], P('shard', 'dp')
- fine_second: float32 [28672, 4096], P('shard', 'dp')
Inputs may be any that keep to these rules, and one draw needn't show every extreme that they name: `partner_device`: within each aligned block of 28672 / 64 fine hidden units, no shard index is named more than 14 times, a bound that some block reaches.
All inputs are finite; a program needn't handle non-finite values.
Results may differ from a plain program's by a relative error of at most 0.0003.
Values sent between devices are 32-bit elements; how exact they have to be, the bound alone decides.
No kernel may reach another device: no remote copies, remote signals or barrier semaphores. Data moves between devices by JAX's collectives and lax.ppermute only.
A program may use at most 64 MiB of HBM per device.

v0:
```python
import jax
import jax.numpy as jnp
from jax import lax
from jax.sharding import PartitionSpec as P

STEP = 20


first_decay = 0.9
second_decay = 0.95
learning_rate = 0.02
weight_decay = 0.1
epsilon = 1e-08
own_share = 0.75


def adamw_update(weight, first, second, grad):
    new_first = first_decay * first + (1.0 - first_decay) * grad
    new_second = second_decay * second + (1.0 - second_decay) * grad * grad
    first_hat = new_first / (1.0 - first_decay**STEP)
    second_hat = new_second / (1.0 - second_decay**STEP)
    new_weight = weight - learning_rate * (
        first_hat / (jnp.sqrt(second_hat) + epsilon) + weight_decay * weight
    )
    return (new_weight, new_first, new_second)


def on_device(
    grad_parts, coarse_weight, first_moment, second_moment, partner_device, partner_column
):
    shard_count = lax.axis_size("shard")
    fine_units = partner_column.shape[0]
    capacity = max(2, 2 * fine_units // shard_count)
    feature_cols = coarse_weight.shape[1]
    grad = lax.psum_scatter(
        grad_parts[0].astype(jnp.float32), "dp", scatter_dimension=1, tiled=True
    )
    source_dev = partner_device[:, 0]
    onehot = (source_dev[:, None] == jnp.arange(shard_count, dtype=jnp.int32)[None, :]).astype(
        jnp.int32
    )
    slot = jnp.sum((jnp.cumsum(onehot, axis=0) - onehot) * onehot, axis=1)
    wanted = jnp.zeros((shard_count, capacity), jnp.int32).at[source_dev, slot].set(partner_column)
    asked = lax.all_to_all(wanted, "shard", split_axis=0, concat_axis=0, tiled=True).reshape(-1)

    def pick(state):
        return jnp.take(state, asked, axis=0).reshape(shard_count, capacity, feature_cols)

    def flatten(state):
        return state.reshape(shard_count * capacity, feature_cols)

    new_weight, new_first, new_second = adamw_update(
        coarse_weight, first_moment, second_moment, grad
    )
    got_weight, got_first, got_second = (
        lax.all_to_all(pick(new_weight), "shard", split_axis=0, concat_axis=0, tiled=True),
        lax.all_to_all(pick(new_first), "shard", split_axis=0, concat_axis=0, tiled=True),
        lax.all_to_all(pick(new_second), "shard", split_axis=0, concat_axis=0, tiled=True),
    )
    far_weight, far_first, far_second = (
        flatten(got_weight),
        flatten(got_first),
        flatten(got_second),
    )
    position = source_dev * capacity + slot

    def expand(near, far):
        mixed = own_share * jnp.repeat(near, 2, axis=0) + (1.0 - own_share) * jnp.take(
            far, position, axis=0
        )
        return jnp.repeat(mixed, 2, axis=1)

    return (
        expand(new_weight, far_weight),
        expand(new_first, far_first),
        expand(new_second, far_second),
    )


def solution(mesh):
    placed = (
        P("dp", "shard", None),
        P("shard", "dp"),
        P("shard", "dp"),
        P("shard", "dp"),
        P("shard", None),
        P("shard"),
    )
    return jax.shard_map(
        on_device,
        mesh=mesh,
        in_specs=placed,
        out_specs=(P("shard", "dp"), P("shard", "dp"), P("shard", "dp")),
        check_vma=False,
    )
```

profile of v0, /device:TPU:2, one launch (start us, length us, event | category | flops | bytes accessed | tf_op | source)
XLA Modules:
  0.0 290.6 jit_solution(7806897930515867185)
XLA Ops:
  7.2 0.0 copy-start.8
  7.2 0.0 reduce-scatter.2.cloned.1.call-start
  7.2 2.6 bitcast_convert_fusion
  9.8 0.0 reduce-scatter.2.cloned.1.call-update
  9.9 0.0 copy-done.8
  9.9 1.2 reduce-window.6
  11.1 0.2 slice_reduce_fusion
  11.4 0.1 bitcast_bitcast_fusion
  11.6 0.0 copy-done.9
  11.6 0.0 copy-start.6
  11.6 0.0 copy-start.7
  11.6 23.7 %scatter_fusion = s32[64,14]{0,1:T(8,128)S(1)} fusion(s32[64,14]{0,1:T(8,128)S(1)} %broadcast_in_dim.43, s32[448]{0:T(512)S(1)} %bitcast.26, s32[448]{0:T(512)S(1)} %copy-done.9), kind=kCustom, calls=%fused_computation.6 | custom fusion | bytes 8960 | tf_op jit(solution)/shard_map/scatter | solution.py:43
  35.4 0.1 copy.20
  35.5 25.4 %all_to_all.24 = s32[64,1,14]{2,1,0:T(1,128)S(1)} all-to-all(s32[64,1,14]{2,1,0:T(1,128)S(1)} %copy.20), channel_id=1, replica_groups=mesh['dp'=4,'shard'=64] {'shard'}, dimensions={0} | all-to-all | bytes 7168 | tf_op jit(solution)/shard_map/all_to_all | solution.py:44
  60.8 0.5 broadcast.123
  61.4 0.7 reduce.5
  62.1 0.1 reshape.86
  62.3 0.0 reduce-scatter.2.cloned.1.call-done
  62.3 0.0 copy-done.6
  62.3 0.0 copy-done.7
  62.3 2.2 broadcast_multiply_fusion.1
  64.6 2.7 gather_fusion.4
  67.3 3.6 %gather_fusion.2 = f32[896,512]{1,0:T(8,128)} fusion(f32[224,512]{1,0:T(8,128)S(1)} %get-tuple-element.14, s32[1024]{0:T(1024)S(1)} %pad_clamp_fusion.1), kind=kCustom, calls=%fused_computation.2.clone | custom fusion | bytes 3673600 | tf_op jit(solution)/shard_map/jit(_take)/gather | solution.py:47
  70.8 2.1 broadcast_multiply_fusion.2
  72.9 3.5 %gather_fusion = f32[896,512]{1,0:T(8,128)} fusion(f32[224,512]{1,0:T(8,128)S(1)} %get-tuple-element.18, s32[1024]{0:T(1024)S(1)} %pad_clamp_fusion.1), kind=kCustom, calls=%fused_computation.clone | custom fusion | bytes 3673600 | tf_op jit(solution)/shard_map/jit(_take)/gather | solution.py:47
  76.5 4.9 %broadcast_select_fusion = (f32[896,512]{1,0:T(8,128)}, f32[896,512]{1,0:T(8,128)}, f32[896,512]{1,0:T(8,128)}) fusion(f32[896,512]{1,0:T(8,128)S(1)} %gather_fusion.4, pred[896]{0:T(1024)(128)(4,1)S(1)} %compare_and_fusion, f32[896,512]{1,0:T(8,128)} %gather_fusion.2, f32[896,512]{1,0:T(8,128)} %gather_fusion), kind=kLoop, calls=%fused_computation.14 | loop fusion | flops 1376256 | bytes 11010944 | tf_op jit(solution)/shard_map/jit(_take)/select_n | solution.py:47
  81.4 2.7 reshape.87
  84.1 5.6 %all-to-all-start.1 = ((f32[64,14,512]{2,1,0:T(8,128)}), f32[64,14,512]{2,1,0:T(8,128)S(1)}, u32[]{:S(2)}, u32[]{:S(2)}) async-start(f32[64,14,512]{2,1,0:T(8,128)} %reshape.87), calls=%async_computation.2 | async-start | bytes 4194304 | tf_op jit(solution)/shard_map/all_to_all | solution.py:56
  89.7 2.7 reshape.90
  92.4 47.8 %all-to-all-done.1 = f32[64,14,512]{2,1,0:T(8,128)S(1)} async-done(((f32[64,14,512]{2,1,0:T(8,128)}), f32[64,14,512]{2,1,0:T(8,128)S(1)}, u32[]{:S(2)}, u32[]{:S(2)}) %all-to-all-start.1) | async-done | bytes 1835040 | tf_op jit(solution)/shard_map/all_to_all | solution.py:56
  140.1 1.3 copy-done
  141.5 7.4 %all-to-all-start.2 = ((f32[64,14,512]{2,1,0:T(8,128)}), f32[64,14,512]{2,1,0:T(8,128)}, u32[]{:S(2)}, u32[]{:S(2)}) async-start(f32[64,14,512]{2,1,0:T(8,128)} %reshape.90), calls=%async_computation.3 | async-start | bytes 4194304 | tf_op jit(solution)/shard_map/all_to_all | solution.py:57
  148.9 2.7 reshape.93
  151.6 47.4 %all-to-all-done.2 = f32[64,14,512]{2,1,0:T(8,128)} async-done(((f32[64,14,512]{2,1,0:T(8,128)}), f32[64,14,512]{2,1,0:T(8,128)}, u32[]{:S(2)}, u32[]{:S(2)}) %all-to-all-start.2) | async-done | bytes 1835040 | tf_op jit(solution)/shard_map/all_to_all | solution.py:57
  199.0 7.5 %all-to-all-start.3 = ((f32[64,14,512]{2,1,0:T(8,128)}), f32[64,14,512]{2,1,0:T(8,128)}, u32[]{:S(2)}, u32[]{:S(2)}) async-start(f32[64,14,512]{2,1,0:T(8,128)} %reshape.93), calls=%async_computation.4 | async-start | bytes 4194304 | tf_op jit(solution)/shard_map/all_to_all | solution.py:58
  206.5 0.0 copy-start.4
  206.6 0.3 broadcast_in_dim.42
  206.9 1.6 mul.81
  208.5 0.0 copy-done.4
  208.5 0.3 broadcast_in_dim.45
  208.8 1.6 mul.86
  210.4 0.3 broadcast_in_dim.47
  210.7 1.6 mul.89
  212.2 1.6 reshape.88
  213.9 1.7 gather_fusion.1
  215.6 1.7 reshape.91
  217.2 2.3 gather_fusion.3
  219.5 37.0 %all-to-all-done.3 = f32[64,14,512]{2,1,0:T(8,128)} async-done(((f32[64,14,512]{2,1,0:T(8,128)}), f32[64,14,512]{2,1,0:T(8,128)}, u32[]{:S(2)}, u32[]{:S(2)}) %all-to-all-start.3) | async-done | bytes 1835040 | tf_op jit(solution)/shard_map/all_to_all | solution.py:58
  256.5 1.6 reshape.94
  258.2 2.3 gather_fusion.5
  260.5 3.9 %fusion = (f32[448,512]{1,0:T(8,128)}, f32[448,512]{1,0:T(8,128)}, f32[448,512]{1,0:T(8,128)S(1)}) fusion(f32[448,512]{1,0:T(8,128)} %mul.89, f32[448,512]{1,0:T(8,128)} %gather_fusion.5, pred[448]{0:T(512)(128)(4,1)S(1)} %get-tuple-element.15, f32[448,512]{1,0:T(8,128)} %mul.86, f32[448,512]{1,0:T(8,128)} %gather_fusion.3, f32[448,512]{1,0:T(8,128)} %mul.81, ...), kind=kLoop, calls=%fused_computation.9 | loop fusion | flops 2064384 | bytes 8257984 | tf_op jit(solution)/shard_map/add | solution.py:68
  264.3 0.3 copy.21
  264.7 0.7 broadcast_in_dim.44
  265.4 2.6 reshape.89
  268.0 2.9 copy.24
  270.9 0.3 copy.22
  271.2 0.7 broadcast_in_dim.46
  271.9 2.6 reshape.92
  274.5 2.9 copy.25
  277.4 0.0 copy-done.1
  277.4 0.3 copy.23
  277.7 0.7 broadcast_in_dim.48
  278.4 2.6 reshape.95
  281.0 2.8 copy.26
  (21 shorter events, 0.2 us)
Async XLA Ops:
  7.2 2.7 copy-start.8
  7.2 55.1 %reduce-scatter.2.cloned.1.call-start = ((), (), s32[]{:S(2)}) async-start(), calls=%async_computation.5 | async-start | bytes 2293760 | tf_op jit(solution)/shard_map/reduce_scatter | solution.py:35
  9.8 1.8 copy-start.9
  11.6 50.7 %copy-start.6 = (f32[224,512]{1,0:T(8,128)S(1)}, f32[224,512]{1,0:T(8,128)}, u32[]{:S(2)}) copy-start(f32[224,512]{1,0:T(8,128)} %param.12) | copy-start | bytes 1376260
  11.6 50.7 %copy-start.7 = (f32[224,512]{1,0:T(8,128)S(1)}, f32[224,512]{1,0:T(8,128)}, u32[]{:S(2)}) copy-start(f32[224,512]{1,0:T(8,128)} %param.13) | copy-start | bytes 1376260
  84.1 56.1 %all-to-all-start.1 = ((f32[64,14,512]{2,1,0:T(8,128)}), f32[64,14,512]{2,1,0:T(8,128)S(1)}, u32[]{:S(2)}, u32[]{:S(2)}) async-start(f32[64,14,512]{2,1,0:T(8,128)} %reshape.87), calls=%async_computation.2 | async-start | bytes 4194304 | tf_op jit(solution)/shard_map/all_to_all | solution.py:56
  140.1 1.3 copy-start
  141.5 57.5 %all-to-all-start.2 = ((f32[64,14,512]{2,1,0:T(8,128)}), f32[64,14,512]{2,1,0:T(8,128)}, u32[]{:S(2)}, u32[]{:S(2)}) async-start(f32[64,14,512]{2,1,0:T(8,128)} %reshape.90), calls=%async_computation.3 | async-start | bytes 4194304 | tf_op jit(solution)/shard_map/all_to_all | solution.py:57
  151.6 55.0 %copy-start.5 = (f32[224,512]{1,0:T(8,128)S(1)}, f32[224,512]{1,0:T(8,128)}, u32[]{:S(2)}) copy-start(f32[224,512]{1,0:T(8,128)} %get-tuple-element.17) | copy-start | bytes 1376260
  199.0 57.5 %all-to-all-start.3 = ((f32[64,14,512]{2,1,0:T(8,128)}), f32[64,14,512]{2,1,0:T(8,128)}, u32[]{:S(2)}, u32[]{:S(2)}) async-start(f32[64,14,512]{2,1,0:T(8,128)} %reshape.93), calls=%async_computation.4 | async-start | bytes 4194304 | tf_op jit(solution)/shard_map/all_to_all | solution.py:58
  206.5 2.0 copy-start.4
  208.5 1.9 copy-start.3
  268.0 2.9 copy-start.2
  274.5 2.9 copy-start.1
Sparse Core Ops, SparseCore 0:
  11.1 31.5 reduce-scatter.1
where the time goes:
time: 292 us; the launch traced here: 291 us
  waiting for transfers between devices  132 us (45%)
  local copies, waits for them, and re-layouts  80.2 us (27%)
  blocking collectives  25.4 us (9%)
  starting transfers between devices  20.6 us (7%)
  other arithmetic  18 us (6%)
  between operations  14.3 us (5%)
    all_to_all x1, waiting for transfers between devices, on_device(): lax.all_to_all(pick(new_weight), 'shard', split_axis=0, concat_axis=0, ti...  47.8 us
    all_to_all x1, waiting for transfers between devices, on_device(): lax.all_to_all(pick(new_first), 'shard', split_axis=0, concat_axis=0, til...  47.4 us
    all_to_all x1, waiting for transfers between devices, on_device(): lax.all_to_all(pick(new_second), 'shard', split_axis=0, concat_axis=0, ti...  37 us
    all_to_all x1, blocking collectives, on_device(): lax.all_to_all(wanted, 'shard', split_axis=0, concat_axis=0, tiled=True)  25.4 us
    scatter x1, local copies, waits for them, and re-layouts, on_device(): jnp.zeros((shard_count, capacity), jnp.int32).at[source_dev, slot]  23.7 us
    unnamed x23, local copies, waits for them, and re-layouts  9.93 us
    gather x3, local copies, waits for them, and re-layouts, pick(): jnp.take(state, asked, axis=0).reshape(shard_count, capacity, feature_cols)  9.8 us
    reshape x3, local copies, waits for them, and re-layouts, pick(): jnp.take(state, asked, axis=0).reshape(shard_count, capacity, feature_cols)  8.05 us
  transfers between devices with their start and end apart: 4, of which 3 were waited for; matrix products, arithmetic and copies ran while one was open for 16% of the time, Pallas kernels for 0%

commit v1 on v0

v1 whole, which is shorter than its diff:
```python
import jax
import jax.numpy as jnp
from jax import lax
from jax.experimental import pallas as pl
from jax.experimental.pallas import tpu as pltpu
from jax.sharding import PartitionSpec as P

STEP = 20

first_decay = 0.9
second_decay = 0.95
learning_rate = 0.02
weight_decay = 0.1
epsilon = 1e-08
own_share = 0.75

F32 = jnp.float32
BF16 = jnp.bfloat16
I32 = jnp.int32

ROWS = 224
FINE = 448
FEATS = 512
HALF = 256
WIDE = 3 * HALF
SLOTS = 16
PLANE = 8
RING = 8

VMEM = pltpu.CompilerParams(vmem_limit_bytes=48 * 1024 * 1024)


def call(kernel, out, *, grid=None, in_specs=None, out_specs=None, flops=0, moved=0):
    extra = {}
    if grid is not None:
        extra = dict(grid=grid, in_specs=in_specs, out_specs=out_specs)
    elif in_specs is not None:
        extra = dict(in_specs=in_specs)
    return pl.pallas_call(
        kernel,
        out_shape=out,
        compiler_params=VMEM,
        cost_estimate=pl.CostEstimate(flops=flops, bytes_accessed=moved, transcendentals=0),
        **extra,
    )


def whole():
    return pl.BlockSpec(memory_space=pltpu.VMEM)


def scalar():
    return pl.BlockSpec(memory_space=pltpu.SMEM)


def split_dot(chosen, values, contract=((1,), (0,))):
    high = values.astype(BF16)
    low = (values - high.astype(F32)).astype(BF16)
    dims = (contract, ((), ()))
    return lax.dot_general(chosen, high, dims, preferred_element_type=F32) + lax.dot_general(
        chosen, low, dims, preferred_element_type=F32
    )


def send_core_kernel(place, grad, out0, out1):
    dp = place[1]
    core, y = lax.rem(dp, 2), lax.div(dp, 2)
    for half, out in enumerate((out0, out1)):
        for part, row in enumerate((1 - y, y)):
            at = pl.multiple_of((row * 2 + 1 - core) * FEATS + half * HALF, HALF)
            out[:, part * HALF : (part + 1) * HALF] = grad[:, pl.ds(at, HALF)].astype(F32)


def send_y_kernel(half, place, grad, got, out):
    dp = place[1]
    core, y = lax.rem(dp, 2), lax.div(dp, 2)
    at = pl.multiple_of(((1 - y) * 2 + core) * FEATS + half * HALF, HALF)
    out[...] = grad[:, pl.ds(at, HALF)].astype(F32) + got[...]


def update_kernel(half, place, grad, got, got_y, weight, first, second, out):
    dp = place[1]
    at = pl.multiple_of(dp * FEATS + half * HALF, HALF)
    total = grad[:, pl.ds(at, HALF)].astype(F32) + got[...] + got_y[...]
    new_first = first_decay * first[...] + (1.0 - first_decay) * total
    new_second = second_decay * second[...] + (1.0 - second_decay) * total * total
    first_hat = new_first / (1.0 - first_decay**STEP)
    second_hat = new_second / (1.0 - second_decay**STEP)
    old = weight[...]
    new_weight = old - learning_rate * (
        first_hat / (jnp.sqrt(second_hat) + epsilon) + weight_decay * old
    )
    out[:, 0:HALF] = new_weight
    out[:, HALF : 2 * HALF] = new_first
    out[:, 2 * HALF : 3 * HALF] = new_second


def index_kernel(place, dev, dev_row, col, wanted, codes):
    shard = place[0]
    plane, me = lax.div(shard, PLANE), lax.rem(shard, PLANE)
    d = dev[...]
    r = dev_row[...]
    earlier = lax.broadcasted_iota(I32, (FINE, FINE), 1) < lax.broadcasted_iota(
        I32, (FINE, FINE), 0
    )
    slot = jnp.sum(jnp.where(earlier & (d == r), 1, 0), axis=1, keepdims=True)
    source_xy, source_z = d & (PLANE - 1), d >> 3
    row_of = ((r & (PLANE - 1)) << 3) + (r >> 3)
    left = jnp.where(lax.broadcasted_iota(I32, (64, FINE), 0) == row_of, 1.0, 0.0).astype(BF16)
    right = jnp.where(
        lax.broadcasted_iota(I32, (FINE, 128), 1) == me * SLOTS + slot, col[...].astype(F32), 0.0
    ).astype(BF16)
    table = jnp.dot(left, right, preferred_element_type=F32)
    wanted[...] = table.astype(I32).reshape(PLANE, RING, 128)
    away = (source_z - plane + RING) & (RING - 1)
    none = -1

    def place_in(rows, offsets):
        at = jnp.full((FINE, 1), none, I32)
        for k, offset in offsets:
            at = jnp.where(away == k, source_xy * rows + offset + slot, at)
        return at

    groups = (
        place_in(48, ((0, 0), (7, 16), (1, 32))),
        place_in(32, ((6, 0), (2, 16))),
        place_in(32, ((5, 0), (3, 16))),
        place_in(16, ((4, 0),)),
    )
    lane = lax.broadcasted_iota(I32, (FINE, 128), 1)
    out = jnp.full((FINE, 128), none, I32)
    for g, at in enumerate(groups):
        out = jnp.where(lane == g, at, out)
    codes[...] = out


def asked_rows(asked, plane):
    table = jnp.sum(asked[...], axis=0)
    here = lax.broadcasted_iota(I32, (RING, 128), 0) == plane
    return jnp.sum(jnp.where(here, table, 0), axis=0, keepdims=True)


def pick_from(asked, plane, values):
    rows = values.shape[0]
    chosen = jnp.where(
        lax.broadcasted_iota(I32, (rows, 128), 0) == asked_rows(asked, plane), 1.0, 0.0
    ).astype(BF16)
    return split_dot(chosen, values, ((0,), (0,)))


def pick_kernel(offsets, place, asked, *refs):
    out = refs[-1]
    plane = lax.div(place[0], PLANE)
    for n, offset in enumerate(offsets):
        from_plane = (plane + offset + RING) & (RING - 1)
        for half in range(2):
            got = pick_from(asked, from_plane, refs[2 * n + half][...])
            for d in range(PLANE):
                out[d, n * SLOTS : (n + 1) * SLOTS, half * WIDE : (half + 1) * WIDE] = got[
                    d * SLOTS : (d + 1) * SLOTS
                ]


def pick_last_kernel(place, asked, low0, low1, high0, high1, out):
    plane = lax.div(place[0], PLANE)
    from_plane = (plane + 4) & (RING - 1)
    for half, (low, high) in enumerate(((low0, high0), (low1, high1))):
        got = pick_from(asked, from_plane, jnp.concatenate([low[...], high[...]], axis=0))
        for d in range(PLANE):
            out[d, :, half * WIDE : (half + 1) * WIDE] = got[d * SLOTS : (d + 1) * SLOTS]


def far_dot(codes, group, far):
    rows = far.shape[0] * far.shape[1]
    at = codes[:, group : group + 1]
    chosen = jnp.where(
        lax.broadcasted_iota(I32, (FINE, rows), 1) == at, 1.0 - own_share, 0.0
    ).astype(BF16)
    return split_dot(chosen, far[...].reshape(rows, far.shape[2]))


def gather_kernel(codes, near0, near1, far1, far2, out):
    i = pl.program_id(0)
    near = jnp.where(i < 3, near0[...], near1[...])
    own = lax.broadcasted_iota(I32, (FINE, ROWS), 0) >> 1
    chosen = jnp.where(
        lax.broadcasted_iota(I32, (FINE, ROWS), 1) == own, own_share, 0.0
    ).astype(BF16)
    out[...] = split_dot(chosen, near) + far_dot(codes, 0, far1) + far_dot(codes, 1, far2)


def final_kernel(codes, *refs):
    lane = lax.broadcasted_iota(I32, (FINE, 128), 1) >> 1
    for state in range(3):
        acc, far3, far4 = refs[state], refs[3 + state], refs[6 + state]
        out = refs[9 + state]
        mixed = acc[...] + far_dot(codes, 2, far3) + far_dot(codes, 3, far4)
        out[:, 0:128] = jnp.take_along_axis(mixed, lane, axis=1)
        out[:, 128:256] = jnp.take_along_axis(mixed, lane + 64, axis=1)


PLANES = [[z * PLANE + p for p in range(PLANE)] for z in range(RING)]
UP = [(z * PLANE + p, ((z + 1) % RING) * PLANE + p) for z in range(RING) for p in range(PLANE)]
DOWN = [(b, a) for a, b in UP]
CORE = [(0, 1), (1, 0), (2, 3), (3, 2)]
NEXT_Y = [(0, 2), (2, 0), (1, 3), (3, 1)]


def shape(*dims, dtype=F32):
    return jax.ShapeDtypeStruct(dims, dtype)


def on_device(grad_parts, weight, first, second, partner_device, partner_column):
    place = jnp.stack([lax.axis_index("shard"), lax.axis_index("dp")]).astype(I32)
    grad = grad_parts[0]

    sends = call(
        send_core_kernel,
        (shape(ROWS, 2 * HALF),) * 2,
        in_specs=[scalar(), whole()],
        moved=3 << 20,
    )(place, grad)
    got_core = [lax.ppermute(s, "dp", CORE) for s in sends]
    state = []
    for half in range(2):
        got = got_core[half]
        passed = call(
            lambda *refs, half=half: send_y_kernel(half, *refs),
            shape(ROWS, HALF),
            grid=(1,),
            in_specs=[
                scalar(),
                pl.BlockSpec((ROWS, 4 * FEATS), lambda i: (0, 0)),
                pl.BlockSpec((ROWS, HALF), lambda i: (0, 0)),
            ],
            out_specs=pl.BlockSpec((ROWS, HALF), lambda i: (0, 0)),
            moved=1 << 20,
        )(place, grad, got)
        got_y = lax.ppermute(passed, "dp", NEXT_Y)
        block = pl.BlockSpec((ROWS, HALF), lambda i, half=half: (0, half))
        state.append(
            call(
                lambda *refs, half=half: update_kernel(half, *refs),
                shape(ROWS, WIDE),
                grid=(1,),
                in_specs=[
                    scalar(),
                    pl.BlockSpec((ROWS, 4 * FEATS), lambda i: (0, 0)),
                    pl.BlockSpec((ROWS, HALF), lambda i: (0, 1)),
                    pl.BlockSpec((ROWS, HALF), lambda i: (0, 0)),
                    block,
                    block,
                    block,
                ],
                out_specs=pl.BlockSpec((ROWS, WIDE), lambda i: (0, 0)),
                moved=2 << 20,
            )(place, grad, got, got_y, weight, first, second)
        )

    wanted, codes = call(
        index_kernel,
        (shape(PLANE, RING, 128, dtype=I32), shape(FINE, 128, dtype=I32)),
        in_specs=[scalar(), whole(), whole(), whole()],
        moved=1 << 20,
    )(
        place,
        partner_device,
        partner_device.reshape(1, FINE),
        partner_column.reshape(FINE, 1),
    )
    asked = lax.all_to_all(
        wanted, "shard", split_axis=0, concat_axis=0, axis_index_groups=PLANES, tiled=True
    )

    up, down = [state], [state]
    for step in range(3):
        nu, nd = [], []
        for half in range(2):
            nu.append(lax.ppermute(up[-1][half], "shard", UP))
            nd.append(lax.ppermute(down[-1][half], "shard", DOWN))
        up.append(nu)
        down.append(nd)
    middle = ROWS // 2
    low = [lax.ppermute(up[3][half][:middle], "shard", UP) for half in range(2)]
    high = [lax.ppermute(down[3][half][middle:], "shard", DOWN) for half in range(2)]

    def pick(offsets, sources):
        rows = SLOTS * len(offsets)
        return call(
            lambda *refs: pick_kernel(offsets, *refs),
            shape(PLANE, rows, 2 * WIDE),
            in_specs=[scalar()] + [whole()] * (1 + len(sources)),
            flops=rows * PLANE * ROWS * WIDE * 8,
            moved=(len(sources) + 2) << 20,
        )(place, asked, *sources)

    def to_plane(rows):
        return lax.all_to_all(
            rows, "shard", split_axis=0, concat_axis=0, axis_index_groups=PLANES, tiled=True
        )

    far1 = to_plane(pick((0, -1, 1), (*state, *up[1], *down[1])))
    far2 = to_plane(pick((-2, 2), (*up[2], *down[2])))
    far3 = to_plane(pick((-3, 3), (*up[3], *down[3])))
    last = call(
        pick_last_kernel,
        shape(PLANE, SLOTS, 2 * WIDE),
        in_specs=[scalar()] + [whole()] * 5,
        flops=SLOTS * PLANE * ROWS * WIDE * 8,
        moved=3 << 20,
    )(place, asked, *low, *high)
    far4 = to_plane(last)

    acc = call(
        gather_kernel,
        shape(FINE, 2 * WIDE),
        grid=(6,),
        in_specs=[
            pl.BlockSpec((FINE, 128), lambda i: (0, 0)),
            pl.BlockSpec((ROWS, HALF), lambda i: (0, jnp.minimum(i, 2))),
            pl.BlockSpec((ROWS, HALF), lambda i: (0, jnp.maximum(i - 3, 0))),
            pl.BlockSpec((PLANE, 48, HALF), lambda i: (0, 0, i)),
            pl.BlockSpec((PLANE, 32, HALF), lambda i: (0, 0, i)),
        ],
        out_specs=pl.BlockSpec((FINE, HALF), lambda i: (0, i)),
        flops=FINE * 864 * 1536 * 4,
        moved=8 << 20,
    )(codes, *state, far1, far2)

    def lanes(block, state):
        n = len(block) - 1
        return pl.BlockSpec(
            block, lambda j: (0,) * n + (lax.div(j, 2) * 6 + state * 2 + lax.rem(j, 2),)
        )

    return call(
        final_kernel,
        (shape(FINE, 2 * FEATS),) * 3,
        grid=(4,),
        in_specs=[pl.BlockSpec((FINE, 128), lambda j: (0, 0))]
        + [lanes((FINE, 128), s) for s in range(3)]
        + [lanes((PLANE, 32, 128), s) for s in range(3)]
        + [lanes((PLANE, 16, 128), s) for s in range(3)],
        out_specs=(pl.BlockSpec((FINE, 256), lambda j: (0, j)),) * 3,
        flops=FINE * 384 * 1536 * 4,
        moved=12 << 20,
    )(codes, acc, acc, acc, far3, far3, far3, far4, far4, far4)


def solution(mesh):
    placed = (
        P("dp", "shard", None),
        P("shard", "dp"),
        P("shard", "dp"),
        P("shard", "dp"),
        P("shard", None),
        P("shard"),
    )
    return jax.shard_map(
        on_device,
        mesh=mesh,
        in_specs=placed,
        out_specs=(P("shard", "dp"), P("shard", "dp"), P("shard", "dp")),
        check_vma=False,
    )
```

time: 292 us -> 210 us (0.72)
  the two profiles are of different devices: /device:TPU:2 before, /device:TPU:96 now
where the time goes in v1:
time: 210 us; the launch traced here: 209 us
  waiting for transfers between devices  105 us (50%)
  starting transfers between devices  49.4 us (24%)
  Pallas kernels  27.5 us (13%)
  blocking collectives  14.4 us (7%)
  local copies, waits for them, and re-layouts  12.1 us (6%)
    ppermute x6, waiting for transfers between devices, on_device(): nu.append(lax.ppermute(up[-1][half], 'shard', UP))  61 us
    all_to_all x4, starting transfers between devices, to_plane(): lax.all_to_all(rows, 'shard', split_axis=0, concat_axis=0, axis_index_gro...  27.1 us
    all_to_all x4, waiting for transfers between devices, to_plane(): lax.all_to_all(rows, 'shard', split_axis=0, concat_axis=0, axis_index_gro...  15.7 us
    all_to_all x1, blocking collectives, on_device(): lax.all_to_all(wanted, 'shard', split_axis=0, concat_axis=0, axis_index_g...  14.4 us
    unnamed x51, local copies, waits for them, and re-layouts  11.9 us
    ppermute x6, waiting for transfers between devices, on_device(): nd.append(lax.ppermute(down[-1][half], 'shard', DOWN))  9.88 us
    ppermute x6, starting transfers between devices, on_device(): nu.append(lax.ppermute(up[-1][half], 'shard', UP))  8.9 us
    pallas_call x3, Pallas kernels, pick(): call(lambda *refs: pick_kernel(offsets, *refs), shape(PLANE, rows, 2 * WI...  7.24 us
  transfers between devices with their start and end apart: 24, of which 16 were waited for; matrix products, arithmetic and copies ran while one was open for 0% of the time, Pallas kernels for 8%

profile of v1, /device:TPU:96, one launch (start us, length us, event | category | flops | bytes accessed | tf_op | source)
XLA Modules:
  0.0 209.2 jit_solution(6874000602775651525)
XLA Ops:
  0.6 0.1 pad_add_fusion.place.refs_0_
  0.7 1.2 copy-done.1
  1.9 0.6 shard_map.86
  2.5 0.0 copy-start.7
  2.5 0.1 collective-permute-start
  2.6 0.5 collective-permute-start.2
  3.1 1.3 collective-permute-done.refs_2_
  4.4 0.6 shard_map.87
  5.0 1.7 collective-permute-start.1
  6.7 0.6 shard_map.89
  7.3 0.5 collective-permute-start.3
  7.8 5.8 %collective-permute-done.1.refs_3_ = f32[224,256]{1,0:T(8,128)S(1)} collective-permute-done((f32[224,256]{1,0:T(8,128)S(1)}, f32[224,256]{1,0:T(8,128)S(1)}, u32[]{:S(2)}, u32[]{:S(2)}) %collective-permute-start.1) | collective-permute-done | bytes 229408 | tf_op jit(solution)/shard_map/ppermute | solution.py:239
  13.6 0.8 shard_map.88.refs_2_.near0
  14.4 3.2 %collective-permute-start.4 = (f32[224,768]{1,0:T(8,128)S(1)}, f32[224,768]{1,0:T(8,128)}, u32[]{:S(2)}, u32[]{:S(2)}) collective-permute-start(f32[224,768]{1,0:T(8,128)S(1)} %shard_map.88.refs_2_.near0), channel_id=1, source_target_pairs={{0,8},{1,9},{2,10},{3,11},{4,12},{5,13},{6,14},{7,15},{8,16},{9,17... | collective-permute-start | bytes 2064392 | tf_op jit(solution)/shard_map/ppermute | solution.py:279
  17.6 0.1 collective-permute-done.3.refs_3_
  17.7 0.8 shard_map.90.refs_3_.near1
  18.4 3.2 %collective-permute-start.5 = (f32[224,768]{1,0:T(8,128)S(1)}, f32[224,768]{1,0:T(8,128)S(1)}, u32[]{:S(2)}, u32[]{:S(2)}) collective-permute-start(f32[224,768]{1,0:T(8,128)S(1)} %shard_map.90.refs_3_.near1), channel_id=1, source_target_pairs={{0,8},{1,9},{2,10},{3,11},{4,12},{5,13},{6,14},{7,15},{8,16},{9,17... | collective-permute-start | bytes 2064392 | tf_op jit(solution)/shard_map/ppermute | solution.py:279
  21.7 0.1 copy.10.dev
  21.8 0.1 copy.11.col
  22.0 1.1 shard_map.85
  23.1 14.4 %all_to_all.25.refs_1_.asked = s32[8,8,128]{2,1,0:T(8,128)S(1)} all-to-all(s32[8,8,128]{2,1,0:T(8,128)S(1)} %get-tuple-element.10), channel_id=1, replica_groups={{0,1,2,3,4,5,6,7},{8,9,10,11,12,13,14,15},{16,17,18,19,20,21,22,23},{24..., dimensions={0} | all-to-all | bytes 65536 | tf_op jit(solution)/shard_map/all_to_all | solution.py:271
  37.6 8.1 %collective-permute-done.5.refs_5_ = f32[224,768]{1,0:T(8,128)S(1)} collective-permute-done((f32[224,768]{1,0:T(8,128)S(1)}, f32[224,768]{1,0:T(8,128)S(1)}, u32[]{:S(2)}, u32[]{:S(2)}) %collective-permute-start.5) | collective-permute-done | bytes 688160 | tf_op jit(solution)/shard_map/ppermute | solution.py:279
  45.7 8.4 %collective-permute-done.7.refs_7_ = f32[224,768]{1,0:T(8,128)} collective-permute-done((f32[224,768]{1,0:T(8,128)S(1)}, f32[224,768]{1,0:T(8,128)}, u32[]{:S(2)}, u32[]{:S(2)}) %collective-permute-start.7) | collective-permute-done | bytes 688160 | tf_op jit(solution)/shard_map/ppermute | solution.py:280
  54.1 3.8 %shard_map.91 = f32[8,48,1536]{2,1,0:T(8,128)} custom-call(s32[2]{0:T(128)S(1)} %pad_add_fusion.place.refs_0_, s32[8,8,128]{2,1,0:T(8,128)S(1)} %all_to_all.25.refs_1_.asked, f32[224,768]{1,0:T(8,128)S(1)} %shard_map.88.refs_2_.near0, f32[224,768]{1,0:T(8,128)S(1)} %shard_map.90.refs_3_.near1, f32[224,768]{1,0:T(8,128)} %collective-permute-done.4.refs_4_, ...), custom_call_target="tpu_custom_call" | custom-call | flops 528482304 | bytes 8388608 | tf_op jit(solution)/shard_map/pallas_call | solution.py:289
  57.9 6.9 %all-to-all-start.1 = ((f32[8,48,1536]{2,1,0:T(8,128)}), f32[8,48,1536]{2,1,0:T(8,128)S(1)}, u32[]{:S(2)}, u32[]{:S(2)}) async-start(f32[8,48,1536]{2,1,0:T(8,128)} %shard_map.91), calls=%async_computation.1 | async-start | bytes 4718592 | tf_op jit(solution)/shard_map/all_to_all | solution.py:298
  64.8 0.8 collective-permute-start.9
  65.6 1.3 collective-permute-start.10
  66.9 1.9 collective-permute-start.11
  68.8 14.5 %collective-permute-done.8.refs_2_ = f32[224,768]{1,0:T(8,128)S(1)} collective-permute-done((f32[224,768]{1,0:T(8,128)}, f32[224,768]{1,0:T(8,128)S(1)}, u32[]{:S(2)}, u32[]{:S(2)}) %collective-permute-start.8) | collective-permute-done | bytes 688160 | tf_op jit(solution)/shard_map/ppermute | solution.py:279
  83.4 11.5 %collective-permute-done.9.refs_3_ = f32[224,768]{1,0:T(8,128)S(1)} collective-permute-done((f32[224,768]{1,0:T(8,128)}, f32[224,768]{1,0:T(8,128)S(1)}, u32[]{:S(2)}, u32[]{:S(2)}) %collective-permute-start.9) | collective-permute-done | bytes 688160 | tf_op jit(solution)/shard_map/ppermute | solution.py:279
  94.9 1.5 collective-permute-done.11.refs_5_
  96.4 0.9 copy-done.18
  97.3 2.3 %shard_map.92 = f32[8,32,1536]{2,1,0:T(8,128)} custom-call(s32[2]{0:T(128)S(1)} %pad_add_fusion.place.refs_0_, s32[8,8,128]{2,1,0:T(8,128)S(1)} %all_to_all.25.refs_1_.asked, f32[224,768]{1,0:T(8,128)S(1)} %collective-permute-done.8.refs_2_, f32[224,768]{1,0:T(8,128)S(1)} %collective-permute-done.9.refs_3_, f32[224,768]{1,0:T(8,128)S(1)} %collective-permute-done.10.refs_4_, ...), custom_call_target="tpu_custom_call" | custom-call | flops 352321536 | bytes 6291456 | tf_op jit(solution)/shard_map/pallas_call | solution.py:289
  99.6 0.8 copy-done.22
  100.4 6.9 %all-to-all-start.2 = ((f32[8,32,1536]{2,1,0:T(8,128)}), f32[8,32,1536]{2,1,0:T(8,128)}, u32[]{:S(2)}, u32[]{:S(2)}) async-start(f32[8,32,1536]{2,1,0:T(8,128)} %shard_map.92), calls=%async_computation.2 | async-start | bytes 3145728 | tf_op jit(solution)/shard_map/all_to_all | solution.py:298
  107.4 1.1 collective-permute-start.12
  108.5 0.5 collective-permute-start.13
  109.0 1.5 collective-permute-start.14
  110.5 0.9 collective-permute-start.15
  111.4 14.5 %collective-permute-done.12.refs_2_ = f32[224,768]{1,0:T(8,128)S(1)} collective-permute-done((f32[224,768]{1,0:T(8,128)}, f32[224,768]{1,0:T(8,128)S(1)}, u32[]{:S(2)}, u32[]{:S(2)}) %collective-permute-start.12) | collective-permute-done | bytes 688160 | tf_op jit(solution)/shard_map/ppermute | solution.py:279
  126.0 2.4 %collective-permute-start.16 = (f32[112,768]{1,0:T(8,128)S(1)}, f32[112,768]{1,0:T(8,128)S(1)}, u32[]{:S(2)}, u32[]{:S(2)}) collective-permute-start(f32[112,768]{1,0:T(8,128)S(1)} %slice.16), channel_id=1, source_target_pairs={{0,8},{1,9},{2,10},{3,11},{4,12},{5,13},{6,14},{7,15},{8,16},{9,17... | collective-permute-start | bytes 1032200 | tf_op jit(solution)/shard_map/ppermute | solution.py:284
  128.4 12.3 %collective-permute-done.13.refs_3_ = f32[224,768]{1,0:T(8,128)S(1)} collective-permute-done((f32[224,768]{1,0:T(8,128)}, f32[224,768]{1,0:T(8,128)S(1)}, u32[]{:S(2)}, u32[]{:S(2)}) %collective-permute-start.13) | collective-permute-done | bytes 688160 | tf_op jit(solution)/shard_map/ppermute | solution.py:279
  140.7 2.4 %collective-permute-start.17 = (f32[112,768]{1,0:T(8,128)S(1)}, f32[112,768]{1,0:T(8,128)S(1)}, u32[]{:S(2)}, u32[]{:S(2)}) collective-permute-start(f32[112,768]{1,0:T(8,128)S(1)} %slice.17), channel_id=1, source_target_pairs={{0,8},{1,9},{2,10},{3,11},{4,12},{5,13},{6,14},{7,15},{8,16},{9,17... | collective-permute-start | bytes 1032200 | tf_op jit(solution)/shard_map/ppermute | solution.py:284
  143.2 0.1 collective-permute-start.18
  143.3 0.7 copy-done.14
  144.0 0.2 copy-done.16
  144.3 2.4 %collective-permute-done.16.low0 = f32[112,768]{1,0:T(8,128)S(1)} collective-permute-done((f32[112,768]{1,0:T(8,128)S(1)}, f32[112,768]{1,0:T(8,128)S(1)}, u32[]{:S(2)}, u32[]{:S(2)}) %collective-permute-start.16) | collective-permute-done | bytes 344096 | tf_op jit(solution)/shard_map/ppermute | solution.py:284
  146.7 3.7 %collective-permute-done.17.low1 = f32[112,768]{1,0:T(8,128)S(1)} collective-permute-done((f32[112,768]{1,0:T(8,128)S(1)}, f32[112,768]{1,0:T(8,128)S(1)}, u32[]{:S(2)}, u32[]{:S(2)}) %collective-permute-start.17) | collective-permute-done | bytes 344096 | tf_op jit(solution)/shard_map/ppermute | solution.py:284
  150.4 1.3 collective-permute-done.18.high0
  151.7 3.7 %collective-permute-done.19.high1 = f32[112,768]{1,0:T(8,128)S(1)} collective-permute-done((f32[112,768]{1,0:T(8,128)S(1)}, f32[112,768]{1,0:T(8,128)S(1)}, u32[]{:S(2)}, u32[]{:S(2)}) %collective-permute-start.19) | collective-permute-done | bytes 344096 | tf_op jit(solution)/shard_map/ppermute | solution.py:285
  155.4 1.8 shard_map.95
  157.2 7.2 %all-to-all-start.4 = ((f32[8,16,1536]{2,1,0:T(8,128)}), f32[8,16,1536]{2,1,0:T(8,128)S(1)}, u32[]{:S(2)}, u32[]{:S(2)}) async-start(f32[8,16,1536]{2,1,0:T(8,128)} %shard_map.95), calls=%async_computation.4 | async-start | bytes 1572864 | tf_op jit(solution)/shard_map/all_to_all | solution.py:298
  164.5 1.1 copy-done.15
  165.6 1.1 copy-done.17
  166.7 1.2 shard_map.94
  167.8 1.1 copy-done.2
  169.0 10.4 %all-to-all-done.4.refs_6_.refs_7_.refs_8_ = f32[8,16,1536]{2,1,0:T(8,128)S(1)} async-done(((f32[8,16,1536]{2,1,0:T(8,128)}), f32[8,16,1536]{2,1,0:T(8,128)S(1)}, u32[]{:S(2)}, u32[]{:S(2)}) %all-to-all-start.4) | async-done | bytes 786464 | tf_op jit(solution)/shard_map/all_to_all | solution.py:298
  179.4 6.1 %all-to-all-start.3 = ((f32[8,32,1536]{2,1,0:T(8,128)}), f32[8,32,1536]{2,1,0:T(8,128)S(1)}, u32[]{:S(2)}, u32[]{:S(2)}) async-start(f32[8,32,1536]{2,1,0:T(8,128)} %copy-done.2), calls=%async_computation.3 | async-start | bytes 3145728 | tf_op jit(solution)/shard_map/all_to_all | solution.py:298
  185.5 1.1 copy-done.4
  186.5 1.7 copy-done.6
  188.2 7.0 %shard_map.93.refs_0_.refs_1_.refs_2_ = f32[448,1536]{1,0:T(8,128)} custom-call(s32[448,128]{1,0:T(8,128)S(1)} %get-tuple-element.7.codes, f32[224,768]{1,0:T(8,128)S(1)} %shard_map.88.refs_2_.near0, f32[224,768]{1,0:T(8,128)S(1)} %copy-done.4, f32[8,48,1536]{2,1,0:T(8,128)S(1)} %copy-done.6, f32[8,32,1536]{2,1,0:T(8,128)} %all-to-all-done.2.far2), custom_call_target="tpu_custom_call" | custom-call | flops 2378170368 | bytes 8388608 | tf_op jit(solution)/shard_map/pallas_call | solution.py:314
  195.2 5.3 %all-to-all-done.3.refs_3_.refs_4_.refs_5_ = f32[8,32,1536]{2,1,0:T(8,128)S(1)} async-done(((f32[8,32,1536]{2,1,0:T(8,128)}), f32[8,32,1536]{2,1,0:T(8,128)S(1)}, u32[]{:S(2)}, u32[]{:S(2)}) %all-to-all-start.3) | async-done | bytes 1572896 | tf_op jit(solution)/shard_map/all_to_all | solution.py:298
  200.4 1.8 copy-done
  202.2 7.0 %shard_map.96 = (f32[448,1024]{1,0:T(8,128)}, f32[448,1024]{1,0:T(8,128)}, f32[448,1024]{1,0:T(8,128)}) custom-call(s32[448,128]{1,0:T(8,128)S(1)} %get-tuple-element.7.codes, f32[448,1536]{1,0:T(8,128)S(1)} %copy-done, f32[448,1536]{1,0:T(8,128)S(1)} %copy-done, f32[448,1536]{1,0:T(8,128)S(1)} %copy-done, ...), custom_call_target="tpu_custom_call" | custom-call | flops 1056964608 | bytes 12582912 | tf_op jit(solution)/shard_map/pallas_call | solution.py:336
  (54 shorter events, 0.2 us)
Async XLA Ops:
  0.7 1.2 copy-start.1
  2.5 11.1 %copy-start.7 = (f32[224,512]{1,0:T(8,128)S(1)}, f32[224,512]{1,0:T(8,128)}, u32[]{:S(2)}) copy-start(f32[224,512]{1,0:T(8,128)} %refs_4_.3) | copy-start | bytes 1376260
  2.5 11.0 %copy-start.8 = (f32[224,512]{1,0:T(8,128)S(1)}, f32[224,512]{1,0:T(8,128)}, u32[]{:S(2)}) copy-start(f32[224,512]{1,0:T(8,128)} %refs_5_.3) | copy-start | bytes 1376260
  2.5 11.0 %copy-start.9 = (f32[224,512]{1,0:T(8,128)S(1)}, f32[224,512]{1,0:T(8,128)}, u32[]{:S(2)}) copy-start(f32[224,512]{1,0:T(8,128)} %refs_6_.3) | copy-start | bytes 1376260
  2.5 1.9 collective-permute-start
  2.6 4.0 %collective-permute-start.2 = (f32[224,512]{1,0:T(8,128)S(1)}, f32[224,512]{1,0:T(8,128)S(1)}, u32[]{:S(2)}, u32[]{:S(2)}) collective-permute-start(f32[224,512]{1,0:T(8,128)S(1)} %get-tuple-element.9), channel_id=1, source_target_pairs={{0,64},{64,0},{128,192},{192,128},{1,65},{65,1},{129,193},{193,129... | collective-permute-start | bytes 1376264 | tf_op jit(solution)/shard_map/ppermute | solution.py:223
  5.0 8.5 %collective-permute-start.1 = (f32[224,256]{1,0:T(8,128)S(1)}, f32[224,256]{1,0:T(8,128)S(1)}, u32[]{:S(2)}, u32[]{:S(2)}) collective-permute-start(f32[224,256]{1,0:T(8,128)S(1)} %shard_map.87), channel_id=1, source_target_pairs={{0,128},{128,0},{64,192},{192,64},{1,129},{129,1},{65,193},{193,65... | collective-permute-start | bytes 688136 | tf_op jit(solution)/shard_map/ppermute | solution.py:239
  7.3 10.4 %collective-permute-start.3 = (f32[224,256]{1,0:T(8,128)S(1)}, f32[224,256]{1,0:T(8,128)S(1)}, u32[]{:S(2)}, u32[]{:S(2)}) collective-permute-start(f32[224,256]{1,0:T(8,128)S(1)} %shard_map.89), channel_id=1, source_target_pairs={{0,128},{128,0},{64,192},{192,64},{1,129},{129,1},{65,193},{193,65... | collective-permute-start | bytes 688136 | tf_op jit(solution)/shard_map/ppermute | solution.py:239
  14.3 7.3 %copy-start.23 = (s32[448,1]{0,1:T(1,128)S(1)}, s32[448,1]{0,1:T(1,128)}, u32[]{:S(2)}) copy-start(s32[448,1]{0,1:T(1,128)} %param.10) | copy-start | bytes 5380
  14.3 7.5 %copy-start.24 = (s32[448]{0:T(512)S(1)}, s32[448]{0:T(512)}, u32[]{:S(2)}) copy-start(s32[448]{0:T(512)} %param.11) | copy-start | bytes 5380
  14.4 23.2 %collective-permute-start.4 = (f32[224,768]{1,0:T(8,128)S(1)}, f32[224,768]{1,0:T(8,128)}, u32[]{:S(2)}, u32[]{:S(2)}) collective-permute-start(f32[224,768]{1,0:T(8,128)S(1)} %shard_map.88.refs_2_.near0), channel_id=1, source_target_pairs={{0,8},{1,9},{2,10},{3,11},{4,12},{5,13},{6,14},{7,15},{8,16},{9,17... | collective-permute-start | bytes 2064392 | tf_op jit(solution)/shard_map/ppermute | solution.py:279
  18.4 39.4 %copy-start.3 = (f32[224,768]{1,0:T(8,128)}, f32[224,768]{1,0:T(8,128)S(1)}, u32[]{:S(2)}) copy-start(f32[224,768]{1,0:T(8,128)S(1)} %shard_map.90.refs_3_.near1) | copy-start | bytes 2064388
  18.4 27.2 %collective-permute-start.5 = (f32[224,768]{1,0:T(8,128)S(1)}, f32[224,768]{1,0:T(8,128)S(1)}, u32[]{:S(2)}, u32[]{:S(2)}) collective-permute-start(f32[224,768]{1,0:T(8,128)S(1)} %shard_map.90.refs_3_.near1), channel_id=1, source_target_pairs={{0,8},{1,9},{2,10},{3,11},{4,12},{5,13},{6,14},{7,15},{8,16},{9,17... | collective-permute-start | bytes 2064392 | tf_op jit(solution)/shard_map/ppermute | solution.py:279
  21.7 24.0 %collective-permute-start.6 = (f32[224,768]{1,0:T(8,128)S(1)}, f32[224,768]{1,0:T(8,128)}, u32[]{:S(2)}, u32[]{:S(2)}) collective-permute-start(f32[224,768]{1,0:T(8,128)S(1)} %shard_map.88.refs_2_.near0), channel_id=1, source_target_pairs={{8,0},{9,1},{10,2},{11,3},{12,4},{13,5},{14,6},{15,7},{16,8},{17,9... | collective-permute-start | bytes 2064392 | tf_op jit(solution)/shard_map/ppermute | solution.py:280
  21.7 32.4 %collective-permute-start.7 = (f32[224,768]{1,0:T(8,128)S(1)}, f32[224,768]{1,0:T(8,128)}, u32[]{:S(2)}, u32[]{:S(2)}) collective-permute-start(f32[224,768]{1,0:T(8,128)S(1)} %shard_map.90.refs_3_.near1), channel_id=1, source_target_pairs={{8,0},{9,1},{10,2},{11,3},{12,4},{13,5},{14,6},{15,7},{16,8},{17,9... | collective-permute-start | bytes 2064392 | tf_op jit(solution)/shard_map/ppermute | solution.py:280
  45.7 12.2 %copy-start.21 = (f32[224,768]{1,0:T(8,128)}, f32[224,768]{1,0:T(8,128)S(1)}, u32[]{:S(2)}) copy-start(f32[224,768]{1,0:T(8,128)S(1)} %collective-permute-done.5.refs_5_) | copy-start | bytes 2064388
  57.9 42.6 %all-to-all-start.1 = ((f32[8,48,1536]{2,1,0:T(8,128)}), f32[8,48,1536]{2,1,0:T(8,128)S(1)}, u32[]{:S(2)}, u32[]{:S(2)}) async-start(f32[8,48,1536]{2,1,0:T(8,128)} %shard_map.91), calls=%async_computation.1 | async-start | bytes 4718592 | tf_op jit(solution)/shard_map/all_to_all | solution.py:298
  64.8 18.6 %collective-permute-start.8 = (f32[224,768]{1,0:T(8,128)}, f32[224,768]{1,0:T(8,128)S(1)}, u32[]{:S(2)}, u32[]{:S(2)}) collective-permute-start(f32[224,768]{1,0:T(8,128)} %collective-permute-done.4.refs_4_), channel_id=1, source_target_pairs={{0,8},{1,9},{2,10},{3,11},{4,12},{5,13},{6,14},{7,15},{8,16},{9,17... | collective-permute-start | bytes 2064392 | tf_op jit(solution)/shard_map/ppermute | solution.py:279
  64.8 30.1 %collective-permute-start.9 = (f32[224,768]{1,0:T(8,128)}, f32[224,768]{1,0:T(8,128)S(1)}, u32[]{:S(2)}, u32[]{:S(2)}) collective-permute-start(f32[224,768]{1,0:T(8,128)} %copy-done.21), channel_id=1, source_target_pairs={{0,8},{1,9},{2,10},{3,11},{4,12},{5,13},{6,14},{7,15},{8,16},{9,17... | collective-permute-start | bytes 2064392 | tf_op jit(solution)/shard_map/ppermute | solution.py:279
  65.6 29.3 %collective-permute-start.10 = (f32[224,768]{1,0:T(8,128)}, f32[224,768]{1,0:T(8,128)S(1)}, u32[]{:S(2)}, u32[]{:S(2)}) collective-permute-start(f32[224,768]{1,0:T(8,128)} %collective-permute-done.6.refs_6_), channel_id=1, source_target_pairs={{8,0},{9,1},{10,2},{11,3},{12,4},{13,5},{14,6},{15,7},{16,8},{17,9... | collective-permute-start | bytes 2064392 | tf_op jit(solution)/shard_map/ppermute | solution.py:280
  66.9 29.5 %collective-permute-start.11 = (f32[224,768]{1,0:T(8,128)}, f32[224,768]{1,0:T(8,128)S(1)}, u32[]{:S(2)}, u32[]{:S(2)}) collective-permute-start(f32[224,768]{1,0:T(8,128)} %collective-permute-done.7.refs_7_), channel_id=1, source_target_pairs={{8,0},{9,1},{10,2},{11,3},{12,4},{13,5},{14,6},{15,7},{16,8},{17,9... | collective-permute-start | bytes 2064392 | tf_op jit(solution)/shard_map/ppermute | solution.py:280
  94.9 1.5 copy-start.20
  94.9 1.5 copy-start.19
  96.4 0.9 copy-start.18
  99.6 0.8 copy-start.22
  100.4 25.5 %copy-start.5 = (f32[8,48,1536]{2,1,0:T(8,128)}, f32[8,48,1536]{2,1,0:T(8,128)S(1)}, u32[]{:S(2)}) copy-start(f32[8,48,1536]{2,1,0:T(8,128)S(1)} %all-to-all-done.1.far1) | copy-start | bytes 7077892
  100.4 56.8 %all-to-all-start.2 = ((f32[8,32,1536]{2,1,0:T(8,128)}), f32[8,32,1536]{2,1,0:T(8,128)}, u32[]{:S(2)}, u32[]{:S(2)}) async-start(f32[8,32,1536]{2,1,0:T(8,128)} %shard_map.92), calls=%async_computation.2 | async-start | bytes 3145728 | tf_op jit(solution)/shard_map/all_to_all | solution.py:298
  107.4 18.6 %collective-permute-start.12 = (f32[224,768]{1,0:T(8,128)}, f32[224,768]{1,0:T(8,128)S(1)}, u32[]{:S(2)}, u32[]{:S(2)}) collective-permute-start(f32[224,768]{1,0:T(8,128)} %copy-done.22), channel_id=1, source_target_pairs={{0,8},{1,9},{2,10},{3,11},{4,12},{5,13},{6,14},{7,15},{8,16},{9,17... | collective-permute-start | bytes 2064392 | tf_op jit(solution)/shard_map/ppermute | solution.py:279
  108.5 32.2 %collective-permute-start.13 = (f32[224,768]{1,0:T(8,128)}, f32[224,768]{1,0:T(8,128)S(1)}, u32[]{:S(2)}, u32[]{:S(2)}) collective-permute-start(f32[224,768]{1,0:T(8,128)} %copy-done.20), channel_id=1, source_target_pairs={{0,8},{1,9},{2,10},{3,11},{4,12},{5,13},{6,14},{7,15},{8,16},{9,17... | collective-permute-start | bytes 2064392 | tf_op jit(solution)/shard_map/ppermute | solution.py:279
  109.0 34.1 %collective-permute-start.14 = (f32[224,768]{1,0:T(8,128)}, f32[224,768]{1,0:T(8,128)S(1)}, u32[]{:S(2)}, u32[]{:S(2)}) collective-permute-start(f32[224,768]{1,0:T(8,128)} %copy-done.19), channel_id=1, source_target_pairs={{8,0},{9,1},{10,2},{11,3},{12,4},{13,5},{14,6},{15,7},{16,8},{17,9... | collective-permute-start | bytes 2064392 | tf_op jit(solution)/shard_map/ppermute | solution.py:280
  110.5 32.7 %collective-permute-start.15 = (f32[224,768]{1,0:T(8,128)}, f32[224,768]{1,0:T(8,128)S(1)}, u32[]{:S(2)}, u32[]{:S(2)}) collective-permute-start(f32[224,768]{1,0:T(8,128)} %copy-done.18), channel_id=1, source_target_pairs={{8,0},{9,1},{10,2},{11,3},{12,4},{13,5},{14,6},{15,7},{16,8},{17,9... | collective-permute-start | bytes 2064392 | tf_op jit(solution)/shard_map/ppermute | solution.py:280
  125.9 2.5 %copy-start.10 = (f32[224,768]{1,0:T(8,128)}, f32[224,768]{1,0:T(8,128)S(1)}, u32[]{:S(2)}) copy-start(f32[224,768]{1,0:T(8,128)S(1)} %collective-permute-done.12.refs_2_) | copy-start | bytes 2064388
  126.0 20.7 %collective-permute-start.16 = (f32[112,768]{1,0:T(8,128)S(1)}, f32[112,768]{1,0:T(8,128)S(1)}, u32[]{:S(2)}, u32[]{:S(2)}) collective-permute-start(f32[112,768]{1,0:T(8,128)S(1)} %slice.16), channel_id=1, source_target_pairs={{0,8},{1,9},{2,10},{3,11},{4,12},{5,13},{6,14},{7,15},{8,16},{9,17... | collective-permute-start | bytes 1032200 | tf_op jit(solution)/shard_map/ppermute | solution.py:284
  140.7 2.6 %copy-start.12 = (f32[224,768]{1,0:T(8,128)}, f32[224,768]{1,0:T(8,128)S(1)}, u32[]{:S(2)}) copy-start(f32[224,768]{1,0:T(8,128)S(1)} %collective-permute-done.13.refs_3_) | copy-start | bytes 2064388
  140.7 9.7 %collective-permute-start.17 = (f32[112,768]{1,0:T(8,128)S(1)}, f32[112,768]{1,0:T(8,128)S(1)}, u32[]{:S(2)}, u32[]{:S(2)}) collective-permute-start(f32[112,768]{1,0:T(8,128)S(1)} %slice.17), channel_id=1, source_target_pairs={{0,8},{1,9},{2,10},{3,11},{4,12},{5,13},{6,14},{7,15},{8,16},{9,17... | collective-permute-start | bytes 1032200 | tf_op jit(solution)/shard_map/ppermute | solution.py:284
  143.1 0.9 copy-start.14
  143.2 8.5 %collective-permute-start.18 = (f32[112,768]{1,0:T(8,128)S(1)}, f32[112,768]{1,0:T(8,128)S(1)}, u32[]{:S(2)}, u32[]{:S(2)}) collective-permute-start(f32[112,768]{1,0:T(8,128)S(1)} %slice.18), channel_id=1, source_target_pairs={{8,0},{9,1},{10,2},{11,3},{12,4},{13,5},{14,6},{15,7},{16,8},{17,9... | collective-permute-start | bytes 1032200 | tf_op jit(solution)/shard_map/ppermute | solution.py:285
  143.3 1.0 copy-start.16
  144.0 20.4 %copy-start.11 = (f32[224,768]{1,0:T(8,128)S(1)}, f32[224,768]{1,0:T(8,128)}, u32[]{:S(2)}) copy-start(f32[224,768]{1,0:T(8,128)} %copy-done.10) | copy-start | bytes 2064388
  144.0 20.4 %copy-start.13 = (f32[224,768]{1,0:T(8,128)S(1)}, f32[224,768]{1,0:T(8,128)}, u32[]{:S(2)}) copy-start(f32[224,768]{1,0:T(8,128)} %copy-done.12) | copy-start | bytes 2064388
  144.0 11.4 %collective-permute-start.19 = (f32[112,768]{1,0:T(8,128)S(1)}, f32[112,768]{1,0:T(8,128)S(1)}, u32[]{:S(2)}, u32[]{:S(2)}) collective-permute-start(f32[112,768]{1,0:T(8,128)S(1)} %slice.19), channel_id=1, source_target_pairs={{8,0},{9,1},{10,2},{11,3},{12,4},{13,5},{14,6},{15,7},{16,8},{17,9... | collective-permute-start | bytes 1032200 | tf_op jit(solution)/shard_map/ppermute | solution.py:285
  157.2 22.1 %all-to-all-start.4 = ((f32[8,16,1536]{2,1,0:T(8,128)}), f32[8,16,1536]{2,1,0:T(8,128)S(1)}, u32[]{:S(2)}, u32[]{:S(2)}) async-start(f32[8,16,1536]{2,1,0:T(8,128)} %shard_map.95), calls=%async_computation.4 | async-start | bytes 1572864 | tf_op jit(solution)/shard_map/all_to_all | solution.py:298
  164.5 1.1 copy-start.15
  165.6 1.1 copy-start.17
  167.8 1.1 copy-start.2
  179.4 21.1 %all-to-all-start.3 = ((f32[8,32,1536]{2,1,0:T(8,128)}), f32[8,32,1536]{2,1,0:T(8,128)S(1)}, u32[]{:S(2)}, u32[]{:S(2)}) async-start(f32[8,32,1536]{2,1,0:T(8,128)} %copy-done.2), calls=%async_computation.3 | async-start | bytes 3145728 | tf_op jit(solution)/shard_map/all_to_all | solution.py:298
  185.4 1.1 copy-start.4
  186.5 1.7 copy-start.6
  200.4 1.8 copy-start

commit v2 on v1

--- a/solution.py
+++ b/solution.py
@@ -45,6 +45,10 @@
     )
 
 
+def shape(*dims, dtype=F32):
+    return jax.ShapeDtypeStruct(dims, dtype)
+
+
 def whole():
     return pl.BlockSpec(memory_space=pltpu.VMEM)
 
@@ -115,17 +119,21 @@
     away = (source_z - plane + RING) & (RING - 1)
     none = -1
 
-    def place_in(rows, offsets):
+    def place_in(offsets):
         at = jnp.full((FINE, 1), none, I32)
         for k, offset in offsets:
-            at = jnp.where(away == k, source_xy * rows + offset + slot, at)
+            at = jnp.where(away == k, source_xy * 64 + offset + slot, at)
         return at
 
     groups = (
-        place_in(48, ((0, 0), (7, 16), (1, 32))),
-        place_in(32, ((6, 0), (2, 16))),
-        place_in(32, ((5, 0), (3, 16))),
-        place_in(16, ((4, 0),)),
+        place_in(((0, 0), (7, 32), (1, 48))),
+        place_in(((6, 32), (2, 48))),
+        place_in(((5, 32), (3, 48))),
+        place_in(((4, 32),)),
+        place_in(((0, 16),)),
+        place_in(((7, 0), (1, 16))),
+        place_in(((6, 0), (2, 16))),
+        place_in(((5, 0), (3, 16), (4, 48))),
     )
     lane = lax.broadcasted_iota(I32, (FINE, 128), 1)
     out = jnp.full((FINE, 128), none, I32)
@@ -148,53 +156,85 @@
     return split_dot(chosen, values, ((0,), (0,)))
 
 
-def pick_kernel(offsets, place, asked, *refs):
+def pick_kernel(parts, place, asked, *refs):
     out = refs[-1]
     plane = lax.div(place[0], PLANE)
-    for n, offset in enumerate(offsets):
-        from_plane = (plane + offset + RING) & (RING - 1)
-        for half in range(2):
-            got = pick_from(asked, from_plane, refs[2 * n + half][...])
-            for d in range(PLANE):
-                out[d, n * SLOTS : (n + 1) * SLOTS, half * WIDE : (half + 1) * WIDE] = got[
-                    d * SLOTS : (d + 1) * SLOTS
-                ]
-
-
-def pick_last_kernel(place, asked, low0, low1, high0, high1, out):
-    plane = lax.div(place[0], PLANE)
-    from_plane = (plane + 4) & (RING - 1)
-    for half, (low, high) in enumerate(((low0, high0), (low1, high1))):
-        got = pick_from(asked, from_plane, jnp.concatenate([low[...], high[...]], axis=0))
+    n = 0
+    for away, row, pieces in parts:
+        values = refs[n][...]
+        if pieces == 2:
+            values = jnp.concatenate([values, refs[n + 1][...]], axis=0)
+        n += pieces
+        got = pick_from(asked, (plane + away + RING) & (RING - 1), values)
         for d in range(PLANE):
-            out[d, :, half * WIDE : (half + 1) * WIDE] = got[d * SLOTS : (d + 1) * SLOTS]
-
-
-def far_dot(codes, group, far):
+            out[d, row : row + SLOTS, :] = got[d * SLOTS : (d + 1) * SLOTS]
+
+
+def held_kernel(*refs):
+    pass
+
+
+def hold(arrays, *until):
+    n = len(arrays)
+    return pl.pallas_call(
+        held_kernel,
+        out_shape=tuple(shape(*a.shape) for a in arrays),
+        in_specs=[pl.BlockSpec(memory_space=pl.ANY)] * (n + len(until)),
+        out_specs=(pl.BlockSpec(memory_space=pl.ANY),) * n,
+        input_output_aliases={i: i for i in range(n)},
+        cost_estimate=pl.CostEstimate(flops=0, bytes_accessed=1 << 20, transcendentals=0),
+    )(*arrays, *until)
+
+
+def token_kernel(*refs):
+    refs[-1][...] = jnp.zeros((8, 128), F32)
+
+
+def token(arrays):
+    return call(
+        token_kernel,
+        shape(8, 128),
+        in_specs=[pl.BlockSpec(memory_space=pl.ANY)] * len(arrays),
+        flops=10**10,
+    )(*arrays)
+
+
+def far_dot(at, far):
     rows = far.shape[0] * far.shape[1]
-    at = codes[:, group : group + 1]
     chosen = jnp.where(
         lax.broadcasted_iota(I32, (FINE, rows), 1) == at, 1.0 - own_share, 0.0
     ).astype(BF16)
-    return split_dot(chosen, far[...].reshape(rows, far.shape[2]))
-
-
-def gather_kernel(codes, near0, near1, far1, far2, out):
-    i = pl.program_id(0)
-    near = jnp.where(i < 3, near0[...], near1[...])
+    return split_dot(chosen, far.reshape(rows, far.shape[2]))
+
+
+def far_part(codes, lane, far, low, high):
+    at = codes[:, lane : lane + 1]
+    xy, row = at >> 6, at & 63
+    here = (at >= 0) & (row >= low) & (row < high)
+    at = jnp.where(here, xy * (high - low) + row - low, -1)
+    return far_dot(at, far[:, low:high, :])
+
+
+def gather_kernel(parts, codes, near, far1, far2, far3, out):
     own = lax.broadcasted_iota(I32, (FINE, ROWS), 0) >> 1
     chosen = jnp.where(
         lax.broadcasted_iota(I32, (FINE, ROWS), 1) == own, own_share, 0.0
     ).astype(BF16)
-    out[...] = split_dot(chosen, near) + far_dot(codes, 0, far1) + far_dot(codes, 1, far2)
+    total = split_dot(chosen, near[...])
+    far = (far1, far2, far3)
+    for lane, exchange, low, high in parts:
+        total = total + far_part(codes, lane, far[exchange], low, high)
+    out[...] = total
 
 
 def final_kernel(codes, *refs):
     lane = lax.broadcasted_iota(I32, (FINE, 128), 1) >> 1
+    first_half = pl.program_id(0) < 2
+    at = jnp.where(first_half, codes[:, 3:4], codes[:, 7:8])
     for state in range(3):
-        acc, far3, far4 = refs[state], refs[3 + state], refs[6 + state]
-        out = refs[9 + state]
-        mixed = acc[...] + far_dot(codes, 2, far3) + far_dot(codes, 3, far4)
+        acc0, acc1, far, out = (refs[3 * k + state] for k in range(4))
+        acc = jnp.where(first_half, acc0[...], acc1[...])
+        mixed = acc + far_dot(at, far[...])
         out[:, 0:128] = jnp.take_along_axis(mixed, lane, axis=1)
         out[:, 128:256] = jnp.take_along_axis(mixed, lane + 64, axis=1)
 
@@ -204,10 +244,6 @@
 DOWN = [(b, a) for a, b in UP]
 CORE = [(0, 1), (1, 0), (2, 3), (3, 2)]
 NEXT_Y = [(0, 2), (2, 0), (1, 3), (3, 1)]
-
-
-def shape(*dims, dtype=F32):
-    return jax.ShapeDtypeStruct(dims, dtype)
 
 
 def on_device(grad_parts, weight, first, second, partner_device, partner_column):
@@ -272,79 +308,87 @@
         wanted, "shard", split_axis=0, concat_axis=0, axis_index_groups=PLANES, tiled=True
     )
 
-    up, down = [state], [state]
-    for step in range(3):
-        nu, nd = [], []
-        for half in range(2):
-            nu.append(lax.ppermute(up[-1][half], "shard", UP))
-            nd.append(lax.ppermute(down[-1][half], "shard", DOWN))
-        up.append(nu)
-        down.append(nd)
-    middle = ROWS // 2
-    low = [lax.ppermute(up[3][half][:middle], "shard", UP) for half in range(2)]
-    high = [lax.ppermute(down[3][half][middle:], "shard", DOWN) for half in range(2)]
-
-    def pick(offsets, sources):
-        rows = SLOTS * len(offsets)
+    def pick(parts, sources, after=()):
         return call(
-            lambda *refs: pick_kernel(offsets, *refs),
-            shape(PLANE, rows, 2 * WIDE),
-            in_specs=[scalar()] + [whole()] * (1 + len(sources)),
-            flops=rows * PLANE * ROWS * WIDE * 8,
+            lambda *refs: pick_kernel(parts, *refs),
+            shape(PLANE, SLOTS * len(parts), WIDE),
+            in_specs=[scalar()]
+            + [whole()] * (1 + len(sources))
+            + [pl.BlockSpec(memory_space=pl.ANY)] * len(after),
+            flops=len(parts) * SLOTS * PLANE * ROWS * WIDE * 4,
             moved=(len(sources) + 2) << 20,
-        )(place, asked, *sources)
+        )(place, asked, *sources, *after)
 
     def to_plane(rows):
         return lax.all_to_all(
             rows, "shard", split_axis=0, concat_axis=0, axis_index_groups=PLANES, tiled=True
         )
 
-    far1 = to_plane(pick((0, -1, 1), (*state, *up[1], *down[1])))
-    far2 = to_plane(pick((-2, 2), (*up[2], *down[2])))
-    far3 = to_plane(pick((-3, 3), (*up[3], *down[3])))
-    last = call(
-        pick_last_kernel,
-        shape(PLANE, SLOTS, 2 * WIDE),
-        in_specs=[scalar()] + [whole()] * 5,
-        flops=SLOTS * PLANE * ROWS * WIDE * 8,
-        moved=3 << 20,
-    )(place, asked, *low, *high)
-    far4 = to_plane(last)
-
-    acc = call(
-        gather_kernel,
-        shape(FINE, 2 * WIDE),
-        grid=(6,),
-        in_specs=[
-            pl.BlockSpec((FINE, 128), lambda i: (0, 0)),
-            pl.BlockSpec((ROWS, HALF), lambda i: (0, jnp.minimum(i, 2))),
-            pl.BlockSpec((ROWS, HALF), lambda i: (0, jnp.maximum(i - 3, 0))),
-            pl.BlockSpec((PLANE, 48, HALF), lambda i: (0, 0, i)),
-            pl.BlockSpec((PLANE, 32, HALF), lambda i: (0, 0, i)),
-        ],
-        out_specs=pl.BlockSpec((FINE, HALF), lambda i: (0, i)),
-        flops=FINE * 864 * 1536 * 4,
-        moved=8 << 20,
-    )(codes, *state, far1, far2)
-
-    def lanes(block, state):
-        n = len(block) - 1
-        return pl.BlockSpec(
-            block, lambda j: (0,) * n + (lax.div(j, 2) * 6 + state * 2 + lax.rem(j, 2),)
+    def around(pair):
+        return lax.ppermute(pair[0], "shard", UP), lax.ppermute(pair[1], "shard", DOWN)
+
+    one = [around((x, x)) for x in state]
+    one[0] = hold(one[0], asked)
+    two = [around(pair) for pair in one]
+    three = [around(pair) for pair in two]
+    far1 = to_plane(pick(((0, 0, 1), (0, 16, 1), (-1, 32, 1), (1, 48, 1)), (*state, *one[0])))
+    far2 = to_plane(
+        pick(((-1, 0, 1), (1, 16, 1), (-2, 32, 1), (2, 48, 1)), (*one[1], *two[0]), (far1, token(two[0])))
+    )
+    far3 = to_plane(
+        pick(((-2, 0, 1), (2, 16, 1), (-3, 32, 1), (3, 48, 1)), (*two[1], *three[0]), (far2, token(three[0])))
+    )
+    middle = ROWS // 2
+    four = [around((pair[0][:middle], pair[1][middle:])) for pair in three]
+    rows = pick(
+        ((-3, 0, 1), (3, 16, 1), (4, 32, 2), (4, 48, 2)), (*three[1], *four[0], *four[1]), (far3, token(four[1]))
+    )
+    far4 = to_plane(rows)
+
+    acc = []
+    for half, parts in enumerate(
+        (
+            ((0, 0, 0, 16), (0, 0, 32, 64), (1, 1, 32, 64), (2, 2, 32, 64)),
+            ((4, 0, 16, 32), (5, 1, 0, 32), (6, 2, 0, 32)),
         )
+    ):
+        acc.append(
+            call(
+                lambda *refs, parts=parts: gather_kernel(parts, *refs),
+                shape(FINE, WIDE),
+                grid=(3,),
+                in_specs=[
+                    pl.BlockSpec((FINE, 128), lambda i: (0, 0)),
+                    pl.BlockSpec((ROWS, HALF), lambda i: (0, i)),
+                ]
+                + [pl.BlockSpec((PLANE, 64, HALF), lambda i: (0, 0, i))] * 3,
+                out_specs=pl.BlockSpec((FINE, HALF), lambda i: (0, i)),
+                flops=FINE * 1120 * WIDE * 4,
+                moved=8 << 20,
+            )(codes, state[half], far1, far2, far3)
+        )
+
+    def acc_block(half, state):
+        def index(j):
+            k = jnp.minimum(j, 1) if half == 0 else jnp.maximum(j - 2, 0)
+            return 0, state * 2 + k
+
+        return pl.BlockSpec((FINE, 128), index)
+
+    def far_block(state):
+        return pl.BlockSpec((PLANE, 64, 128), lambda j: (0, 0, state * 2 + lax.rem(j, 2)))
 
     return call(
         final_kernel,
         (shape(FINE, 2 * FEATS),) * 3,
         grid=(4,),
         in_specs=[pl.BlockSpec((FINE, 128), lambda j: (0, 0))]
-        + [lanes((FINE, 128), s) for s in range(3)]
-        + [lanes((PLANE, 32, 128), s) for s in range(3)]
-        + [lanes((PLANE, 16, 128), s) for s in range(3)],
+        + [acc_block(half, s) for half in range(2) for s in range(3)]
+        + [far_block(s) for s in range(3)],
         out_specs=(pl.BlockSpec((FINE, 256), lambda j: (0, j)),) * 3,
-        flops=FINE * 384 * 1536 * 4,
+        flops=FINE * 512 * 1536 * 4,
         moved=12 << 20,
-    )(codes, acc, acc, acc, far3, far3, far3, far4, far4, far4)
+    )(codes, acc[0], acc[0], acc[0], acc[1], acc[1], acc[1], far4, far4, far4)
 
 
 def solution(mesh):

time: 210 us -> 180 us (0.86)
  the two profiles are of different devices: /device:TPU:96 before, /device:TPU:2 now
where the time goes in v2:
time: 180 us; the launch traced here: 176 us
  starting transfers between devices  66.4 us (37%)
  waiting for transfers between devices  46.3 us (26%)
  Pallas kernels  31.9 us (18%)
  local copies, waits for them, and re-layouts  30.8 us (17%)
    ppermute x8, waiting for transfers between devices, around(): lax.ppermute(pair[0], 'shard', UP)  30.2 us
    all_to_all x4, starting transfers between devices, to_plane(): lax.all_to_all(rows, 'shard', split_axis=0, concat_axis=0, axis_index_gro...  26.9 us
    ppermute x8, starting transfers between devices, around(): lax.ppermute(pair[1], 'shard', DOWN)  26.8 us
    unnamed x81, local copies, waits for them, and re-layouts  25.9 us
    pallas_call x4, Pallas kernels, pick(): call(lambda *refs: pick_kernel(parts, *refs), shape(PLANE, SLOTS * len(pa...  10.6 us
    pallas_call x2, Pallas kernels, on_device(): call(lambda *refs, parts=parts: gather_kernel(parts, *refs), shape(FINE,...  8 us
    all_to_all x4, waiting for transfers between devices, to_plane(): lax.all_to_all(rows, 'shard', split_axis=0, concat_axis=0, axis_index_gro...  7.8 us
    all_to_all x1, starting transfers between devices, on_device(): lax.all_to_all(wanted, 'shard', split_axis=0, concat_axis=0, axis_index_g...  7.17 us
  transfers between devices with their start and end apart: 25, of which 13 were waited for; matrix products, arithmetic and copies ran while one was open for 3% of the time, Pallas kernels for 12%

profile of v2, /device:TPU:2, one launch (start us, length us, event | category | flops | bytes accessed | tf_op | source)
XLA Modules:
  0.0 176.5 jit_solution(829730711562353058)
XLA Ops:
  0.7 1.2 copy-done.3
  2.6 1.8 %collective-permute-done.refs_2_ = f32[224,512]{1,0:T(8,128)S(1)} collective-permute-done((f32[224,512]{1,0:T(8,128)S(1)}, f32[224,512]{1,0:T(8,128)S(1)}, u32[]{:S(2)}, u32[]{:S(2)}) %collective-permute-start) | collective-permute-done | bytes 458784 | tf_op jit(solution)/shard_map/ppermute | solution.py:259
  5.0 1.7 collective-permute-start.1
  6.7 6.1 %collective-permute-done.1.refs_3_ = f32[224,256]{1,0:T(8,128)S(1)} collective-permute-done((f32[224,256]{1,0:T(8,128)S(1)}, f32[224,256]{1,0:T(8,128)S(1)}, u32[]{:S(2)}, u32[]{:S(2)}) %collective-permute-start.1) | collective-permute-done | bytes 229408 | tf_op jit(solution)/shard_map/ppermute | solution.py:275
  12.7 0.8 shard_map.88.refs_2_.refs_1_
  13.5 2.0 %collective-permute-start.4 = (f32[224,768]{1,0:T(8,128)S(1)}, f32[224,768]{1,0:T(8,128)S(1)}, u32[]{:S(2)}, u32[]{:S(2)}) collective-permute-start(f32[224,768]{1,0:T(8,128)S(1)} %shard_map.88.refs_2_.refs_1_), channel_id=1, source_target_pairs={{0,8},{1,9},{2,10},{3,11},{4,12},{5,13},{6,14},{7,15},{8,16},{9,17... | collective-permute-start | bytes 2064392 | tf_op jit(solution)/shard_map/ppermute | solution.py:328
  15.5 4.0 %collective-permute-start.5 = (f32[224,768]{1,0:T(8,128)S(1)}, f32[224,768]{1,0:T(8,128)}, u32[]{:S(2)}, u32[]{:S(2)}) collective-permute-start(f32[224,768]{1,0:T(8,128)S(1)} %shard_map.88.refs_2_.refs_1_), channel_id=1, source_target_pairs={{8,0},{9,1},{10,2},{11,3},{12,4},{13,5},{14,6},{15,7},{16,8},{17,9... | collective-permute-start | bytes 2064392 | tf_op jit(solution)/shard_map/ppermute | solution.py:328
  19.6 1.3 shard_map.89
  20.8 1.6 collective-permute-start.3
  22.6 0.8 copy.13.col
  23.4 0.9 copy-done.29
  24.3 1.9 %shard_map.85 = (s32[8,8,128]{2,1,0:T(8,128)}, s32[448,128]{1,0:T(8,128)S(1)}) custom-call(s32[2]{0:T(128)S(1)} %pad_add_fusion.place.refs_0_, s32[448,1]{1,0:T(8,128)S(1)} %copy.12.dev, s32[1,448]{1,0:T(1,128)S(1)} %bitcast.10, s32[448,1]{1,0:T(8,128)S(1)} %copy-done.29), custom_call_target="tpu_custom_call" | custom-call | bytes 1048576 | tf_op jit(solution)/shard_map/pallas_call | solution.py:296
  26.2 7.2 %all-to-all-start = ((s32[8,8,128]{2,1,0:T(8,128)}), s32[8,8,128]{2,1,0:T(8,128)S(1)}, u32[]{:S(2)}, u32[]{:S(2)}) async-start(s32[8,8,128]{2,1,0:T(8,128)} %get-tuple-element.11), calls=%async_computation | async-start | bytes 65536 | tf_op jit(solution)/shard_map/all_to_all | solution.py:307
  33.4 1.0 copy-done.19
  34.5 1.0 copy-done.21
  35.5 1.0 copy-done.23
  36.5 1.0 copy-done.25
  37.5 1.2 shard_map.90.refs_3_.refs_1_
  38.8 3.2 %collective-permute-start.7 = (f32[224,768]{1,0:T(8,128)S(1)}, f32[224,768]{1,0:T(8,128)}, u32[]{:S(2)}, u32[]{:S(2)}) collective-permute-start(f32[224,768]{1,0:T(8,128)S(1)} %shard_map.90.refs_3_.refs_1_), channel_id=1, source_target_pairs={{8,0},{9,1},{10,2},{11,3},{12,4},{13,5},{14,6},{15,7},{16,8},{17,9... | collective-permute-start | bytes 2064392 | tf_op jit(solution)/shard_map/ppermute | solution.py:328
  42.9 3.2 %collective-permute-start.9 = (f32[224,768]{1,0:T(8,128)}, f32[224,768]{1,0:T(8,128)}, u32[]{:S(2)}, u32[]{:S(2)}) collective-permute-start(f32[224,768]{1,0:T(8,128)} %get-tuple-element.14.refs_5_), channel_id=1, source_target_pairs={{8,0},{9,1},{10,2},{11,3},{12,4},{13,5},{14,6},{15,7},{16,8},{17,9... | collective-permute-start | bytes 2064392 | tf_op jit(solution)/shard_map/ppermute | solution.py:328
  46.1 1.1 copy-done.17
  47.2 0.8 copy-done.27
  48.0 2.9 %shard_map.92 = f32[8,64,768]{2,1,0:T(8,128)} custom-call(s32[2]{0:T(128)S(1)} %pad_add_fusion.place.refs_0_, s32[8,8,128]{2,1,0:T(8,128)S(1)} %copy-done.27, f32[224,768]{1,0:T(8,128)S(1)} %shard_map.88.refs_2_.refs_1_, f32[224,768]{1,0:T(8,128)S(1)} %shard_map.90.refs_3_.refs_1_, f32[224,768]{1,0:T(8,128)S(1)} %copy-done.17, ...), custom_call_target="tpu_custom_call" | custom-call | flops 352321536 | bytes 6291456 | tf_op jit(solution)/shard_map/pallas_call | solution.py:312
  50.9 7.2 %all-to-all-start.1 = ((f32[8,64,768]{2,1,0:T(8,128)}), f32[8,64,768]{2,1,0:T(8,128)S(1)}, u32[]{:S(2)}, u32[]{:S(2)}) async-start(f32[8,64,768]{2,1,0:T(8,128)} %shard_map.92), calls=%async_computation.1 | async-start | bytes 3145728 | tf_op jit(solution)/shard_map/all_to_all | solution.py:323
  58.5 3.2 %collective-permute-start.11 = (f32[224,768]{1,0:T(8,128)}, f32[224,768]{1,0:T(8,128)}, u32[]{:S(2)}, u32[]{:S(2)}) collective-permute-start(f32[224,768]{1,0:T(8,128)} %collective-permute-done.7.refs_3_), channel_id=1, source_target_pairs={{8,0},{9,1},{10,2},{11,3},{12,4},{13,5},{14,6},{15,7},{16,8},{17,9... | collective-permute-start | bytes 2064392 | tf_op jit(solution)/shard_map/ppermute | solution.py:328
  61.7 11.5 %collective-permute-done.8.refs_0_.refs_4_ = f32[224,768]{1,0:T(8,128)} collective-permute-done((f32[224,768]{1,0:T(8,128)}, f32[224,768]{1,0:T(8,128)}, u32[]{:S(2)}, u32[]{:S(2)}) %collective-permute-start.8) | collective-permute-done | bytes 688160 | tf_op jit(solution)/shard_map/ppermute | solution.py:328
  73.2 3.2 %collective-permute-start.13 = (f32[224,768]{1,0:T(8,128)}, f32[224,768]{1,0:T(8,128)}, u32[]{:S(2)}, u32[]{:S(2)}) collective-permute-start(f32[224,768]{1,0:T(8,128)} %collective-permute-done.9.refs_1_.refs_5_), channel_id=1, source_target_pairs={{8,0},{9,1},{10,2},{11,3},{12,4},{13,5},{14,6},{15,7},{16,8},{17,9... | collective-permute-start | bytes 2064392 | tf_op jit(solution)/shard_map/ppermute | solution.py:328
  76.5 2.4 %shard_map.94 = f32[8,64,768]{2,1,0:T(8,128)S(1)} custom-call(s32[2]{0:T(128)S(1)} %pad_add_fusion.place.refs_0_, s32[8,8,128]{2,1,0:T(8,128)S(1)} %copy-done.28, f32[224,768]{1,0:T(8,128)} %collective-permute-done.6.refs_2_, f32[224,768]{1,0:T(8,128)} %collective-permute-done.7.refs_3_, f32[224,768]{1,0:T(8,128)} %collective-permute-done.8.refs_0_.refs_4_, ...), custom_call_target="tpu_custom_call" | custom-call | flops 352321536 | bytes 6291456 | tf_op jit(solution)/shard_map/pallas_call | solution.py:312
  78.8 1.1 copy-done.10
  80.0 7.2 %all-to-all-start.2 = ((f32[8,64,768]{2,1,0:T(8,128)}), f32[8,64,768]{2,1,0:T(8,128)S(1)}, u32[]{:S(2)}, u32[]{:S(2)}) async-start(f32[8,64,768]{2,1,0:T(8,128)} %copy-done.10), calls=%async_computation.2 | async-start | bytes 3145728 | tf_op jit(solution)/shard_map/all_to_all | solution.py:323
  87.2 0.8 collective-permute-done.10.refs_2_
  88.0 3.2 %collective-permute-start.15 = (f32[224,768]{1,0:T(8,128)}, f32[224,768]{1,0:T(8,128)}, u32[]{:S(2)}, u32[]{:S(2)}) collective-permute-start(f32[224,768]{1,0:T(8,128)} %collective-permute-done.11.refs_3_), channel_id=1, source_target_pairs={{8,0},{9,1},{10,2},{11,3},{12,4},{13,5},{14,6},{15,7},{16,8},{17,9... | collective-permute-start | bytes 2064392 | tf_op jit(solution)/shard_map/ppermute | solution.py:328
  91.2 11.5 %collective-permute-done.12.refs_0_.refs_4_ = f32[224,768]{1,0:T(8,128)} collective-permute-done((f32[224,768]{1,0:T(8,128)}, f32[224,768]{1,0:T(8,128)}, u32[]{:S(2)}, u32[]{:S(2)}) %collective-permute-start.12) | collective-permute-done | bytes 688160 | tf_op jit(solution)/shard_map/ppermute | solution.py:328
  102.7 1.8 %all-to-all-done.2.refs_6_.refs_3_ = f32[8,64,768]{2,1,0:T(8,128)S(1)} async-done(((f32[8,64,768]{2,1,0:T(8,128)}), f32[8,64,768]{2,1,0:T(8,128)S(1)}, u32[]{:S(2)}, u32[]{:S(2)}) %all-to-all-start.2) | async-done | bytes 1572896 | tf_op jit(solution)/shard_map/all_to_all | solution.py:323
  104.5 2.9 %shard_map.96 = f32[8,64,768]{2,1,0:T(8,128)S(1)} custom-call(s32[2]{0:T(128)S(1)} %pad_add_fusion.place.refs_0_, s32[8,8,128]{2,1,0:T(8,128)S(1)} %copy-done.28, f32[224,768]{1,0:T(8,128)} %collective-permute-done.10.refs_2_, f32[224,768]{1,0:T(8,128)} %collective-permute-done.11.refs_3_, f32[224,768]{1,0:T(8,128)} %collective-permute-done.12.refs_0_.refs_4_, ...), custom_call_target="tpu_custom_call" | custom-call | flops 352321536 | bytes 6291456 | tf_op jit(solution)/shard_map/pallas_call | solution.py:312
  107.4 1.1 copy-done.9
  108.6 5.8 %all-to-all-start.3 = ((f32[8,64,768]{2,1,0:T(8,128)}), f32[8,64,768]{2,1,0:T(8,128)S(1)}, u32[]{:S(2)}, u32[]{:S(2)}) async-start(f32[8,64,768]{2,1,0:T(8,128)} %copy-done.9), calls=%async_computation.3 | async-start | bytes 3145728 | tf_op jit(solution)/shard_map/all_to_all | solution.py:323
  114.6 1.0 slice.18
  115.7 1.0 slice.19
  116.7 3.3 %collective-permute-start.19 = (f32[112,768]{1,0:T(8,128)S(1)}, f32[112,768]{1,0:T(8,128)S(1)}, u32[]{:S(2)}, u32[]{:S(2)}) collective-permute-start(f32[112,768]{1,0:T(8,128)S(1)} %slice.19), channel_id=1, source_target_pairs={{8,0},{9,1},{10,2},{11,3},{12,4},{13,5},{14,6},{15,7},{16,8},{17,9... | collective-permute-start | bytes 1032200 | tf_op jit(solution)/shard_map/ppermute | solution.py:328
  120.0 1.0 slice.16
  121.1 1.0 slice.17
  122.1 3.3 %collective-permute-start.17 = (f32[112,768]{1,0:T(8,128)S(1)}, f32[112,768]{1,0:T(8,128)S(1)}, u32[]{:S(2)}, u32[]{:S(2)}) collective-permute-start(f32[112,768]{1,0:T(8,128)S(1)} %slice.17), channel_id=1, source_target_pairs={{8,0},{9,1},{10,2},{11,3},{12,4},{13,5},{14,6},{15,7},{16,8},{17,9... | collective-permute-start | bytes 1032200 | tf_op jit(solution)/shard_map/ppermute | solution.py:328
  125.4 2.0 %collective-permute-done.18.refs_0_.refs_6_ = f32[112,768]{1,0:T(8,128)S(1)} collective-permute-done((f32[112,768]{1,0:T(8,128)S(1)}, f32[112,768]{1,0:T(8,128)S(1)}, u32[]{:S(2)}, u32[]{:S(2)}) %collective-permute-start.18) | collective-permute-done | bytes 344096 | tf_op jit(solution)/shard_map/ppermute | solution.py:328
  128.4 3.8 %collective-permute-done.16.refs_4_ = f32[112,768]{1,0:T(8,128)S(1)} collective-permute-done((f32[112,768]{1,0:T(8,128)S(1)}, f32[112,768]{1,0:T(8,128)S(1)}, u32[]{:S(2)}, u32[]{:S(2)}) %collective-permute-start.16) | collective-permute-done | bytes 344096 | tf_op jit(solution)/shard_map/ppermute | solution.py:328
  132.3 0.7 copy-done.34
  133.0 0.7 copy-done.36
  134.2 1.0 copy-done.31
  135.2 1.0 copy-done.33
  136.2 1.0 copy-done.35
  137.2 1.0 copy-done.37
  138.2 2.5 %shard_map.100 = f32[8,64,768]{2,1,0:T(8,128)S(1)} custom-call(s32[2]{0:T(128)S(1)} %pad_add_fusion.place.refs_0_, s32[8,8,128]{2,1,0:T(8,128)S(1)} %copy-done.28, f32[224,768]{1,0:T(8,128)} %collective-permute-done.14.refs_2_, f32[224,768]{1,0:T(8,128)} %collective-permute-done.15.refs_3_, f32[112,768]{1,0:T(8,128)S(1)} %copy-done.35, ...), custom_call_target="tpu_custom_call" | custom-call | flops 352321536 | bytes 8388608 | tf_op jit(solution)/shard_map/pallas_call | solution.py:312
  140.7 1.1 copy-done.11
  141.8 6.7 %all-to-all-start.4 = ((f32[8,64,768]{2,1,0:T(8,128)}), f32[8,64,768]{2,1,0:T(8,128)S(1)}, u32[]{:S(2)}, u32[]{:S(2)}) async-start(f32[8,64,768]{2,1,0:T(8,128)} %copy-done.11), calls=%async_computation.4 | async-start | bytes 3145728 | tf_op jit(solution)/shard_map/all_to_all | solution.py:323
  148.5 1.4 copy-done.1
  149.9 1.1 copy-done.15
  151.0 3.9 %shard_map.98.refs_3_.refs_4_.refs_5_ = f32[448,768]{1,0:T(8,128)S(1)} custom-call(s32[448,128]{1,0:T(8,128)S(1)} %get-tuple-element.9.refs_0_.codes, f32[224,768]{1,0:T(8,128)S(1)} %copy-done.15, f32[8,64,768]{2,1,0:T(8,128)S(1)} %all-to-all-done.1.refs_6_.refs_2_, f32[8,64,768]{2,1,0:T(8,128)S(1)} %copy-done.1, f32[8,64,768]{2,1,0:T(8,128)} %copy-done.2), custom_call_target="tpu_custom_call" | custom-call | flops 1541406720 | bytes 8388608 | tf_op jit(solution)/shard_map/pallas_call | solution.py:356
  155.0 1.1 copy-done.5
  156.1 4.1 %shard_map.97.refs_0_.refs_1_.refs_2_ = f32[448,768]{1,0:T(8,128)S(1)} custom-call(s32[448,128]{1,0:T(8,128)S(1)} %get-tuple-element.9.refs_0_.codes, f32[224,768]{1,0:T(8,128)S(1)} %copy-done.13, f32[8,64,768]{2,1,0:T(8,128)S(1)} %all-to-all-done.1.refs_6_.refs_2_, f32[8,64,768]{2,1,0:T(8,128)S(1)} %copy-done.1, f32[8,64,768]{2,1,0:T(8,128)} %copy-done.2), custom_call_target="tpu_custom_call" | custom-call | flops 1541406720 | bytes 8388608 | tf_op jit(solution)/shard_map/pallas_call | solution.py:356
  160.2 1.1 copy-done.7
  161.3 5.5 %all-to-all-done.4.refs_6_.refs_7_.refs_8_ = f32[8,64,768]{2,1,0:T(8,128)S(1)} async-done(((f32[8,64,768]{2,1,0:T(8,128)}), f32[8,64,768]{2,1,0:T(8,128)S(1)}, u32[]{:S(2)}, u32[]{:S(2)}) %all-to-all-start.4) | async-done | bytes 1572896 | tf_op jit(solution)/shard_map/all_to_all | solution.py:323
  166.8 1.3 copy-done.6
  168.1 1.3 copy-done.8
  169.5 7.0 %shard_map.101 = (f32[448,1024]{1,0:T(8,128)}, f32[448,1024]{1,0:T(8,128)}, f32[448,1024]{1,0:T(8,128)}) custom-call(s32[448,128]{1,0:T(8,128)S(1)} %get-tuple-element.9.refs_0_.codes, f32[448,768]{1,0:T(8,128)S(1)} %copy-done.8, f32[448,768]{1,0:T(8,128)S(1)} %copy-done.8, f32[448,768]{1,0:T(8,128)S(1)} %copy-done.8, f32[448,768]{1,0:T(8,128)S(1)} %copy-done.6, ...), custom_call_target="tpu_custom_call" | custom-call | flops 1409286144 | bytes 12582912 | tf_op jit(solution)/shard_map/pallas_call | solution.py:381
  (90 shorter events, 5.0 us)
Async XLA Ops:
  0.7 1.2 copy-start.3
  1.9 10.8 %copy-start.20 = (f32[224,512]{1,0:T(8,128)S(1)}, f32[224,512]{1,0:T(8,128)}, u32[]{:S(2)}) copy-start(f32[224,512]{1,0:T(8,128)} %refs_4_.3) | copy-start | bytes 1376260
  1.9 10.8 %copy-start.22 = (f32[224,512]{1,0:T(8,128)S(1)}, f32[224,512]{1,0:T(8,128)}, u32[]{:S(2)}) copy-start(f32[224,512]{1,0:T(8,128)} %refs_5_.3) | copy-start | bytes 1376260
  1.9 10.8 %copy-start.24 = (f32[224,512]{1,0:T(8,128)S(1)}, f32[224,512]{1,0:T(8,128)}, u32[]{:S(2)}) copy-start(f32[224,512]{1,0:T(8,128)} %refs_6_.3) | copy-start | bytes 1376260
  2.5 1.9 %collective-permute-start = (f32[224,512]{1,0:T(8,128)S(1)}, f32[224,512]{1,0:T(8,128)S(1)}, u32[]{:S(2)}, u32[]{:S(2)}) collective-permute-start(f32[224,512]{1,0:T(8,128)S(1)} %get-tuple-element.10), channel_id=1, source_target_pairs={{0,64},{64,0},{128,192},{192,128},{1,65},{65,1},{129,193},{193,129... | collective-permute-start | bytes 1376264 | tf_op jit(solution)/shard_map/ppermute | solution.py:259
  5.0 7.7 %collective-permute-start.1 = (f32[224,256]{1,0:T(8,128)S(1)}, f32[224,256]{1,0:T(8,128)S(1)}, u32[]{:S(2)}, u32[]{:S(2)}) collective-permute-start(f32[224,256]{1,0:T(8,128)S(1)} %shard_map.87), channel_id=1, source_target_pairs={{0,128},{128,0},{64,192},{192,64},{1,129},{129,1},{65,193},{193,65... | collective-permute-start | bytes 688136 | tf_op jit(solution)/shard_map/ppermute | solution.py:275
  6.7 12.9 %collective-permute-start.2 = (f32[224,512]{1,0:T(8,128)S(1)}, f32[224,512]{1,0:T(8,128)S(1)}, u32[]{:S(2)}, u32[]{:S(2)}) collective-permute-start(f32[224,512]{1,0:T(8,128)S(1)} %get-tuple-element.12), channel_id=1, source_target_pairs={{0,64},{64,0},{128,192},{192,128},{1,65},{65,1},{129,193},{193,129... | collective-permute-start | bytes 1376264 | tf_op jit(solution)/shard_map/ppermute | solution.py:259
  13.5 32.6 %copy-start.12 = (f32[224,768]{1,0:T(8,128)}, f32[224,768]{1,0:T(8,128)S(1)}, u32[]{:S(2)}) copy-start(f32[224,768]{1,0:T(8,128)S(1)} %shard_map.88.refs_2_.refs_1_) | copy-start | bytes 2064388
  13.5 8.9 %copy-start.38 = (s32[448,1]{0,1:T(1,128)S(1)}, s32[448,1]{0,1:T(1,128)}, u32[]{:S(2)}) copy-start(s32[448,1]{0,1:T(1,128)} %param.10) | copy-start | bytes 5380
  13.5 9.0 %copy-start.39 = (s32[448]{0:T(512)S(1)}, s32[448]{0:T(512)}, u32[]{:S(2)}) copy-start(s32[448]{0:T(512)} %param.11) | copy-start | bytes 5380
  13.5 19.9 %copy-start.4 = (bf16[1,224,2048]{2,1,0:T(8,128)(2,1)S(1)}, bf16[1,224,2048]{2,1,0:T(8,128)(2,1)}, u32[]{:S(2)}) copy-start(bf16[1,224,2048]{2,1,0:T(8,128)(2,1)} %param.6) | copy-start | bytes 2752516
  13.5 28.5 %collective-permute-start.4 = (f32[224,768]{1,0:T(8,128)S(1)}, f32[224,768]{1,0:T(8,128)S(1)}, u32[]{:S(2)}, u32[]{:S(2)}) collective-permute-start(f32[224,768]{1,0:T(8,128)S(1)} %shard_map.88.refs_2_.refs_1_), channel_id=1, source_target_pairs={{0,8},{1,9},{2,10},{3,11},{4,12},{5,13},{6,14},{7,15},{8,16},{9,17... | collective-permute-start | bytes 2064392 | tf_op jit(solution)/shard_map/ppermute | solution.py:328
  15.5 26.5 %collective-permute-start.5 = (f32[224,768]{1,0:T(8,128)S(1)}, f32[224,768]{1,0:T(8,128)}, u32[]{:S(2)}, u32[]{:S(2)}) collective-permute-start(f32[224,768]{1,0:T(8,128)S(1)} %shard_map.88.refs_2_.refs_1_), channel_id=1, source_target_pairs={{8,0},{9,1},{10,2},{11,3},{12,4},{13,5},{14,6},{15,7},{16,8},{17,9... | collective-permute-start | bytes 2064392 | tf_op jit(solution)/shard_map/ppermute | solution.py:328
  19.6 13.8 %copy-start.18 = (f32[224,512]{1,0:T(8,128)}, f32[224,512]{1,0:T(8,128)S(1)}, u32[]{:S(2)}) copy-start(f32[224,512]{1,0:T(8,128)S(1)} %collective-permute-done.2.refs_2_) | copy-start | bytes 1376260
  20.8 12.6 %collective-permute-start.3 = (f32[224,256]{1,0:T(8,128)}, f32[224,256]{1,0:T(8,128)}, u32[]{:S(2)}, u32[]{:S(2)}) collective-permute-start(f32[224,256]{1,0:T(8,128)} %shard_map.89), channel_id=1, source_target_pairs={{0,128},{128,0},{64,192},{192,64},{1,129},{129,1},{65,193},{193,65... | collective-permute-start | bytes 688136 | tf_op jit(solution)/shard_map/ppermute | solution.py:275
  23.4 0.9 copy-start.29
  26.2 15.8 %all-to-all-start = ((s32[8,8,128]{2,1,0:T(8,128)}), s32[8,8,128]{2,1,0:T(8,128)S(1)}, u32[]{:S(2)}, u32[]{:S(2)}) async-start(s32[8,8,128]{2,1,0:T(8,128)} %get-tuple-element.11), calls=%async_computation | async-start | bytes 65536 | tf_op jit(solution)/shard_map/all_to_all | solution.py:307
  33.4 1.0 copy-start.19
  34.5 1.0 copy-start.21
  35.5 1.0 copy-start.23
  36.5 1.0 copy-start.25
  38.7 12.2 %copy-start.14 = (f32[224,768]{1,0:T(8,128)}, f32[224,768]{1,0:T(8,128)S(1)}, u32[]{:S(2)}) copy-start(f32[224,768]{1,0:T(8,128)S(1)} %shard_map.90.refs_3_.refs_1_) | copy-start | bytes 2064388
  38.7 19.8 %collective-permute-start.6 = (f32[224,768]{1,0:T(8,128)S(1)}, f32[224,768]{1,0:T(8,128)}, u32[]{:S(2)}, u32[]{:S(2)}) collective-permute-start(f32[224,768]{1,0:T(8,128)S(1)} %shard_map.90.refs_3_.refs_1_), channel_id=1, source_target_pairs={{0,8},{1,9},{2,10},{3,11},{4,12},{5,13},{6,14},{7,15},{8,16},{9,17... | collective-permute-start | bytes 2064392 | tf_op jit(solution)/shard_map/ppermute | solution.py:328
  38.8 19.7 %collective-permute-start.7 = (f32[224,768]{1,0:T(8,128)S(1)}, f32[224,768]{1,0:T(8,128)}, u32[]{:S(2)}, u32[]{:S(2)}) collective-permute-start(f32[224,768]{1,0:T(8,128)S(1)} %shard_map.90.refs_3_.refs_1_), channel_id=1, source_target_pairs={{8,0},{9,1},{10,2},{11,3},{12,4},{13,5},{14,6},{15,7},{16,8},{17,9... | collective-permute-start | bytes 2064392 | tf_op jit(solution)/shard_map/ppermute | solution.py:328
  42.0 0.9 copy-start.16
  42.9 30.3 %collective-permute-start.8 = (f32[224,768]{1,0:T(8,128)}, f32[224,768]{1,0:T(8,128)}, u32[]{:S(2)}, u32[]{:S(2)}) collective-permute-start(f32[224,768]{1,0:T(8,128)} %get-tuple-element.13.refs_4_), channel_id=1, source_target_pairs={{0,8},{1,9},{2,10},{3,11},{4,12},{5,13},{6,14},{7,15},{8,16},{9,17... | collective-permute-start | bytes 2064392 | tf_op jit(solution)/shard_map/ppermute | solution.py:328
  42.9 30.3 %collective-permute-start.9 = (f32[224,768]{1,0:T(8,128)}, f32[224,768]{1,0:T(8,128)}, u32[]{:S(2)}, u32[]{:S(2)}) collective-permute-start(f32[224,768]{1,0:T(8,128)} %get-tuple-element.14.refs_5_), channel_id=1, source_target_pairs={{8,0},{9,1},{10,2},{11,3},{12,4},{13,5},{14,6},{15,7},{16,8},{17,9... | collective-permute-start | bytes 2064392 | tf_op jit(solution)/shard_map/ppermute | solution.py:328
  46.1 1.1 copy-start.17
  47.2 0.8 copy-start.27
  50.9 25.6 %all-to-all-start.1 = ((f32[8,64,768]{2,1,0:T(8,128)}), f32[8,64,768]{2,1,0:T(8,128)S(1)}, u32[]{:S(2)}, u32[]{:S(2)}) async-start(f32[8,64,768]{2,1,0:T(8,128)} %shard_map.92), calls=%async_computation.1 | async-start | bytes 3145728 | tf_op jit(solution)/shard_map/all_to_all | solution.py:323
  58.1 18.4 %copy-start.28 = (s32[8,8,128]{2,1,0:T(8,128)S(1)}, s32[8,8,128]{2,1,0:T(8,128)}, u32[]{:S(2)}) copy-start(s32[8,8,128]{2,1,0:T(8,128)} %copy-done.26) | copy-start | bytes 98308
  58.5 29.5 %collective-permute-start.10 = (f32[224,768]{1,0:T(8,128)}, f32[224,768]{1,0:T(8,128)}, u32[]{:S(2)}, u32[]{:S(2)}) collective-permute-start(f32[224,768]{1,0:T(8,128)} %collective-permute-done.6.refs_2_), channel_id=1, source_target_pairs={{0,8},{1,9},{2,10},{3,11},{4,12},{5,13},{6,14},{7,15},{8,16},{9,17... | collective-permute-start | bytes 2064392 | tf_op jit(solution)/shard_map/ppermute | solution.py:328
  58.5 29.5 %collective-permute-start.11 = (f32[224,768]{1,0:T(8,128)}, f32[224,768]{1,0:T(8,128)}, u32[]{:S(2)}, u32[]{:S(2)}) collective-permute-start(f32[224,768]{1,0:T(8,128)} %collective-permute-done.7.refs_3_), channel_id=1, source_target_pairs={{8,0},{9,1},{10,2},{11,3},{12,4},{13,5},{14,6},{15,7},{16,8},{17,9... | collective-permute-start | bytes 2064392 | tf_op jit(solution)/shard_map/ppermute | solution.py:328
  73.2 29.5 %collective-permute-start.12 = (f32[224,768]{1,0:T(8,128)}, f32[224,768]{1,0:T(8,128)}, u32[]{:S(2)}, u32[]{:S(2)}) collective-permute-start(f32[224,768]{1,0:T(8,128)} %collective-permute-done.8.refs_0_.refs_4_), channel_id=1, source_target_pairs={{0,8},{1,9},{2,10},{3,11},{4,12},{5,13},{6,14},{7,15},{8,16},{9,17... | collective-permute-start | bytes 2064392 | tf_op jit(solution)/shard_map/ppermute | solution.py:328
  73.2 29.5 %collective-permute-start.13 = (f32[224,768]{1,0:T(8,128)}, f32[224,768]{1,0:T(8,128)}, u32[]{:S(2)}, u32[]{:S(2)}) collective-permute-start(f32[224,768]{1,0:T(8,128)} %collective-permute-done.9.refs_1_.refs_5_), channel_id=1, source_target_pairs={{8,0},{9,1},{10,2},{11,3},{12,4},{13,5},{14,6},{15,7},{16,8},{17,9... | collective-permute-start | bytes 2064392 | tf_op jit(solution)/shard_map/ppermute | solution.py:328
  78.8 1.1 copy-start.10
  80.0 24.5 %all-to-all-start.2 = ((f32[8,64,768]{2,1,0:T(8,128)}), f32[8,64,768]{2,1,0:T(8,128)S(1)}, u32[]{:S(2)}, u32[]{:S(2)}) async-start(f32[8,64,768]{2,1,0:T(8,128)} %copy-done.10), calls=%async_computation.2 | async-start | bytes 3145728 | tf_op jit(solution)/shard_map/all_to_all | solution.py:323
  88.0 26.7 %collective-permute-start.14 = (f32[224,768]{1,0:T(8,128)}, f32[224,768]{1,0:T(8,128)}, u32[]{:S(2)}, u32[]{:S(2)}) collective-permute-start(f32[224,768]{1,0:T(8,128)} %collective-permute-done.10.refs_2_), channel_id=1, source_target_pairs={{0,8},{1,9},{2,10},{3,11},{4,12},{5,13},{6,14},{7,15},{8,16},{9,17... | collective-permute-start | bytes 2064392 | tf_op jit(solution)/shard_map/ppermute | solution.py:328
  88.0 27.7 %collective-permute-start.15 = (f32[224,768]{1,0:T(8,128)}, f32[224,768]{1,0:T(8,128)}, u32[]{:S(2)}, u32[]{:S(2)}) collective-permute-start(f32[224,768]{1,0:T(8,128)} %collective-permute-done.11.refs_3_), channel_id=1, source_target_pairs={{8,0},{9,1},{10,2},{11,3},{12,4},{13,5},{14,6},{15,7},{16,8},{17,9... | collective-permute-start | bytes 2064392 | tf_op jit(solution)/shard_map/ppermute | solution.py:328
  104.5 2.9 %copy-start = (f32[8,64,768]{2,1,0:T(8,128)}, f32[8,64,768]{2,1,0:T(8,128)S(1)}, u32[]{:S(2)}) copy-start(f32[8,64,768]{2,1,0:T(8,128)S(1)} %all-to-all-done.2.refs_6_.refs_3_) | copy-start | bytes 4718596
  107.4 1.1 copy-start.9
  108.6 25.7 %all-to-all-start.3 = ((f32[8,64,768]{2,1,0:T(8,128)}), f32[8,64,768]{2,1,0:T(8,128)S(1)}, u32[]{:S(2)}, u32[]{:S(2)}) async-start(f32[8,64,768]{2,1,0:T(8,128)} %copy-done.9), calls=%async_computation.3 | async-start | bytes 3145728 | tf_op jit(solution)/shard_map/all_to_all | solution.py:323
  115.6 11.8 %collective-permute-start.18 = (f32[112,768]{1,0:T(8,128)S(1)}, f32[112,768]{1,0:T(8,128)S(1)}, u32[]{:S(2)}, u32[]{:S(2)}) collective-permute-start(f32[112,768]{1,0:T(8,128)S(1)} %slice.18), channel_id=1, source_target_pairs={{0,8},{1,9},{2,10},{3,11},{4,12},{5,13},{6,14},{7,15},{8,16},{9,17... | collective-permute-start | bytes 1032200 | tf_op jit(solution)/shard_map/ppermute | solution.py:328
  116.7 11.0 %collective-permute-start.19 = (f32[112,768]{1,0:T(8,128)S(1)}, f32[112,768]{1,0:T(8,128)S(1)}, u32[]{:S(2)}, u32[]{:S(2)}) collective-permute-start(f32[112,768]{1,0:T(8,128)S(1)} %slice.19), channel_id=1, source_target_pairs={{8,0},{9,1},{10,2},{11,3},{12,4},{13,5},{14,6},{15,7},{16,8},{17,9... | collective-permute-start | bytes 1032200 | tf_op jit(solution)/shard_map/ppermute | solution.py:328
  121.0 11.3 %collective-permute-start.16 = (f32[112,768]{1,0:T(8,128)S(1)}, f32[112,768]{1,0:T(8,128)S(1)}, u32[]{:S(2)}, u32[]{:S(2)}) collective-permute-start(f32[112,768]{1,0:T(8,128)S(1)} %slice.16), channel_id=1, source_target_pairs={{0,8},{1,9},{2,10},{3,11},{4,12},{5,13},{6,14},{7,15},{8,16},{9,17... | collective-permute-start | bytes 1032200 | tf_op jit(solution)/shard_map/ppermute | solution.py:328
  122.1 10.9 %collective-permute-start.17 = (f32[112,768]{1,0:T(8,128)S(1)}, f32[112,768]{1,0:T(8,128)S(1)}, u32[]{:S(2)}, u32[]{:S(2)}) collective-permute-start(f32[112,768]{1,0:T(8,128)S(1)} %slice.17), channel_id=1, source_target_pairs={{8,0},{9,1},{10,2},{11,3},{12,4},{13,5},{14,6},{15,7},{16,8},{17,9... | collective-permute-start | bytes 1032200 | tf_op jit(solution)/shard_map/ppermute | solution.py:328
  127.4 0.7 copy-start.30
  127.7 0.7 copy-start.32
  132.3 0.7 copy-start.34
  133.0 0.7 copy-start.36
  134.2 1.0 copy-start.31
  135.2 1.0 copy-start.33
  136.2 1.0 copy-start.35
  137.2 1.0 copy-start.37
  138.1 2.5 %copy-start.2 = (f32[8,64,768]{2,1,0:T(8,128)}, f32[8,64,768]{2,1,0:T(8,128)S(1)}, u32[]{:S(2)}) copy-start(f32[8,64,768]{2,1,0:T(8,128)S(1)} %all-to-all-done.3.refs_4_.refs_8_) | copy-start | bytes 4718596
  140.7 1.1 copy-start.11
  141.8 25.0 %all-to-all-start.4 = ((f32[8,64,768]{2,1,0:T(8,128)}), f32[8,64,768]{2,1,0:T(8,128)S(1)}, u32[]{:S(2)}, u32[]{:S(2)}) async-start(f32[8,64,768]{2,1,0:T(8,128)} %copy-done.11), calls=%async_computation.4 | async-start | bytes 3145728 | tf_op jit(solution)/shard_map/all_to_all | solution.py:323
  148.5 1.4 copy-start.1
  149.9 1.1 copy-start.15
  151.0 5.0 %copy-start.13 = (f32[224,768]{1,0:T(8,128)S(1)}, f32[224,768]{1,0:T(8,128)}, u32[]{:S(2)}) copy-start(f32[224,768]{1,0:T(8,128)} %copy-done.12) | copy-start | bytes 2064388
  155.0 1.1 copy-start.5
  160.2 1.1 copy-start.7
  166.8 1.3 copy-start.6
  168.1 1.3 copy-start.8
  (1 other events, 0.6 us)

commit v3 on v2

--- a/solution.py
+++ b/solution.py
@@ -27,7 +27,7 @@
 PLANE = 8
 RING = 8
 
-VMEM = pltpu.CompilerParams(vmem_limit_bytes=48 * 1024 * 1024)
+VMEM = pltpu.CompilerParams(vmem_limit_bytes=12 * 1024 * 1024)
 
 
 def call(kernel, out, *, grid=None, in_specs=None, out_specs=None, flops=0, moved=0):
@@ -82,7 +82,8 @@
     out[...] = grad[:, pl.ds(at, HALF)].astype(F32) + got[...]
 
 
-def update_kernel(half, place, grad, got, got_y, weight, first, second, out):
+def update_kernel(half, place, grad, got, got_y, weight, first, second, *refs):
+    out = refs[-1]
     dp = place[1]
     at = pl.multiple_of(dp * FEATS + half * HALF, HALF)
     total = grad[:, pl.ds(at, HALF)].astype(F32) + got[...] + got_y[...]
@@ -129,11 +130,11 @@
         place_in(((0, 0), (7, 32), (1, 48))),
         place_in(((6, 32), (2, 48))),
         place_in(((5, 32), (3, 48))),
-        place_in(((4, 32),)),
+        place_in(((4, 0),)),
         place_in(((0, 16),)),
         place_in(((7, 0), (1, 16))),
         place_in(((6, 0), (2, 16))),
-        place_in(((5, 0), (3, 16), (4, 48))),
+        place_in(((5, 0), (3, 16))),
     )
     lane = lax.broadcasted_iota(I32, (FINE, 128), 1)
     out = jnp.full((FINE, 128), none, I32)
@@ -170,22 +171,6 @@
             out[d, row : row + SLOTS, :] = got[d * SLOTS : (d + 1) * SLOTS]
 
 
-def held_kernel(*refs):
-    pass
-
-
-def hold(arrays, *until):
-    n = len(arrays)
-    return pl.pallas_call(
-        held_kernel,
-        out_shape=tuple(shape(*a.shape) for a in arrays),
-        in_specs=[pl.BlockSpec(memory_space=pl.ANY)] * (n + len(until)),
-        out_specs=(pl.BlockSpec(memory_space=pl.ANY),) * n,
-        input_output_aliases={i: i for i in range(n)},
-        cost_estimate=pl.CostEstimate(flops=0, bytes_accessed=1 << 20, transcendentals=0),
-    )(*arrays, *until)
-
-
 def token_kernel(*refs):
     refs[-1][...] = jnp.zeros((8, 128), F32)
 
@@ -207,34 +192,33 @@
     return split_dot(chosen, far.reshape(rows, far.shape[2]))
 
 
-def far_part(codes, lane, far, low, high):
-    at = codes[:, lane : lane + 1]
+def far_part(at, far, low, high):
     xy, row = at >> 6, at & 63
     here = (at >= 0) & (row >= low) & (row < high)
     at = jnp.where(here, xy * (high - low) + row - low, -1)
     return far_dot(at, far[:, low:high, :])
 
 
-def gather_kernel(parts, codes, near, far1, far2, far3, out):
+def gather_kernel(parts, codes, near, *refs):
     own = lax.broadcasted_iota(I32, (FINE, ROWS), 0) >> 1
     chosen = jnp.where(
         lax.broadcasted_iota(I32, (FINE, ROWS), 1) == own, own_share, 0.0
     ).astype(BF16)
     total = split_dot(chosen, near[...])
-    far = (far1, far2, far3)
     for lane, exchange, low, high in parts:
-        total = total + far_part(codes, lane, far[exchange], low, high)
-    out[...] = total
+        total = total + far_part(codes[:, lane : lane + 1], refs[exchange], low, high)
+    refs[-1][...] = total
 
 
 def final_kernel(codes, *refs):
     lane = lax.broadcasted_iota(I32, (FINE, 128), 1) >> 1
     first_half = pl.program_id(0) < 2
-    at = jnp.where(first_half, codes[:, 3:4], codes[:, 7:8])
+    at = codes[:, 3:4]
     for state in range(3):
         acc0, acc1, far, out = (refs[3 * k + state] for k in range(4))
         acc = jnp.where(first_half, acc0[...], acc1[...])
-        mixed = acc + far_dot(at, far[...])
+        rows = jnp.where(first_half, far[:, 0:16, :], far[:, 16:32, :])
+        mixed = acc + far_part(at, rows, 0, 16)
         out[:, 0:128] = jnp.take_along_axis(mixed, lane, axis=1)
         out[:, 128:256] = jnp.take_along_axis(mixed, lane + 64, axis=1)
 
@@ -249,6 +233,21 @@
 def on_device(grad_parts, weight, first, second, partner_device, partner_column):
     place = jnp.stack([lax.axis_index("shard"), lax.axis_index("dp")]).astype(I32)
     grad = grad_parts[0]
+
+    wanted, codes = call(
+        index_kernel,
+        (shape(PLANE, RING, 128, dtype=I32), shape(FINE, 128, dtype=I32)),
+        in_specs=[scalar(), whole(), whole(), whole()],
+        moved=1 << 20,
+    )(
+        place,
+        partner_device,
+        partner_device.reshape(1, FINE),
+        partner_column.reshape(FINE, 1),
+    )
+    asked = lax.all_to_all(
+        wanted, "shard", split_axis=0, concat_axis=0, axis_index_groups=PLANES, tiled=True
+    )
 
     sends = call(
         send_core_kernel,
@@ -287,26 +286,12 @@
                     block,
                     block,
                     block,
-                ],
+                ]
+                + [pl.BlockSpec(memory_space=pl.ANY)] * half,
                 out_specs=pl.BlockSpec((ROWS, WIDE), lambda i: (0, 0)),
                 moved=2 << 20,
-            )(place, grad, got, got_y, weight, first, second)
+            )(place, grad, got, got_y, weight, first, second, *[asked] * half)
         )
-
-    wanted, codes = call(
-        index_kernel,
-        (shape(PLANE, RING, 128, dtype=I32), shape(FINE, 128, dtype=I32)),
-        in_specs=[scalar(), whole(), whole(), whole()],
-        moved=1 << 20,
-    )(
-        place,
-        partner_device,
-        partner_device.reshape(1, FINE),
-        partner_column.reshape(FINE, 1),
-    )
-    asked = lax.all_to_all(
-        wanted, "shard", split_axis=0, concat_axis=0, axis_index_groups=PLANES, tiled=True
-    )
 
     def pick(parts, sources, after=()):
         return call(
@@ -328,28 +313,28 @@
         return lax.ppermute(pair[0], "shard", UP), lax.ppermute(pair[1], "shard", DOWN)
 
     one = [around((x, x)) for x in state]
-    one[0] = hold(one[0], asked)
     two = [around(pair) for pair in one]
     three = [around(pair) for pair in two]
     far1 = to_plane(pick(((0, 0, 1), (0, 16, 1), (-1, 32, 1), (1, 48, 1)), (*state, *one[0])))
     far2 = to_plane(
-        pick(((-1, 0, 1), (1, 16, 1), (-2, 32, 1), (2, 48, 1)), (*one[1], *two[0]), (far1, token(two[0])))
+        pick(((-1, 0, 1), (1, 16, 1), (-2, 32, 1), (2, 48, 1)), (*one[1], *two[0]), (far1, token((*one[1], *two[0]))))
     )
     far3 = to_plane(
-        pick(((-2, 0, 1), (2, 16, 1), (-3, 32, 1), (3, 48, 1)), (*two[1], *three[0]), (far2, token(three[0])))
+        pick(((-2, 0, 1), (2, 16, 1), (-3, 32, 1), (3, 48, 1)), (*two[1], *three[0]), (far2, token((*two[1], *three[0]))))
     )
     middle = ROWS // 2
     four = [around((pair[0][:middle], pair[1][middle:])) for pair in three]
-    rows = pick(
-        ((-3, 0, 1), (3, 16, 1), (4, 32, 2), (4, 48, 2)), (*three[1], *four[0], *four[1]), (far3, token(four[1]))
-    )
-    far4 = to_plane(rows)
+    far4 = to_plane(pick(((-3, 0, 1), (3, 16, 1)), three[1], (far3, token(three[1]))))
+    far5 = to_plane(pick(((4, 0, 2), (4, 16, 2)), (*four[0], *four[1]), (far4, token((*four[0], *four[1])))))
 
     acc = []
-    for half, parts in enumerate(
+    for half, (parts, far) in enumerate(
         (
-            ((0, 0, 0, 16), (0, 0, 32, 64), (1, 1, 32, 64), (2, 2, 32, 64)),
-            ((4, 0, 16, 32), (5, 1, 0, 32), (6, 2, 0, 32)),
+            (((0, 0, 0, 16), (0, 0, 32, 64), (1, 1, 32, 64), (2, 2, 32, 64)), (far1, far2, far3)),
+            (
+                ((4, 0, 16, 32), (5, 1, 0, 32), (6, 2, 0, 32), (7, 3, 0, 32)),
+                (far1, far2, far3, far4),
+            ),
         )
     ):
         acc.append(
@@ -361,11 +346,11 @@
                     pl.BlockSpec((FINE, 128), lambda i: (0, 0)),
                     pl.BlockSpec((ROWS, HALF), lambda i: (0, i)),
                 ]
-                + [pl.BlockSpec((PLANE, 64, HALF), lambda i: (0, 0, i))] * 3,
+                + [pl.BlockSpec((PLANE, a.shape[1], HALF), lambda i: (0, 0, i)) for a in far],
                 out_specs=pl.BlockSpec((FINE, HALF), lambda i: (0, i)),
                 flops=FINE * 1120 * WIDE * 4,
                 moved=8 << 20,
-            )(codes, state[half], far1, far2, far3)
+            )(codes, state[half], *far)
         )
 
     def acc_block(half, state):
@@ -376,7 +361,7 @@
         return pl.BlockSpec((FINE, 128), index)
 
     def far_block(state):
-        return pl.BlockSpec((PLANE, 64, 128), lambda j: (0, 0, state * 2 + lax.rem(j, 2)))
+        return pl.BlockSpec((PLANE, 32, 128), lambda j: (0, 0, state * 2 + lax.rem(j, 2)))
 
     return call(
         final_kernel,
@@ -388,7 +373,7 @@
         out_specs=(pl.BlockSpec((FINE, 256), lambda j: (0, j)),) * 3,
         flops=FINE * 512 * 1536 * 4,
         moved=12 << 20,
-    )(codes, acc[0], acc[0], acc[0], acc[1], acc[1], acc[1], far4, far4, far4)
+    )(codes, acc[0], acc[0], acc[0], acc[1], acc[1], acc[1], far5, far5, far5)
 
 
 def solution(mesh):

time: 180 us -> 180 us (level); the launches traced: 176 us -> 178 us
  blocking collectives: 0 us -> 13.2 us
  local copies, waits for them, and re-layouts: 30.8 us -> 23 us
  starting transfers between devices: 66.4 us -> 59.7 us
  waiting for transfers between devices: 46.3 us -> 49.5 us
    all_to_all x0 -> x1, blocking collectives: none -> 13.2 us  [on_device(): lax.all_to_all(wanted, 'shard', split_axis=0, concat_axis=0, axis_index_g...]
    unnamed x81 -> x45, local copies, waits for them, and re-layouts: 25.9 us -> 16 us
    all_to_all x1 -> x0, starting transfers between devices: 7.17 us -> none  [on_device(): lax.all_to_all(wanted, 'shard', split_axis=0, concat_axis=0, axis_index_g...]
    slice x4, local copies, waits for them, and re-layouts: 4.01 us -> 6.91 us  [on_device(): four = [around((pair[0][:middle], pair[1][middle:])) for pair in three]]
    all_to_all x4 -> x5, waiting for transfers between devices: 7.8 us -> 10.4 us  [to_plane(): lax.all_to_all(rows, 'shard', split_axis=0, concat_axis=0, axis_index_gro...]
    pallas_call x4 -> x5, Pallas kernels: 10.6 us -> 11.4 us  [pick(): call(lambda *refs: pick_kernel(parts, *refs), shape(PLANE, SLOTS * len(pa...]
    all_to_all x4 -> x5, starting transfers between devices: 26.9 us -> 27.7 us  [to_plane(): lax.all_to_all(rows, 'shard', split_axis=0, concat_axis=0, axis_index_gro...]
  transfers between devices with their start and end apart: 25 -> 25, of which waited for: 13 -> 8; matrix products, arithmetic and copies ran while one was open for 3% -> 4% of each run, Pallas kernels for 12% -> 13%
where the time goes in v3:
time: 180 us; the launch traced here: 178 us
  starting transfers between devices  59.7 us (33%)
  waiting for transfers between devices  49.5 us (28%)
  Pallas kernels  32 us (18%)
  local copies, waits for them, and re-layouts  23 us (13%)
  blocking collectives  13.2 us (7%)
    ppermute x8, waiting for transfers between devices, around(): lax.ppermute(pair[0], 'shard', UP)  31.2 us
    all_to_all x5, starting transfers between devices, to_plane(): lax.all_to_all(rows, 'shard', split_axis=0, concat_axis=0, axis_index_gro...  27.7 us
    ppermute x8, starting transfers between devices, around(): lax.ppermute(pair[1], 'shard', DOWN)  26.7 us
    unnamed x45, local copies, waits for them, and re-layouts  16 us
    all_to_all x1, blocking collectives, on_device(): lax.all_to_all(wanted, 'shard', split_axis=0, concat_axis=0, axis_index_g...  13.2 us
    pallas_call x5, Pallas kernels, pick(): call(lambda *refs: pick_kernel(parts, *refs), shape(PLANE, SLOTS * len(pa...  11.4 us
    all_to_all x5, waiting for transfers between devices, to_plane(): lax.all_to_all(rows, 'shard', split_axis=0, concat_axis=0, axis_index_gro...  10.4 us
    pallas_call x2, Pallas kernels, on_device(): call(lambda *refs, parts=parts: gather_kernel(parts, *refs), shape(FINE,...  8.45 us
  transfers between devices with their start and end apart: 25, of which 8 were waited for; matrix products, arithmetic and copies ran while one was open for 4% of the time, Pallas kernels for 13%

profile of v3, /device:TPU:2, one launch (start us, length us, event | category | flops | bytes accessed | tf_op | source)
XLA Modules:
  0.0 178.5 jit_solution(15560766350267390918)
XLA Ops:
  0.6 0.1 pad_add_fusion.place.refs_0_
  0.7 1.2 copy-done
  1.9 0.6 shard_map.86
  2.5 0.1 collective-permute-start
  2.6 1.8 %collective-permute-done.refs_2_ = f32[224,512]{1,0:T(8,128)S(1)} collective-permute-done((f32[224,512]{1,0:T(8,128)S(1)}, f32[224,512]{1,0:T(8,128)S(1)}, u32[]{:S(2)}, u32[]{:S(2)}) %collective-permute-start) | collective-permute-done | bytes 458784 | tf_op jit(solution)/shard_map/ppermute | solution.py:258
  4.4 0.6 shard_map.87
  5.0 1.7 collective-permute-start.1
  6.7 6.1 %collective-permute-done.1.refs_3_ = f32[224,256]{1,0:T(8,128)S(1)} collective-permute-done((f32[224,256]{1,0:T(8,128)S(1)}, f32[224,256]{1,0:T(8,128)S(1)}, u32[]{:S(2)}, u32[]{:S(2)}) %collective-permute-start.1) | collective-permute-done | bytes 229408 | tf_op jit(solution)/shard_map/ppermute | solution.py:274
  12.7 0.8 shard_map.88.refs_2_.refs_1_
  13.5 0.0 copy-start.21
  13.5 0.0 copy-start.1
  13.5 2.0 %collective-permute-start.4 = (f32[224,768]{1,0:T(8,128)S(1)}, f32[224,768]{1,0:T(8,128)}, u32[]{:S(2)}, u32[]{:S(2)}) collective-permute-start(f32[224,768]{1,0:T(8,128)S(1)} %shard_map.88.refs_2_.refs_1_), channel_id=1, source_target_pairs={{0,8},{1,9},{2,10},{3,11},{4,12},{5,13},{6,14},{7,15},{8,16},{9,17... | collective-permute-start | bytes 2064392 | tf_op jit(solution)/shard_map/ppermute | solution.py:313
  15.5 4.0 %collective-permute-start.5 = (f32[224,768]{1,0:T(8,128)S(1)}, f32[224,768]{1,0:T(8,128)}, u32[]{:S(2)}, u32[]{:S(2)}) collective-permute-start(f32[224,768]{1,0:T(8,128)S(1)} %shard_map.88.refs_2_.refs_1_), channel_id=1, source_target_pairs={{8,0},{9,1},{10,2},{11,3},{12,4},{13,5},{14,6},{15,7},{16,8},{17,9... | collective-permute-start | bytes 2064392 | tf_op jit(solution)/shard_map/ppermute | solution.py:313
  19.6 1.3 shard_map.89
  20.8 1.6 collective-permute-start.3
  22.4 0.1 copy.10.dev
  22.6 0.1 copy.11.col
  22.7 1.3 shard_map.85
  24.1 13.2 %all_to_all.30.refs_7_.refs_1_ = s32[8,8,128]{2,1,0:T(8,128)S(1)} all-to-all(s32[8,8,128]{2,1,0:T(8,128)S(1)} %get-tuple-element.9), channel_id=1, replica_groups={{0,1,2,3,4,5,6,7},{8,9,10,11,12,13,14,15},{16,17,18,19,20,21,22,23},{24..., dimensions={0} | all-to-all | bytes 65536 | tf_op jit(solution)/shard_map/all_to_all | solution.py:248
  37.3 0.7 copy-done.18
  38.0 1.0 copy-done.13
  39.0 1.0 copy-done.15
  40.0 1.0 copy-done.17
  41.0 0.9 copy-done.19
  42.0 1.6 shard_map.90.refs_3_.refs_1_
  43.6 3.2 %collective-permute-start.7 = (f32[224,768]{1,0:T(8,128)}, f32[224,768]{1,0:T(8,128)}, u32[]{:S(2)}, u32[]{:S(2)}) collective-permute-start(f32[224,768]{1,0:T(8,128)} %shard_map.90.refs_3_.refs_1_), channel_id=1, source_target_pairs={{8,0},{9,1},{10,2},{11,3},{12,4},{13,5},{14,6},{15,7},{16,8},{17,9... | collective-permute-start | bytes 2064392 | tf_op jit(solution)/shard_map/ppermute | solution.py:313
  46.8 3.2 %collective-permute-start.9 = (f32[224,768]{1,0:T(8,128)}, f32[224,768]{1,0:T(8,128)}, u32[]{:S(2)}, u32[]{:S(2)}) collective-permute-start(f32[224,768]{1,0:T(8,128)} %collective-permute-done.5.refs_5_), channel_id=1, source_target_pairs={{8,0},{9,1},{10,2},{11,3},{12,4},{13,5},{14,6},{15,7},{16,8},{17,9... | collective-permute-start | bytes 2064392 | tf_op jit(solution)/shard_map/ppermute | solution.py:313
  50.1 3.3 %shard_map.91 = f32[8,64,768]{2,1,0:T(8,128)} custom-call(s32[2]{0:T(128)S(1)} %pad_add_fusion.place.refs_0_, s32[8,8,128]{2,1,0:T(8,128)S(1)} %all_to_all.30.refs_7_.refs_1_, f32[224,768]{1,0:T(8,128)S(1)} %shard_map.88.refs_2_.refs_1_, f32[224,768]{1,0:T(8,128)} %shard_map.90.refs_3_.refs_1_, f32[224,768]{1,0:T(8,128)} %collective-permute-done.4.refs_4_, ...), custom_call_target="tpu_custom_call" | custom-call | flops 352321536 | bytes 6291456 | tf_op jit(solution)/shard_map/pallas_call | solution.py:297
  53.4 4.9 %all-to-all-start.1 = ((f32[8,64,768]{2,1,0:T(8,128)}), f32[8,64,768]{2,1,0:T(8,128)S(1)}, u32[]{:S(2)}, u32[]{:S(2)}) async-start(f32[8,64,768]{2,1,0:T(8,128)} %shard_map.91), calls=%async_computation.1 | async-start | bytes 3145728 | tf_op jit(solution)/shard_map/all_to_all | solution.py:308
  58.3 5.2 %collective-permute-done.6.refs_0_.refs_2_ = f32[224,768]{1,0:T(8,128)} collective-permute-done((f32[224,768]{1,0:T(8,128)}, f32[224,768]{1,0:T(8,128)}, u32[]{:S(2)}, u32[]{:S(2)}) %collective-permute-start.6) | collective-permute-done | bytes 688160 | tf_op jit(solution)/shard_map/ppermute | solution.py:313
  63.5 3.2 %collective-permute-start.11 = (f32[224,768]{1,0:T(8,128)}, f32[224,768]{1,0:T(8,128)}, u32[]{:S(2)}, u32[]{:S(2)}) collective-permute-start(f32[224,768]{1,0:T(8,128)} %collective-permute-done.7.refs_1_.refs_3_), channel_id=1, source_target_pairs={{8,0},{9,1},{10,2},{11,3},{12,4},{13,5},{14,6},{15,7},{16,8},{17,9... | collective-permute-start | bytes 2064392 | tf_op jit(solution)/shard_map/ppermute | solution.py:313
  66.7 11.5 %collective-permute-done.8.refs_2_.refs_4_ = f32[224,768]{1,0:T(8,128)} collective-permute-done((f32[224,768]{1,0:T(8,128)}, f32[224,768]{1,0:T(8,128)}, u32[]{:S(2)}, u32[]{:S(2)}) %collective-permute-start.8) | collective-permute-done | bytes 688160 | tf_op jit(solution)/shard_map/ppermute | solution.py:313
  78.2 3.2 %collective-permute-start.13 = (f32[224,768]{1,0:T(8,128)}, f32[224,768]{1,0:T(8,128)}, u32[]{:S(2)}, u32[]{:S(2)}) collective-permute-start(f32[224,768]{1,0:T(8,128)} %collective-permute-done.9.refs_3_.refs_5_), channel_id=1, source_target_pairs={{8,0},{9,1},{10,2},{11,3},{12,4},{13,5},{14,6},{15,7},{16,8},{17,9... | collective-permute-start | bytes 2064392 | tf_op jit(solution)/shard_map/ppermute | solution.py:313
  81.5 2.4 %shard_map.93 = f32[8,64,768]{2,1,0:T(8,128)S(1)} custom-call(s32[2]{0:T(128)S(1)} %pad_add_fusion.place.refs_0_, s32[8,8,128]{2,1,0:T(8,128)S(1)} %all_to_all.30.refs_7_.refs_1_, f32[224,768]{1,0:T(8,128)} %collective-permute-done.6.refs_0_.refs_2_, f32[224,768]{1,0:T(8,128)} %collective-permute-done.7.refs_1_.refs_3_, ...), custom_call_target="tpu_custom_call" | custom-call | flops 352321536 | bytes 6291456 | tf_op jit(solution)/shard_map/pallas_call | solution.py:297
  83.9 1.1 copy-done.7
  85.0 5.0 %all-to-all-start.2 = ((f32[8,64,768]{2,1,0:T(8,128)}), f32[8,64,768]{2,1,0:T(8,128)S(1)}, u32[]{:S(2)}, u32[]{:S(2)}) async-start(f32[8,64,768]{2,1,0:T(8,128)} %copy-done.7), calls=%async_computation.2 | async-start | bytes 3145728 | tf_op jit(solution)/shard_map/all_to_all | solution.py:308
  89.9 3.0 %collective-permute-done.10.refs_0_.refs_2_ = f32[224,768]{1,0:T(8,128)} collective-permute-done((f32[224,768]{1,0:T(8,128)}, f32[224,768]{1,0:T(8,128)}, u32[]{:S(2)}, u32[]{:S(2)}) %collective-permute-start.10) | collective-permute-done | bytes 688160 | tf_op jit(solution)/shard_map/ppermute | solution.py:313
  93.0 3.2 %collective-permute-start.15 = (f32[224,768]{1,0:T(8,128)}, f32[224,768]{1,0:T(8,128)}, u32[]{:S(2)}, u32[]{:S(2)}) collective-permute-start(f32[224,768]{1,0:T(8,128)} %collective-permute-done.11.refs_1_.refs_3_), channel_id=1, source_target_pairs={{8,0},{9,1},{10,2},{11,3},{12,4},{13,5},{14,6},{15,7},{16,8},{17,9... | collective-permute-start | bytes 2064392 | tf_op jit(solution)/shard_map/ppermute | solution.py:313
  96.2 11.5 %collective-permute-done.12.refs_2_.refs_4_ = f32[224,768]{1,0:T(8,128)} collective-permute-done((f32[224,768]{1,0:T(8,128)}, f32[224,768]{1,0:T(8,128)}, u32[]{:S(2)}, u32[]{:S(2)}) %collective-permute-start.12) | collective-permute-done | bytes 688160 | tf_op jit(solution)/shard_map/ppermute | solution.py:313
  107.7 2.4 %shard_map.95 = f32[8,64,768]{2,1,0:T(8,128)S(1)} custom-call(s32[2]{0:T(128)S(1)} %pad_add_fusion.place.refs_0_, s32[8,8,128]{2,1,0:T(8,128)S(1)} %all_to_all.30.refs_7_.refs_1_, f32[224,768]{1,0:T(8,128)} %collective-permute-done.10.refs_0_.refs_2_, f32[224,768]{1,0:T(8,128)} %collective-permute-done.11.refs_1_.refs_3_, ...), custom_call_target="tpu_custom_call" | custom-call | flops 352321536 | bytes 6291456 | tf_op jit(solution)/shard_map/pallas_call | solution.py:297
  110.1 1.1 copy-done.6
  111.2 5.6 %all-to-all-start.3 = ((f32[8,64,768]{2,1,0:T(8,128)}), f32[8,64,768]{2,1,0:T(8,128)}, u32[]{:S(2)}, u32[]{:S(2)}) async-start(f32[8,64,768]{2,1,0:T(8,128)} %copy-done.6), calls=%async_computation.3 | async-start | bytes 3145728 | tf_op jit(solution)/shard_map/all_to_all | solution.py:308
  116.9 1.7 slice.16
  118.6 1.7 slice.17
  120.4 3.2 %collective-permute-start.17 = (f32[112,768]{1,0:T(8,128)}, f32[112,768]{1,0:T(8,128)}, u32[]{:S(2)}, u32[]{:S(2)}) collective-permute-start(f32[112,768]{1,0:T(8,128)} %slice.17), channel_id=1, source_target_pairs={{8,0},{9,1},{10,2},{11,3},{12,4},{13,5},{14,6},{15,7},{16,8},{17,9... | collective-permute-start | bytes 1032200 | tf_op jit(solution)/shard_map/ppermute | solution.py:313
  123.6 1.7 slice.18
  125.3 1.7 slice.19
  127.0 3.2 %collective-permute-start.19 = (f32[112,768]{1,0:T(8,128)}, f32[112,768]{1,0:T(8,128)}, u32[]{:S(2)}, u32[]{:S(2)}) collective-permute-start(f32[112,768]{1,0:T(8,128)} %slice.19), channel_id=1, source_target_pairs={{8,0},{9,1},{10,2},{11,3},{12,4},{13,5},{14,6},{15,7},{16,8},{17,9... | collective-permute-start | bytes 1032200 | tf_op jit(solution)/shard_map/ppermute | solution.py:313
  130.3 0.9 all-to-all-done.3.refs_4_
  131.1 1.7 shard_map.98
  132.9 0.9 copy-done.10
  133.7 6.6 %all-to-all-start.4 = ((f32[8,32,768]{2,1,0:T(8,128)}), f32[8,32,768]{2,1,0:T(8,128)}, u32[]{:S(2)}, u32[]{:S(2)}) async-start(f32[8,32,768]{2,1,0:T(8,128)} %copy-done.10), calls=%async_computation.4 | async-start | bytes 1572864 | tf_op jit(solution)/shard_map/all_to_all | solution.py:308
  140.4 9.5 %all-to-all-done.4.refs_5_.refs_6_ = f32[8,32,768]{2,1,0:T(8,128)} async-done(((f32[8,32,768]{2,1,0:T(8,128)}), f32[8,32,768]{2,1,0:T(8,128)}, u32[]{:S(2)}, u32[]{:S(2)}) %all-to-all-start.4) | async-done | bytes 786464 | tf_op jit(solution)/shard_map/all_to_all | solution.py:308
  149.9 1.7 shard_map.101
  151.6 0.9 copy-done.11
  152.5 5.6 %all-to-all-start.5 = ((f32[8,32,768]{2,1,0:T(8,128)}), f32[8,32,768]{2,1,0:T(8,128)}, u32[]{:S(2)}, u32[]{:S(2)}) async-start(f32[8,32,768]{2,1,0:T(8,128)} %copy-done.11), calls=%async_computation.5 | async-start | bytes 1572864 | tf_op jit(solution)/shard_map/all_to_all | solution.py:308
  158.1 1.1 copy-done.9
  159.2 4.1 %shard_map.96.refs_0_.refs_1_.refs_2_ = f32[448,768]{1,0:T(8,128)S(1)} custom-call(s32[448,128]{1,0:T(8,128)S(1)} %get-tuple-element.7.refs_0_.codes, f32[224,768]{1,0:T(8,128)S(1)} %copy-done.9, f32[8,64,768]{2,1,0:T(8,128)S(1)} %all-to-all-done.1.refs_6_.refs_2_, f32[8,64,768]{2,1,0:T(8,128)S(1)} %all-to-all-done.2.refs_6_.refs_3_, ...), custom_call_target="tpu_custom_call" | custom-call | flops 1541406720 | bytes 8388608 | tf_op jit(solution)/shard_map/pallas_call | solution.py:341
  163.3 1.1 copy-done.2
  164.4 4.4 %shard_map.99.refs_3_.refs_4_.refs_5_ = f32[448,768]{1,0:T(8,128)S(1)} custom-call(s32[448,128]{1,0:T(8,128)S(1)} %get-tuple-element.7.refs_0_.codes, f32[224,768]{1,0:T(8,128)} %shard_map.90.refs_3_.refs_1_, f32[8,64,768]{2,1,0:T(8,128)S(1)} %all-to-all-done.1.refs_6_.refs_2_, f32[8,64,768]{2,1,0:T(8,128)S(1)} %all-to-all-done.2.refs_6_.refs_3_, ...), custom_call_target="tpu_custom_call" | custom-call | flops 1541406720 | bytes 8388608 | tf_op jit(solution)/shard_map/pallas_call | solution.py:341
  168.7 1.1 copy-done.4
  169.8 1.3 copy-done.3
  171.2 1.3 copy-done.5
  172.5 6.0 %shard_map.102 = (f32[448,1024]{1,0:T(8,128)}, f32[448,1024]{1,0:T(8,128)}, f32[448,1024]{1,0:T(8,128)}) custom-call(s32[448,128]{1,0:T(8,128)S(1)} %get-tuple-element.7.refs_0_.codes, f32[448,768]{1,0:T(8,128)S(1)} %copy-done.3, f32[448,768]{1,0:T(8,128)S(1)} %copy-done.3, f32[448,768]{1,0:T(8,128)S(1)} %copy-done.3, f32[448,768]{1,0:T(8,128)S(1)} %copy-done.5, ...), custom_call_target="tpu_custom_call" | custom-call | flops 1409286144 | bytes 12582912 | tf_op jit(solution)/shard_map/pallas_call | solution.py:366
  (56 shorter events, 0.1 us)
Async XLA Ops:
  0.7 1.2 copy-start
  1.9 10.8 %copy-start.12 = (f32[224,512]{1,0:T(8,128)S(1)}, f32[224,512]{1,0:T(8,128)}, u32[]{:S(2)}) copy-start(f32[224,512]{1,0:T(8,128)} %refs_4_.3) | copy-start | bytes 1376260
  1.9 10.8 %copy-start.14 = (f32[224,512]{1,0:T(8,128)S(1)}, f32[224,512]{1,0:T(8,128)}, u32[]{:S(2)}) copy-start(f32[224,512]{1,0:T(8,128)} %refs_5_.3) | copy-start | bytes 1376260
  1.9 10.8 %copy-start.16 = (f32[224,512]{1,0:T(8,128)S(1)}, f32[224,512]{1,0:T(8,128)}, u32[]{:S(2)}) copy-start(f32[224,512]{1,0:T(8,128)} %refs_6_.3) | copy-start | bytes 1376260
  2.5 1.9 %collective-permute-start = (f32[224,512]{1,0:T(8,128)S(1)}, f32[224,512]{1,0:T(8,128)S(1)}, u32[]{:S(2)}, u32[]{:S(2)}) collective-permute-start(f32[224,512]{1,0:T(8,128)S(1)} %get-tuple-element.8), channel_id=1, source_target_pairs={{0,64},{64,0},{128,192},{192,128},{1,65},{65,1},{129,193},{193,129... | collective-permute-start | bytes 1376264 | tf_op jit(solution)/shard_map/ppermute | solution.py:258
  5.0 7.7 %collective-permute-start.1 = (f32[224,256]{1,0:T(8,128)S(1)}, f32[224,256]{1,0:T(8,128)S(1)}, u32[]{:S(2)}, u32[]{:S(2)}) collective-permute-start(f32[224,256]{1,0:T(8,128)S(1)} %shard_map.87), channel_id=1, source_target_pairs={{0,128},{128,0},{64,192},{192,64},{1,129},{129,1},{65,193},{193,65... | collective-permute-start | bytes 688136 | tf_op jit(solution)/shard_map/ppermute | solution.py:274
  6.7 12.9 %collective-permute-start.2 = (f32[224,512]{1,0:T(8,128)S(1)}, f32[224,512]{1,0:T(8,128)S(1)}, u32[]{:S(2)}, u32[]{:S(2)}) collective-permute-start(f32[224,512]{1,0:T(8,128)S(1)} %get-tuple-element.10), channel_id=1, source_target_pairs={{0,64},{64,0},{128,192},{192,128},{1,65},{65,1},{129,193},{193,129... | collective-permute-start | bytes 1376264 | tf_op jit(solution)/shard_map/ppermute | solution.py:258
  13.5 36.6 %copy-start.8 = (f32[224,768]{1,0:T(8,128)}, f32[224,768]{1,0:T(8,128)S(1)}, u32[]{:S(2)}) copy-start(f32[224,768]{1,0:T(8,128)S(1)} %shard_map.88.refs_2_.refs_1_) | copy-start | bytes 2064388
  13.5 8.9 %copy-start.20 = (s32[448,1]{0,1:T(1,128)S(1)}, s32[448,1]{0,1:T(1,128)}, u32[]{:S(2)}) copy-start(s32[448,1]{0,1:T(1,128)} %param.10) | copy-start | bytes 5380
  13.5 9.0 %copy-start.21 = (s32[448]{0:T(512)S(1)}, s32[448]{0:T(512)}, u32[]{:S(2)}) copy-start(s32[448]{0:T(512)} %param.11) | copy-start | bytes 5380
  13.5 24.5 %copy-start.1 = (bf16[1,224,2048]{2,1,0:T(8,128)(2,1)S(1)}, bf16[1,224,2048]{2,1,0:T(8,128)(2,1)}, u32[]{:S(2)}) copy-start(bf16[1,224,2048]{2,1,0:T(8,128)(2,1)} %param.6) | copy-start | bytes 2752516
  13.5 33.3 %collective-permute-start.4 = (f32[224,768]{1,0:T(8,128)S(1)}, f32[224,768]{1,0:T(8,128)}, u32[]{:S(2)}, u32[]{:S(2)}) collective-permute-start(f32[224,768]{1,0:T(8,128)S(1)} %shard_map.88.refs_2_.refs_1_), channel_id=1, source_target_pairs={{0,8},{1,9},{2,10},{3,11},{4,12},{5,13},{6,14},{7,15},{8,16},{9,17... | collective-permute-start | bytes 2064392 | tf_op jit(solution)/shard_map/ppermute | solution.py:313
  15.5 31.3 %collective-permute-start.5 = (f32[224,768]{1,0:T(8,128)S(1)}, f32[224,768]{1,0:T(8,128)}, u32[]{:S(2)}, u32[]{:S(2)}) collective-permute-start(f32[224,768]{1,0:T(8,128)S(1)} %shard_map.88.refs_2_.refs_1_), channel_id=1, source_target_pairs={{8,0},{9,1},{10,2},{11,3},{12,4},{13,5},{14,6},{15,7},{16,8},{17,9... | collective-permute-start | bytes 2064392 | tf_op jit(solution)/shard_map/ppermute | solution.py:313
  20.8 16.5 %collective-permute-start.3 = (f32[224,256]{1,0:T(8,128)}, f32[224,256]{1,0:T(8,128)S(1)}, u32[]{:S(2)}, u32[]{:S(2)}) collective-permute-start(f32[224,256]{1,0:T(8,128)} %shard_map.89), channel_id=1, source_target_pairs={{0,128},{128,0},{64,192},{192,64},{1,129},{129,1},{65,193},{193,65... | collective-permute-start | bytes 688136 | tf_op jit(solution)/shard_map/ppermute | solution.py:274
  37.3 0.7 copy-start.18
  38.0 1.0 copy-start.13
  39.0 1.0 copy-start.15
  40.0 1.0 copy-start.17
  41.0 0.9 copy-start.19
  43.6 19.9 %collective-permute-start.6 = (f32[224,768]{1,0:T(8,128)}, f32[224,768]{1,0:T(8,128)}, u32[]{:S(2)}, u32[]{:S(2)}) collective-permute-start(f32[224,768]{1,0:T(8,128)} %shard_map.90.refs_3_.refs_1_), channel_id=1, source_target_pairs={{0,8},{1,9},{2,10},{3,11},{4,12},{5,13},{6,14},{7,15},{8,16},{9,17... | collective-permute-start | bytes 2064392 | tf_op jit(solution)/shard_map/ppermute | solution.py:313
  43.6 19.9 %collective-permute-start.7 = (f32[224,768]{1,0:T(8,128)}, f32[224,768]{1,0:T(8,128)}, u32[]{:S(2)}, u32[]{:S(2)}) collective-permute-start(f32[224,768]{1,0:T(8,128)} %shard_map.90.refs_3_.refs_1_), channel_id=1, source_target_pairs={{8,0},{9,1},{10,2},{11,3},{12,4},{13,5},{14,6},{15,7},{16,8},{17,9... | collective-permute-start | bytes 2064392 | tf_op jit(solution)/shard_map/ppermute | solution.py:313
  46.8 31.4 %collective-permute-start.8 = (f32[224,768]{1,0:T(8,128)}, f32[224,768]{1,0:T(8,128)}, u32[]{:S(2)}, u32[]{:S(2)}) collective-permute-start(f32[224,768]{1,0:T(8,128)} %collective-permute-done.4.refs_4_), channel_id=1, source_target_pairs={{0,8},{1,9},{2,10},{3,11},{4,12},{5,13},{6,14},{7,15},{8,16},{9,17... | collective-permute-start | bytes 2064392 | tf_op jit(solution)/shard_map/ppermute | solution.py:313
  46.8 31.4 %collective-permute-start.9 = (f32[224,768]{1,0:T(8,128)}, f32[224,768]{1,0:T(8,128)}, u32[]{:S(2)}, u32[]{:S(2)}) collective-permute-start(f32[224,768]{1,0:T(8,128)} %collective-permute-done.5.refs_5_), channel_id=1, source_target_pairs={{8,0},{9,1},{10,2},{11,3},{12,4},{13,5},{14,6},{15,7},{16,8},{17,9... | collective-permute-start | bytes 2064392 | tf_op jit(solution)/shard_map/ppermute | solution.py:313
  53.4 28.1 %all-to-all-start.1 = ((f32[8,64,768]{2,1,0:T(8,128)}), f32[8,64,768]{2,1,0:T(8,128)S(1)}, u32[]{:S(2)}, u32[]{:S(2)}) async-start(f32[8,64,768]{2,1,0:T(8,128)} %shard_map.91), calls=%async_computation.1 | async-start | bytes 3145728 | tf_op jit(solution)/shard_map/all_to_all | solution.py:308
  63.5 29.5 %collective-permute-start.10 = (f32[224,768]{1,0:T(8,128)}, f32[224,768]{1,0:T(8,128)}, u32[]{:S(2)}, u32[]{:S(2)}) collective-permute-start(f32[224,768]{1,0:T(8,128)} %collective-permute-done.6.refs_0_.refs_2_), channel_id=1, source_target_pairs={{0,8},{1,9},{2,10},{3,11},{4,12},{5,13},{6,14},{7,15},{8,16},{9,17... | collective-permute-start | bytes 2064392 | tf_op jit(solution)/shard_map/ppermute | solution.py:313
  63.5 29.5 %collective-permute-start.11 = (f32[224,768]{1,0:T(8,128)}, f32[224,768]{1,0:T(8,128)}, u32[]{:S(2)}, u32[]{:S(2)}) collective-permute-start(f32[224,768]{1,0:T(8,128)} %collective-permute-done.7.refs_1_.refs_3_), channel_id=1, source_target_pairs={{8,0},{9,1},{10,2},{11,3},{12,4},{13,5},{14,6},{15,7},{16,8},{17,9... | collective-permute-start | bytes 2064392 | tf_op jit(solution)/shard_map/ppermute | solution.py:313
  78.2 29.5 %collective-permute-start.12 = (f32[224,768]{1,0:T(8,128)}, f32[224,768]{1,0:T(8,128)}, u32[]{:S(2)}, u32[]{:S(2)}) collective-permute-start(f32[224,768]{1,0:T(8,128)} %collective-permute-done.8.refs_2_.refs_4_), channel_id=1, source_target_pairs={{0,8},{1,9},{2,10},{3,11},{4,12},{5,13},{6,14},{7,15},{8,16},{9,17... | collective-permute-start | bytes 2064392 | tf_op jit(solution)/shard_map/ppermute | solution.py:313
  78.2 29.5 %collective-permute-start.13 = (f32[224,768]{1,0:T(8,128)}, f32[224,768]{1,0:T(8,128)}, u32[]{:S(2)}, u32[]{:S(2)}) collective-permute-start(f32[224,768]{1,0:T(8,128)} %collective-permute-done.9.refs_3_.refs_5_), channel_id=1, source_target_pairs={{8,0},{9,1},{10,2},{11,3},{12,4},{13,5},{14,6},{15,7},{16,8},{17,9... | collective-permute-start | bytes 2064392 | tf_op jit(solution)/shard_map/ppermute | solution.py:313
  83.8 1.1 copy-start.7
  85.0 22.8 %all-to-all-start.2 = ((f32[8,64,768]{2,1,0:T(8,128)}), f32[8,64,768]{2,1,0:T(8,128)S(1)}, u32[]{:S(2)}, u32[]{:S(2)}) async-start(f32[8,64,768]{2,1,0:T(8,128)} %copy-done.7), calls=%async_computation.2 | async-start | bytes 3145728 | tf_op jit(solution)/shard_map/all_to_all | solution.py:308
  93.0 30.6 %collective-permute-start.14 = (f32[224,768]{1,0:T(8,128)}, f32[224,768]{1,0:T(8,128)}, u32[]{:S(2)}, u32[]{:S(2)}) collective-permute-start(f32[224,768]{1,0:T(8,128)} %collective-permute-done.10.refs_0_.refs_2_), channel_id=1, source_target_pairs={{0,8},{1,9},{2,10},{3,11},{4,12},{5,13},{6,14},{7,15},{8,16},{9,17... | collective-permute-start | bytes 2064392 | tf_op jit(solution)/shard_map/ppermute | solution.py:313
  93.0 32.3 %collective-permute-start.15 = (f32[224,768]{1,0:T(8,128)}, f32[224,768]{1,0:T(8,128)}, u32[]{:S(2)}, u32[]{:S(2)}) collective-permute-start(f32[224,768]{1,0:T(8,128)} %collective-permute-done.11.refs_1_.refs_3_), channel_id=1, source_target_pairs={{8,0},{9,1},{10,2},{11,3},{12,4},{13,5},{14,6},{15,7},{16,8},{17,9... | collective-permute-start | bytes 2064392 | tf_op jit(solution)/shard_map/ppermute | solution.py:313
  110.1 1.1 copy-start.6
  111.2 19.9 %all-to-all-start.3 = ((f32[8,64,768]{2,1,0:T(8,128)}), f32[8,64,768]{2,1,0:T(8,128)}, u32[]{:S(2)}, u32[]{:S(2)}) async-start(f32[8,64,768]{2,1,0:T(8,128)} %copy-done.6), calls=%async_computation.3 | async-start | bytes 3145728 | tf_op jit(solution)/shard_map/all_to_all | solution.py:308
  118.6 21.7 %collective-permute-start.16 = (f32[112,768]{1,0:T(8,128)}, f32[112,768]{1,0:T(8,128)}, u32[]{:S(2)}, u32[]{:S(2)}) collective-permute-start(f32[112,768]{1,0:T(8,128)} %slice.16), channel_id=1, source_target_pairs={{0,8},{1,9},{2,10},{3,11},{4,12},{5,13},{6,14},{7,15},{8,16},{9,17... | collective-permute-start | bytes 1032200 | tf_op jit(solution)/shard_map/ppermute | solution.py:313
  120.4 20.0 %collective-permute-start.17 = (f32[112,768]{1,0:T(8,128)}, f32[112,768]{1,0:T(8,128)}, u32[]{:S(2)}, u32[]{:S(2)}) collective-permute-start(f32[112,768]{1,0:T(8,128)} %slice.17), channel_id=1, source_target_pairs={{8,0},{9,1},{10,2},{11,3},{12,4},{13,5},{14,6},{15,7},{16,8},{17,9... | collective-permute-start | bytes 1032200 | tf_op jit(solution)/shard_map/ppermute | solution.py:313
  125.3 15.0 %collective-permute-start.18 = (f32[112,768]{1,0:T(8,128)}, f32[112,768]{1,0:T(8,128)}, u32[]{:S(2)}, u32[]{:S(2)}) collective-permute-start(f32[112,768]{1,0:T(8,128)} %slice.18), channel_id=1, source_target_pairs={{0,8},{1,9},{2,10},{3,11},{4,12},{5,13},{6,14},{7,15},{8,16},{9,17... | collective-permute-start | bytes 1032200 | tf_op jit(solution)/shard_map/ppermute | solution.py:313
  127.0 13.3 %collective-permute-start.19 = (f32[112,768]{1,0:T(8,128)}, f32[112,768]{1,0:T(8,128)}, u32[]{:S(2)}, u32[]{:S(2)}) collective-permute-start(f32[112,768]{1,0:T(8,128)} %slice.19), channel_id=1, source_target_pairs={{8,0},{9,1},{10,2},{11,3},{12,4},{13,5},{14,6},{15,7},{16,8},{17,9... | collective-permute-start | bytes 1032200 | tf_op jit(solution)/shard_map/ppermute | solution.py:313
  132.9 0.9 copy-start.10
  133.7 16.2 %all-to-all-start.4 = ((f32[8,32,768]{2,1,0:T(8,128)}), f32[8,32,768]{2,1,0:T(8,128)}, u32[]{:S(2)}, u32[]{:S(2)}) async-start(f32[8,32,768]{2,1,0:T(8,128)} %copy-done.10), calls=%async_computation.4 | async-start | bytes 1572864 | tf_op jit(solution)/shard_map/all_to_all | solution.py:308
  151.6 0.9 copy-start.11
  152.5 17.3 %all-to-all-start.5 = ((f32[8,32,768]{2,1,0:T(8,128)}), f32[8,32,768]{2,1,0:T(8,128)}, u32[]{:S(2)}, u32[]{:S(2)}) async-start(f32[8,32,768]{2,1,0:T(8,128)} %copy-done.11), calls=%async_computation.5 | async-start | bytes 1572864 | tf_op jit(solution)/shard_map/all_to_all | solution.py:308
  158.1 1.1 copy-start.9
  163.3 1.1 copy-start.2
  168.7 1.1 copy-start.4
  169.8 1.3 copy-start.3
  171.1 1.3 copy-start.5

commit v4 on v2

--- a/solution.py
+++ b/solution.py
@@ -24,13 +24,15 @@
 HALF = 256
 WIDE = 3 * HALF
 SLOTS = 16
+USED = 14
+SENT = 4 * USED
 PLANE = 8
 RING = 8
 
-VMEM = pltpu.CompilerParams(vmem_limit_bytes=48 * 1024 * 1024)
-
-
-def call(kernel, out, *, grid=None, in_specs=None, out_specs=None, flops=0, moved=0):
+VMEM = pltpu.CompilerParams(vmem_limit_bytes=12 * 1024 * 1024)
+
+
+def call(kernel, out, *, grid=None, in_specs=None, out_specs=None, flops=0, moved=0, aliases=None):
     extra = {}
     if grid is not None:
         extra = dict(grid=grid, in_specs=in_specs, out_specs=out_specs)
@@ -40,6 +42,7 @@
         kernel,
         out_shape=out,
         compiler_params=VMEM,
+        input_output_aliases=aliases or {},
         cost_estimate=pl.CostEstimate(flops=flops, bytes_accessed=moved, transcendentals=0),
         **extra,
     )
@@ -122,18 +125,18 @@
     def place_in(offsets):
         at = jnp.full((FINE, 1), none, I32)
         for k, offset in offsets:
-            at = jnp.where(away == k, source_xy * 64 + offset + slot, at)
+            at = jnp.where(away == k, source_xy * 128 + offset + slot, at)
         return at
 
     groups = (
-        place_in(((0, 0), (7, 32), (1, 48))),
-        place_in(((6, 32), (2, 48))),
-        place_in(((5, 32), (3, 48))),
-        place_in(((4, 32),)),
-        place_in(((0, 16),)),
-        place_in(((7, 0), (1, 16))),
-        place_in(((6, 0), (2, 16))),
-        place_in(((5, 0), (3, 16), (4, 48))),
+        place_in(((0, 0), (7, 28), (1, 42))),
+        place_in(((6, 28), (2, 42))),
+        place_in(((5, 28), (3, 42))),
+        place_in(((4, 28),)),
+        place_in(((0, 14),)),
+        place_in(((7, 0), (1, 14))),
+        place_in(((6, 0), (2, 14))),
+        place_in(((5, 0), (3, 14), (4, 42))),
     )
     lane = lax.broadcasted_iota(I32, (FINE, 128), 1)
     out = jnp.full((FINE, 128), none, I32)
@@ -143,9 +146,8 @@
 
 
 def asked_rows(asked, plane):
-    table = jnp.sum(asked[...], axis=0)
     here = lax.broadcasted_iota(I32, (RING, 128), 0) == plane
-    return jnp.sum(jnp.where(here, table, 0), axis=0, keepdims=True)
+    return jnp.sum(jnp.where(here, asked[...], 0), axis=0, keepdims=True)
 
 
 def pick_from(asked, plane, values):
@@ -156,18 +158,13 @@
     return split_dot(chosen, values, ((0,), (0,)))
 
 
-def pick_kernel(parts, place, asked, *refs):
+def pick_kernel(planes, place, asked, *refs):
     out = refs[-1]
     plane = lax.div(place[0], PLANE)
-    n = 0
-    for away, row, pieces in parts:
-        values = refs[n][...]
-        if pieces == 2:
-            values = jnp.concatenate([values, refs[n + 1][...]], axis=0)
-        n += pieces
-        got = pick_from(asked, (plane + away + RING) & (RING - 1), values)
+    for n, away in enumerate(planes):
+        got = pick_from(asked, (plane + away + RING) & (RING - 1), refs[n][...])
         for d in range(PLANE):
-            out[d, row : row + SLOTS, :] = got[d * SLOTS : (d + 1) * SLOTS]
+            out[d, n * USED : (n + 1) * USED, :] = got[d * SLOTS : d * SLOTS + USED]
 
 
 def held_kernel(*refs):
@@ -182,7 +179,6 @@
         in_specs=[pl.BlockSpec(memory_space=pl.ANY)] * (n + len(until)),
         out_specs=(pl.BlockSpec(memory_space=pl.ANY),) * n,
         input_output_aliases={i: i for i in range(n)},
-        cost_estimate=pl.CostEstimate(flops=0, bytes_accessed=1 << 20, transcendentals=0),
     )(*arrays, *until)
 
 
@@ -209,34 +205,46 @@
 
 def far_part(codes, lane, far, low, high):
     at = codes[:, lane : lane + 1]
-    xy, row = at >> 6, at & 63
+    xy, row = at >> 7, at & 127
     here = (at >= 0) & (row >= low) & (row < high)
     at = jnp.where(here, xy * (high - low) + row - low, -1)
     return far_dot(at, far[:, low:high, :])
 
 
-def gather_kernel(parts, codes, near, far1, far2, far3, out):
+def near_part(near):
     own = lax.broadcasted_iota(I32, (FINE, ROWS), 0) >> 1
     chosen = jnp.where(
         lax.broadcasted_iota(I32, (FINE, ROWS), 1) == own, own_share, 0.0
     ).astype(BF16)
-    total = split_dot(chosen, near[...])
-    far = (far1, far2, far3)
+    return split_dot(chosen, near[...])
+
+
+def gather_kernel(parts, codes, near, *refs):
+    total = near_part(near)
     for lane, exchange, low, high in parts:
-        total = total + far_part(codes, lane, far[exchange], low, high)
-    out[...] = total
+        total = total + far_part(codes, lane, refs[exchange], low, high)
+    refs[-1][...] = total
+
+
+def doubled(values):
+    row = lax.broadcasted_iota(I32, (128, 256), 0)
+    lane = lax.broadcasted_iota(I32, (128, 256), 1) >> 1
+    twice = jnp.where(row == lane, 1.0, 0.0).astype(BF16)
+    high = values.astype(BF16)
+    low = (values - high.astype(F32)).astype(BF16)
+    return jnp.dot(high, twice, preferred_element_type=F32) + jnp.dot(
+        low, twice, preferred_element_type=F32
+    )
 
 
 def final_kernel(codes, *refs):
-    lane = lax.broadcasted_iota(I32, (FINE, 128), 1) >> 1
     first_half = pl.program_id(0) < 2
     at = jnp.where(first_half, codes[:, 3:4], codes[:, 7:8])
+    at = jnp.where(at >= 0, (at >> 7) * SENT + (at & 127), -1)
     for state in range(3):
         acc0, acc1, far, out = (refs[3 * k + state] for k in range(4))
         acc = jnp.where(first_half, acc0[...], acc1[...])
-        mixed = acc + far_dot(at, far[...])
-        out[:, 0:128] = jnp.take_along_axis(mixed, lane, axis=1)
-        out[:, 128:256] = jnp.take_along_axis(mixed, lane + 64, axis=1)
+        out[...] = doubled(acc + far_dot(at, far[...]))
 
 
 PLANES = [[z * PLANE + p for p in range(PLANE)] for z in range(RING)]
@@ -250,6 +258,23 @@
     place = jnp.stack([lax.axis_index("shard"), lax.axis_index("dp")]).astype(I32)
     grad = grad_parts[0]
 
+    wanted, codes = call(
+        index_kernel,
+        (shape(PLANE, RING, 128, dtype=I32), shape(FINE, 128, dtype=I32)),
+        in_specs=[scalar(), whole(), whole(), whole()],
+        moved=1 << 20,
+    )(
+        place,
+        partner_device,
+        partner_device.reshape(1, FINE),
+        partner_column.reshape(FINE, 1),
+    )
+    asked = jnp.sum(
+        lax.all_to_all(
+            wanted, "shard", split_axis=0, concat_axis=0, axis_index_groups=PLANES, tiled=True
+        ),
+        axis=0,
+    )
     sends = call(
         send_core_kernel,
         (shape(ROWS, 2 * HALF),) * 2,
@@ -293,30 +318,16 @@
             )(place, grad, got, got_y, weight, first, second)
         )
 
-    wanted, codes = call(
-        index_kernel,
-        (shape(PLANE, RING, 128, dtype=I32), shape(FINE, 128, dtype=I32)),
-        in_specs=[scalar(), whole(), whole(), whole()],
-        moved=1 << 20,
-    )(
-        place,
-        partner_device,
-        partner_device.reshape(1, FINE),
-        partner_column.reshape(FINE, 1),
-    )
-    asked = lax.all_to_all(
-        wanted, "shard", split_axis=0, concat_axis=0, axis_index_groups=PLANES, tiled=True
-    )
-
-    def pick(parts, sources, after=()):
+    def pick(planes, sources, after=()):
+        after = (*after, token(sources))
         return call(
-            lambda *refs: pick_kernel(parts, *refs),
-            shape(PLANE, SLOTS * len(parts), WIDE),
+            lambda *refs: pick_kernel(planes, *refs),
+            shape(PLANE, SENT, WIDE),
             in_specs=[scalar()]
             + [whole()] * (1 + len(sources))
             + [pl.BlockSpec(memory_space=pl.ANY)] * len(after),
-            flops=len(parts) * SLOTS * PLANE * ROWS * WIDE * 4,
-            moved=(len(sources) + 2) << 20,
+            flops=4 * SLOTS * PLANE * ROWS * WIDE * 4,
+            moved=5 << 20,
         )(place, asked, *sources, *after)
 
     def to_plane(rows):
@@ -331,25 +342,20 @@
     one[0] = hold(one[0], asked)
     two = [around(pair) for pair in one]
     three = [around(pair) for pair in two]
-    far1 = to_plane(pick(((0, 0, 1), (0, 16, 1), (-1, 32, 1), (1, 48, 1)), (*state, *one[0])))
-    far2 = to_plane(
-        pick(((-1, 0, 1), (1, 16, 1), (-2, 32, 1), (2, 48, 1)), (*one[1], *two[0]), (far1, token(two[0])))
-    )
-    far3 = to_plane(
-        pick(((-2, 0, 1), (2, 16, 1), (-3, 32, 1), (3, 48, 1)), (*two[1], *three[0]), (far2, token(three[0])))
-    )
-    middle = ROWS // 2
-    four = [around((pair[0][:middle], pair[1][middle:])) for pair in three]
-    rows = pick(
-        ((-3, 0, 1), (3, 16, 1), (4, 32, 2), (4, 48, 2)), (*three[1], *four[0], *four[1]), (far3, token(four[1]))
-    )
-    far4 = to_plane(rows)
+    four = (
+        lax.ppermute(three[0][0], "shard", UP),
+        lax.ppermute(three[1][1], "shard", DOWN),
+    )
+    far1 = to_plane(pick((0, 0, -1, 1), (*state, *one[0])))
+    far2 = to_plane(pick((-1, 1, -2, 2), (*one[1], *two[0]), (far1,)))
+    far3 = to_plane(pick((-2, 2, -3, 3), (*two[1], *three[0]), (far2,)))
+    far4 = to_plane(pick((-3, 3, 4, 4), (*three[1], *four), (far3,)))
 
     acc = []
     for half, parts in enumerate(
         (
-            ((0, 0, 0, 16), (0, 0, 32, 64), (1, 1, 32, 64), (2, 2, 32, 64)),
-            ((4, 0, 16, 32), (5, 1, 0, 32), (6, 2, 0, 32)),
+            ((0, 0, 0, 56), (1, 1, 24, 56), (2, 2, 24, 56)),
+            ((4, 0, 8, 32), (5, 1, 0, 32), (6, 2, 0, 32)),
         )
     ):
         acc.append(
@@ -361,7 +367,7 @@
                     pl.BlockSpec((FINE, 128), lambda i: (0, 0)),
                     pl.BlockSpec((ROWS, HALF), lambda i: (0, i)),
                 ]
-                + [pl.BlockSpec((PLANE, 64, HALF), lambda i: (0, 0, i))] * 3,
+                + [pl.BlockSpec((PLANE, SENT, HALF), lambda i: (0, 0, i))] * 3,
                 out_specs=pl.BlockSpec((FINE, HALF), lambda i: (0, i)),
                 flops=FINE * 1120 * WIDE * 4,
                 moved=8 << 20,
@@ -376,7 +382,7 @@
         return pl.BlockSpec((FINE, 128), index)
 
     def far_block(state):
-        return pl.BlockSpec((PLANE, 64, 128), lambda j: (0, 0, state * 2 + lax.rem(j, 2)))
+        return pl.BlockSpec((PLANE, SENT, 128), lambda j: (0, 0, state * 2 + lax.rem(j, 2)))
 
     return call(
         final_kernel,

time: 180 us -> 175 us (0.972); the launches traced: 176 us -> 174 us
  local copies, waits for them, and re-layouts: 30.8 us -> 16.9 us
  blocking collectives: 0 us -> 13.5 us
  starting transfers between devices: 66.4 us -> 57.7 us
  waiting for transfers between devices: 46.3 us -> 54.6 us
  Pallas kernels: 31.9 us -> 29.7 us
    ppermute x8 -> x6, waiting for transfers between devices: 30.2 us -> 16.3 us  [around(): lax.ppermute(pair[0], 'shard', UP)]
    all_to_all x0 -> x1, blocking collectives: none -> 13.5 us  [on_device(): lax.all_to_all(wanted, 'shard', split_axis=0, concat_axis=0, axis_index_g...]
    ppermute x8 -> x6, waiting for transfers between devices: 0.37 us -> 10.1 us  [around(): lax.ppermute(pair[1], 'shard', DOWN)]
    unnamed x81 -> x59, local copies, waits for them, and re-layouts: 25.9 us -> 16.8 us
    ppermute x0 -> x2, waiting for transfers between devices: none -> 8.36 us  [the longest x1 8.35 us: on_device(): lax.ppermute(three[0][0], 'shard', UP)]
    all_to_all x1 -> x0, starting transfers between devices: 7.17 us -> none  [on_device(): lax.all_to_all(wanted, 'shard', split_axis=0, concat_axis=0, axis_index_g...]
    ppermute x8 -> x6, starting transfers between devices: 26.8 us -> 21.2 us  [around(): lax.ppermute(pair[1], 'shard', DOWN)]
    all_to_all x4, waiting for transfers between devices: 7.8 us -> 12.7 us  [to_plane(): lax.all_to_all(rows, 'shard', split_axis=0, concat_axis=0, axis_index_gro...]
  transfers between devices with their start and end apart: 25 -> 22, of which waited for: 13 -> 10; matrix products, arithmetic and copies ran while one was open for 3% -> 1% of each run, Pallas kernels for 12% -> 10%
where the time goes in v4:
time: 175 us; the launch traced here: 174 us
  starting transfers between devices  57.7 us (33%)
  waiting for transfers between devices  54.6 us (31%)
  Pallas kernels  29.7 us (17%)
  local copies, waits for them, and re-layouts  16.9 us (10%)
  blocking collectives  13.5 us (8%)
    all_to_all x4, starting transfers between devices, to_plane(): lax.all_to_all(rows, 'shard', split_axis=0, concat_axis=0, axis_index_gro...  28 us
    ppermute x6, starting transfers between devices, around(): lax.ppermute(pair[1], 'shard', DOWN)  21.2 us
    unnamed x59, local copies, waits for them, and re-layouts  16.8 us
    ppermute x6, waiting for transfers between devices, around(): lax.ppermute(pair[0], 'shard', UP)  16.3 us
    all_to_all x1, blocking collectives, on_device(): lax.all_to_all(wanted, 'shard', split_axis=0, concat_axis=0, axis_index_g...  13.5 us
    all_to_all x4, waiting for transfers between devices, to_plane(): lax.all_to_all(rows, 'shard', split_axis=0, concat_axis=0, axis_index_gro...  12.7 us
    pallas_call x4, Pallas kernels, pick(): call(lambda *refs: pick_kernel(planes, *refs), shape(PLANE, SENT, WIDE),...  11.5 us
    ppermute x6, waiting for transfers between devices, around(): lax.ppermute(pair[1], 'shard', DOWN)  10.1 us
  transfers between devices with their start and end apart: 22, of which 10 were waited for; matrix products, arithmetic and copies ran while one was open for 1% of the time, Pallas kernels for 10%

profile of v4, /device:TPU:2, one launch (start us, length us, event | category | flops | bytes accessed | tf_op | source)
XLA Modules:
  0.0 174.0 jit_solution(7700531992234447348)
XLA Ops:
  0.6 0.1 pad_add_fusion.place.refs_0_
  0.7 1.2 copy-done
  1.9 0.6 shard_map.86
  2.5 0.1 collective-permute-start
  2.6 0.0 copy-start.23
  2.6 0.0 copy-start.24
  2.6 0.5 collective-permute-start.2
  3.1 1.3 collective-permute-done.refs_2_
  4.4 0.6 shard_map.87
  5.0 1.7 collective-permute-start.1
  6.7 0.6 shard_map.89
  7.2 0.5 collective-permute-start.3
  7.8 5.8 %collective-permute-done.1.refs_3_ = f32[224,256]{1,0:T(8,128)S(1)} collective-permute-done((f32[224,256]{1,0:T(8,128)S(1)}, f32[224,256]{1,0:T(8,128)S(1)}, u32[]{:S(2)}, u32[]{:S(2)}) %collective-permute-start.1) | collective-permute-done | bytes 229408 | tf_op jit(solution)/shard_map/ppermute | solution.py:300
  13.5 0.8 shard_map.88.refs_0_.refs_2_.refs_1_
  14.3 2.0 %collective-permute-start.4 = (f32[224,768]{1,0:T(8,128)S(1)}, f32[224,768]{1,0:T(8,128)S(1)}, u32[]{:S(2)}, u32[]{:S(2)}) collective-permute-start(f32[224,768]{1,0:T(8,128)S(1)} %shard_map.88.refs_0_.refs_2_.refs_1_), channel_id=1, source_target_pairs={{0,8},{1,9},{2,10},{3,11},{4,12},{5,13},{6,14},{7,15},{8,16},{9,17... | collective-permute-start | bytes 2064392 | tf_op jit(solution)/shard_map/ppermute | solution.py:339
  16.3 4.0 %collective-permute-start.5 = (f32[224,768]{1,0:T(8,128)S(1)}, f32[224,768]{1,0:T(8,128)S(1)}, u32[]{:S(2)}, u32[]{:S(2)}) collective-permute-start(f32[224,768]{1,0:T(8,128)S(1)} %shard_map.88.refs_0_.refs_2_.refs_1_), channel_id=1, source_target_pairs={{8,0},{9,1},{10,2},{11,3},{12,4},{13,5},{14,6},{15,7},{16,8},{17,9... | collective-permute-start | bytes 2064392 | tf_op jit(solution)/shard_map/ppermute | solution.py:339
  20.3 0.8 shard_map.90.refs_1_.refs_3_
  21.1 3.2 %collective-permute-start.7 = (f32[224,768]{1,0:T(8,128)S(1)}, f32[224,768]{1,0:T(8,128)}, u32[]{:S(2)}, u32[]{:S(2)}) collective-permute-start(f32[224,768]{1,0:T(8,128)S(1)} %shard_map.90.refs_1_.refs_3_), channel_id=1, source_target_pairs={{8,0},{9,1},{10,2},{11,3},{12,4},{13,5},{14,6},{15,7},{16,8},{17,9... | collective-permute-start | bytes 2064392 | tf_op jit(solution)/shard_map/ppermute | solution.py:339
  24.3 0.1 copy.12.dev
  24.5 0.1 copy.13.col
  24.6 1.4 shard_map.85
  26.0 0.7 copy-done.19
  26.7 13.5 %all_to_all.25 = s32[8,8,128]{2,1,0:T(8,128)S(1)} all-to-all(s32[8,8,128]{2,1,0:T(8,128)S(1)} %get-tuple-element.11), channel_id=1, replica_groups={{0,1,2,3,4,5,6,7},{8,9,10,11,12,13,14,15},{16,17,18,19,20,21,22,23},{24..., dimensions={0} | all-to-all | bytes 65536 | tf_op jit(solution)/shard_map/all_to_all | solution.py:273
  40.2 0.6 reduce_sum.9.refs_2_.refs_1_
  40.8 0.8 copy-done.13
  41.7 0.8 copy-done.16
  42.5 3.2 %collective-permute-start.9 = (f32[224,768]{1,0:T(8,128)}, f32[224,768]{1,0:T(8,128)}, u32[]{:S(2)}, u32[]{:S(2)}) collective-permute-start(f32[224,768]{1,0:T(8,128)} %get-tuple-element.14.refs_3_.refs_5_), channel_id=1, source_target_pairs={{8,0},{9,1},{10,2},{11,3},{12,4},{13,5},{14,6},{15,7},{16,8},{17,9... | collective-permute-start | bytes 2064392 | tf_op jit(solution)/shard_map/ppermute | solution.py:339
  45.8 5.2 %collective-permute-done.7.refs_1_.refs_3_ = f32[224,768]{1,0:T(8,128)} collective-permute-done((f32[224,768]{1,0:T(8,128)S(1)}, f32[224,768]{1,0:T(8,128)}, u32[]{:S(2)}, u32[]{:S(2)}) %collective-permute-start.7) | collective-permute-done | bytes 688160 | tf_op jit(solution)/shard_map/ppermute | solution.py:339
  51.0 3.8 %collective-permute-start.11 = (f32[224,768]{1,0:T(8,128)}, f32[224,768]{1,0:T(8,128)}, u32[]{:S(2)}, u32[]{:S(2)}) collective-permute-start(f32[224,768]{1,0:T(8,128)} %collective-permute-done.7.refs_1_.refs_3_), channel_id=1, source_target_pairs={{8,0},{9,1},{10,2},{11,3},{12,4},{13,5},{14,6},{15,7},{16,8},{17,9... | collective-permute-start | bytes 2064392 | tf_op jit(solution)/shard_map/ppermute | solution.py:339
  54.8 1.1 copy-done.14
  55.9 1.1 copy-done.17
  57.0 1.1 copy-done.15
  58.1 0.2 copy-done.18
  58.3 1.2 shard_map.93
  59.5 1.1 copy-done.11
  60.5 7.5 %all-to-all-start.1 = ((f32[8,56,768]{2,1,0:T(8,128)}), f32[8,56,768]{2,1,0:T(8,128)S(1)}, u32[]{:S(2)}, u32[]{:S(2)}) async-start(f32[8,56,768]{2,1,0:T(8,128)} %copy-done.11), calls=%async_computation.1 | async-start | bytes 2752512 | tf_op jit(solution)/shard_map/all_to_all | solution.py:334
  68.0 7.2 %collective-permute-done.8.refs_2_.refs_4_ = f32[224,768]{1,0:T(8,128)} collective-permute-done((f32[224,768]{1,0:T(8,128)}, f32[224,768]{1,0:T(8,128)}, u32[]{:S(2)}, u32[]{:S(2)}) %collective-permute-start.8) | collective-permute-done | bytes 688160 | tf_op jit(solution)/shard_map/ppermute | solution.py:339
  75.3 3.2 %collective-permute-start.13 = (f32[224,768]{1,0:T(8,128)}, f32[224,768]{1,0:T(8,128)}, u32[]{:S(2)}, u32[]{:S(2)}) collective-permute-start(f32[224,768]{1,0:T(8,128)} %collective-permute-done.9.refs_3_.refs_5_), channel_id=1, source_target_pairs={{8,0},{9,1},{10,2},{11,3},{12,4},{13,5},{14,6},{15,7},{16,8},{17,9... | collective-permute-start | bytes 2064392 | tf_op jit(solution)/shard_map/ppermute | solution.py:339
  78.5 2.1 %collective-permute-done.11.refs_1_.refs_3_ = f32[224,768]{1,0:T(8,128)} collective-permute-done((f32[224,768]{1,0:T(8,128)}, f32[224,768]{1,0:T(8,128)}, u32[]{:S(2)}, u32[]{:S(2)}) %collective-permute-start.11) | collective-permute-done | bytes 688160 | tf_op jit(solution)/shard_map/ppermute | solution.py:339
  80.6 3.7 %collective-permute-start.15 = (f32[224,768]{1,0:T(8,128)}, f32[224,768]{1,0:T(8,128)}, u32[]{:S(2)}, u32[]{:S(2)}) collective-permute-start(f32[224,768]{1,0:T(8,128)} %collective-permute-done.11.refs_1_.refs_3_), channel_id=1, source_target_pairs={{8,0},{9,1},{10,2},{11,3},{12,4},{13,5},{14,6},{15,7},{16,8},{17,9... | collective-permute-start | bytes 2064392 | tf_op jit(solution)/shard_map/ppermute | solution.py:339
  84.3 2.8 %shard_map.95 = f32[8,56,768]{2,1,0:T(8,128)S(1)} custom-call(s32[2]{0:T(128)S(1)} %pad_add_fusion.place.refs_0_, s32[8,128]{1,0:T(8,128)S(1)} %copy-done.26, f32[224,768]{1,0:T(8,128)} %collective-permute-done.6.refs_0_.refs_2_, f32[224,768]{1,0:T(8,128)} %collective-permute-done.7.refs_1_.refs_3_, f32[224,768]{1,0:T(8,128)} %collective-permute-done.8.refs_2_.refs_4_, ...), custom_call_target="tpu_custom_call" | custom-call | flops 352321536 | bytes 5242880 | tf_op jit(solution)/shard_map/pallas_call | solution.py:323
  87.1 0.0 copy-start.12
  87.2 1.1 copy-done.12
  88.2 7.5 %all-to-all-start.2 = ((f32[8,56,768]{2,1,0:T(8,128)}), f32[8,56,768]{2,1,0:T(8,128)S(1)}, u32[]{:S(2)}, u32[]{:S(2)}) async-start(f32[8,56,768]{2,1,0:T(8,128)} %copy-done.12), calls=%async_computation.2 | async-start | bytes 2752512 | tf_op jit(solution)/shard_map/all_to_all | solution.py:334
  95.7 9.1 %collective-permute-done.12.refs_2_.refs_4_ = f32[224,768]{1,0:T(8,128)} collective-permute-done((f32[224,768]{1,0:T(8,128)}, f32[224,768]{1,0:T(8,128)}, u32[]{:S(2)}, u32[]{:S(2)}) %collective-permute-start.12) | collective-permute-done | bytes 688160 | tf_op jit(solution)/shard_map/ppermute | solution.py:339
  104.8 2.8 %collective-permute-done.15.refs_1_.refs_3_ = f32[224,768]{1,0:T(8,128)} collective-permute-done((f32[224,768]{1,0:T(8,128)}, f32[224,768]{1,0:T(8,128)}, u32[]{:S(2)}, u32[]{:S(2)}) %collective-permute-start.15) | collective-permute-done | bytes 688160 | tf_op jit(solution)/shard_map/ppermute | solution.py:339
  107.5 3.7 %collective-permute-start.17 = (f32[224,768]{1,0:T(8,128)}, f32[224,768]{1,0:T(8,128)}, u32[]{:S(2)}, u32[]{:S(2)}) collective-permute-start(f32[224,768]{1,0:T(8,128)} %collective-permute-done.15.refs_1_.refs_3_), channel_id=1, source_target_pairs={{8,0},{9,1},{10,2},{11,3},{12,4},{13,5},{14,6},{15,7},{16,8},{17,9... | collective-permute-start | bytes 2064392 | tf_op jit(solution)/shard_map/ppermute | solution.py:347
  111.3 3.7 %shard_map.97 = f32[8,56,768]{2,1,0:T(8,128)} custom-call(s32[2]{0:T(128)S(1)} %pad_add_fusion.place.refs_0_, s32[8,128]{1,0:T(8,128)S(1)} %copy-done.26, f32[224,768]{1,0:T(8,128)S(1)} %collective-permute-done.10.refs_0_.refs_2_, f32[224,768]{1,0:T(8,128)} %collective-permute-done.11.refs_1_.refs_3_, f32[224,768]{1,0:T(8,128)} %collective-permute-done.12.refs_2_.refs_4_, ...), custom_call_target="tpu_custom_call" | custom-call | flops 352321536 | bytes 5242880 | tf_op jit(solution)/shard_map/pallas_call | solution.py:323
  115.0 7.5 %all-to-all-start.3 = ((f32[8,56,768]{2,1,0:T(8,128)}), f32[8,56,768]{2,1,0:T(8,128)S(1)}, u32[]{:S(2)}, u32[]{:S(2)}) async-start(f32[8,56,768]{2,1,0:T(8,128)} %shard_map.97), calls=%async_computation.3 | async-start | bytes 2752512 | tf_op jit(solution)/shard_map/all_to_all | solution.py:334
  122.5 8.4 %collective-permute-done.16.refs_2_.refs_4_ = f32[224,768]{1,0:T(8,128)} collective-permute-done((f32[224,768]{1,0:T(8,128)}, f32[224,768]{1,0:T(8,128)}, u32[]{:S(2)}, u32[]{:S(2)}) %collective-permute-start.16) | collective-permute-done | bytes 688160 | tf_op jit(solution)/shard_map/ppermute | solution.py:346
  130.8 7.2 %all-to-all-done.3.refs_4_.refs_6_ = f32[8,56,768]{2,1,0:T(8,128)S(1)} async-done(((f32[8,56,768]{2,1,0:T(8,128)}), f32[8,56,768]{2,1,0:T(8,128)S(1)}, u32[]{:S(2)}, u32[]{:S(2)}) %all-to-all-start.3) | async-done | bytes 1376288 | tf_op jit(solution)/shard_map/all_to_all | solution.py:334
  138.0 3.8 %shard_map.101 = f32[8,56,768]{2,1,0:T(8,128)} custom-call(s32[2]{0:T(128)S(1)} %pad_add_fusion.place.refs_0_, s32[8,128]{1,0:T(8,128)S(1)} %copy-done.26, f32[224,768]{1,0:T(8,128)S(1)} %collective-permute-done.14.refs_0_.refs_2_, f32[224,768]{1,0:T(8,128)} %collective-permute-done.15.refs_1_.refs_3_, f32[224,768]{1,0:T(8,128)} %collective-permute-done.16.refs_2_.refs_4_, ...), custom_call_target="tpu_custom_call" | custom-call | flops 352321536 | bytes 5242880 | tf_op jit(solution)/shard_map/pallas_call | solution.py:323
  141.8 5.6 %all-to-all-start.4 = ((f32[8,56,768]{2,1,0:T(8,128)}), f32[8,56,768]{2,1,0:T(8,128)S(1)}, u32[]{:S(2)}, u32[]{:S(2)}) async-start(f32[8,56,768]{2,1,0:T(8,128)} %shard_map.101), calls=%async_computation.4 | async-start | bytes 2752512 | tf_op jit(solution)/shard_map/all_to_all | solution.py:334
  147.4 1.3 copy-done.4
  148.8 1.3 copy-done.6
  150.1 1.3 copy-done.8
  151.4 0.9 copy-done.20
  152.4 3.2 %shard_map.98.refs_0_.refs_1_.refs_2_ = f32[448,768]{1,0:T(8,128)S(1)} custom-call(s32[448,128]{1,0:T(8,128)S(1)} %copy-done.20, f32[224,768]{1,0:T(8,128)S(1)} %shard_map.88.refs_0_.refs_2_.refs_1_, f32[8,56,768]{2,1,0:T(8,128)S(1)} %copy-done.4, f32[8,56,768]{2,1,0:T(8,128)S(1)} %copy-done.6, f32[8,56,768]{2,1,0:T(8,128)S(1)} %copy-done.8), custom_call_target="tpu_custom_call" | custom-call | flops 1541406720 | bytes 8388608 | tf_op jit(solution)/shard_map/pallas_call | solution.py:362
  155.6 2.8 %shard_map.99.refs_3_.refs_4_.refs_5_ = f32[448,768]{1,0:T(8,128)S(1)} custom-call(s32[448,128]{1,0:T(8,128)S(1)} %copy-done.21, f32[224,768]{1,0:T(8,128)S(1)} %copy-done.10, f32[8,56,768]{2,1,0:T(8,128)S(1)} %copy-done.4, f32[8,56,768]{2,1,0:T(8,128)S(1)} %copy-done.6, f32[8,56,768]{2,1,0:T(8,128)S(1)} %copy-done.8), custom_call_target="tpu_custom_call" | custom-call | flops 1541406720 | bytes 8388608 | tf_op jit(solution)/shard_map/pallas_call | solution.py:362
  158.4 0.0 copy-start.1
  158.4 1.1 copy-done.1
  159.5 5.6 %all-to-all-done.4.refs_6_.refs_7_.refs_8_ = f32[8,56,768]{2,1,0:T(8,128)S(1)} async-done(((f32[8,56,768]{2,1,0:T(8,128)}), f32[8,56,768]{2,1,0:T(8,128)S(1)}, u32[]{:S(2)}, u32[]{:S(2)}) %all-to-all-start.4) | async-done | bytes 1376288 | tf_op jit(solution)/shard_map/all_to_all | solution.py:334
  165.1 1.3 copy-done.2
  166.4 7.6 %shard_map.102 = (f32[448,1024]{1,0:T(8,128)}, f32[448,1024]{1,0:T(8,128)}, f32[448,1024]{1,0:T(8,128)}) custom-call(s32[448,128]{1,0:T(8,128)S(1)} %copy-done.22, f32[448,768]{1,0:T(8,128)S(1)} %shard_map.98.refs_0_.refs_1_.refs_2_, f32[448,768]{1,0:T(8,128)S(1)} %shard_map.98.refs_0_.refs_1_.refs_2_, f32[448,768]{1,0:T(8,128)S(1)} %shard_map.98.refs_0_.refs_1_.refs_2_, ...), custom_call_target="tpu_custom_call" | custom-call | flops 1409286144 | bytes 12582912 | tf_op jit(solution)/shard_map/pallas_call | solution.py:387
  (61 shorter events, 0.1 us)
Async XLA Ops:
  0.7 1.2 copy-start
  2.5 1.9 %collective-permute-start = (f32[224,512]{1,0:T(8,128)S(1)}, f32[224,512]{1,0:T(8,128)S(1)}, u32[]{:S(2)}, u32[]{:S(2)}) collective-permute-start(f32[224,512]{1,0:T(8,128)S(1)} %get-tuple-element.10), channel_id=1, source_target_pairs={{0,64},{64,0},{128,192},{192,128},{1,65},{65,1},{129,193},{193,129... | collective-permute-start | bytes 1376264 | tf_op jit(solution)/shard_map/ppermute | solution.py:284
  2.6 10.9 %copy-start.23 = (f32[224,512]{1,0:T(8,128)S(1)}, f32[224,512]{1,0:T(8,128)}, u32[]{:S(2)}) copy-start(f32[224,512]{1,0:T(8,128)} %refs_4_.3) | copy-start | bytes 1376260
  2.6 10.9 %copy-start.24 = (f32[224,512]{1,0:T(8,128)S(1)}, f32[224,512]{1,0:T(8,128)}, u32[]{:S(2)}) copy-start(f32[224,512]{1,0:T(8,128)} %refs_5_.3) | copy-start | bytes 1376260
  2.6 10.9 %copy-start.25 = (f32[224,512]{1,0:T(8,128)S(1)}, f32[224,512]{1,0:T(8,128)}, u32[]{:S(2)}) copy-start(f32[224,512]{1,0:T(8,128)} %refs_6_.3) | copy-start | bytes 1376260
  2.6 4.0 %collective-permute-start.2 = (f32[224,512]{1,0:T(8,128)S(1)}, f32[224,512]{1,0:T(8,128)S(1)}, u32[]{:S(2)}, u32[]{:S(2)}) collective-permute-start(f32[224,512]{1,0:T(8,128)S(1)} %get-tuple-element.12), channel_id=1, source_target_pairs={{0,64},{64,0},{128,192},{192,128},{1,65},{65,1},{129,193},{193,129... | collective-permute-start | bytes 1376264 | tf_op jit(solution)/shard_map/ppermute | solution.py:284
  5.0 8.5 %collective-permute-start.1 = (f32[224,256]{1,0:T(8,128)S(1)}, f32[224,256]{1,0:T(8,128)S(1)}, u32[]{:S(2)}, u32[]{:S(2)}) collective-permute-start(f32[224,256]{1,0:T(8,128)S(1)} %shard_map.87), channel_id=1, source_target_pairs={{0,128},{128,0},{64,192},{192,64},{1,129},{129,1},{65,193},{193,65... | collective-permute-start | bytes 688136 | tf_op jit(solution)/shard_map/ppermute | solution.py:300
  7.2 13.1 %collective-permute-start.3 = (f32[224,256]{1,0:T(8,128)S(1)}, f32[224,256]{1,0:T(8,128)S(1)}, u32[]{:S(2)}, u32[]{:S(2)}) collective-permute-start(f32[224,256]{1,0:T(8,128)S(1)} %shard_map.89), channel_id=1, source_target_pairs={{0,128},{128,0},{64,192},{192,64},{1,129},{129,1},{65,193},{193,65... | collective-permute-start | bytes 688136 | tf_op jit(solution)/shard_map/ppermute | solution.py:300
  14.3 10.0 %copy-start.27 = (s32[448,1]{0,1:T(1,128)S(1)}, s32[448,1]{0,1:T(1,128)}, u32[]{:S(2)}) copy-start(s32[448,1]{0,1:T(1,128)} %param.10) | copy-start | bytes 5380
  14.3 10.2 %copy-start.28 = (s32[448]{0:T(512)S(1)}, s32[448]{0:T(512)}, u32[]{:S(2)}) copy-start(s32[448]{0:T(512)} %param.11) | copy-start | bytes 5380
  14.3 26.5 %collective-permute-start.4 = (f32[224,768]{1,0:T(8,128)S(1)}, f32[224,768]{1,0:T(8,128)S(1)}, u32[]{:S(2)}, u32[]{:S(2)}) collective-permute-start(f32[224,768]{1,0:T(8,128)S(1)} %shard_map.88.refs_0_.refs_2_.refs_1_), channel_id=1, source_target_pairs={{0,8},{1,9},{2,10},{3,11},{4,12},{5,13},{6,14},{7,15},{8,16},{9,17... | collective-permute-start | bytes 2064392 | tf_op jit(solution)/shard_map/ppermute | solution.py:339
  16.3 24.5 %collective-permute-start.5 = (f32[224,768]{1,0:T(8,128)S(1)}, f32[224,768]{1,0:T(8,128)S(1)}, u32[]{:S(2)}, u32[]{:S(2)}) collective-permute-start(f32[224,768]{1,0:T(8,128)S(1)} %shard_map.88.refs_0_.refs_2_.refs_1_), channel_id=1, source_target_pairs={{8,0},{9,1},{10,2},{11,3},{12,4},{13,5},{14,6},{15,7},{16,8},{17,9... | collective-permute-start | bytes 2064392 | tf_op jit(solution)/shard_map/ppermute | solution.py:339
  21.1 35.9 %copy-start.9 = (f32[224,768]{1,0:T(8,128)}, f32[224,768]{1,0:T(8,128)S(1)}, u32[]{:S(2)}) copy-start(f32[224,768]{1,0:T(8,128)S(1)} %shard_map.90.refs_1_.refs_3_) | copy-start | bytes 2064388
  21.1 29.9 %collective-permute-start.7 = (f32[224,768]{1,0:T(8,128)S(1)}, f32[224,768]{1,0:T(8,128)}, u32[]{:S(2)}, u32[]{:S(2)}) collective-permute-start(f32[224,768]{1,0:T(8,128)S(1)} %shard_map.90.refs_1_.refs_3_), channel_id=1, source_target_pairs={{8,0},{9,1},{10,2},{11,3},{12,4},{13,5},{14,6},{15,7},{16,8},{17,9... | collective-permute-start | bytes 2064392 | tf_op jit(solution)/shard_map/ppermute | solution.py:339
  26.0 0.7 copy-start.19
  40.8 27.2 %collective-permute-start.6 = (f32[224,768]{1,0:T(8,128)S(1)}, f32[224,768]{1,0:T(8,128)}, u32[]{:S(2)}, u32[]{:S(2)}) collective-permute-start(f32[224,768]{1,0:T(8,128)S(1)} %shard_map.90.refs_1_.refs_3_), channel_id=1, source_target_pairs={{0,8},{1,9},{2,10},{3,11},{4,12},{5,13},{6,14},{7,15},{8,16},{9,17... | collective-permute-start | bytes 2064392 | tf_op jit(solution)/shard_map/ppermute | solution.py:339
  40.8 0.8 copy-start.13
  41.7 0.8 copy-start.16
  42.5 32.7 %collective-permute-start.8 = (f32[224,768]{1,0:T(8,128)}, f32[224,768]{1,0:T(8,128)}, u32[]{:S(2)}, u32[]{:S(2)}) collective-permute-start(f32[224,768]{1,0:T(8,128)} %get-tuple-element.13.refs_2_.refs_4_), channel_id=1, source_target_pairs={{0,8},{1,9},{2,10},{3,11},{4,12},{5,13},{6,14},{7,15},{8,16},{9,17... | collective-permute-start | bytes 2064392 | tf_op jit(solution)/shard_map/ppermute | solution.py:339
  42.5 32.7 %collective-permute-start.9 = (f32[224,768]{1,0:T(8,128)}, f32[224,768]{1,0:T(8,128)}, u32[]{:S(2)}, u32[]{:S(2)}) collective-permute-start(f32[224,768]{1,0:T(8,128)} %get-tuple-element.14.refs_3_.refs_5_), channel_id=1, source_target_pairs={{8,0},{9,1},{10,2},{11,3},{12,4},{13,5},{14,6},{15,7},{16,8},{17,9... | collective-permute-start | bytes 2064392 | tf_op jit(solution)/shard_map/ppermute | solution.py:339
  51.0 29.6 %collective-permute-start.11 = (f32[224,768]{1,0:T(8,128)}, f32[224,768]{1,0:T(8,128)}, u32[]{:S(2)}, u32[]{:S(2)}) collective-permute-start(f32[224,768]{1,0:T(8,128)} %collective-permute-done.7.refs_1_.refs_3_), channel_id=1, source_target_pairs={{8,0},{9,1},{10,2},{11,3},{12,4},{13,5},{14,6},{15,7},{16,8},{17,9... | collective-permute-start | bytes 2064392 | tf_op jit(solution)/shard_map/ppermute | solution.py:339
  54.8 1.1 copy-start.14
  55.9 1.1 copy-start.17
  57.0 1.1 copy-start.15
  57.0 1.3 copy-start.18
  57.0 1.3 copy-start.26
  59.5 1.1 copy-start.11
  60.5 23.7 %all-to-all-start.1 = ((f32[8,56,768]{2,1,0:T(8,128)}), f32[8,56,768]{2,1,0:T(8,128)S(1)}, u32[]{:S(2)}, u32[]{:S(2)}) async-start(f32[8,56,768]{2,1,0:T(8,128)} %copy-done.11), calls=%async_computation.1 | async-start | bytes 2752512 | tf_op jit(solution)/shard_map/all_to_all | solution.py:334
  68.0 27.7 %collective-permute-start.10 = (f32[224,768]{1,0:T(8,128)}, f32[224,768]{1,0:T(8,128)S(1)}, u32[]{:S(2)}, u32[]{:S(2)}) collective-permute-start(f32[224,768]{1,0:T(8,128)} %collective-permute-done.6.refs_0_.refs_2_), channel_id=1, source_target_pairs={{0,8},{1,9},{2,10},{3,11},{4,12},{5,13},{6,14},{7,15},{8,16},{9,17... | collective-permute-start | bytes 2064392 | tf_op jit(solution)/shard_map/ppermute | solution.py:339
  75.3 29.5 %collective-permute-start.12 = (f32[224,768]{1,0:T(8,128)}, f32[224,768]{1,0:T(8,128)}, u32[]{:S(2)}, u32[]{:S(2)}) collective-permute-start(f32[224,768]{1,0:T(8,128)} %collective-permute-done.8.refs_2_.refs_4_), channel_id=1, source_target_pairs={{0,8},{1,9},{2,10},{3,11},{4,12},{5,13},{6,14},{7,15},{8,16},{9,17... | collective-permute-start | bytes 2064392 | tf_op jit(solution)/shard_map/ppermute | solution.py:339
  75.3 36.0 %collective-permute-start.13 = (f32[224,768]{1,0:T(8,128)}, f32[224,768]{1,0:T(8,128)}, u32[]{:S(2)}, u32[]{:S(2)}) collective-permute-start(f32[224,768]{1,0:T(8,128)} %collective-permute-done.9.refs_3_.refs_5_), channel_id=1, source_target_pairs={{8,0},{9,1},{10,2},{11,3},{12,4},{13,5},{14,6},{15,7},{16,8},{17,9... | collective-permute-start | bytes 2064392 | tf_op jit(solution)/shard_map/ppermute | solution.py:339
  80.6 27.0 %collective-permute-start.15 = (f32[224,768]{1,0:T(8,128)}, f32[224,768]{1,0:T(8,128)}, u32[]{:S(2)}, u32[]{:S(2)}) collective-permute-start(f32[224,768]{1,0:T(8,128)} %collective-permute-done.11.refs_1_.refs_3_), channel_id=1, source_target_pairs={{8,0},{9,1},{10,2},{11,3},{12,4},{13,5},{14,6},{15,7},{16,8},{17,9... | collective-permute-start | bytes 2064392 | tf_op jit(solution)/shard_map/ppermute | solution.py:339
  84.3 2.9 %copy-start.3 = (f32[8,56,768]{2,1,0:T(8,128)}, f32[8,56,768]{2,1,0:T(8,128)S(1)}, u32[]{:S(2)}) copy-start(f32[8,56,768]{2,1,0:T(8,128)S(1)} %all-to-all-done.1.refs_6_.refs_2_) | copy-start | bytes 4128772
  87.1 1.1 copy-start.12
  88.2 23.0 %all-to-all-start.2 = ((f32[8,56,768]{2,1,0:T(8,128)}), f32[8,56,768]{2,1,0:T(8,128)S(1)}, u32[]{:S(2)}, u32[]{:S(2)}) async-start(f32[8,56,768]{2,1,0:T(8,128)} %copy-done.12), calls=%async_computation.2 | async-start | bytes 2752512 | tf_op jit(solution)/shard_map/all_to_all | solution.py:334
  95.7 26.8 %collective-permute-start.14 = (f32[224,768]{1,0:T(8,128)S(1)}, f32[224,768]{1,0:T(8,128)S(1)}, u32[]{:S(2)}, u32[]{:S(2)}) collective-permute-start(f32[224,768]{1,0:T(8,128)S(1)} %collective-permute-done.10.refs_0_.refs_2_), channel_id=1, source_target_pairs={{0,8},{1,9},{2,10},{3,11},{4,12},{5,13},{6,14},{7,15},{8,16},{9,17... | collective-permute-start | bytes 2064392 | tf_op jit(solution)/shard_map/ppermute | solution.py:339
  104.8 26.1 %collective-permute-start.16 = (f32[224,768]{1,0:T(8,128)}, f32[224,768]{1,0:T(8,128)}, u32[]{:S(2)}, u32[]{:S(2)}) collective-permute-start(f32[224,768]{1,0:T(8,128)} %collective-permute-done.12.refs_2_.refs_4_), channel_id=1, source_target_pairs={{0,8},{1,9},{2,10},{3,11},{4,12},{5,13},{6,14},{7,15},{8,16},{9,17... | collective-permute-start | bytes 2064392 | tf_op jit(solution)/shard_map/ppermute | solution.py:346
  107.5 23.3 %collective-permute-start.17 = (f32[224,768]{1,0:T(8,128)}, f32[224,768]{1,0:T(8,128)}, u32[]{:S(2)}, u32[]{:S(2)}) collective-permute-start(f32[224,768]{1,0:T(8,128)} %collective-permute-done.15.refs_1_.refs_3_), channel_id=1, source_target_pairs={{8,0},{9,1},{10,2},{11,3},{12,4},{13,5},{14,6},{15,7},{16,8},{17,9... | collective-permute-start | bytes 2064392 | tf_op jit(solution)/shard_map/ppermute | solution.py:347
  111.2 3.7 %copy-start.5 = (f32[8,56,768]{2,1,0:T(8,128)}, f32[8,56,768]{2,1,0:T(8,128)S(1)}, u32[]{:S(2)}) copy-start(f32[8,56,768]{2,1,0:T(8,128)S(1)} %all-to-all-done.2.refs_6_.refs_3_) | copy-start | bytes 4128772
  115.0 23.0 %all-to-all-start.3 = ((f32[8,56,768]{2,1,0:T(8,128)}), f32[8,56,768]{2,1,0:T(8,128)S(1)}, u32[]{:S(2)}, u32[]{:S(2)}) async-start(f32[8,56,768]{2,1,0:T(8,128)} %shard_map.97), calls=%async_computation.3 | async-start | bytes 2752512 | tf_op jit(solution)/shard_map/all_to_all | solution.py:334
  138.0 3.8 %copy-start.7 = (f32[8,56,768]{2,1,0:T(8,128)}, f32[8,56,768]{2,1,0:T(8,128)S(1)}, u32[]{:S(2)}) copy-start(f32[8,56,768]{2,1,0:T(8,128)S(1)} %all-to-all-done.3.refs_4_.refs_6_) | copy-start | bytes 4128772
  141.8 23.3 %all-to-all-start.4 = ((f32[8,56,768]{2,1,0:T(8,128)}), f32[8,56,768]{2,1,0:T(8,128)S(1)}, u32[]{:S(2)}, u32[]{:S(2)}) async-start(f32[8,56,768]{2,1,0:T(8,128)} %shard_map.101), calls=%async_computation.4 | async-start | bytes 2752512 | tf_op jit(solution)/shard_map/all_to_all | solution.py:334
  147.4 1.3 copy-start.4
  148.8 1.3 copy-start.6
  150.1 1.3 copy-start.8
  151.4 0.9 copy-start.20
  152.4 3.2 %copy-start.10 = (f32[224,768]{1,0:T(8,128)S(1)}, f32[224,768]{1,0:T(8,128)}, u32[]{:S(2)}) copy-start(f32[224,768]{1,0:T(8,128)} %copy-done.9) | copy-start | bytes 2064388
  152.4 3.2 %copy-start.21 = (s32[448,128]{1,0:T(8,128)S(1)}, s32[448,128]{1,0:T(8,128)}, u32[]{:S(2)}) copy-start(s32[448,128]{1,0:T(8,128)} %copy-done.19) | copy-start | bytes 688132
  155.6 9.4 %copy-start.22 = (s32[448,128]{1,0:T(8,128)S(1)}, s32[448,128]{1,0:T(8,128)}, u32[]{:S(2)}) copy-start(s32[448,128]{1,0:T(8,128)} %copy-done.19) | copy-start | bytes 688132
  158.4 1.1 copy-start.1
  165.1 1.3 copy-start.2

commit v5 on v4

--- a/solution.py
+++ b/solution.py
@@ -60,10 +60,14 @@
     return pl.BlockSpec(memory_space=pltpu.SMEM)
 
 
+def halves(values):
+    high = values.astype(BF16)
+    return high, (values - high.astype(F32)).astype(BF16)
+
+
 def split_dot(chosen, values, contract=((1,), (0,))):
-    high = values.astype(BF16)
-    low = (values - high.astype(F32)).astype(BF16)
     dims = (contract, ((), ()))
+    high, low = halves(values)
     return lax.dot_general(chosen, high, dims, preferred_element_type=F32) + lax.dot_general(
         chosen, low, dims, preferred_element_type=F32
     )
@@ -85,7 +89,8 @@
     out[...] = grad[:, pl.ds(at, HALF)].astype(F32) + got[...]
 
 
-def update_kernel(half, place, grad, got, got_y, weight, first, second, out):
+def update_kernel(half, place, grad, got, got_y, weight, first, second, *refs):
+    out = refs[-1]
     dp = place[1]
     at = pl.multiple_of(dp * FEATS + half * HALF, HALF)
     total = grad[:, pl.ds(at, HALF)].astype(F32) + got[...] + got_y[...]
@@ -226,25 +231,27 @@
     refs[-1][...] = total
 
 
-def doubled(values):
-    row = lax.broadcasted_iota(I32, (128, 256), 0)
-    lane = lax.broadcasted_iota(I32, (128, 256), 1) >> 1
-    twice = jnp.where(row == lane, 1.0, 0.0).astype(BF16)
-    high = values.astype(BF16)
-    low = (values - high.astype(F32)).astype(BF16)
-    return jnp.dot(high, twice, preferred_element_type=F32) + jnp.dot(
-        low, twice, preferred_element_type=F32
-    )
-
-
 def final_kernel(codes, *refs):
     first_half = pl.program_id(0) < 2
     at = jnp.where(first_half, codes[:, 3:4], codes[:, 7:8])
     at = jnp.where(at >= 0, (at >> 7) * SENT + (at & 127), -1)
+    rows = PLANE * SENT
+    chosen = jnp.where(
+        lax.broadcasted_iota(I32, (FINE, rows), 1) == at, 1.0 - own_share, 0.0
+    ).astype(BF16)
+    row = lax.broadcasted_iota(I32, (256, 256), 0) & 127
+    lane = lax.broadcasted_iota(I32, (256, 256), 1) >> 1
+    twice = jnp.where(row == lane, 1.0, 0.0).astype(BF16)
+    far = [piece for k in range(3) for piece in halves(refs[6 + k][...].reshape(rows, 128))]
+    far = jnp.dot(chosen, jnp.concatenate(far, axis=1), preferred_element_type=F32)
     for state in range(3):
-        acc0, acc1, far, out = (refs[3 * k + state] for k in range(4))
-        acc = jnp.where(first_half, acc0[...], acc1[...])
-        out[...] = doubled(acc + far_dot(at, far[...]))
+        acc0, acc1, out = (refs[3 * k + state] for k in (0, 1, 3))
+        at = state * 256
+        mixed = jnp.where(first_half, acc0[...], acc1[...])
+        mixed = mixed + far[:, at : at + 128] + far[:, at + 128 : at + 256]
+        out[...] = jnp.dot(
+            jnp.concatenate(halves(mixed), axis=1), twice, preferred_element_type=F32
+        )
 
 
 PLANES = [[z * PLANE + p for p in range(PLANE)] for z in range(RING)]
@@ -312,14 +319,16 @@
                     block,
                     block,
                     block,
-                ],
+                ]
+                + [pl.BlockSpec(memory_space=pl.ANY)] * half,
                 out_specs=pl.BlockSpec((ROWS, WIDE), lambda i: (0, 0)),
                 moved=2 << 20,
-            )(place, grad, got, got_y, weight, first, second)
+            )(place, grad, got, got_y, weight, first, second, *[wanted] * half)
         )
 
     def pick(planes, sources, after=()):
-        after = (*after, token(sources))
+        if after:
+            after = (*after, token(sources))
         return call(
             lambda *refs: pick_kernel(planes, *refs),
             shape(PLANE, SENT, WIDE),
@@ -339,7 +348,7 @@
         return lax.ppermute(pair[0], "shard", UP), lax.ppermute(pair[1], "shard", DOWN)
 
     one = [around((x, x)) for x in state]
-    one[0] = hold(one[0], asked)
+    one[1] = hold(one[1], asked)
     two = [around(pair) for pair in one]
     three = [around(pair) for pair in two]
     four = (

time: 175 us -> 177 us (1.011)
  waiting for transfers between devices: 54.6 us -> 58.8 us
  local copies, waits for them, and re-layouts: 16.9 us -> 14.4 us
    ppermute x6, waiting for transfers between devices: 10.1 us -> 23.1 us  [around(): lax.ppermute(pair[1], 'shard', DOWN)]
    ppermute x1, waiting for transfers between devices: 8.35 us -> 0.62 us  [on_device(): lax.ppermute(three[0][0], 'shard', UP)]
    all_to_all x4, waiting for transfers between devices: 12.7 us -> 19.8 us  [to_plane(): lax.all_to_all(rows, 'shard', split_axis=0, concat_axis=0, axis_index_gro...]
    ppermute x6, waiting for transfers between devices: 16.3 us -> 9.58 us  [around(): lax.ppermute(pair[0], 'shard', UP)]
    unnamed x59 -> x55, local copies, waits for them, and re-layouts: 16.8 us -> 14.2 us
    pallas_call x1, Pallas kernels: 7.55 us -> 5.26 us  [on_device(): call(final_kernel, (shape(FINE, 2 * FEATS),) * 3, grid=(4,), in_specs=[pl...]
    ppermute x2, waiting for transfers between devices: 5.76 us -> 3.71 us  [on_device(): got_y = lax.ppermute(passed, 'dp', NEXT_Y)]
  transfers between devices with their start and end apart: 22 -> 22, of which waited for: 10 -> 9; matrix products, arithmetic and copies ran while one was open for 1% -> 0% of each run, Pallas kernels for 10% -> 12%
where the time goes in v5:
time: 177 us; the launch traced here: 175 us
  waiting for transfers between devices  58.8 us (33%)
  starting transfers between devices  56.8 us (32%)
  Pallas kernels  30.1 us (17%)
  local copies, waits for them, and re-layouts  14.4 us (8%)
  blocking collectives  13.5 us (8%)
    all_to_all x4, starting transfers between devices, to_plane(): lax.all_to_all(rows, 'shard', split_axis=0, concat_axis=0, axis_index_gro...  28.2 us
    ppermute x6, waiting for transfers between devices, around(): lax.ppermute(pair[1], 'shard', DOWN)  23.1 us
    ppermute x6, starting transfers between devices, around(): lax.ppermute(pair[1], 'shard', DOWN)  20 us
    all_to_all x4, waiting for transfers between devices, to_plane(): lax.all_to_all(rows, 'shard', split_axis=0, concat_axis=0, axis_index_gro...  19.8 us
    unnamed x55, local copies, waits for them, and re-layouts  14.2 us
    all_to_all x1, blocking collectives, on_device(): lax.all_to_all(wanted, 'shard', split_axis=0, concat_axis=0, axis_index_g...  13.5 us
    pallas_call x4, Pallas kernels, pick(): call(lambda *refs: pick_kernel(planes, *refs), shape(PLANE, SENT, WIDE),...  13.2 us
    ppermute x6, waiting for transfers between devices, around(): lax.ppermute(pair[0], 'shard', UP)  9.58 us
  transfers between devices with their start and end apart: 22, of which 9 were waited for; matrix products, arithmetic and copies ran while one was open for 0% of the time, Pallas kernels for 12%

profile of v5, /device:TPU:2, one launch (start us, length us, event | category | flops | bytes accessed | tf_op | source)
XLA Modules:
  0.0 175.2 jit_solution(619397039696671118)
XLA Ops:
  0.6 0.1 pad_add_fusion.place.refs_0_
  0.7 1.2 copy-done
  1.9 0.6 shard_map.86
  2.5 0.1 collective-permute-start
  2.6 0.0 copy-start.25
  2.6 0.0 copy-start.26
  2.6 0.5 collective-permute-start.2
  3.1 1.3 collective-permute-done.refs_2_
  4.4 1.3 shard_map.87
  5.7 1.6 collective-permute-start.1
  7.3 0.6 shard_map.89
  7.8 0.5 collective-permute-start.3
  8.4 0.1 copy.12.dev
  8.5 0.1 copy.13.col
  8.7 1.4 shard_map.85
  10.0 0.7 copy-done.17
  10.7 3.7 %collective-permute-done.1.refs_3_ = f32[224,256]{1,0:T(8,128)} collective-permute-done((f32[224,256]{1,0:T(8,128)}, f32[224,256]{1,0:T(8,128)}, u32[]{:S(2)}, u32[]{:S(2)}) %collective-permute-start.1) | collective-permute-done | bytes 229408 | tf_op jit(solution)/shard_map/ppermute | solution.py:307
  14.4 1.0 copy-done.22
  15.5 1.0 copy-done.23
  16.5 1.2 shard_map.88.refs_2_.refs_1_
  17.7 2.0 %collective-permute-start.4 = (f32[224,768]{1,0:T(8,128)S(1)}, f32[224,768]{1,0:T(8,128)}, u32[]{:S(2)}, u32[]{:S(2)}) collective-permute-start(f32[224,768]{1,0:T(8,128)S(1)} %shard_map.88.refs_2_.refs_1_), channel_id=1, source_target_pairs={{0,8},{1,9},{2,10},{3,11},{4,12},{5,13},{6,14},{7,15},{8,16},{9,17... | collective-permute-start | bytes 2064392 | tf_op jit(solution)/shard_map/ppermute | solution.py:348
  19.7 4.0 %collective-permute-start.5 = (f32[224,768]{1,0:T(8,128)S(1)}, f32[224,768]{1,0:T(8,128)}, u32[]{:S(2)}, u32[]{:S(2)}) collective-permute-start(f32[224,768]{1,0:T(8,128)S(1)} %shard_map.88.refs_2_.refs_1_), channel_id=1, source_target_pairs={{8,0},{9,1},{10,2},{11,3},{12,4},{13,5},{14,6},{15,7},{16,8},{17,9... | collective-permute-start | bytes 2064392 | tf_op jit(solution)/shard_map/ppermute | solution.py:348
  23.7 0.8 shard_map.90.refs_3_.refs_1_
  24.5 0.1 collective-permute-start.6
  24.5 3.2 %collective-permute-start.7 = (f32[224,768]{1,0:T(8,128)S(1)}, f32[224,768]{1,0:T(8,128)S(1)}, u32[]{:S(2)}, u32[]{:S(2)}) collective-permute-start(f32[224,768]{1,0:T(8,128)S(1)} %shard_map.90.refs_3_.refs_1_), channel_id=1, source_target_pairs={{8,0},{9,1},{10,2},{11,3},{12,4},{13,5},{14,6},{15,7},{16,8},{17,9... | collective-permute-start | bytes 2064392 | tf_op jit(solution)/shard_map/ppermute | solution.py:348
  27.8 13.5 %all_to_all.25 = s32[8,8,128]{2,1,0:T(8,128)S(1)} all-to-all(s32[8,8,128]{2,1,0:T(8,128)S(1)} %get-tuple-element.11.refs_7_), channel_id=1, replica_groups={{0,1,2,3,4,5,6,7},{8,9,10,11,12,13,14,15},{16,17,18,19,20,21,22,23},{24..., dimensions={0} | all-to-all | bytes 65536 | tf_op jit(solution)/shard_map/all_to_all | solution.py:280
  41.3 0.6 reduce_sum.9.refs_1_.refs_2_
  41.9 3.2 %collective-permute-start.9 = (f32[224,768]{1,0:T(8,128)}, f32[224,768]{1,0:T(8,128)}, u32[]{:S(2)}, u32[]{:S(2)}) collective-permute-start(f32[224,768]{1,0:T(8,128)} %collective-permute-done.5.refs_5_), channel_id=1, source_target_pairs={{8,0},{9,1},{10,2},{11,3},{12,4},{13,5},{14,6},{15,7},{16,8},{17,9... | collective-permute-start | bytes 2064392 | tf_op jit(solution)/shard_map/ppermute | solution.py:348
  45.1 9.6 %collective-permute-done.6.refs_0_ = f32[224,768]{1,0:T(8,128)S(1)} collective-permute-done((f32[224,768]{1,0:T(8,128)S(1)}, f32[224,768]{1,0:T(8,128)S(1)}, u32[]{:S(2)}, u32[]{:S(2)}) %collective-permute-start.6) | collective-permute-done | bytes 688160 | tf_op jit(solution)/shard_map/ppermute | solution.py:348
  54.7 0.8 copy-done.13
  55.5 0.8 copy-done.15
  56.4 2.5 %collective-permute-start.11 = (f32[224,768]{1,0:T(8,128)}, f32[224,768]{1,0:T(8,128)}, u32[]{:S(2)}, u32[]{:S(2)}) collective-permute-start(f32[224,768]{1,0:T(8,128)} %get-tuple-element.14.refs_1_.refs_3_), channel_id=1, source_target_pairs={{8,0},{9,1},{10,2},{11,3},{12,4},{13,5},{14,6},{15,7},{16,8},{17,9... | collective-permute-start | bytes 2064392 | tf_op jit(solution)/shard_map/ppermute | solution.py:348
  58.9 1.9 %shard_map.91 = f32[8,56,768]{2,1,0:T(8,128)S(1)} custom-call(s32[2]{0:T(128)S(1)} %pad_add_fusion.place.refs_0_, s32[8,128]{1,0:T(8,128)S(1)} %copy-done.24, f32[224,768]{1,0:T(8,128)S(1)} %shard_map.88.refs_2_.refs_1_, f32[224,768]{1,0:T(8,128)S(1)} %shard_map.90.refs_3_.refs_1_, f32[224,768]{1,0:T(8,128)} %collective-permute-done.4.refs_4_, ...), custom_call_target="tpu_custom_call" | custom-call | flops 352321536 | bytes 5242880 | tf_op jit(solution)/shard_map/pallas_call | solution.py:332
  60.8 0.0 copy-start.12
  60.8 1.1 copy-done.12
  61.9 7.6 %all-to-all-start.1 = ((f32[8,56,768]{2,1,0:T(8,128)}), f32[8,56,768]{2,1,0:T(8,128)S(1)}, u32[]{:S(2)}, u32[]{:S(2)}) async-start(f32[8,56,768]{2,1,0:T(8,128)} %copy-done.12), calls=%async_computation.1 | async-start | bytes 2752512 | tf_op jit(solution)/shard_map/all_to_all | solution.py:343
  69.5 0.1 collective-permute-start.12
  69.6 3.4 %collective-permute-start.13 = (f32[224,768]{1,0:T(8,128)}, f32[224,768]{1,0:T(8,128)}, u32[]{:S(2)}, u32[]{:S(2)}) collective-permute-start(f32[224,768]{1,0:T(8,128)} %collective-permute-done.9.refs_3_.refs_5_), channel_id=1, source_target_pairs={{8,0},{9,1},{10,2},{11,3},{12,4},{13,5},{14,6},{15,7},{16,8},{17,9... | collective-permute-start | bytes 2064392 | tf_op jit(solution)/shard_map/ppermute | solution.py:348
  73.0 10.9 %collective-permute-done.11.refs_1_.refs_3_ = f32[224,768]{1,0:T(8,128)} collective-permute-done((f32[224,768]{1,0:T(8,128)}, f32[224,768]{1,0:T(8,128)}, u32[]{:S(2)}, u32[]{:S(2)}) %collective-permute-start.11) | collective-permute-done | bytes 688160 | tf_op jit(solution)/shard_map/ppermute | solution.py:348
  83.9 3.7 %collective-permute-start.15 = (f32[224,768]{1,0:T(8,128)}, f32[224,768]{1,0:T(8,128)}, u32[]{:S(2)}, u32[]{:S(2)}) collective-permute-start(f32[224,768]{1,0:T(8,128)} %collective-permute-done.11.refs_1_.refs_3_), channel_id=1, source_target_pairs={{8,0},{9,1},{10,2},{11,3},{12,4},{13,5},{14,6},{15,7},{16,8},{17,9... | collective-permute-start | bytes 2064392 | tf_op jit(solution)/shard_map/ppermute | solution.py:348
  87.6 3.5 %shard_map.94 = f32[8,56,768]{2,1,0:T(8,128)} custom-call(s32[2]{0:T(128)S(1)} %pad_add_fusion.place.refs_0_, s32[8,128]{1,0:T(8,128)S(1)} %copy-done.24, f32[224,768]{1,0:T(8,128)S(1)} %copy-done.14, f32[224,768]{1,0:T(8,128)S(1)} %copy-done.16, f32[224,768]{1,0:T(8,128)} %collective-permute-done.8.refs_2_.refs_4_, ...), custom_call_target="tpu_custom_call" | custom-call | flops 352321536 | bytes 5242880 | tf_op jit(solution)/shard_map/pallas_call | solution.py:332
  91.1 7.5 %all-to-all-start.2 = ((f32[8,56,768]{2,1,0:T(8,128)}), f32[8,56,768]{2,1,0:T(8,128)S(1)}, u32[]{:S(2)}, u32[]{:S(2)}) async-start(f32[8,56,768]{2,1,0:T(8,128)} %shard_map.94), calls=%async_computation.2 | async-start | bytes 2752512 | tf_op jit(solution)/shard_map/all_to_all | solution.py:343
  98.6 0.1 collective-permute-start.16
  98.7 12.2 %collective-permute-done.15.refs_1_.refs_3_ = f32[224,768]{1,0:T(8,128)} collective-permute-done((f32[224,768]{1,0:T(8,128)}, f32[224,768]{1,0:T(8,128)}, u32[]{:S(2)}, u32[]{:S(2)}) %collective-permute-start.15) | collective-permute-done | bytes 688160 | tf_op jit(solution)/shard_map/ppermute | solution.py:348
  110.9 3.7 %collective-permute-start.17 = (f32[224,768]{1,0:T(8,128)}, f32[224,768]{1,0:T(8,128)}, u32[]{:S(2)}, u32[]{:S(2)}) collective-permute-start(f32[224,768]{1,0:T(8,128)} %collective-permute-done.15.refs_1_.refs_3_), channel_id=1, source_target_pairs={{8,0},{9,1},{10,2},{11,3},{12,4},{13,5},{14,6},{15,7},{16,8},{17,9... | collective-permute-start | bytes 2064392 | tf_op jit(solution)/shard_map/ppermute | solution.py:356
  114.6 0.0 copy-start.6
  114.6 3.9 %shard_map.96 = f32[8,56,768]{2,1,0:T(8,128)} custom-call(s32[2]{0:T(128)S(1)} %pad_add_fusion.place.refs_0_, s32[8,128]{1,0:T(8,128)S(1)} %copy-done.24, f32[224,768]{1,0:T(8,128)} %collective-permute-done.10.refs_0_.refs_2_, f32[224,768]{1,0:T(8,128)} %collective-permute-done.11.refs_1_.refs_3_, f32[224,768]{1,0:T(8,128)} %collective-permute-done.12.refs_2_.refs_4_, ...), custom_call_target="tpu_custom_call" | custom-call | flops 352321536 | bytes 5242880 | tf_op jit(solution)/shard_map/pallas_call | solution.py:332
  118.5 7.5 %all-to-all-start.3 = ((f32[8,56,768]{2,1,0:T(8,128)}), f32[8,56,768]{2,1,0:T(8,128)S(1)}, u32[]{:S(2)}, u32[]{:S(2)}) async-start(f32[8,56,768]{2,1,0:T(8,128)} %shard_map.96), calls=%async_computation.3 | async-start | bytes 2752512 | tf_op jit(solution)/shard_map/all_to_all | solution.py:343
  126.0 0.6 collective-permute-done.16.refs_2_.refs_4_
  126.6 0.7 collective-permute-done.17.refs_3_.refs_5_
  127.3 14.2 %all-to-all-done.3.refs_4_.refs_6_ = f32[8,56,768]{2,1,0:T(8,128)S(1)} async-done(((f32[8,56,768]{2,1,0:T(8,128)}), f32[8,56,768]{2,1,0:T(8,128)S(1)}, u32[]{:S(2)}, u32[]{:S(2)}) %all-to-all-start.3) | async-done | bytes 1376288 | tf_op jit(solution)/shard_map/all_to_all | solution.py:343
  141.6 3.8 %shard_map.100 = f32[8,56,768]{2,1,0:T(8,128)} custom-call(s32[2]{0:T(128)S(1)} %pad_add_fusion.place.refs_0_, s32[8,128]{1,0:T(8,128)S(1)} %copy-done.24, f32[224,768]{1,0:T(8,128)S(1)} %collective-permute-done.14.refs_0_.refs_2_, f32[224,768]{1,0:T(8,128)} %collective-permute-done.15.refs_1_.refs_3_, f32[224,768]{1,0:T(8,128)} %collective-permute-done.16.refs_2_.refs_4_, ...), custom_call_target="tpu_custom_call" | custom-call | flops 352321536 | bytes 5242880 | tf_op jit(solution)/shard_map/pallas_call | solution.py:332
  145.3 5.6 %all-to-all-start.4 = ((f32[8,56,768]{2,1,0:T(8,128)}), f32[8,56,768]{2,1,0:T(8,128)S(1)}, u32[]{:S(2)}, u32[]{:S(2)}) async-start(f32[8,56,768]{2,1,0:T(8,128)} %shard_map.100), calls=%async_computation.4 | async-start | bytes 2752512 | tf_op jit(solution)/shard_map/all_to_all | solution.py:343
  151.0 1.3 copy-done.5
  152.3 1.3 copy-done.7
  153.7 1.3 copy-done.9
  155.0 0.9 copy-done.18
  155.9 3.2 %shard_map.97.refs_0_.refs_1_.refs_2_ = f32[448,768]{1,0:T(8,128)S(1)} custom-call(s32[448,128]{1,0:T(8,128)S(1)} %copy-done.18, f32[224,768]{1,0:T(8,128)S(1)} %shard_map.88.refs_2_.refs_1_, f32[8,56,768]{2,1,0:T(8,128)S(1)} %copy-done.5, f32[8,56,768]{2,1,0:T(8,128)S(1)} %copy-done.7, f32[8,56,768]{2,1,0:T(8,128)S(1)} %copy-done.9), custom_call_target="tpu_custom_call" | custom-call | flops 1541406720 | bytes 8388608 | tf_op jit(solution)/shard_map/pallas_call | solution.py:371
  159.2 2.8 %shard_map.98.refs_3_.refs_4_.refs_5_ = f32[448,768]{1,0:T(8,128)S(1)} custom-call(s32[448,128]{1,0:T(8,128)S(1)} %copy-done.19, f32[224,768]{1,0:T(8,128)S(1)} %copy-done.11, f32[8,56,768]{2,1,0:T(8,128)S(1)} %copy-done.5, f32[8,56,768]{2,1,0:T(8,128)S(1)} %copy-done.7, f32[8,56,768]{2,1,0:T(8,128)S(1)} %copy-done.9), custom_call_target="tpu_custom_call" | custom-call | flops 1541406720 | bytes 8388608 | tf_op jit(solution)/shard_map/pallas_call | solution.py:371
  162.0 0.0 copy-start.2
  162.0 1.1 copy-done.2
  163.1 5.6 %all-to-all-done.4.refs_6_.refs_7_.refs_8_ = f32[8,56,768]{2,1,0:T(8,128)S(1)} async-done(((f32[8,56,768]{2,1,0:T(8,128)}), f32[8,56,768]{2,1,0:T(8,128)S(1)}, u32[]{:S(2)}, u32[]{:S(2)}) %all-to-all-start.4) | async-done | bytes 1376288 | tf_op jit(solution)/shard_map/all_to_all | solution.py:343
  168.6 1.3 copy-done.3
  170.0 5.3 %shard_map.101 = (f32[448,1024]{1,0:T(8,128)}, f32[448,1024]{1,0:T(8,128)}, f32[448,1024]{1,0:T(8,128)}) custom-call(s32[448,128]{1,0:T(8,128)S(1)} %copy-done.20, f32[448,768]{1,0:T(8,128)S(1)} %shard_map.97.refs_0_.refs_1_.refs_2_, f32[448,768]{1,0:T(8,128)S(1)} %shard_map.97.refs_0_.refs_1_.refs_2_, f32[448,768]{1,0:T(8,128)S(1)} %shard_map.97.refs_0_.refs_1_.refs_2_, ...), custom_call_target="tpu_custom_call" | custom-call | flops 1409286144 | bytes 12582912 | tf_op jit(solution)/shard_map/pallas_call | solution.py:396
  (56 shorter events, 0.1 us)
Async XLA Ops:
  0.7 1.2 copy-start
  2.5 1.9 %collective-permute-start = (f32[224,512]{1,0:T(8,128)S(1)}, f32[224,512]{1,0:T(8,128)S(1)}, u32[]{:S(2)}, u32[]{:S(2)}) collective-permute-start(f32[224,512]{1,0:T(8,128)S(1)} %get-tuple-element.10), channel_id=1, source_target_pairs={{0,64},{64,0},{128,192},{192,128},{1,65},{65,1},{129,193},{193,129... | collective-permute-start | bytes 1376264 | tf_op jit(solution)/shard_map/ppermute | solution.py:291
  2.6 5.8 %copy-start.25 = (s32[448,1]{0,1:T(1,128)S(1)}, s32[448,1]{0,1:T(1,128)}, u32[]{:S(2)}) copy-start(s32[448,1]{0,1:T(1,128)} %param.10) | copy-start | bytes 5380
  2.6 5.9 %copy-start.26 = (s32[448]{0:T(512)S(1)}, s32[448]{0:T(512)}, u32[]{:S(2)}) copy-start(s32[448]{0:T(512)} %param.11) | copy-start | bytes 5380
  2.6 4.6 %collective-permute-start.2 = (f32[224,512]{1,0:T(8,128)S(1)}, f32[224,512]{1,0:T(8,128)S(1)}, u32[]{:S(2)}, u32[]{:S(2)}) collective-permute-start(f32[224,512]{1,0:T(8,128)S(1)} %get-tuple-element.12), channel_id=1, source_target_pairs={{0,64},{64,0},{128,192},{192,128},{1,65},{65,1},{129,193},{193,129... | collective-permute-start | bytes 1376264 | tf_op jit(solution)/shard_map/ppermute | solution.py:291
  5.7 8.8 %copy-start.1 = (bf16[1,224,2048]{2,1,0:T(8,128)(2,1)S(1)}, bf16[1,224,2048]{2,1,0:T(8,128)(2,1)}, u32[]{:S(2)}) copy-start(bf16[1,224,2048]{2,1,0:T(8,128)(2,1)} %param.6) | copy-start | bytes 2752516
  5.7 8.8 %copy-start.21 = (f32[224,512]{1,0:T(8,128)S(1)}, f32[224,512]{1,0:T(8,128)}, u32[]{:S(2)}) copy-start(f32[224,512]{1,0:T(8,128)} %refs_4_.3) | copy-start | bytes 1376260
  5.7 8.8 %collective-permute-start.1 = (f32[224,256]{1,0:T(8,128)}, f32[224,256]{1,0:T(8,128)}, u32[]{:S(2)}, u32[]{:S(2)}) collective-permute-start(f32[224,256]{1,0:T(8,128)} %shard_map.87), channel_id=1, source_target_pairs={{0,128},{128,0},{64,192},{192,64},{1,129},{129,1},{65,193},{193,65... | collective-permute-start | bytes 688136 | tf_op jit(solution)/shard_map/ppermute | solution.py:307
  7.8 15.9 %collective-permute-start.3 = (f32[224,256]{1,0:T(8,128)S(1)}, f32[224,256]{1,0:T(8,128)S(1)}, u32[]{:S(2)}, u32[]{:S(2)}) collective-permute-start(f32[224,256]{1,0:T(8,128)S(1)} %shard_map.89), channel_id=1, source_target_pairs={{0,128},{128,0},{64,192},{192,64},{1,129},{129,1},{65,193},{193,65... | collective-permute-start | bytes 688136 | tf_op jit(solution)/shard_map/ppermute | solution.py:307
  10.0 0.7 copy-start.17
  14.4 1.0 copy-start.22
  15.5 1.0 copy-start.23
  17.7 24.2 %collective-permute-start.4 = (f32[224,768]{1,0:T(8,128)S(1)}, f32[224,768]{1,0:T(8,128)}, u32[]{:S(2)}, u32[]{:S(2)}) collective-permute-start(f32[224,768]{1,0:T(8,128)S(1)} %shard_map.88.refs_2_.refs_1_), channel_id=1, source_target_pairs={{0,8},{1,9},{2,10},{3,11},{4,12},{5,13},{6,14},{7,15},{8,16},{9,17... | collective-permute-start | bytes 2064392 | tf_op jit(solution)/shard_map/ppermute | solution.py:348
  19.7 22.2 %collective-permute-start.5 = (f32[224,768]{1,0:T(8,128)S(1)}, f32[224,768]{1,0:T(8,128)}, u32[]{:S(2)}, u32[]{:S(2)}) collective-permute-start(f32[224,768]{1,0:T(8,128)S(1)} %shard_map.88.refs_2_.refs_1_), channel_id=1, source_target_pairs={{8,0},{9,1},{10,2},{11,3},{12,4},{13,5},{14,6},{15,7},{16,8},{17,9... | collective-permute-start | bytes 2064392 | tf_op jit(solution)/shard_map/ppermute | solution.py:348
  24.4 36.4 %copy-start.10 = (f32[224,768]{1,0:T(8,128)}, f32[224,768]{1,0:T(8,128)S(1)}, u32[]{:S(2)}) copy-start(f32[224,768]{1,0:T(8,128)S(1)} %shard_map.90.refs_3_.refs_1_) | copy-start | bytes 2064388
  24.5 30.2 %collective-permute-start.6 = (f32[224,768]{1,0:T(8,128)S(1)}, f32[224,768]{1,0:T(8,128)S(1)}, u32[]{:S(2)}, u32[]{:S(2)}) collective-permute-start(f32[224,768]{1,0:T(8,128)S(1)} %shard_map.90.refs_3_.refs_1_), channel_id=1, source_target_pairs={{0,8},{1,9},{2,10},{3,11},{4,12},{5,13},{6,14},{7,15},{8,16},{9,17... | collective-permute-start | bytes 2064392 | tf_op jit(solution)/shard_map/ppermute | solution.py:348
  24.5 30.1 %collective-permute-start.7 = (f32[224,768]{1,0:T(8,128)S(1)}, f32[224,768]{1,0:T(8,128)S(1)}, u32[]{:S(2)}, u32[]{:S(2)}) collective-permute-start(f32[224,768]{1,0:T(8,128)S(1)} %shard_map.90.refs_3_.refs_1_), channel_id=1, source_target_pairs={{8,0},{9,1},{10,2},{11,3},{12,4},{13,5},{14,6},{15,7},{16,8},{17,9... | collective-permute-start | bytes 2064392 | tf_op jit(solution)/shard_map/ppermute | solution.py:348
  41.9 17.0 %copy-start.24 = (s32[8,128]{1,0:T(8,128)S(1)}, s32[8,128]{1,0:T(8,128)}, u32[]{:S(2)}) copy-start(s32[8,128]{1,0:T(8,128)} %reduce_sum.9.refs_1_.refs_2_) | copy-start | bytes 12292
  41.9 27.6 %collective-permute-start.8 = (f32[224,768]{1,0:T(8,128)}, f32[224,768]{1,0:T(8,128)}, u32[]{:S(2)}, u32[]{:S(2)}) collective-permute-start(f32[224,768]{1,0:T(8,128)} %collective-permute-done.4.refs_4_), channel_id=1, source_target_pairs={{0,8},{1,9},{2,10},{3,11},{4,12},{5,13},{6,14},{7,15},{8,16},{9,17... | collective-permute-start | bytes 2064392 | tf_op jit(solution)/shard_map/ppermute | solution.py:348
  41.9 27.7 %collective-permute-start.9 = (f32[224,768]{1,0:T(8,128)}, f32[224,768]{1,0:T(8,128)}, u32[]{:S(2)}, u32[]{:S(2)}) collective-permute-start(f32[224,768]{1,0:T(8,128)} %collective-permute-done.5.refs_5_), channel_id=1, source_target_pairs={{8,0},{9,1},{10,2},{11,3},{12,4},{13,5},{14,6},{15,7},{16,8},{17,9... | collective-permute-start | bytes 2064392 | tf_op jit(solution)/shard_map/ppermute | solution.py:348
  54.7 0.8 copy-start.13
  55.5 0.8 copy-start.15
  56.4 27.5 %collective-permute-start.11 = (f32[224,768]{1,0:T(8,128)}, f32[224,768]{1,0:T(8,128)}, u32[]{:S(2)}, u32[]{:S(2)}) collective-permute-start(f32[224,768]{1,0:T(8,128)} %get-tuple-element.14.refs_1_.refs_3_), channel_id=1, source_target_pairs={{8,0},{9,1},{10,2},{11,3},{12,4},{13,5},{14,6},{15,7},{16,8},{17,9... | collective-permute-start | bytes 2064392 | tf_op jit(solution)/shard_map/ppermute | solution.py:348
  60.8 1.1 copy-start.12
  61.9 7.6 %copy-start.14 = (f32[224,768]{1,0:T(8,128)S(1)}, f32[224,768]{1,0:T(8,128)}, u32[]{:S(2)}) copy-start(f32[224,768]{1,0:T(8,128)} %get-tuple-element.13.refs_0_.refs_2_) | copy-start | bytes 2064388
  61.9 25.7 %copy-start.16 = (f32[224,768]{1,0:T(8,128)S(1)}, f32[224,768]{1,0:T(8,128)}, u32[]{:S(2)}) copy-start(f32[224,768]{1,0:T(8,128)} %get-tuple-element.14.refs_1_.refs_3_) | copy-start | bytes 2064388
  61.9 25.7 %all-to-all-start.1 = ((f32[8,56,768]{2,1,0:T(8,128)}), f32[8,56,768]{2,1,0:T(8,128)S(1)}, u32[]{:S(2)}, u32[]{:S(2)}) async-start(f32[8,56,768]{2,1,0:T(8,128)} %copy-done.12), calls=%async_computation.1 | async-start | bytes 2752512 | tf_op jit(solution)/shard_map/all_to_all | solution.py:343
  69.5 29.1 %collective-permute-start.10 = (f32[224,768]{1,0:T(8,128)S(1)}, f32[224,768]{1,0:T(8,128)}, u32[]{:S(2)}, u32[]{:S(2)}) collective-permute-start(f32[224,768]{1,0:T(8,128)S(1)} %copy-done.14), channel_id=1, source_target_pairs={{0,8},{1,9},{2,10},{3,11},{4,12},{5,13},{6,14},{7,15},{8,16},{9,17... | collective-permute-start | bytes 2064392 | tf_op jit(solution)/shard_map/ppermute | solution.py:348
  69.5 29.1 %collective-permute-start.12 = (f32[224,768]{1,0:T(8,128)}, f32[224,768]{1,0:T(8,128)}, u32[]{:S(2)}, u32[]{:S(2)}) collective-permute-start(f32[224,768]{1,0:T(8,128)} %collective-permute-done.8.refs_2_.refs_4_), channel_id=1, source_target_pairs={{0,8},{1,9},{2,10},{3,11},{4,12},{5,13},{6,14},{7,15},{8,16},{9,17... | collective-permute-start | bytes 2064392 | tf_op jit(solution)/shard_map/ppermute | solution.py:348
  69.6 45.0 %collective-permute-start.13 = (f32[224,768]{1,0:T(8,128)}, f32[224,768]{1,0:T(8,128)}, u32[]{:S(2)}, u32[]{:S(2)}) collective-permute-start(f32[224,768]{1,0:T(8,128)} %collective-permute-done.9.refs_3_.refs_5_), channel_id=1, source_target_pairs={{8,0},{9,1},{10,2},{11,3},{12,4},{13,5},{14,6},{15,7},{16,8},{17,9... | collective-permute-start | bytes 2064392 | tf_op jit(solution)/shard_map/ppermute | solution.py:348
  83.9 27.0 %collective-permute-start.15 = (f32[224,768]{1,0:T(8,128)}, f32[224,768]{1,0:T(8,128)}, u32[]{:S(2)}, u32[]{:S(2)}) collective-permute-start(f32[224,768]{1,0:T(8,128)} %collective-permute-done.11.refs_1_.refs_3_), channel_id=1, source_target_pairs={{8,0},{9,1},{10,2},{11,3},{12,4},{13,5},{14,6},{15,7},{16,8},{17,9... | collective-permute-start | bytes 2064392 | tf_op jit(solution)/shard_map/ppermute | solution.py:348
  87.6 3.5 %copy-start.4 = (f32[8,56,768]{2,1,0:T(8,128)}, f32[8,56,768]{2,1,0:T(8,128)S(1)}, u32[]{:S(2)}) copy-start(f32[8,56,768]{2,1,0:T(8,128)S(1)} %all-to-all-done.1.refs_6_.refs_2_) | copy-start | bytes 4128772
  91.1 23.4 %all-to-all-start.2 = ((f32[8,56,768]{2,1,0:T(8,128)}), f32[8,56,768]{2,1,0:T(8,128)S(1)}, u32[]{:S(2)}, u32[]{:S(2)}) async-start(f32[8,56,768]{2,1,0:T(8,128)} %shard_map.94), calls=%async_computation.2 | async-start | bytes 2752512 | tf_op jit(solution)/shard_map/all_to_all | solution.py:343
  98.6 27.4 %collective-permute-start.14 = (f32[224,768]{1,0:T(8,128)}, f32[224,768]{1,0:T(8,128)S(1)}, u32[]{:S(2)}, u32[]{:S(2)}) collective-permute-start(f32[224,768]{1,0:T(8,128)} %collective-permute-done.10.refs_0_.refs_2_), channel_id=1, source_target_pairs={{0,8},{1,9},{2,10},{3,11},{4,12},{5,13},{6,14},{7,15},{8,16},{9,17... | collective-permute-start | bytes 2064392 | tf_op jit(solution)/shard_map/ppermute | solution.py:348
  98.6 28.0 %collective-permute-start.16 = (f32[224,768]{1,0:T(8,128)}, f32[224,768]{1,0:T(8,128)}, u32[]{:S(2)}, u32[]{:S(2)}) collective-permute-start(f32[224,768]{1,0:T(8,128)} %collective-permute-done.12.refs_2_.refs_4_), channel_id=1, source_target_pairs={{0,8},{1,9},{2,10},{3,11},{4,12},{5,13},{6,14},{7,15},{8,16},{9,17... | collective-permute-start | bytes 2064392 | tf_op jit(solution)/shard_map/ppermute | solution.py:355
  110.9 16.5 %collective-permute-start.17 = (f32[224,768]{1,0:T(8,128)}, f32[224,768]{1,0:T(8,128)}, u32[]{:S(2)}, u32[]{:S(2)}) collective-permute-start(f32[224,768]{1,0:T(8,128)} %collective-permute-done.15.refs_1_.refs_3_), channel_id=1, source_target_pairs={{8,0},{9,1},{10,2},{11,3},{12,4},{13,5},{14,6},{15,7},{16,8},{17,9... | collective-permute-start | bytes 2064392 | tf_op jit(solution)/shard_map/ppermute | solution.py:356
  114.6 3.9 %copy-start.6 = (f32[8,56,768]{2,1,0:T(8,128)}, f32[8,56,768]{2,1,0:T(8,128)S(1)}, u32[]{:S(2)}) copy-start(f32[8,56,768]{2,1,0:T(8,128)S(1)} %all-to-all-done.2.refs_6_.refs_3_) | copy-start | bytes 4128772
  118.5 23.0 %all-to-all-start.3 = ((f32[8,56,768]{2,1,0:T(8,128)}), f32[8,56,768]{2,1,0:T(8,128)S(1)}, u32[]{:S(2)}, u32[]{:S(2)}) async-start(f32[8,56,768]{2,1,0:T(8,128)} %shard_map.96), calls=%async_computation.3 | async-start | bytes 2752512 | tf_op jit(solution)/shard_map/all_to_all | solution.py:343
  141.6 3.8 %copy-start.8 = (f32[8,56,768]{2,1,0:T(8,128)}, f32[8,56,768]{2,1,0:T(8,128)S(1)}, u32[]{:S(2)}) copy-start(f32[8,56,768]{2,1,0:T(8,128)S(1)} %all-to-all-done.3.refs_4_.refs_6_) | copy-start | bytes 4128772
  145.3 23.3 %all-to-all-start.4 = ((f32[8,56,768]{2,1,0:T(8,128)}), f32[8,56,768]{2,1,0:T(8,128)S(1)}, u32[]{:S(2)}, u32[]{:S(2)}) async-start(f32[8,56,768]{2,1,0:T(8,128)} %shard_map.100), calls=%async_computation.4 | async-start | bytes 2752512 | tf_op jit(solution)/shard_map/all_to_all | solution.py:343
  151.0 1.3 copy-start.5
  152.3 1.3 copy-start.7
  153.7 1.3 copy-start.9
  155.0 0.9 copy-start.18
  155.9 3.2 %copy-start.11 = (f32[224,768]{1,0:T(8,128)S(1)}, f32[224,768]{1,0:T(8,128)}, u32[]{:S(2)}) copy-start(f32[224,768]{1,0:T(8,128)} %copy-done.10) | copy-start | bytes 2064388
  155.9 3.2 %copy-start.19 = (s32[448,128]{1,0:T(8,128)S(1)}, s32[448,128]{1,0:T(8,128)}, u32[]{:S(2)}) copy-start(s32[448,128]{1,0:T(8,128)} %copy-done.17) | copy-start | bytes 688132
  159.2 9.4 %copy-start.20 = (s32[448,128]{1,0:T(8,128)S(1)}, s32[448,128]{1,0:T(8,128)}, u32[]{:S(2)}) copy-start(s32[448,128]{1,0:T(8,128)} %copy-done.17) | copy-start | bytes 688132
  162.0 1.1 copy-start.2
  168.6 1.3 copy-start.3

commit v6 on v5

--- a/solution.py
+++ b/solution.py
@@ -152,7 +152,7 @@
 
 def asked_rows(asked, plane):
     here = lax.broadcasted_iota(I32, (RING, 128), 0) == plane
-    return jnp.sum(jnp.where(here, asked[...], 0), axis=0, keepdims=True)
+    return jnp.sum(jnp.where(here, jnp.sum(asked[...], axis=0), 0), axis=0, keepdims=True)
 
 
 def pick_from(asked, plane, values):
@@ -176,7 +176,7 @@
     pass
 
 
-def hold(arrays, *until):
+def hold(arrays, *until, wait=0):
     n = len(arrays)
     return pl.pallas_call(
         held_kernel,
@@ -184,6 +184,7 @@
         in_specs=[pl.BlockSpec(memory_space=pl.ANY)] * (n + len(until)),
         out_specs=(pl.BlockSpec(memory_space=pl.ANY),) * n,
         input_output_aliases={i: i for i in range(n)},
+        cost_estimate=pl.CostEstimate(flops=wait * 10**9, bytes_accessed=0, transcendentals=0),
     )(*arrays, *until)
 
 
@@ -191,12 +192,12 @@
     refs[-1][...] = jnp.zeros((8, 128), F32)
 
 
-def token(arrays):
+def token(arrays, wait):
     return call(
         token_kernel,
         shape(8, 128),
         in_specs=[pl.BlockSpec(memory_space=pl.ANY)] * len(arrays),
-        flops=10**10,
+        flops=wait * 10**9,
     )(*arrays)
 
 
@@ -276,11 +277,8 @@
         partner_device.reshape(1, FINE),
         partner_column.reshape(FINE, 1),
     )
-    asked = jnp.sum(
-        lax.all_to_all(
-            wanted, "shard", split_axis=0, concat_axis=0, axis_index_groups=PLANES, tiled=True
-        ),
-        axis=0,
+    asked = lax.all_to_all(
+        wanted, "shard", split_axis=0, concat_axis=0, axis_index_groups=PLANES, tiled=True
     )
     sends = call(
         send_core_kernel,
@@ -326,9 +324,9 @@
             )(place, grad, got, got_y, weight, first, second, *[wanted] * half)
         )
 
-    def pick(planes, sources, after=()):
-        if after:
-            after = (*after, token(sources))
+    def pick(planes, sources, wait, after=()):
+        if wait:
+            after = (*after, token(sources, wait))
         return call(
             lambda *refs: pick_kernel(planes, *refs),
             shape(PLANE, SENT, WIDE),
@@ -348,17 +346,18 @@
         return lax.ppermute(pair[0], "shard", UP), lax.ppermute(pair[1], "shard", DOWN)
 
     one = [around((x, x)) for x in state]
-    one[1] = hold(one[1], asked)
+    rows = pick((0, 0, -1, 1), (*state, *one[0]), 10)
+    far1 = to_plane(rows)
+    one = [hold(one[0], rows), hold(one[1], wait=10)]
     two = [around(pair) for pair in one]
     three = [around(pair) for pair in two]
     four = (
         lax.ppermute(three[0][0], "shard", UP),
         lax.ppermute(three[1][1], "shard", DOWN),
     )
-    far1 = to_plane(pick((0, 0, -1, 1), (*state, *one[0])))
-    far2 = to_plane(pick((-1, 1, -2, 2), (*one[1], *two[0]), (far1,)))
-    far3 = to_plane(pick((-2, 2, -3, 3), (*two[1], *three[0]), (far2,)))
-    far4 = to_plane(pick((-3, 3, 4, 4), (*three[1], *four), (far3,)))
+    far2 = to_plane(pick((-1, 1, -2, 2), (*one[1], *two[0]), 5, (far1,)))
+    far3 = to_plane(pick((-2, 2, -3, 3), (*two[1], *three[0]), 10, (far2,)))
+    far4 = to_plane(pick((-3, 3, 4, 4), (*three[1], *four), 10, (far3,)))
 
     acc = []
     for half, parts in enumerate(

time: 177 us -> 179 us (1.011)
  blocking collectives: 13.5 us -> 0 us
  starting transfers between devices: 56.8 us -> 64 us
  waiting for transfers between devices: 58.8 us -> 65.6 us
    all_to_all x1 -> x0, blocking collectives: 13.5 us -> none  [on_device(): lax.all_to_all(wanted, 'shard', split_axis=0, concat_axis=0, axis_index_g...]
    all_to_all x0 -> x1, starting transfers between devices: none -> 7.17 us  [on_device(): lax.all_to_all(wanted, 'shard', split_axis=0, concat_axis=0, axis_index_g...]
    ppermute x6, waiting for transfers between devices: 9.58 us -> 13.7 us  [around(): lax.ppermute(pair[0], 'shard', UP)]
    ppermute x2, waiting for transfers between devices: 3.71 us -> 6.07 us  [on_device(): got_y = lax.ppermute(passed, 'dp', NEXT_Y)]
    unnamed x55 -> x57, local copies, waits for them, and re-layouts: 14.2 us -> 15.2 us
  transfers between devices with their start and end apart: 22 -> 23, of which waited for: 9 -> 10; matrix products, arithmetic and copies ran while one was open for 0% -> 0% of each run, Pallas kernels for 12% -> 12%
where the time goes in v6:
time: 179 us; the launch traced here: 177 us
  waiting for transfers between devices  65.6 us (37%)
  starting transfers between devices  64 us (36%)
  Pallas kernels  31.4 us (18%)
  local copies, waits for them, and re-layouts  15.4 us (9%)
    all_to_all x4, starting transfers between devices, to_plane(): lax.all_to_all(rows, 'shard', split_axis=0, concat_axis=0, axis_index_gro...  27.3 us
    ppermute x6, waiting for transfers between devices, around(): lax.ppermute(pair[1], 'shard', DOWN)  23.1 us
    ppermute x6, starting transfers between devices, around(): lax.ppermute(pair[1], 'shard', DOWN)  20.4 us
    all_to_all x4, waiting for transfers between devices, to_plane(): lax.all_to_all(rows, 'shard', split_axis=0, concat_axis=0, axis_index_gro...  19.3 us
    unnamed x57, local copies, waits for them, and re-layouts  15.2 us
    pallas_call x4, Pallas kernels, pick(): call(lambda *refs: pick_kernel(planes, *refs), shape(PLANE, SENT, WIDE),...  14.3 us
    ppermute x6, waiting for transfers between devices, around(): lax.ppermute(pair[0], 'shard', UP)  13.7 us
    all_to_all x1, starting transfers between devices, on_device(): lax.all_to_all(wanted, 'shard', split_axis=0, concat_axis=0, axis_index_g...  7.17 us
  transfers between devices with their start and end apart: 23, of which 10 were waited for; matrix products, arithmetic and copies ran while one was open for 0% of the time, Pallas kernels for 12%

profile of v6, /device:TPU:2, one launch (start us, length us, event | category | flops | bytes accessed | tf_op | source)
XLA Modules:
  0.0 177.4 jit_solution(12311425873138122642)
XLA Ops:
  0.6 0.1 pad_add_fusion.place.refs_0_
  0.7 1.2 copy-done
  1.9 0.6 shard_map.86
  2.5 0.1 collective-permute-start
  2.6 1.8 %collective-permute-done.refs_2_ = f32[224,512]{1,0:T(8,128)S(1)} collective-permute-done((f32[224,512]{1,0:T(8,128)S(1)}, f32[224,512]{1,0:T(8,128)S(1)}, u32[]{:S(2)}, u32[]{:S(2)}) %collective-permute-start) | collective-permute-done | bytes 458784 | tf_op jit(solution)/shard_map/ppermute | solution.py:289
  4.4 0.6 shard_map.87
  5.0 1.7 collective-permute-start.1
  6.7 0.0 collective-permute-start.2
  6.7 6.1 %collective-permute-done.1.refs_3_ = f32[224,256]{1,0:T(8,128)S(1)} collective-permute-done((f32[224,256]{1,0:T(8,128)S(1)}, f32[224,256]{1,0:T(8,128)S(1)}, u32[]{:S(2)}, u32[]{:S(2)}) %collective-permute-start.1) | collective-permute-done | bytes 229408 | tf_op jit(solution)/shard_map/ppermute | solution.py:305
  12.7 0.8 shard_map.88.refs_0_.refs_2_.refs_1_
  13.5 0.0 copy-start.26
  13.5 0.0 copy-start.27
  13.5 0.0 copy-start.1
  13.5 2.0 %collective-permute-start.4 = (f32[224,768]{1,0:T(8,128)S(1)}, f32[224,768]{1,0:T(8,128)S(1)}, u32[]{:S(2)}, u32[]{:S(2)}) collective-permute-start(f32[224,768]{1,0:T(8,128)S(1)} %shard_map.88.refs_0_.refs_2_.refs_1_), channel_id=1, source_target_pairs={{0,8},{1,9},{2,10},{3,11},{4,12},{5,13},{6,14},{7,15},{8,16},{9,17... | collective-permute-start | bytes 2064392 | tf_op jit(solution)/shard_map/ppermute | solution.py:346
  15.5 4.0 %collective-permute-start.5 = (f32[224,768]{1,0:T(8,128)S(1)}, f32[224,768]{1,0:T(8,128)}, u32[]{:S(2)}, u32[]{:S(2)}) collective-permute-start(f32[224,768]{1,0:T(8,128)S(1)} %shard_map.88.refs_0_.refs_2_.refs_1_), channel_id=1, source_target_pairs={{8,0},{9,1},{10,2},{11,3},{12,4},{13,5},{14,6},{15,7},{16,8},{17,9... | collective-permute-start | bytes 2064392 | tf_op jit(solution)/shard_map/ppermute | solution.py:346
  19.6 1.3 shard_map.89
  20.8 1.6 collective-permute-start.3
  22.4 0.1 copy.14.dev
  22.6 0.1 copy.15.col
  22.7 1.9 %shard_map.85 = (s32[8,8,128]{2,1,0:T(8,128)}, s32[448,128]{1,0:T(8,128)S(1)}) custom-call(s32[2]{0:T(128)S(1)} %pad_add_fusion.place.refs_0_, s32[448,1]{1,0:T(8,128)S(1)} %copy.14.dev, s32[1,448]{1,0:T(1,128)S(1)} %bitcast.10, s32[448,1]{1,0:T(8,128)S(1)} %copy.15.col), custom_call_target="tpu_custom_call" | custom-call | bytes 1048576 | tf_op jit(solution)/shard_map/pallas_call | solution.py:269
  24.6 7.2 %all-to-all-start = ((s32[8,8,128]{2,1,0:T(8,128)}), s32[8,8,128]{2,1,0:T(8,128)S(1)}, u32[]{:S(2)}, u32[]{:S(2)}) async-start(s32[8,8,128]{2,1,0:T(8,128)} %get-tuple-element.13.refs_7_), calls=%async_computation | async-start | bytes 65536 | tf_op jit(solution)/shard_map/all_to_all | solution.py:280
  31.8 0.7 copy-done.24
  32.5 1.0 copy-done.17
  33.5 1.0 copy-done.19
  34.5 1.0 copy-done.21
  35.5 1.0 copy-done.23
  36.6 0.9 copy-done.25
  37.5 0.8 shard_map.90.refs_1_.refs_3_
  38.3 0.1 collective-permute-start.6
  38.4 3.2 %collective-permute-start.7 = (f32[224,768]{1,0:T(8,128)S(1)}, f32[224,768]{1,0:T(8,128)}, u32[]{:S(2)}, u32[]{:S(2)}) collective-permute-start(f32[224,768]{1,0:T(8,128)S(1)} %shard_map.90.refs_1_.refs_3_), channel_id=1, source_target_pairs={{8,0},{9,1},{10,2},{11,3},{12,4},{13,5},{14,6},{15,7},{16,8},{17,9... | collective-permute-start | bytes 2064392 | tf_op jit(solution)/shard_map/ppermute | solution.py:346
  41.6 0.8 copy-done.12
  42.4 2.8 %shard_map.92.refs_2_ = f32[8,56,768]{2,1,0:T(8,128)} custom-call(s32[2]{0:T(128)S(1)} %pad_add_fusion.place.refs_0_, s32[8,8,128]{2,1,0:T(8,128)S(1)} %all-to-all-done.refs_1_, f32[224,768]{1,0:T(8,128)S(1)} %shard_map.88.refs_0_.refs_2_.refs_1_, f32[224,768]{1,0:T(8,128)S(1)} %shard_map.90.refs_1_.refs_3_, ...), custom_call_target="tpu_custom_call" | custom-call | flops 352321536 | bytes 5242880 | tf_op jit(solution)/shard_map/pallas_call | solution.py:330
  45.3 7.2 %all-to-all-start.1 = ((f32[8,56,768]{2,1,0:T(8,128)}), f32[8,56,768]{2,1,0:T(8,128)S(1)}, u32[]{:S(2)}, u32[]{:S(2)}) async-start(f32[8,56,768]{2,1,0:T(8,128)} %shard_map.92.refs_2_), calls=%async_computation.1 | async-start | bytes 2752512 | tf_op jit(solution)/shard_map/all_to_all | solution.py:341
  52.5 3.2 %collective-permute-start.9 = (f32[224,768]{1,0:T(8,128)}, f32[224,768]{1,0:T(8,128)S(1)}, u32[]{:S(2)}, u32[]{:S(2)}) collective-permute-start(f32[224,768]{1,0:T(8,128)} %get-tuple-element.18), channel_id=1, source_target_pairs={{8,0},{9,1},{10,2},{11,3},{12,4},{13,5},{14,6},{15,7},{16,8},{17,9... | collective-permute-start | bytes 2064392 | tf_op jit(solution)/shard_map/ppermute | solution.py:346
  55.7 1.0 collective-permute-done.6.refs_0_
  56.7 3.0 %collective-permute-start.11 = (f32[224,768]{1,0:T(8,128)}, f32[224,768]{1,0:T(8,128)}, u32[]{:S(2)}, u32[]{:S(2)}) collective-permute-start(f32[224,768]{1,0:T(8,128)} %get-tuple-element.16.refs_1_.refs_3_), channel_id=1, source_target_pairs={{8,0},{9,1},{10,2},{11,3},{12,4},{13,5},{14,6},{15,7},{16,8},{17,9... | collective-permute-start | bytes 2064392 | tf_op jit(solution)/shard_map/ppermute | solution.py:346
  59.6 12.7 %collective-permute-done.8.refs_2_.refs_4_ = f32[224,768]{1,0:T(8,128)} collective-permute-done((f32[224,768]{1,0:T(8,128)}, f32[224,768]{1,0:T(8,128)}, u32[]{:S(2)}, u32[]{:S(2)}) %collective-permute-start.8) | collective-permute-done | bytes 688160 | tf_op jit(solution)/shard_map/ppermute | solution.py:346
  72.4 3.2 %collective-permute-start.13 = (f32[224,768]{1,0:T(8,128)S(1)}, f32[224,768]{1,0:T(8,128)}, u32[]{:S(2)}, u32[]{:S(2)}) collective-permute-start(f32[224,768]{1,0:T(8,128)S(1)} %collective-permute-done.9.refs_3_.refs_5_), channel_id=1, source_target_pairs={{8,0},{9,1},{10,2},{11,3},{12,4},{13,5},{14,6},{15,7},{16,8},{17,9... | collective-permute-start | bytes 2064392 | tf_op jit(solution)/shard_map/ppermute | solution.py:346
  75.6 11.0 %collective-permute-done.11.refs_1_.refs_3_ = f32[224,768]{1,0:T(8,128)} collective-permute-done((f32[224,768]{1,0:T(8,128)}, f32[224,768]{1,0:T(8,128)}, u32[]{:S(2)}, u32[]{:S(2)}) %collective-permute-start.11) | collective-permute-done | bytes 688160 | tf_op jit(solution)/shard_map/ppermute | solution.py:346
  86.6 3.7 %collective-permute-start.15 = (f32[224,768]{1,0:T(8,128)}, f32[224,768]{1,0:T(8,128)}, u32[]{:S(2)}, u32[]{:S(2)}) collective-permute-start(f32[224,768]{1,0:T(8,128)} %collective-permute-done.11.refs_1_.refs_3_), channel_id=1, source_target_pairs={{8,0},{9,1},{10,2},{11,3},{12,4},{13,5},{14,6},{15,7},{16,8},{17,9... | collective-permute-start | bytes 2064392 | tf_op jit(solution)/shard_map/ppermute | solution.py:346
  90.3 3.7 %shard_map.96 = f32[8,56,768]{2,1,0:T(8,128)} custom-call(s32[2]{0:T(128)S(1)} %pad_add_fusion.place.refs_0_, s32[8,8,128]{2,1,0:T(8,128)S(1)} %all-to-all-done.refs_1_, f32[224,768]{1,0:T(8,128)} %get-tuple-element.15.refs_0_.refs_2_, f32[224,768]{1,0:T(8,128)} %get-tuple-element.16.refs_1_.refs_3_, f32[224,768]{1,0:T(8,128)} %collective-permute-done.8.refs_2_.refs_4_, ...), custom_call_target="tpu_custom_call" | custom-call | flops 352321536 | bytes 5242880 | tf_op jit(solution)/shard_map/pallas_call | solution.py:330
  94.1 7.2 %all-to-all-start.2 = ((f32[8,56,768]{2,1,0:T(8,128)}), f32[8,56,768]{2,1,0:T(8,128)S(1)}, u32[]{:S(2)}, u32[]{:S(2)}) async-start(f32[8,56,768]{2,1,0:T(8,128)} %shard_map.96), calls=%async_computation.2 | async-start | bytes 2752512 | tf_op jit(solution)/shard_map/all_to_all | solution.py:341
  101.3 0.1 collective-permute-start.16
  101.4 12.0 %collective-permute-done.15.refs_1_.refs_3_ = f32[224,768]{1,0:T(8,128)} collective-permute-done((f32[224,768]{1,0:T(8,128)}, f32[224,768]{1,0:T(8,128)}, u32[]{:S(2)}, u32[]{:S(2)}) %collective-permute-start.15) | collective-permute-done | bytes 688160 | tf_op jit(solution)/shard_map/ppermute | solution.py:346
  113.4 3.7 %collective-permute-start.17 = (f32[224,768]{1,0:T(8,128)}, f32[224,768]{1,0:T(8,128)}, u32[]{:S(2)}, u32[]{:S(2)}) collective-permute-start(f32[224,768]{1,0:T(8,128)} %collective-permute-done.15.refs_1_.refs_3_), channel_id=1, source_target_pairs={{8,0},{9,1},{10,2},{11,3},{12,4},{13,5},{14,6},{15,7},{16,8},{17,9... | collective-permute-start | bytes 2064392 | tf_op jit(solution)/shard_map/ppermute | solution.py:356
  117.1 0.0 copy-start.6
  117.2 3.7 %shard_map.98 = f32[8,56,768]{2,1,0:T(8,128)} custom-call(s32[2]{0:T(128)S(1)} %pad_add_fusion.place.refs_0_, s32[8,8,128]{2,1,0:T(8,128)S(1)} %all-to-all-done.refs_1_, f32[224,768]{1,0:T(8,128)S(1)} %collective-permute-done.10.refs_0_.refs_2_, f32[224,768]{1,0:T(8,128)} %collective-permute-done.11.refs_1_.refs_3_, ...), custom_call_target="tpu_custom_call" | custom-call | flops 352321536 | bytes 5242880 | tf_op jit(solution)/shard_map/pallas_call | solution.py:330
  120.9 7.2 %all-to-all-start.3 = ((f32[8,56,768]{2,1,0:T(8,128)}), f32[8,56,768]{2,1,0:T(8,128)S(1)}, u32[]{:S(2)}, u32[]{:S(2)}) async-start(f32[8,56,768]{2,1,0:T(8,128)} %shard_map.98), calls=%async_computation.3 | async-start | bytes 2752512 | tf_op jit(solution)/shard_map/all_to_all | solution.py:341
  128.1 0.8 collective-permute-done.16.refs_2_.refs_4_
  128.9 0.8 collective-permute-done.17.refs_3_.refs_5_
  129.7 13.8 %all-to-all-done.3.refs_4_.refs_6_ = f32[8,56,768]{2,1,0:T(8,128)S(1)} async-done(((f32[8,56,768]{2,1,0:T(8,128)}), f32[8,56,768]{2,1,0:T(8,128)S(1)}, u32[]{:S(2)}, u32[]{:S(2)}) %all-to-all-start.3) | async-done | bytes 1376288 | tf_op jit(solution)/shard_map/all_to_all | solution.py:341
  143.5 4.0 %shard_map.102 = f32[8,56,768]{2,1,0:T(8,128)} custom-call(s32[2]{0:T(128)S(1)} %pad_add_fusion.place.refs_0_, s32[8,8,128]{2,1,0:T(8,128)S(1)} %all-to-all-done.refs_1_, f32[224,768]{1,0:T(8,128)} %collective-permute-done.14.refs_0_.refs_2_, f32[224,768]{1,0:T(8,128)} %collective-permute-done.15.refs_1_.refs_3_, ...), custom_call_target="tpu_custom_call" | custom-call | flops 352321536 | bytes 5242880 | tf_op jit(solution)/shard_map/pallas_call | solution.py:330
  147.5 5.7 %all-to-all-start.4 = ((f32[8,56,768]{2,1,0:T(8,128)}), f32[8,56,768]{2,1,0:T(8,128)S(1)}, u32[]{:S(2)}, u32[]{:S(2)}) async-start(f32[8,56,768]{2,1,0:T(8,128)} %shard_map.102), calls=%async_computation.4 | async-start | bytes 2752512 | tf_op jit(solution)/shard_map/all_to_all | solution.py:341
  153.1 1.3 copy-done.5
  154.5 1.3 copy-done.7
  155.8 1.3 copy-done.9
  157.2 0.9 copy-done.14
  158.1 3.2 %shard_map.99.refs_0_.refs_1_.refs_2_ = f32[448,768]{1,0:T(8,128)S(1)} custom-call(s32[448,128]{1,0:T(8,128)S(1)} %copy-done.14, f32[224,768]{1,0:T(8,128)S(1)} %shard_map.88.refs_0_.refs_2_.refs_1_, f32[8,56,768]{2,1,0:T(8,128)S(1)} %copy-done.5, f32[8,56,768]{2,1,0:T(8,128)S(1)} %copy-done.7, f32[8,56,768]{2,1,0:T(8,128)S(1)} %copy-done.9), custom_call_target="tpu_custom_call" | custom-call | flops 1541406720 | bytes 8388608 | tf_op jit(solution)/shard_map/pallas_call | solution.py:370
  161.3 2.8 %shard_map.100.refs_3_.refs_4_.refs_5_ = f32[448,768]{1,0:T(8,128)S(1)} custom-call(s32[448,128]{1,0:T(8,128)S(1)} %copy-done.14, f32[224,768]{1,0:T(8,128)S(1)} %copy-done.11, f32[8,56,768]{2,1,0:T(8,128)S(1)} %copy-done.5, f32[8,56,768]{2,1,0:T(8,128)S(1)} %copy-done.7, f32[8,56,768]{2,1,0:T(8,128)S(1)} %copy-done.9), custom_call_target="tpu_custom_call" | custom-call | flops 1541406720 | bytes 8388608 | tf_op jit(solution)/shard_map/pallas_call | solution.py:370
  164.1 0.0 copy-start.2
  164.1 1.1 copy-done.2
  165.2 5.6 %all-to-all-done.4.refs_6_.refs_7_.refs_8_ = f32[8,56,768]{2,1,0:T(8,128)S(1)} async-done(((f32[8,56,768]{2,1,0:T(8,128)}), f32[8,56,768]{2,1,0:T(8,128)S(1)}, u32[]{:S(2)}, u32[]{:S(2)}) %all-to-all-start.4) | async-done | bytes 1376288 | tf_op jit(solution)/shard_map/all_to_all | solution.py:341
  170.8 1.3 copy-done.3
  172.1 5.3 %shard_map.103 = (f32[448,1024]{1,0:T(8,128)}, f32[448,1024]{1,0:T(8,128)}, f32[448,1024]{1,0:T(8,128)}) custom-call(s32[448,128]{1,0:T(8,128)S(1)} %copy-done.15, f32[448,768]{1,0:T(8,128)S(1)} %shard_map.99.refs_0_.refs_1_.refs_2_, f32[448,768]{1,0:T(8,128)S(1)} %shard_map.99.refs_0_.refs_1_.refs_2_, f32[448,768]{1,0:T(8,128)S(1)} %shard_map.99.refs_0_.refs_1_.refs_2_, ...), custom_call_target="tpu_custom_call" | custom-call | flops 1409286144 | bytes 12582912 | tf_op jit(solution)/shard_map/pallas_call | solution.py:395
  (60 shorter events, 0.1 us)
Async XLA Ops:
  0.7 1.2 copy-start
  1.9 10.8 %copy-start.18 = (f32[224,512]{1,0:T(8,128)S(1)}, f32[224,512]{1,0:T(8,128)}, u32[]{:S(2)}) copy-start(f32[224,512]{1,0:T(8,128)} %refs_4_.3) | copy-start | bytes 1376260
  1.9 10.8 %copy-start.20 = (f32[224,512]{1,0:T(8,128)S(1)}, f32[224,512]{1,0:T(8,128)}, u32[]{:S(2)}) copy-start(f32[224,512]{1,0:T(8,128)} %refs_5_.3) | copy-start | bytes 1376260
  1.9 10.8 %copy-start.22 = (f32[224,512]{1,0:T(8,128)S(1)}, f32[224,512]{1,0:T(8,128)}, u32[]{:S(2)}) copy-start(f32[224,512]{1,0:T(8,128)} %refs_6_.3) | copy-start | bytes 1376260
  2.5 1.9 %collective-permute-start = (f32[224,512]{1,0:T(8,128)S(1)}, f32[224,512]{1,0:T(8,128)S(1)}, u32[]{:S(2)}, u32[]{:S(2)}) collective-permute-start(f32[224,512]{1,0:T(8,128)S(1)} %get-tuple-element.12), channel_id=1, source_target_pairs={{0,64},{64,0},{128,192},{192,128},{1,65},{65,1},{129,193},{193,129... | collective-permute-start | bytes 1376264 | tf_op jit(solution)/shard_map/ppermute | solution.py:289
  5.0 7.7 %collective-permute-start.1 = (f32[224,256]{1,0:T(8,128)S(1)}, f32[224,256]{1,0:T(8,128)S(1)}, u32[]{:S(2)}, u32[]{:S(2)}) collective-permute-start(f32[224,256]{1,0:T(8,128)S(1)} %shard_map.87), channel_id=1, source_target_pairs={{0,128},{128,0},{64,192},{192,64},{1,129},{129,1},{65,193},{193,65... | collective-permute-start | bytes 688136 | tf_op jit(solution)/shard_map/ppermute | solution.py:305
  6.7 12.9 %collective-permute-start.2 = (f32[224,512]{1,0:T(8,128)S(1)}, f32[224,512]{1,0:T(8,128)S(1)}, u32[]{:S(2)}, u32[]{:S(2)}) collective-permute-start(f32[224,512]{1,0:T(8,128)S(1)} %get-tuple-element.14), channel_id=1, source_target_pairs={{0,64},{64,0},{128,192},{192,128},{1,65},{65,1},{129,193},{193,129... | collective-permute-start | bytes 1376264 | tf_op jit(solution)/shard_map/ppermute | solution.py:289
  13.5 8.9 %copy-start.26 = (s32[448,1]{0,1:T(1,128)S(1)}, s32[448,1]{0,1:T(1,128)}, u32[]{:S(2)}) copy-start(s32[448,1]{0,1:T(1,128)} %param.10) | copy-start | bytes 5380
  13.5 9.0 %copy-start.27 = (s32[448]{0:T(512)S(1)}, s32[448]{0:T(512)}, u32[]{:S(2)}) copy-start(s32[448]{0:T(512)} %param.11) | copy-start | bytes 5380
  13.5 19.0 %copy-start.1 = (bf16[1,224,2048]{2,1,0:T(8,128)(2,1)S(1)}, bf16[1,224,2048]{2,1,0:T(8,128)(2,1)}, u32[]{:S(2)}) copy-start(bf16[1,224,2048]{2,1,0:T(8,128)(2,1)} %param.6) | copy-start | bytes 2752516
  13.5 28.1 %collective-permute-start.4 = (f32[224,768]{1,0:T(8,128)S(1)}, f32[224,768]{1,0:T(8,128)S(1)}, u32[]{:S(2)}, u32[]{:S(2)}) collective-permute-start(f32[224,768]{1,0:T(8,128)S(1)} %shard_map.88.refs_0_.refs_2_.refs_1_), channel_id=1, source_target_pairs={{0,8},{1,9},{2,10},{3,11},{4,12},{5,13},{6,14},{7,15},{8,16},{9,17... | collective-permute-start | bytes 2064392 | tf_op jit(solution)/shard_map/ppermute | solution.py:346
  15.5 26.1 %collective-permute-start.5 = (f32[224,768]{1,0:T(8,128)S(1)}, f32[224,768]{1,0:T(8,128)}, u32[]{:S(2)}, u32[]{:S(2)}) collective-permute-start(f32[224,768]{1,0:T(8,128)S(1)} %shard_map.88.refs_0_.refs_2_.refs_1_), channel_id=1, source_target_pairs={{8,0},{9,1},{10,2},{11,3},{12,4},{13,5},{14,6},{15,7},{16,8},{17,9... | collective-permute-start | bytes 2064392 | tf_op jit(solution)/shard_map/ppermute | solution.py:346
  19.6 3.1 %copy-start.16 = (f32[224,512]{1,0:T(8,128)}, f32[224,512]{1,0:T(8,128)S(1)}, u32[]{:S(2)}) copy-start(f32[224,512]{1,0:T(8,128)S(1)} %collective-permute-done.2.refs_2_) | copy-start | bytes 1376260
  20.8 11.0 %collective-permute-start.3 = (f32[224,256]{1,0:T(8,128)}, f32[224,256]{1,0:T(8,128)S(1)}, u32[]{:S(2)}, u32[]{:S(2)}) collective-permute-start(f32[224,256]{1,0:T(8,128)} %shard_map.89), channel_id=1, source_target_pairs={{0,128},{128,0},{64,192},{192,64},{1,129},{129,1},{65,193},{193,65... | collective-permute-start | bytes 688136 | tf_op jit(solution)/shard_map/ppermute | solution.py:305
  24.6 13.6 %copy-start.13 = (s32[448,128]{1,0:T(8,128)}, s32[448,128]{1,0:T(8,128)S(1)}, u32[]{:S(2)}) copy-start(s32[448,128]{1,0:T(8,128)S(1)} %get-tuple-element.11.refs_0_.codes) | copy-start | bytes 688132
  24.6 17.0 %all-to-all-start = ((s32[8,8,128]{2,1,0:T(8,128)}), s32[8,8,128]{2,1,0:T(8,128)S(1)}, u32[]{:S(2)}, u32[]{:S(2)}) async-start(s32[8,8,128]{2,1,0:T(8,128)} %get-tuple-element.13.refs_7_), calls=%async_computation | async-start | bytes 65536 | tf_op jit(solution)/shard_map/all_to_all | solution.py:280
  31.8 0.7 copy-start.24
  32.5 1.0 copy-start.17
  33.5 1.0 copy-start.19
  34.5 1.0 copy-start.21
  35.5 1.0 copy-start.23
  36.6 0.9 copy-start.25
  38.3 3.4 %copy-start.10 = (f32[224,768]{1,0:T(8,128)}, f32[224,768]{1,0:T(8,128)S(1)}, u32[]{:S(2)}) copy-start(f32[224,768]{1,0:T(8,128)S(1)} %shard_map.90.refs_1_.refs_3_) | copy-start | bytes 2064388
  38.3 18.4 %collective-permute-start.6 = (f32[224,768]{1,0:T(8,128)S(1)}, f32[224,768]{1,0:T(8,128)}, u32[]{:S(2)}, u32[]{:S(2)}) collective-permute-start(f32[224,768]{1,0:T(8,128)S(1)} %shard_map.90.refs_1_.refs_3_), channel_id=1, source_target_pairs={{0,8},{1,9},{2,10},{3,11},{4,12},{5,13},{6,14},{7,15},{8,16},{9,17... | collective-permute-start | bytes 2064392 | tf_op jit(solution)/shard_map/ppermute | solution.py:346
  38.4 18.3 %collective-permute-start.7 = (f32[224,768]{1,0:T(8,128)S(1)}, f32[224,768]{1,0:T(8,128)}, u32[]{:S(2)}, u32[]{:S(2)}) collective-permute-start(f32[224,768]{1,0:T(8,128)S(1)} %shard_map.90.refs_1_.refs_3_), channel_id=1, source_target_pairs={{8,0},{9,1},{10,2},{11,3},{12,4},{13,5},{14,6},{15,7},{16,8},{17,9... | collective-permute-start | bytes 2064392 | tf_op jit(solution)/shard_map/ppermute | solution.py:346
  41.6 0.8 copy-start.12
  45.3 45.1 %all-to-all-start.1 = ((f32[8,56,768]{2,1,0:T(8,128)}), f32[8,56,768]{2,1,0:T(8,128)S(1)}, u32[]{:S(2)}, u32[]{:S(2)}) async-start(f32[8,56,768]{2,1,0:T(8,128)} %shard_map.92.refs_2_), calls=%async_computation.1 | async-start | bytes 2752512 | tf_op jit(solution)/shard_map/all_to_all | solution.py:341
  52.5 19.9 %collective-permute-start.8 = (f32[224,768]{1,0:T(8,128)}, f32[224,768]{1,0:T(8,128)}, u32[]{:S(2)}, u32[]{:S(2)}) collective-permute-start(f32[224,768]{1,0:T(8,128)} %get-tuple-element.17), channel_id=1, source_target_pairs={{0,8},{1,9},{2,10},{3,11},{4,12},{5,13},{6,14},{7,15},{8,16},{9,17... | collective-permute-start | bytes 2064392 | tf_op jit(solution)/shard_map/ppermute | solution.py:346
  52.5 19.9 %collective-permute-start.9 = (f32[224,768]{1,0:T(8,128)}, f32[224,768]{1,0:T(8,128)S(1)}, u32[]{:S(2)}, u32[]{:S(2)}) collective-permute-start(f32[224,768]{1,0:T(8,128)} %get-tuple-element.18), channel_id=1, source_target_pairs={{8,0},{9,1},{10,2},{11,3},{12,4},{13,5},{14,6},{15,7},{16,8},{17,9... | collective-permute-start | bytes 2064392 | tf_op jit(solution)/shard_map/ppermute | solution.py:346
  56.7 30.0 %collective-permute-start.11 = (f32[224,768]{1,0:T(8,128)}, f32[224,768]{1,0:T(8,128)}, u32[]{:S(2)}, u32[]{:S(2)}) collective-permute-start(f32[224,768]{1,0:T(8,128)} %get-tuple-element.16.refs_1_.refs_3_), channel_id=1, source_target_pairs={{8,0},{9,1},{10,2},{11,3},{12,4},{13,5},{14,6},{15,7},{16,8},{17,9... | collective-permute-start | bytes 2064392 | tf_op jit(solution)/shard_map/ppermute | solution.py:346
  59.6 41.7 %collective-permute-start.10 = (f32[224,768]{1,0:T(8,128)}, f32[224,768]{1,0:T(8,128)S(1)}, u32[]{:S(2)}, u32[]{:S(2)}) collective-permute-start(f32[224,768]{1,0:T(8,128)} %get-tuple-element.15.refs_0_.refs_2_), channel_id=1, source_target_pairs={{0,8},{1,9},{2,10},{3,11},{4,12},{5,13},{6,14},{7,15},{8,16},{9,17... | collective-permute-start | bytes 2064392 | tf_op jit(solution)/shard_map/ppermute | solution.py:346
  72.4 29.0 %collective-permute-start.12 = (f32[224,768]{1,0:T(8,128)}, f32[224,768]{1,0:T(8,128)}, u32[]{:S(2)}, u32[]{:S(2)}) collective-permute-start(f32[224,768]{1,0:T(8,128)} %collective-permute-done.8.refs_2_.refs_4_), channel_id=1, source_target_pairs={{0,8},{1,9},{2,10},{3,11},{4,12},{5,13},{6,14},{7,15},{8,16},{9,17... | collective-permute-start | bytes 2064392 | tf_op jit(solution)/shard_map/ppermute | solution.py:346
  72.4 44.8 %collective-permute-start.13 = (f32[224,768]{1,0:T(8,128)S(1)}, f32[224,768]{1,0:T(8,128)}, u32[]{:S(2)}, u32[]{:S(2)}) collective-permute-start(f32[224,768]{1,0:T(8,128)S(1)} %collective-permute-done.9.refs_3_.refs_5_), channel_id=1, source_target_pairs={{8,0},{9,1},{10,2},{11,3},{12,4},{13,5},{14,6},{15,7},{16,8},{17,9... | collective-permute-start | bytes 2064392 | tf_op jit(solution)/shard_map/ppermute | solution.py:346
  86.6 26.8 %collective-permute-start.15 = (f32[224,768]{1,0:T(8,128)}, f32[224,768]{1,0:T(8,128)}, u32[]{:S(2)}, u32[]{:S(2)}) collective-permute-start(f32[224,768]{1,0:T(8,128)} %collective-permute-done.11.refs_1_.refs_3_), channel_id=1, source_target_pairs={{8,0},{9,1},{10,2},{11,3},{12,4},{13,5},{14,6},{15,7},{16,8},{17,9... | collective-permute-start | bytes 2064392 | tf_op jit(solution)/shard_map/ppermute | solution.py:346
  90.3 3.7 %copy-start.4 = (f32[8,56,768]{2,1,0:T(8,128)}, f32[8,56,768]{2,1,0:T(8,128)S(1)}, u32[]{:S(2)}) copy-start(f32[8,56,768]{2,1,0:T(8,128)S(1)} %all-to-all-done.1.refs_6_.refs_2_) | copy-start | bytes 4128772
  94.1 23.1 %all-to-all-start.2 = ((f32[8,56,768]{2,1,0:T(8,128)}), f32[8,56,768]{2,1,0:T(8,128)S(1)}, u32[]{:S(2)}, u32[]{:S(2)}) async-start(f32[8,56,768]{2,1,0:T(8,128)} %shard_map.96), calls=%async_computation.2 | async-start | bytes 2752512 | tf_op jit(solution)/shard_map/all_to_all | solution.py:341
  101.3 26.8 %collective-permute-start.14 = (f32[224,768]{1,0:T(8,128)S(1)}, f32[224,768]{1,0:T(8,128)}, u32[]{:S(2)}, u32[]{:S(2)}) collective-permute-start(f32[224,768]{1,0:T(8,128)S(1)} %collective-permute-done.10.refs_0_.refs_2_), channel_id=1, source_target_pairs={{0,8},{1,9},{2,10},{3,11},{4,12},{5,13},{6,14},{7,15},{8,16},{9,17... | collective-permute-start | bytes 2064392 | tf_op jit(solution)/shard_map/ppermute | solution.py:346
  101.3 27.6 %collective-permute-start.16 = (f32[224,768]{1,0:T(8,128)}, f32[224,768]{1,0:T(8,128)}, u32[]{:S(2)}, u32[]{:S(2)}) collective-permute-start(f32[224,768]{1,0:T(8,128)} %collective-permute-done.12.refs_2_.refs_4_), channel_id=1, source_target_pairs={{0,8},{1,9},{2,10},{3,11},{4,12},{5,13},{6,14},{7,15},{8,16},{9,17... | collective-permute-start | bytes 2064392 | tf_op jit(solution)/shard_map/ppermute | solution.py:355
  113.4 16.3 %collective-permute-start.17 = (f32[224,768]{1,0:T(8,128)}, f32[224,768]{1,0:T(8,128)}, u32[]{:S(2)}, u32[]{:S(2)}) collective-permute-start(f32[224,768]{1,0:T(8,128)} %collective-permute-done.15.refs_1_.refs_3_), channel_id=1, source_target_pairs={{8,0},{9,1},{10,2},{11,3},{12,4},{13,5},{14,6},{15,7},{16,8},{17,9... | collective-permute-start | bytes 2064392 | tf_op jit(solution)/shard_map/ppermute | solution.py:356
  117.1 3.7 %copy-start.6 = (f32[8,56,768]{2,1,0:T(8,128)}, f32[8,56,768]{2,1,0:T(8,128)S(1)}, u32[]{:S(2)}) copy-start(f32[8,56,768]{2,1,0:T(8,128)S(1)} %all-to-all-done.2.refs_6_.refs_3_) | copy-start | bytes 4128772
  120.9 22.6 %all-to-all-start.3 = ((f32[8,56,768]{2,1,0:T(8,128)}), f32[8,56,768]{2,1,0:T(8,128)S(1)}, u32[]{:S(2)}, u32[]{:S(2)}) async-start(f32[8,56,768]{2,1,0:T(8,128)} %shard_map.98), calls=%async_computation.3 | async-start | bytes 2752512 | tf_op jit(solution)/shard_map/all_to_all | solution.py:341
  143.5 4.0 %copy-start.8 = (f32[8,56,768]{2,1,0:T(8,128)}, f32[8,56,768]{2,1,0:T(8,128)S(1)}, u32[]{:S(2)}) copy-start(f32[8,56,768]{2,1,0:T(8,128)S(1)} %all-to-all-done.3.refs_4_.refs_6_) | copy-start | bytes 4128772
  147.5 23.3 %all-to-all-start.4 = ((f32[8,56,768]{2,1,0:T(8,128)}), f32[8,56,768]{2,1,0:T(8,128)S(1)}, u32[]{:S(2)}, u32[]{:S(2)}) async-start(f32[8,56,768]{2,1,0:T(8,128)} %shard_map.102), calls=%async_computation.4 | async-start | bytes 2752512 | tf_op jit(solution)/shard_map/all_to_all | solution.py:341
  153.1 1.3 copy-start.5
  154.5 1.3 copy-start.7
  155.8 1.3 copy-start.9
  157.2 0.9 copy-start.14
  158.1 3.2 %copy-start.11 = (f32[224,768]{1,0:T(8,128)S(1)}, f32[224,768]{1,0:T(8,128)}, u32[]{:S(2)}) copy-start(f32[224,768]{1,0:T(8,128)} %copy-done.10) | copy-start | bytes 2064388
  161.3 9.4 %copy-start.15 = (s32[448,128]{1,0:T(8,128)S(1)}, s32[448,128]{1,0:T(8,128)}, u32[]{:S(2)}) copy-start(s32[448,128]{1,0:T(8,128)} %copy-done.13) | copy-start | bytes 688132
  164.1 1.1 copy-start.2
  170.8 1.3 copy-start.3

commit v7 on v6

--- a/solution.py
+++ b/solution.py
@@ -346,18 +346,22 @@
         return lax.ppermute(pair[0], "shard", UP), lax.ppermute(pair[1], "shard", DOWN)
 
     one = [around((x, x)) for x in state]
-    rows = pick((0, 0, -1, 1), (*state, *one[0]), 10)
+    rows = pick((0, 0, -1, 1), (*state, *one[0]), 4)
     far1 = to_plane(rows)
     one = [hold(one[0], rows), hold(one[1], wait=10)]
     two = [around(pair) for pair in one]
+    rows = pick((-1, 1, -2, 2), (*one[1], *two[0]), 5, (far1,))
+    far2 = to_plane(rows)
+    two = [hold(two[0], rows), hold(two[1], wait=10)]
     three = [around(pair) for pair in two]
+    rows = pick((-2, 2, -3, 3), (*two[1], *three[0]), 5, (far2,))
+    far3 = to_plane(rows)
+    three = [hold(three[0], rows), hold(three[1], wait=10)]
     four = (
         lax.ppermute(three[0][0], "shard", UP),
         lax.ppermute(three[1][1], "shard", DOWN),
     )
-    far2 = to_plane(pick((-1, 1, -2, 2), (*one[1], *two[0]), 5, (far1,)))
-    far3 = to_plane(pick((-2, 2, -3, 3), (*two[1], *three[0]), 10, (far2,)))
-    far4 = to_plane(pick((-3, 3, 4, 4), (*three[1], *four), 10, (far3,)))
+    far4 = to_plane(pick((-3, 3, 4, 4), (*three[1], *four), 5, (far3,)))
 
     acc = []
     for half, parts in enumerate(

time: 179 us -> 170 us (0.950)
  waiting for transfers between devices: 65.6 us -> 55.6 us
  local copies, waits for them, and re-layouts: 15.4 us -> 18.5 us
    ppermute x6, waiting for transfers between devices: 23.1 us -> 0.02 us  [around(): lax.ppermute(pair[1], 'shard', DOWN)]
    all_to_all x4, waiting for transfers between devices: 19.3 us -> 0.01 us  [to_plane(): lax.all_to_all(rows, 'shard', split_axis=0, concat_axis=0, axis_index_gro...]
    ppermute x6, waiting for transfers between devices: 13.7 us -> 26.6 us  [around(): lax.ppermute(pair[0], 'shard', UP)]
    ppermute x1, waiting for transfers between devices: 0.8 us -> 8.77 us  [on_device(): lax.ppermute(three[1][1], 'shard', DOWN)]
    all_to_all x1, waiting for transfers between devices: 0.01 us -> 6.23 us  [on_device(): lax.all_to_all(wanted, 'shard', split_axis=0, concat_axis=0, axis_index_g...]
    unnamed x57 -> x63, local copies, waits for them, and re-layouts: 15.2 us -> 18.4 us
    ppermute x2, waiting for transfers between devices: 6.07 us -> 9.02 us  [on_device(): got_y = lax.ppermute(passed, 'dp', NEXT_Y)]
    ppermute x1, waiting for transfers between devices: 0.82 us -> 3.59 us  [on_device(): lax.ppermute(three[0][0], 'shard', UP)]
  transfers between devices with their start and end apart: 23 -> 23, of which waited for: 10 -> 8; matrix products, arithmetic and copies ran while one was open for 0% -> 0% of each run, Pallas kernels for 12% -> 13%
where the time goes in v7:
time: 170 us; the launch traced here: 169 us
  starting transfers between devices  63.1 us (37%)
  waiting for transfers between devices  55.6 us (33%)
  Pallas kernels  30.8 us (18%)
  local copies, waits for them, and re-layouts  18.5 us (11%)
    ppermute x6, waiting for transfers between devices, around(): lax.ppermute(pair[0], 'shard', UP)  26.6 us
    all_to_all x4, starting transfers between devices, to_plane(): lax.all_to_all(rows, 'shard', split_axis=0, concat_axis=0, axis_index_gro...  26.6 us
    ppermute x6, starting transfers between devices, around(): lax.ppermute(pair[1], 'shard', DOWN)  20.2 us
    unnamed x63, local copies, waits for them, and re-layouts  18.4 us
    pallas_call x4, Pallas kernels, pick(): call(lambda *refs: pick_kernel(planes, *refs), shape(PLANE, SENT, WIDE),...  13.6 us
    ppermute x2, waiting for transfers between devices, on_device(): got_y = lax.ppermute(passed, 'dp', NEXT_Y)  9.02 us
    ppermute x1, waiting for transfers between devices, on_device(): lax.ppermute(three[1][1], 'shard', DOWN)  8.77 us
    all_to_all x1, starting transfers between devices, on_device(): lax.all_to_all(wanted, 'shard', split_axis=0, concat_axis=0, axis_index_g...  7.46 us
  transfers between devices with their start and end apart: 23, of which 8 were waited for; matrix products, arithmetic and copies ran while one was open for 0% of the time, Pallas kernels for 13%

profile of v7, /device:TPU:2, one launch (start us, length us, event | category | flops | bytes accessed | tf_op | source)
XLA Modules:
  0.0 168.9 jit_solution(7070119507340515120)
XLA Ops:
  0.6 0.1 pad_add_fusion.place.refs_0_
  0.7 1.2 copy-done
  1.9 0.6 shard_map.86
  2.5 0.1 collective-permute-start
  2.6 0.5 collective-permute-start.2
  3.1 1.3 collective-permute-done.refs_2_
  4.4 0.6 shard_map.87
  5.0 1.7 collective-permute-start.1
  6.7 6.1 %collective-permute-done.1.refs_3_ = f32[224,256]{1,0:T(8,128)S(1)} collective-permute-done((f32[224,256]{1,0:T(8,128)S(1)}, f32[224,256]{1,0:T(8,128)S(1)}, u32[]{:S(2)}, u32[]{:S(2)}) %collective-permute-start.1) | collective-permute-done | bytes 229408 | tf_op jit(solution)/shard_map/ppermute | solution.py:305
  12.7 0.8 shard_map.88.refs_0_.refs_2_.refs_1_
  13.5 0.0 copy-start.29
  13.5 0.0 copy-start.30
  13.5 0.0 copy-start.1
  13.5 2.0 %collective-permute-start.4 = (f32[224,768]{1,0:T(8,128)S(1)}, f32[224,768]{1,0:T(8,128)S(1)}, u32[]{:S(2)}, u32[]{:S(2)}) collective-permute-start(f32[224,768]{1,0:T(8,128)S(1)} %shard_map.88.refs_0_.refs_2_.refs_1_), channel_id=1, source_target_pairs={{0,8},{1,9},{2,10},{3,11},{4,12},{5,13},{6,14},{7,15},{8,16},{9,17... | collective-permute-start | bytes 2064392 | tf_op jit(solution)/shard_map/ppermute | solution.py:346
  15.5 4.0 %collective-permute-start.5 = (f32[224,768]{1,0:T(8,128)S(1)}, f32[224,768]{1,0:T(8,128)}, u32[]{:S(2)}, u32[]{:S(2)}) collective-permute-start(f32[224,768]{1,0:T(8,128)S(1)} %shard_map.88.refs_0_.refs_2_.refs_1_), channel_id=1, source_target_pairs={{8,0},{9,1},{10,2},{11,3},{12,4},{13,5},{14,6},{15,7},{16,8},{17,9... | collective-permute-start | bytes 2064392 | tf_op jit(solution)/shard_map/ppermute | solution.py:346
  19.6 1.3 shard_map.89
  20.8 1.6 collective-permute-start.3
  22.4 0.1 copy.22.dev
  22.6 0.1 copy.23.col
  22.7 1.9 %shard_map.85 = (s32[8,8,128]{2,1,0:T(8,128)}, s32[448,128]{1,0:T(8,128)S(1)}) custom-call(s32[2]{0:T(128)S(1)} %pad_add_fusion.place.refs_0_, s32[448,1]{1,0:T(8,128)S(1)} %copy.22.dev, s32[1,448]{1,0:T(1,128)S(1)} %bitcast.10, s32[448,1]{1,0:T(8,128)S(1)} %copy.23.col), custom_call_target="tpu_custom_call" | custom-call | bytes 1048576 | tf_op jit(solution)/shard_map/pallas_call | solution.py:269
  24.6 3.0 %collective-permute-done.3.refs_3_ = f32[224,256]{1,0:T(8,128)S(1)} collective-permute-done((f32[224,256]{1,0:T(8,128)}, f32[224,256]{1,0:T(8,128)S(1)}, u32[]{:S(2)}, u32[]{:S(2)}) %collective-permute-start.3) | collective-permute-done | bytes 229408 | tf_op jit(solution)/shard_map/ppermute | solution.py:305
  27.6 0.7 copy-done.27
  28.3 1.0 copy-done.20
  29.3 1.0 copy-done.22
  30.3 1.0 copy-done.24
  31.3 1.0 copy-done.26
  32.3 0.9 copy-done.28
  33.3 0.8 shard_map.90.refs_1_.refs_3_
  34.1 0.1 collective-permute-start.6
  34.1 3.2 %collective-permute-start.7 = (f32[224,768]{1,0:T(8,128)S(1)}, f32[224,768]{1,0:T(8,128)}, u32[]{:S(2)}, u32[]{:S(2)}) collective-permute-start(f32[224,768]{1,0:T(8,128)S(1)} %shard_map.90.refs_1_.refs_3_), channel_id=1, source_target_pairs={{8,0},{9,1},{10,2},{11,3},{12,4},{13,5},{14,6},{15,7},{16,8},{17,9... | collective-permute-start | bytes 2064392 | tf_op jit(solution)/shard_map/ppermute | solution.py:346
  37.4 7.5 %all-to-all-start = ((s32[8,8,128]{2,1,0:T(8,128)}), s32[8,8,128]{2,1,0:T(8,128)S(1)}, u32[]{:S(2)}, u32[]{:S(2)}) async-start(s32[8,8,128]{2,1,0:T(8,128)} %get-tuple-element.20.refs_7_), calls=%async_computation | async-start | bytes 65536 | tf_op jit(solution)/shard_map/all_to_all | solution.py:280
  44.9 6.2 %all-to-all-done.refs_1_ = s32[8,8,128]{2,1,0:T(8,128)S(1)} async-done(((s32[8,8,128]{2,1,0:T(8,128)}), s32[8,8,128]{2,1,0:T(8,128)S(1)}, u32[]{:S(2)}, u32[]{:S(2)}) %all-to-all-start) | async-done | bytes 32800 | tf_op jit(solution)/shard_map/all_to_all | solution.py:280
  51.1 2.8 %shard_map.92.refs_2_ = f32[8,56,768]{2,1,0:T(8,128)} custom-call(s32[2]{0:T(128)S(1)} %pad_add_fusion.place.refs_0_, s32[8,8,128]{2,1,0:T(8,128)S(1)} %all-to-all-done.refs_1_, f32[224,768]{1,0:T(8,128)S(1)} %shard_map.88.refs_0_.refs_2_.refs_1_, f32[224,768]{1,0:T(8,128)S(1)} %shard_map.90.refs_1_.refs_3_, ...), custom_call_target="tpu_custom_call" | custom-call | flops 352321536 | bytes 5242880 | tf_op jit(solution)/shard_map/pallas_call | solution.py:330
  53.9 4.9 %all-to-all-start.1 = ((f32[8,56,768]{2,1,0:T(8,128)}), f32[8,56,768]{2,1,0:T(8,128)S(1)}, u32[]{:S(2)}, u32[]{:S(2)}) async-start(f32[8,56,768]{2,1,0:T(8,128)} %shard_map.92.refs_2_), calls=%async_computation.1 | async-start | bytes 2752512 | tf_op jit(solution)/shard_map/all_to_all | solution.py:341
  58.9 3.2 %collective-permute-start.9 = (f32[224,768]{1,0:T(8,128)}, f32[224,768]{1,0:T(8,128)}, u32[]{:S(2)}, u32[]{:S(2)}) collective-permute-start(f32[224,768]{1,0:T(8,128)} %get-tuple-element.25), channel_id=1, source_target_pairs={{8,0},{9,1},{10,2},{11,3},{12,4},{13,5},{14,6},{15,7},{16,8},{17,9... | collective-permute-start | bytes 2064392 | tf_op jit(solution)/shard_map/ppermute | solution.py:346
  62.1 3.2 %collective-permute-start.11 = (f32[224,768]{1,0:T(8,128)}, f32[224,768]{1,0:T(8,128)}, u32[]{:S(2)}, u32[]{:S(2)}) collective-permute-start(f32[224,768]{1,0:T(8,128)} %get-tuple-element.23.refs_1_.refs_3_), channel_id=1, source_target_pairs={{8,0},{9,1},{10,2},{11,3},{12,4},{13,5},{14,6},{15,7},{16,8},{17,9... | collective-permute-start | bytes 2064392 | tf_op jit(solution)/shard_map/ppermute | solution.py:346
  65.3 13.3 %collective-permute-done.8.refs_2_.refs_4_.refs_0_ = f32[224,768]{1,0:T(8,128)S(1)} collective-permute-done((f32[224,768]{1,0:T(8,128)}, f32[224,768]{1,0:T(8,128)S(1)}, u32[]{:S(2)}, u32[]{:S(2)}) %collective-permute-start.8) | collective-permute-done | bytes 688160 | tf_op jit(solution)/shard_map/ppermute | solution.py:346
  78.7 0.8 copy-done.15
  79.5 3.7 %shard_map.96.refs_2_ = f32[8,56,768]{2,1,0:T(8,128)} custom-call(s32[2]{0:T(128)S(1)} %pad_add_fusion.place.refs_0_, s32[8,8,128]{2,1,0:T(8,128)S(1)} %all-to-all-done.refs_1_, f32[224,768]{1,0:T(8,128)} %get-tuple-element.22.refs_0_.refs_2_, f32[224,768]{1,0:T(8,128)} %get-tuple-element.23.refs_1_.refs_3_, ...), custom_call_target="tpu_custom_call" | custom-call | flops 352321536 | bytes 5242880 | tf_op jit(solution)/shard_map/pallas_call | solution.py:330
  83.2 7.2 %all-to-all-start.2 = ((f32[8,56,768]{2,1,0:T(8,128)}), f32[8,56,768]{2,1,0:T(8,128)S(1)}, u32[]{:S(2)}, u32[]{:S(2)}) async-start(f32[8,56,768]{2,1,0:T(8,128)} %shard_map.96.refs_2_), calls=%async_computation.2 | async-start | bytes 2752512 | tf_op jit(solution)/shard_map/all_to_all | solution.py:341
  90.5 3.2 %collective-permute-start.13 = (f32[224,768]{1,0:T(8,128)}, f32[224,768]{1,0:T(8,128)S(1)}, u32[]{:S(2)}, u32[]{:S(2)}) collective-permute-start(f32[224,768]{1,0:T(8,128)} %get-tuple-element.29), channel_id=1, source_target_pairs={{8,0},{9,1},{10,2},{11,3},{12,4},{13,5},{14,6},{15,7},{16,8},{17,9... | collective-permute-start | bytes 2064392 | tf_op jit(solution)/shard_map/ppermute | solution.py:346
  93.7 3.2 %collective-permute-start.15 = (f32[224,768]{1,0:T(8,128)}, f32[224,768]{1,0:T(8,128)}, u32[]{:S(2)}, u32[]{:S(2)}) collective-permute-start(f32[224,768]{1,0:T(8,128)} %get-tuple-element.27.refs_1_.refs_3_), channel_id=1, source_target_pairs={{8,0},{9,1},{10,2},{11,3},{12,4},{13,5},{14,6},{15,7},{16,8},{17,9... | collective-permute-start | bytes 2064392 | tf_op jit(solution)/shard_map/ppermute | solution.py:346
  96.9 13.3 %collective-permute-done.12.refs_2_.refs_4_.refs_0_ = f32[224,768]{1,0:T(8,128)S(1)} collective-permute-done((f32[224,768]{1,0:T(8,128)}, f32[224,768]{1,0:T(8,128)S(1)}, u32[]{:S(2)}, u32[]{:S(2)}) %collective-permute-start.12) | collective-permute-done | bytes 688160 | tf_op jit(solution)/shard_map/ppermute | solution.py:346
  110.3 0.8 copy-done.12
  111.1 0.2 copy-done.13
  111.4 3.5 %shard_map.100.refs_2_ = f32[8,56,768]{2,1,0:T(8,128)} custom-call(s32[2]{0:T(128)S(1)} %pad_add_fusion.place.refs_0_, s32[8,8,128]{2,1,0:T(8,128)S(1)} %all-to-all-done.refs_1_, f32[224,768]{1,0:T(8,128)} %get-tuple-element.26.refs_0_.refs_2_, f32[224,768]{1,0:T(8,128)} %get-tuple-element.27.refs_1_.refs_3_, ...), custom_call_target="tpu_custom_call" | custom-call | flops 352321536 | bytes 5242880 | tf_op jit(solution)/shard_map/pallas_call | solution.py:330
  114.9 7.2 %all-to-all-start.3 = ((f32[8,56,768]{2,1,0:T(8,128)}), f32[8,56,768]{2,1,0:T(8,128)S(1)}, u32[]{:S(2)}, u32[]{:S(2)}) async-start(f32[8,56,768]{2,1,0:T(8,128)} %shard_map.100.refs_2_), calls=%async_computation.3 | async-start | bytes 2752512 | tf_op jit(solution)/shard_map/all_to_all | solution.py:341
  122.1 3.0 %collective-permute-start.17 = (f32[224,768]{1,0:T(8,128)}, f32[224,768]{1,0:T(8,128)S(1)}, u32[]{:S(2)}, u32[]{:S(2)}) collective-permute-start(f32[224,768]{1,0:T(8,128)} %get-tuple-element.31.refs_1_.refs_3_), channel_id=1, source_target_pairs={{8,0},{9,1},{10,2},{11,3},{12,4},{13,5},{14,6},{15,7},{16,8},{17,9... | collective-permute-start | bytes 2064392 | tf_op jit(solution)/shard_map/ppermute | solution.py:362
  125.1 8.8 %collective-permute-done.17.refs_3_.refs_5_ = f32[224,768]{1,0:T(8,128)S(1)} collective-permute-done((f32[224,768]{1,0:T(8,128)}, f32[224,768]{1,0:T(8,128)S(1)}, u32[]{:S(2)}, u32[]{:S(2)}) %collective-permute-start.17) | collective-permute-done | bytes 688160 | tf_op jit(solution)/shard_map/ppermute | solution.py:362
  133.9 3.6 %collective-permute-done.16.refs_2_.refs_4_ = f32[224,768]{1,0:T(8,128)S(1)} collective-permute-done((f32[224,768]{1,0:T(8,128)}, f32[224,768]{1,0:T(8,128)S(1)}, u32[]{:S(2)}, u32[]{:S(2)}) %collective-permute-start.16) | collective-permute-done | bytes 688160 | tf_op jit(solution)/shard_map/ppermute | solution.py:361
  137.5 3.5 %shard_map.106 = f32[8,56,768]{2,1,0:T(8,128)} custom-call(s32[2]{0:T(128)S(1)} %pad_add_fusion.place.refs_0_, s32[8,8,128]{2,1,0:T(8,128)S(1)} %all-to-all-done.refs_1_, f32[224,768]{1,0:T(8,128)} %get-tuple-element.30.refs_0_.refs_2_, f32[224,768]{1,0:T(8,128)} %get-tuple-element.31.refs_1_.refs_3_, ...), custom_call_target="tpu_custom_call" | custom-call | flops 352321536 | bytes 5242880 | tf_op jit(solution)/shard_map/pallas_call | solution.py:330
  141.0 7.2 %all-to-all-start.4 = ((f32[8,56,768]{2,1,0:T(8,128)}), f32[8,56,768]{2,1,0:T(8,128)S(1)}, u32[]{:S(2)}, u32[]{:S(2)}) async-start(f32[8,56,768]{2,1,0:T(8,128)} %shard_map.106), calls=%async_computation.4 | async-start | bytes 2752512 | tf_op jit(solution)/shard_map/all_to_all | solution.py:341
  148.2 1.3 copy-done.5
  149.6 1.3 copy-done.7
  150.9 1.3 copy-done.9
  152.3 1.1 copy-done.11
  153.4 0.9 copy-done.17
  154.3 2.8 %shard_map.102.refs_3_.refs_4_.refs_5_ = f32[448,768]{1,0:T(8,128)S(1)} custom-call(s32[448,128]{1,0:T(8,128)S(1)} %copy-done.17, f32[224,768]{1,0:T(8,128)S(1)} %copy-done.11, f32[8,56,768]{2,1,0:T(8,128)S(1)} %copy-done.5, f32[8,56,768]{2,1,0:T(8,128)S(1)} %copy-done.7, f32[8,56,768]{2,1,0:T(8,128)S(1)} %copy-done.9), custom_call_target="tpu_custom_call" | custom-call | flops 1541406720 | bytes 8388608 | tf_op jit(solution)/shard_map/pallas_call | solution.py:374
  157.1 3.2 %shard_map.101.refs_0_.refs_1_.refs_2_ = f32[448,768]{1,0:T(8,128)S(1)} custom-call(s32[448,128]{1,0:T(8,128)S(1)} %copy-done.17, f32[224,768]{1,0:T(8,128)S(1)} %shard_map.88.refs_0_.refs_2_.refs_1_, f32[8,56,768]{2,1,0:T(8,128)S(1)} %copy-done.5, f32[8,56,768]{2,1,0:T(8,128)S(1)} %copy-done.7, f32[8,56,768]{2,1,0:T(8,128)S(1)} %copy-done.9), custom_call_target="tpu_custom_call" | custom-call | flops 1541406720 | bytes 8388608 | tf_op jit(solution)/shard_map/pallas_call | solution.py:374
  160.3 0.0 copy-start.2
  160.3 1.1 copy-done.2
  161.4 1.3 copy-done.3
  162.7 0.9 copy-done.18
  163.7 5.3 %shard_map.107 = (f32[448,1024]{1,0:T(8,128)}, f32[448,1024]{1,0:T(8,128)}, f32[448,1024]{1,0:T(8,128)}) custom-call(s32[448,128]{1,0:T(8,128)S(1)} %copy-done.18, f32[448,768]{1,0:T(8,128)S(1)} %copy-done.3, f32[448,768]{1,0:T(8,128)S(1)} %copy-done.3, f32[448,768]{1,0:T(8,128)S(1)} %copy-done.3, f32[448,768]{1,0:T(8,128)S(1)} %shard_map.102.refs_3_.refs_4_.refs_5_, ...), custom_call_target="tpu_custom_call" | custom-call | flops 1409286144 | bytes 12582912 | tf_op jit(solution)/shard_map/pallas_call | solution.py:399
  (70 shorter events, 0.1 us)
Async XLA Ops:
  0.7 1.2 copy-start
  1.9 10.8 %copy-start.21 = (f32[224,512]{1,0:T(8,128)S(1)}, f32[224,512]{1,0:T(8,128)}, u32[]{:S(2)}) copy-start(f32[224,512]{1,0:T(8,128)} %refs_4_.3) | copy-start | bytes 1376260
  1.9 10.8 %copy-start.23 = (f32[224,512]{1,0:T(8,128)S(1)}, f32[224,512]{1,0:T(8,128)}, u32[]{:S(2)}) copy-start(f32[224,512]{1,0:T(8,128)} %refs_5_.3) | copy-start | bytes 1376260
  1.9 10.8 %copy-start.25 = (f32[224,512]{1,0:T(8,128)S(1)}, f32[224,512]{1,0:T(8,128)}, u32[]{:S(2)}) copy-start(f32[224,512]{1,0:T(8,128)} %refs_6_.3) | copy-start | bytes 1376260
  2.5 1.9 %collective-permute-start = (f32[224,512]{1,0:T(8,128)S(1)}, f32[224,512]{1,0:T(8,128)S(1)}, u32[]{:S(2)}, u32[]{:S(2)}) collective-permute-start(f32[224,512]{1,0:T(8,128)S(1)} %get-tuple-element.19), channel_id=1, source_target_pairs={{0,64},{64,0},{128,192},{192,128},{1,65},{65,1},{129,193},{193,129... | collective-permute-start | bytes 1376264 | tf_op jit(solution)/shard_map/ppermute | solution.py:289
  2.6 16.9 %collective-permute-start.2 = (f32[224,512]{1,0:T(8,128)S(1)}, f32[224,512]{1,0:T(8,128)S(1)}, u32[]{:S(2)}, u32[]{:S(2)}) collective-permute-start(f32[224,512]{1,0:T(8,128)S(1)} %get-tuple-element.21), channel_id=1, source_target_pairs={{0,64},{64,0},{128,192},{192,128},{1,65},{65,1},{129,193},{193,129... | collective-permute-start | bytes 1376264 | tf_op jit(solution)/shard_map/ppermute | solution.py:289
  5.0 7.7 %collective-permute-start.1 = (f32[224,256]{1,0:T(8,128)S(1)}, f32[224,256]{1,0:T(8,128)S(1)}, u32[]{:S(2)}, u32[]{:S(2)}) collective-permute-start(f32[224,256]{1,0:T(8,128)S(1)} %shard_map.87), channel_id=1, source_target_pairs={{0,128},{128,0},{64,192},{192,64},{1,129},{129,1},{65,193},{193,65... | collective-permute-start | bytes 688136 | tf_op jit(solution)/shard_map/ppermute | solution.py:305
  13.5 8.9 %copy-start.29 = (s32[448,1]{0,1:T(1,128)S(1)}, s32[448,1]{0,1:T(1,128)}, u32[]{:S(2)}) copy-start(s32[448,1]{0,1:T(1,128)} %param.10) | copy-start | bytes 5380
  13.5 9.0 %copy-start.30 = (s32[448]{0:T(512)S(1)}, s32[448]{0:T(512)}, u32[]{:S(2)}) copy-start(s32[448]{0:T(512)} %param.11) | copy-start | bytes 5380
  13.5 14.7 %copy-start.1 = (bf16[1,224,2048]{2,1,0:T(8,128)(2,1)S(1)}, bf16[1,224,2048]{2,1,0:T(8,128)(2,1)}, u32[]{:S(2)}) copy-start(bf16[1,224,2048]{2,1,0:T(8,128)(2,1)} %param.6) | copy-start | bytes 2752516
  13.5 31.3 %collective-permute-start.4 = (f32[224,768]{1,0:T(8,128)S(1)}, f32[224,768]{1,0:T(8,128)S(1)}, u32[]{:S(2)}, u32[]{:S(2)}) collective-permute-start(f32[224,768]{1,0:T(8,128)S(1)} %shard_map.88.refs_0_.refs_2_.refs_1_), channel_id=1, source_target_pairs={{0,8},{1,9},{2,10},{3,11},{4,12},{5,13},{6,14},{7,15},{8,16},{9,17... | collective-permute-start | bytes 2064392 | tf_op jit(solution)/shard_map/ppermute | solution.py:346
  15.5 29.3 %collective-permute-start.5 = (f32[224,768]{1,0:T(8,128)S(1)}, f32[224,768]{1,0:T(8,128)}, u32[]{:S(2)}, u32[]{:S(2)}) collective-permute-start(f32[224,768]{1,0:T(8,128)S(1)} %shard_map.88.refs_0_.refs_2_.refs_1_), channel_id=1, source_target_pairs={{8,0},{9,1},{10,2},{11,3},{12,4},{13,5},{14,6},{15,7},{16,8},{17,9... | collective-permute-start | bytes 2064392 | tf_op jit(solution)/shard_map/ppermute | solution.py:346
  19.6 3.1 %copy-start.19 = (f32[224,512]{1,0:T(8,128)}, f32[224,512]{1,0:T(8,128)S(1)}, u32[]{:S(2)}) copy-start(f32[224,512]{1,0:T(8,128)S(1)} %collective-permute-done.2.refs_2_) | copy-start | bytes 1376260
  20.8 6.7 %collective-permute-start.3 = (f32[224,256]{1,0:T(8,128)}, f32[224,256]{1,0:T(8,128)S(1)}, u32[]{:S(2)}, u32[]{:S(2)}) collective-permute-start(f32[224,256]{1,0:T(8,128)} %shard_map.89), channel_id=1, source_target_pairs={{0,128},{128,0},{64,192},{192,64},{1,129},{129,1},{65,193},{193,65... | collective-permute-start | bytes 688136 | tf_op jit(solution)/shard_map/ppermute | solution.py:305
  24.6 9.4 %copy-start.16 = (s32[448,128]{1,0:T(8,128)}, s32[448,128]{1,0:T(8,128)S(1)}, u32[]{:S(2)}) copy-start(s32[448,128]{1,0:T(8,128)S(1)} %get-tuple-element.18.refs_0_.codes) | copy-start | bytes 688132
  27.6 0.7 copy-start.27
  28.3 1.0 copy-start.20
  29.3 1.0 copy-start.22
  30.3 1.0 copy-start.24
  31.3 1.0 copy-start.26
  32.3 0.9 copy-start.28
  34.0 17.1 %copy-start.10 = (f32[224,768]{1,0:T(8,128)}, f32[224,768]{1,0:T(8,128)S(1)}, u32[]{:S(2)}) copy-start(f32[224,768]{1,0:T(8,128)S(1)} %shard_map.90.refs_1_.refs_3_) | copy-start | bytes 2064388
  34.1 28.0 %collective-permute-start.6 = (f32[224,768]{1,0:T(8,128)S(1)}, f32[224,768]{1,0:T(8,128)}, u32[]{:S(2)}, u32[]{:S(2)}) collective-permute-start(f32[224,768]{1,0:T(8,128)S(1)} %shard_map.90.refs_1_.refs_3_), channel_id=1, source_target_pairs={{0,8},{1,9},{2,10},{3,11},{4,12},{5,13},{6,14},{7,15},{8,16},{9,17... | collective-permute-start | bytes 2064392 | tf_op jit(solution)/shard_map/ppermute | solution.py:346
  34.1 28.0 %collective-permute-start.7 = (f32[224,768]{1,0:T(8,128)S(1)}, f32[224,768]{1,0:T(8,128)}, u32[]{:S(2)}, u32[]{:S(2)}) collective-permute-start(f32[224,768]{1,0:T(8,128)S(1)} %shard_map.90.refs_1_.refs_3_), channel_id=1, source_target_pairs={{8,0},{9,1},{10,2},{11,3},{12,4},{13,5},{14,6},{15,7},{16,8},{17,9... | collective-permute-start | bytes 2064392 | tf_op jit(solution)/shard_map/ppermute | solution.py:346
  37.4 13.7 %all-to-all-start = ((s32[8,8,128]{2,1,0:T(8,128)}), s32[8,8,128]{2,1,0:T(8,128)S(1)}, u32[]{:S(2)}, u32[]{:S(2)}) async-start(s32[8,8,128]{2,1,0:T(8,128)} %get-tuple-element.20.refs_7_), calls=%async_computation | async-start | bytes 65536 | tf_op jit(solution)/shard_map/all_to_all | solution.py:280
  44.8 6.3 %copy-start.14 = (f32[224,768]{1,0:T(8,128)}, f32[224,768]{1,0:T(8,128)S(1)}, u32[]{:S(2)}) copy-start(f32[224,768]{1,0:T(8,128)S(1)} %collective-permute-done.4.refs_2_.refs_4_.refs_0_) | copy-start | bytes 2064388
  53.9 24.7 %all-to-all-start.1 = ((f32[8,56,768]{2,1,0:T(8,128)}), f32[8,56,768]{2,1,0:T(8,128)S(1)}, u32[]{:S(2)}, u32[]{:S(2)}) async-start(f32[8,56,768]{2,1,0:T(8,128)} %shard_map.92.refs_2_), calls=%async_computation.1 | async-start | bytes 2752512 | tf_op jit(solution)/shard_map/all_to_all | solution.py:341
  58.9 19.8 %collective-permute-start.8 = (f32[224,768]{1,0:T(8,128)}, f32[224,768]{1,0:T(8,128)S(1)}, u32[]{:S(2)}, u32[]{:S(2)}) collective-permute-start(f32[224,768]{1,0:T(8,128)} %get-tuple-element.24), channel_id=1, source_target_pairs={{0,8},{1,9},{2,10},{3,11},{4,12},{5,13},{6,14},{7,15},{8,16},{9,17... | collective-permute-start | bytes 2064392 | tf_op jit(solution)/shard_map/ppermute | solution.py:346
  58.9 19.8 %collective-permute-start.9 = (f32[224,768]{1,0:T(8,128)}, f32[224,768]{1,0:T(8,128)}, u32[]{:S(2)}, u32[]{:S(2)}) collective-permute-start(f32[224,768]{1,0:T(8,128)} %get-tuple-element.25), channel_id=1, source_target_pairs={{8,0},{9,1},{10,2},{11,3},{12,4},{13,5},{14,6},{15,7},{16,8},{17,9... | collective-permute-start | bytes 2064392 | tf_op jit(solution)/shard_map/ppermute | solution.py:346
  62.1 31.6 %collective-permute-start.10 = (f32[224,768]{1,0:T(8,128)}, f32[224,768]{1,0:T(8,128)}, u32[]{:S(2)}, u32[]{:S(2)}) collective-permute-start(f32[224,768]{1,0:T(8,128)} %get-tuple-element.22.refs_0_.refs_2_), channel_id=1, source_target_pairs={{0,8},{1,9},{2,10},{3,11},{4,12},{5,13},{6,14},{7,15},{8,16},{9,17... | collective-permute-start | bytes 2064392 | tf_op jit(solution)/shard_map/ppermute | solution.py:346
  62.1 31.6 %collective-permute-start.11 = (f32[224,768]{1,0:T(8,128)}, f32[224,768]{1,0:T(8,128)}, u32[]{:S(2)}, u32[]{:S(2)}) collective-permute-start(f32[224,768]{1,0:T(8,128)} %get-tuple-element.23.refs_1_.refs_3_), channel_id=1, source_target_pairs={{8,0},{9,1},{10,2},{11,3},{12,4},{13,5},{14,6},{15,7},{16,8},{17,9... | collective-permute-start | bytes 2064392 | tf_op jit(solution)/shard_map/ppermute | solution.py:346
  78.7 0.8 copy-start.15
  79.5 3.7 %copy-start.4 = (f32[8,56,768]{2,1,0:T(8,128)}, f32[8,56,768]{2,1,0:T(8,128)S(1)}, u32[]{:S(2)}) copy-start(f32[8,56,768]{2,1,0:T(8,128)S(1)} %all-to-all-done.1.refs_6_.refs_2_) | copy-start | bytes 4128772
  83.2 27.0 %all-to-all-start.2 = ((f32[8,56,768]{2,1,0:T(8,128)}), f32[8,56,768]{2,1,0:T(8,128)S(1)}, u32[]{:S(2)}, u32[]{:S(2)}) async-start(f32[8,56,768]{2,1,0:T(8,128)} %shard_map.96.refs_2_), calls=%async_computation.2 | async-start | bytes 2752512 | tf_op jit(solution)/shard_map/all_to_all | solution.py:341
  90.5 19.8 %collective-permute-start.12 = (f32[224,768]{1,0:T(8,128)}, f32[224,768]{1,0:T(8,128)S(1)}, u32[]{:S(2)}, u32[]{:S(2)}) collective-permute-start(f32[224,768]{1,0:T(8,128)} %get-tuple-element.28), channel_id=1, source_target_pairs={{0,8},{1,9},{2,10},{3,11},{4,12},{5,13},{6,14},{7,15},{8,16},{9,17... | collective-permute-start | bytes 2064392 | tf_op jit(solution)/shard_map/ppermute | solution.py:346
  90.5 19.8 %collective-permute-start.13 = (f32[224,768]{1,0:T(8,128)}, f32[224,768]{1,0:T(8,128)S(1)}, u32[]{:S(2)}, u32[]{:S(2)}) collective-permute-start(f32[224,768]{1,0:T(8,128)} %get-tuple-element.29), channel_id=1, source_target_pairs={{8,0},{9,1},{10,2},{11,3},{12,4},{13,5},{14,6},{15,7},{16,8},{17,9... | collective-permute-start | bytes 2064392 | tf_op jit(solution)/shard_map/ppermute | solution.py:346
  93.7 28.4 %collective-permute-start.14 = (f32[224,768]{1,0:T(8,128)}, f32[224,768]{1,0:T(8,128)}, u32[]{:S(2)}, u32[]{:S(2)}) collective-permute-start(f32[224,768]{1,0:T(8,128)} %get-tuple-element.26.refs_0_.refs_2_), channel_id=1, source_target_pairs={{0,8},{1,9},{2,10},{3,11},{4,12},{5,13},{6,14},{7,15},{8,16},{9,17... | collective-permute-start | bytes 2064392 | tf_op jit(solution)/shard_map/ppermute | solution.py:346
  93.7 28.4 %collective-permute-start.15 = (f32[224,768]{1,0:T(8,128)}, f32[224,768]{1,0:T(8,128)}, u32[]{:S(2)}, u32[]{:S(2)}) collective-permute-start(f32[224,768]{1,0:T(8,128)} %get-tuple-element.27.refs_1_.refs_3_), channel_id=1, source_target_pairs={{8,0},{9,1},{10,2},{11,3},{12,4},{13,5},{14,6},{15,7},{16,8},{17,9... | collective-permute-start | bytes 2064392 | tf_op jit(solution)/shard_map/ppermute | solution.py:346
  110.3 0.9 copy-start.12
  110.3 1.1 copy-start.13
  111.4 3.5 %copy-start.6 = (f32[8,56,768]{2,1,0:T(8,128)}, f32[8,56,768]{2,1,0:T(8,128)S(1)}, u32[]{:S(2)}) copy-start(f32[8,56,768]{2,1,0:T(8,128)S(1)} %all-to-all-done.2.refs_6_.refs_3_) | copy-start | bytes 4128772
  114.9 22.6 %all-to-all-start.3 = ((f32[8,56,768]{2,1,0:T(8,128)}), f32[8,56,768]{2,1,0:T(8,128)S(1)}, u32[]{:S(2)}, u32[]{:S(2)}) async-start(f32[8,56,768]{2,1,0:T(8,128)} %shard_map.100.refs_2_), calls=%async_computation.3 | async-start | bytes 2752512 | tf_op jit(solution)/shard_map/all_to_all | solution.py:341
  122.1 11.8 %collective-permute-start.17 = (f32[224,768]{1,0:T(8,128)}, f32[224,768]{1,0:T(8,128)S(1)}, u32[]{:S(2)}, u32[]{:S(2)}) collective-permute-start(f32[224,768]{1,0:T(8,128)} %get-tuple-element.31.refs_1_.refs_3_), channel_id=1, source_target_pairs={{8,0},{9,1},{10,2},{11,3},{12,4},{13,5},{14,6},{15,7},{16,8},{17,9... | collective-permute-start | bytes 2064392 | tf_op jit(solution)/shard_map/ppermute | solution.py:362
  125.1 12.4 %collective-permute-start.16 = (f32[224,768]{1,0:T(8,128)}, f32[224,768]{1,0:T(8,128)S(1)}, u32[]{:S(2)}, u32[]{:S(2)}) collective-permute-start(f32[224,768]{1,0:T(8,128)} %get-tuple-element.32), channel_id=1, source_target_pairs={{0,8},{1,9},{2,10},{3,11},{4,12},{5,13},{6,14},{7,15},{8,16},{9,17... | collective-permute-start | bytes 2064392 | tf_op jit(solution)/shard_map/ppermute | solution.py:361
  137.5 3.6 %copy-start.8 = (f32[8,56,768]{2,1,0:T(8,128)}, f32[8,56,768]{2,1,0:T(8,128)S(1)}, u32[]{:S(2)}) copy-start(f32[8,56,768]{2,1,0:T(8,128)S(1)} %all-to-all-done.3.refs_4_.refs_6_) | copy-start | bytes 4128772
  141.0 20.4 %all-to-all-start.4 = ((f32[8,56,768]{2,1,0:T(8,128)}), f32[8,56,768]{2,1,0:T(8,128)S(1)}, u32[]{:S(2)}, u32[]{:S(2)}) async-start(f32[8,56,768]{2,1,0:T(8,128)} %shard_map.106), calls=%async_computation.4 | async-start | bytes 2752512 | tf_op jit(solution)/shard_map/all_to_all | solution.py:341
  148.2 1.3 copy-start.5
  149.6 1.3 copy-start.7
  150.9 1.3 copy-start.9
  152.3 1.1 copy-start.11
  153.4 0.9 copy-start.17
  160.3 1.1 copy-start.2
  161.4 1.3 copy-start.3
  162.7 0.9 copy-start.18

commit v8 on v7

--- a/solution.py
+++ b/solution.py
@@ -287,10 +287,8 @@
         moved=3 << 20,
     )(place, grad)
     got_core = [lax.ppermute(s, "dp", CORE) for s in sends]
-    state = []
-    for half in range(2):
-        got = got_core[half]
-        passed = call(
+    passed = [
+        call(
             lambda *refs, half=half: send_y_kernel(half, *refs),
             shape(ROWS, HALF),
             grid=(1,),
@@ -301,9 +299,14 @@
             ],
             out_specs=pl.BlockSpec((ROWS, HALF), lambda i: (0, 0)),
             moved=1 << 20,
-        )(place, grad, got)
-        got_y = lax.ppermute(passed, "dp", NEXT_Y)
+        )(place, grad, got_core[half])
+        for half in range(2)
+    ]
+    got_y = [lax.ppermute(p, "dp", NEXT_Y) for p in passed]
+    state = []
+    for half in range(2):
         block = pl.BlockSpec((ROWS, HALF), lambda i, half=half: (0, half))
+        after = (got_y[1], wanted) if half == 0 else ()
         state.append(
             call(
                 lambda *refs, half=half: update_kernel(half, *refs),
@@ -318,10 +321,10 @@
                     block,
                     block,
                 ]
-                + [pl.BlockSpec(memory_space=pl.ANY)] * half,
+                + [pl.BlockSpec(memory_space=pl.ANY)] * len(after),
                 out_specs=pl.BlockSpec((ROWS, WIDE), lambda i: (0, 0)),
                 moved=2 << 20,
-            )(place, grad, got, got_y, weight, first, second, *[wanted] * half)
+            )(place, grad, got_core[half], got_y[half], weight, first, second, *after)
         )
 
     def pick(planes, sources, wait, after=()):

time: 170 us -> 167 us (0.982)
  waiting for transfers between devices: 55.6 us -> 53.1 us
    ppermute x6, waiting for transfers between devices: 26.6 us -> 30.5 us  [around(): lax.ppermute(pair[0], 'shard', UP)]
    all_to_all x1, waiting for transfers between devices: 6.23 us -> 2.41 us  [on_device(): lax.all_to_all(wanted, 'shard', split_axis=0, concat_axis=0, axis_index_g...]
    ppermute x2, waiting for transfers between devices: 9.02 us -> 6.37 us  [on_device(): got_y = [lax.ppermute(p, 'dp', NEXT_Y) for p in passed]]
    ppermute x6, starting transfers between devices: 20.2 us -> 18 us  [around(): lax.ppermute(pair[1], 'shard', DOWN)]
    ppermute x6, starting transfers between devices: 2.09 us -> 4.11 us  [around(): lax.ppermute(pair[0], 'shard', UP)]
    unnamed x63 -> x61, local copies, waits for them, and re-layouts: 18.4 us -> 18.5 us
  transfers between devices with their start and end apart: 23 -> 23, of which waited for: 8 -> 11; matrix products, arithmetic and copies ran while one was open for 0% -> 0% of each run, Pallas kernels for 13% -> 12%
where the time goes in v8:
time: 167 us; the launch traced here: 166 us
  starting transfers between devices  62.8 us (38%)
  waiting for transfers between devices  53.1 us (32%)
  Pallas kernels  30.8 us (18%)
  local copies, waits for them, and re-layouts  18.7 us (11%)
    ppermute x6, waiting for transfers between devices, around(): lax.ppermute(pair[0], 'shard', UP)  30.5 us
    all_to_all x4, starting transfers between devices, to_plane(): lax.all_to_all(rows, 'shard', split_axis=0, concat_axis=0, axis_index_gro...  27.6 us
    unnamed x61, local copies, waits for them, and re-layouts  18.5 us
    ppermute x6, starting transfers between devices, around(): lax.ppermute(pair[1], 'shard', DOWN)  18 us
    pallas_call x4, Pallas kernels, pick(): call(lambda *refs: pick_kernel(planes, *refs), shape(PLANE, SENT, WIDE),...  13.7 us
    ppermute x1, waiting for transfers between devices, on_device(): lax.ppermute(three[1][1], 'shard', DOWN)  8.96 us
    all_to_all x1, starting transfers between devices, on_device(): lax.all_to_all(wanted, 'shard', split_axis=0, concat_axis=0, axis_index_g...  7.46 us
    ppermute x2, waiting for transfers between devices, on_device(): got_y = [lax.ppermute(p, 'dp', NEXT_Y) for p in passed]  6.37 us
  transfers between devices with their start and end apart: 23, of which 11 were waited for; matrix products, arithmetic and copies ran while one was open for 0% of the time, Pallas kernels for 12%

profile of v8, /device:TPU:2, one launch (start us, length us, event | category | flops | bytes accessed | tf_op | source)
XLA Modules:
  0.0 166.3 jit_solution(2149716174032883164)
XLA Ops:
  0.7 1.2 copy-done
  1.9 0.6 shard_map.86
  2.5 0.1 collective-permute-start.2
  2.6 0.5 collective-permute-start
  3.1 1.3 collective-permute-done.2.refs_2_
  4.4 0.6 shard_map.88
  5.0 1.7 %collective-permute-start.3 = (f32[224,256]{1,0:T(8,128)S(1)}, f32[224,256]{1,0:T(8,128)S(1)}, u32[]{:S(2)}, u32[]{:S(2)}) collective-permute-start(f32[224,256]{1,0:T(8,128)S(1)} %shard_map.88), channel_id=1, source_target_pairs={{0,128},{128,0},{64,192},{192,64},{1,129},{129,1},{65,193},{193,65... | collective-permute-start | bytes 688136 | tf_op jit(solution)/shard_map/ppermute | solution.py:305
  6.7 1.3 shard_map.87
  7.9 0.4 collective-permute-start.1
  8.4 0.1 copy.22.dev
  8.5 0.1 copy.23.col
  8.7 1.9 %shard_map.85 = (s32[8,8,128]{2,1,0:T(8,128)}, s32[448,128]{1,0:T(8,128)S(1)}) custom-call(s32[2]{0:T(128)S(1)} %pad_add_fusion.place.refs_0_, s32[448,1]{1,0:T(8,128)S(1)} %copy.22.dev, s32[1,448]{1,0:T(1,128)S(1)} %bitcast.10, s32[448,1]{1,0:T(8,128)S(1)} %copy.23.col), custom_call_target="tpu_custom_call" | custom-call | bytes 1048576 | tf_op jit(solution)/shard_map/pallas_call | solution.py:269
  10.6 0.7 copy-done.16
  11.3 2.3 %collective-permute-done.3.refs_7_.refs_3_ = f32[224,256]{1,0:T(8,128)S(1)} collective-permute-done((f32[224,256]{1,0:T(8,128)S(1)}, f32[224,256]{1,0:T(8,128)S(1)}, u32[]{:S(2)}, u32[]{:S(2)}) %collective-permute-start.3) | collective-permute-done | bytes 229408 | tf_op jit(solution)/shard_map/ppermute | solution.py:305
  13.5 4.1 %collective-permute-done.1.refs_3_ = f32[224,256]{1,0:T(8,128)S(1)} collective-permute-done((f32[224,256]{1,0:T(8,128)}, f32[224,256]{1,0:T(8,128)S(1)}, u32[]{:S(2)}, u32[]{:S(2)}) %collective-permute-start.1) | collective-permute-done | bytes 229408 | tf_op jit(solution)/shard_map/ppermute | solution.py:305
  17.7 0.7 copy-done.26
  18.4 1.0 copy-done.22
  19.4 1.0 copy-done.23
  20.4 0.9 copy-done.27
  21.3 0.8 shard_map.89.refs_0_.refs_2_.refs_1_
  22.1 0.7 copy-done.24
  22.8 1.9 %collective-permute-start.4 = (f32[224,768]{1,0:T(8,128)S(1)}, f32[224,768]{1,0:T(8,128)S(1)}, u32[]{:S(2)}, u32[]{:S(2)}) collective-permute-start(f32[224,768]{1,0:T(8,128)S(1)} %shard_map.89.refs_0_.refs_2_.refs_1_), channel_id=1, source_target_pairs={{0,8},{1,9},{2,10},{3,11},{4,12},{5,13},{6,14},{7,15},{8,16},{9,17... | collective-permute-start | bytes 2064392 | tf_op jit(solution)/shard_map/ppermute | solution.py:349
  24.7 3.9 %collective-permute-start.5 = (f32[224,768]{1,0:T(8,128)S(1)}, f32[224,768]{1,0:T(8,128)}, u32[]{:S(2)}, u32[]{:S(2)}) collective-permute-start(f32[224,768]{1,0:T(8,128)S(1)} %shard_map.89.refs_0_.refs_2_.refs_1_), channel_id=1, source_target_pairs={{8,0},{9,1},{10,2},{11,3},{12,4},{13,5},{14,6},{15,7},{16,8},{17,9... | collective-permute-start | bytes 2064392 | tf_op jit(solution)/shard_map/ppermute | solution.py:349
  28.6 0.9 copy-done.25
  29.6 0.8 shard_map.90.refs_1_.refs_3_
  30.4 3.2 %collective-permute-start.7 = (f32[224,768]{1,0:T(8,128)S(1)}, f32[224,768]{1,0:T(8,128)}, u32[]{:S(2)}, u32[]{:S(2)}) collective-permute-start(f32[224,768]{1,0:T(8,128)S(1)} %shard_map.90.refs_1_.refs_3_), channel_id=1, source_target_pairs={{8,0},{9,1},{10,2},{11,3},{12,4},{13,5},{14,6},{15,7},{16,8},{17,9... | collective-permute-start | bytes 2064392 | tf_op jit(solution)/shard_map/ppermute | solution.py:349
  33.7 7.5 %all-to-all-start = ((s32[8,8,128]{2,1,0:T(8,128)}), s32[8,8,128]{2,1,0:T(8,128)S(1)}, u32[]{:S(2)}, u32[]{:S(2)}) async-start(s32[8,8,128]{2,1,0:T(8,128)} %get-tuple-element.21.refs_8_), calls=%async_computation | async-start | bytes 65536 | tf_op jit(solution)/shard_map/all_to_all | solution.py:280
  41.1 3.8 %collective-permute-done.4.refs_2_.refs_4_.refs_0_ = f32[224,768]{1,0:T(8,128)S(1)} collective-permute-done((f32[224,768]{1,0:T(8,128)S(1)}, f32[224,768]{1,0:T(8,128)S(1)}, u32[]{:S(2)}, u32[]{:S(2)}) %collective-permute-start.4) | collective-permute-done | bytes 688160 | tf_op jit(solution)/shard_map/ppermute | solution.py:349
  45.0 2.4 %all-to-all-done.refs_1_ = s32[8,8,128]{2,1,0:T(8,128)S(1)} async-done(((s32[8,8,128]{2,1,0:T(8,128)}), s32[8,8,128]{2,1,0:T(8,128)S(1)}, u32[]{:S(2)}, u32[]{:S(2)}) %all-to-all-start) | async-done | bytes 32800 | tf_op jit(solution)/shard_map/all_to_all | solution.py:280
  47.4 2.8 %shard_map.92.refs_2_ = f32[8,56,768]{2,1,0:T(8,128)} custom-call(s32[2]{0:T(128)S(1)} %pad_add_fusion.place.refs_0_, s32[8,8,128]{2,1,0:T(8,128)S(1)} %all-to-all-done.refs_1_, f32[224,768]{1,0:T(8,128)S(1)} %shard_map.89.refs_0_.refs_2_.refs_1_, f32[224,768]{1,0:T(8,128)S(1)} %shard_map.90.refs_1_.refs_3_, ...), custom_call_target="tpu_custom_call" | custom-call | flops 352321536 | bytes 5242880 | tf_op jit(solution)/shard_map/pallas_call | solution.py:333
  50.2 5.9 %all-to-all-start.1 = ((f32[8,56,768]{2,1,0:T(8,128)}), f32[8,56,768]{2,1,0:T(8,128)S(1)}, u32[]{:S(2)}, u32[]{:S(2)}) async-start(f32[8,56,768]{2,1,0:T(8,128)} %shard_map.92.refs_2_), calls=%async_computation.1 | async-start | bytes 2752512 | tf_op jit(solution)/shard_map/all_to_all | solution.py:344
  56.1 3.2 %collective-permute-start.9 = (f32[224,768]{1,0:T(8,128)}, f32[224,768]{1,0:T(8,128)}, u32[]{:S(2)}, u32[]{:S(2)}) collective-permute-start(f32[224,768]{1,0:T(8,128)} %get-tuple-element.25), channel_id=1, source_target_pairs={{8,0},{9,1},{10,2},{11,3},{12,4},{13,5},{14,6},{15,7},{16,8},{17,9... | collective-permute-start | bytes 2064392 | tf_op jit(solution)/shard_map/ppermute | solution.py:349
  59.3 0.5 collective-permute-done.6.refs_0_
  59.8 3.2 %collective-permute-start.11 = (f32[224,768]{1,0:T(8,128)}, f32[224,768]{1,0:T(8,128)}, u32[]{:S(2)}, u32[]{:S(2)}) collective-permute-start(f32[224,768]{1,0:T(8,128)} %get-tuple-element.23.refs_1_.refs_3_), channel_id=1, source_target_pairs={{8,0},{9,1},{10,2},{11,3},{12,4},{13,5},{14,6},{15,7},{16,8},{17,9... | collective-permute-start | bytes 2064392 | tf_op jit(solution)/shard_map/ppermute | solution.py:349
  63.1 12.8 %collective-permute-done.8.refs_2_.refs_4_.refs_0_ = f32[224,768]{1,0:T(8,128)S(1)} collective-permute-done((f32[224,768]{1,0:T(8,128)}, f32[224,768]{1,0:T(8,128)S(1)}, u32[]{:S(2)}, u32[]{:S(2)}) %collective-permute-start.8) | collective-permute-done | bytes 688160 | tf_op jit(solution)/shard_map/ppermute | solution.py:349
  75.9 0.8 copy-done.14
  76.7 3.7 %shard_map.96.refs_2_ = f32[8,56,768]{2,1,0:T(8,128)} custom-call(s32[2]{0:T(128)S(1)} %pad_add_fusion.place.refs_0_, s32[8,8,128]{2,1,0:T(8,128)S(1)} %all-to-all-done.refs_1_, f32[224,768]{1,0:T(8,128)} %get-tuple-element.22.refs_0_.refs_2_, f32[224,768]{1,0:T(8,128)} %get-tuple-element.23.refs_1_.refs_3_, ...), custom_call_target="tpu_custom_call" | custom-call | flops 352321536 | bytes 5242880 | tf_op jit(solution)/shard_map/pallas_call | solution.py:333
  80.5 7.2 %all-to-all-start.2 = ((f32[8,56,768]{2,1,0:T(8,128)}), f32[8,56,768]{2,1,0:T(8,128)S(1)}, u32[]{:S(2)}, u32[]{:S(2)}) async-start(f32[8,56,768]{2,1,0:T(8,128)} %shard_map.96.refs_2_), calls=%async_computation.2 | async-start | bytes 2752512 | tf_op jit(solution)/shard_map/all_to_all | solution.py:344
  87.7 1.6 collective-permute-start.12
  89.3 1.6 collective-permute-start.13
  90.9 0.5 collective-permute-start.14
  91.4 2.7 %collective-permute-start.15 = (f32[224,768]{1,0:T(8,128)}, f32[224,768]{1,0:T(8,128)}, u32[]{:S(2)}, u32[]{:S(2)}) collective-permute-start(f32[224,768]{1,0:T(8,128)} %get-tuple-element.27.refs_1_.refs_3_), channel_id=1, source_target_pairs={{8,0},{9,1},{10,2},{11,3},{12,4},{13,5},{14,6},{15,7},{16,8},{17,9... | collective-permute-start | bytes 2064392 | tf_op jit(solution)/shard_map/ppermute | solution.py:349
  94.2 13.3 %collective-permute-done.12.refs_2_.refs_4_.refs_0_ = f32[224,768]{1,0:T(8,128)S(1)} collective-permute-done((f32[224,768]{1,0:T(8,128)}, f32[224,768]{1,0:T(8,128)S(1)}, u32[]{:S(2)}, u32[]{:S(2)}) %collective-permute-start.12) | collective-permute-done | bytes 688160 | tf_op jit(solution)/shard_map/ppermute | solution.py:349
  107.5 0.1 collective-permute-done.13.refs_3_.refs_5_.refs_1_
  107.6 0.7 copy-done.12
  108.4 0.2 copy-done.13
  108.6 3.5 %shard_map.100.refs_2_ = f32[8,56,768]{2,1,0:T(8,128)} custom-call(s32[2]{0:T(128)S(1)} %pad_add_fusion.place.refs_0_, s32[8,8,128]{2,1,0:T(8,128)S(1)} %all-to-all-done.refs_1_, f32[224,768]{1,0:T(8,128)} %get-tuple-element.26.refs_0_.refs_2_, f32[224,768]{1,0:T(8,128)} %get-tuple-element.27.refs_1_.refs_3_, ...), custom_call_target="tpu_custom_call" | custom-call | flops 352321536 | bytes 5242880 | tf_op jit(solution)/shard_map/pallas_call | solution.py:333
  112.1 7.4 %all-to-all-start.3 = ((f32[8,56,768]{2,1,0:T(8,128)}), f32[8,56,768]{2,1,0:T(8,128)S(1)}, u32[]{:S(2)}, u32[]{:S(2)}) async-start(f32[8,56,768]{2,1,0:T(8,128)} %shard_map.100.refs_2_), calls=%async_computation.3 | async-start | bytes 2752512 | tf_op jit(solution)/shard_map/all_to_all | solution.py:344
  119.5 2.9 %collective-permute-start.17 = (f32[224,768]{1,0:T(8,128)}, f32[224,768]{1,0:T(8,128)S(1)}, u32[]{:S(2)}, u32[]{:S(2)}) collective-permute-start(f32[224,768]{1,0:T(8,128)} %get-tuple-element.31.refs_1_.refs_3_), channel_id=1, source_target_pairs={{8,0},{9,1},{10,2},{11,3},{12,4},{13,5},{14,6},{15,7},{16,8},{17,9... | collective-permute-start | bytes 2064392 | tf_op jit(solution)/shard_map/ppermute | solution.py:365
  122.4 9.0 %collective-permute-done.17.refs_3_.refs_5_ = f32[224,768]{1,0:T(8,128)S(1)} collective-permute-done((f32[224,768]{1,0:T(8,128)}, f32[224,768]{1,0:T(8,128)S(1)}, u32[]{:S(2)}, u32[]{:S(2)}) %collective-permute-start.17) | collective-permute-done | bytes 688160 | tf_op jit(solution)/shard_map/ppermute | solution.py:365
  131.4 3.4 %collective-permute-done.16.refs_2_.refs_4_ = f32[224,768]{1,0:T(8,128)S(1)} collective-permute-done((f32[224,768]{1,0:T(8,128)}, f32[224,768]{1,0:T(8,128)S(1)}, u32[]{:S(2)}, u32[]{:S(2)}) %collective-permute-start.16) | collective-permute-done | bytes 688160 | tf_op jit(solution)/shard_map/ppermute | solution.py:364
  134.8 3.6 %shard_map.106 = f32[8,56,768]{2,1,0:T(8,128)} custom-call(s32[2]{0:T(128)S(1)} %pad_add_fusion.place.refs_0_, s32[8,8,128]{2,1,0:T(8,128)S(1)} %all-to-all-done.refs_1_, f32[224,768]{1,0:T(8,128)} %get-tuple-element.30.refs_0_.refs_2_, f32[224,768]{1,0:T(8,128)} %get-tuple-element.31.refs_1_.refs_3_, ...), custom_call_target="tpu_custom_call" | custom-call | flops 352321536 | bytes 5242880 | tf_op jit(solution)/shard_map/pallas_call | solution.py:333
  138.4 7.2 %all-to-all-start.4 = ((f32[8,56,768]{2,1,0:T(8,128)}), f32[8,56,768]{2,1,0:T(8,128)S(1)}, u32[]{:S(2)}, u32[]{:S(2)}) async-start(f32[8,56,768]{2,1,0:T(8,128)} %shard_map.106), calls=%async_computation.4 | async-start | bytes 2752512 | tf_op jit(solution)/shard_map/all_to_all | solution.py:344
  145.6 1.3 copy-done.5
  146.9 1.3 copy-done.7
  148.2 1.3 copy-done.9
  149.6 1.1 copy-done.11
  150.7 0.9 copy-done.17
  151.6 2.8 %shard_map.102.refs_3_.refs_4_.refs_5_ = f32[448,768]{1,0:T(8,128)S(1)} custom-call(s32[448,128]{1,0:T(8,128)S(1)} %copy-done.17, f32[224,768]{1,0:T(8,128)S(1)} %copy-done.11, f32[8,56,768]{2,1,0:T(8,128)S(1)} %copy-done.5, f32[8,56,768]{2,1,0:T(8,128)S(1)} %copy-done.7, f32[8,56,768]{2,1,0:T(8,128)S(1)} %copy-done.9), custom_call_target="tpu_custom_call" | custom-call | flops 1541406720 | bytes 8388608 | tf_op jit(solution)/shard_map/pallas_call | solution.py:377
  154.4 3.2 %shard_map.101.refs_0_.refs_1_.refs_2_ = f32[448,768]{1,0:T(8,128)S(1)} custom-call(s32[448,128]{1,0:T(8,128)S(1)} %copy-done.18, f32[224,768]{1,0:T(8,128)S(1)} %shard_map.89.refs_0_.refs_2_.refs_1_, f32[8,56,768]{2,1,0:T(8,128)S(1)} %copy-done.5, f32[8,56,768]{2,1,0:T(8,128)S(1)} %copy-done.7, f32[8,56,768]{2,1,0:T(8,128)S(1)} %copy-done.9), custom_call_target="tpu_custom_call" | custom-call | flops 1541406720 | bytes 8388608 | tf_op jit(solution)/shard_map/pallas_call | solution.py:377
  157.6 1.1 copy-done.2
  158.7 1.3 copy-done.3
  160.1 0.9 copy-done.19
  161.0 5.3 %shard_map.107 = (f32[448,1024]{1,0:T(8,128)}, f32[448,1024]{1,0:T(8,128)}, f32[448,1024]{1,0:T(8,128)}) custom-call(s32[448,128]{1,0:T(8,128)S(1)} %copy-done.19, f32[448,768]{1,0:T(8,128)S(1)} %copy-done.3, f32[448,768]{1,0:T(8,128)S(1)} %copy-done.3, f32[448,768]{1,0:T(8,128)S(1)} %copy-done.3, f32[448,768]{1,0:T(8,128)S(1)} %shard_map.102.refs_3_.refs_4_.refs_5_, ...), custom_call_target="tpu_custom_call" | custom-call | flops 1409286144 | bytes 12582912 | tf_op jit(solution)/shard_map/pallas_call | solution.py:402
  (68 shorter events, 0.3 us)
Async XLA Ops:
  0.7 1.2 copy-start
  2.5 1.9 %collective-permute-start.2 = (f32[224,512]{1,0:T(8,128)S(1)}, f32[224,512]{1,0:T(8,128)S(1)}, u32[]{:S(2)}, u32[]{:S(2)}) collective-permute-start(f32[224,512]{1,0:T(8,128)S(1)} %get-tuple-element.20), channel_id=1, source_target_pairs={{0,64},{64,0},{128,192},{192,128},{1,65},{65,1},{129,193},{193,129... | collective-permute-start | bytes 1376264 | tf_op jit(solution)/shard_map/ppermute | solution.py:289
  2.6 5.8 %copy-start.28 = (s32[448,1]{0,1:T(1,128)S(1)}, s32[448,1]{0,1:T(1,128)}, u32[]{:S(2)}) copy-start(s32[448,1]{0,1:T(1,128)} %param.10) | copy-start | bytes 5380
  2.6 5.9 %copy-start.29 = (s32[448]{0:T(512)S(1)}, s32[448]{0:T(512)}, u32[]{:S(2)}) copy-start(s32[448]{0:T(512)} %param.11) | copy-start | bytes 5380
  2.6 4.0 %collective-permute-start = (f32[224,512]{1,0:T(8,128)S(1)}, f32[224,512]{1,0:T(8,128)S(1)}, u32[]{:S(2)}, u32[]{:S(2)}) collective-permute-start(f32[224,512]{1,0:T(8,128)S(1)} %get-tuple-element.19), channel_id=1, source_target_pairs={{0,64},{64,0},{128,192},{192,128},{1,65},{65,1},{129,193},{193,129... | collective-permute-start | bytes 1376264 | tf_op jit(solution)/shard_map/ppermute | solution.py:289
  5.0 13.4 %copy-start.1 = (bf16[1,224,2048]{2,1,0:T(8,128)(2,1)S(1)}, bf16[1,224,2048]{2,1,0:T(8,128)(2,1)}, u32[]{:S(2)}) copy-start(bf16[1,224,2048]{2,1,0:T(8,128)(2,1)} %param.6) | copy-start | bytes 2752516
  5.0 13.4 %copy-start.20 = (f32[224,512]{1,0:T(8,128)S(1)}, f32[224,512]{1,0:T(8,128)}, u32[]{:S(2)}) copy-start(f32[224,512]{1,0:T(8,128)} %refs_4_.3) | copy-start | bytes 1376260
  5.0 8.5 %collective-permute-start.3 = (f32[224,256]{1,0:T(8,128)S(1)}, f32[224,256]{1,0:T(8,128)S(1)}, u32[]{:S(2)}, u32[]{:S(2)}) collective-permute-start(f32[224,256]{1,0:T(8,128)S(1)} %shard_map.88), channel_id=1, source_target_pairs={{0,128},{128,0},{64,192},{192,64},{1,129},{129,1},{65,193},{193,65... | collective-permute-start | bytes 688136 | tf_op jit(solution)/shard_map/ppermute | solution.py:305
  7.9 9.7 %collective-permute-start.1 = (f32[224,256]{1,0:T(8,128)}, f32[224,256]{1,0:T(8,128)S(1)}, u32[]{:S(2)}, u32[]{:S(2)}) collective-permute-start(f32[224,256]{1,0:T(8,128)} %shard_map.87), channel_id=1, source_target_pairs={{0,128},{128,0},{64,192},{192,64},{1,129},{129,1},{65,193},{193,65... | collective-permute-start | bytes 688136 | tf_op jit(solution)/shard_map/ppermute | solution.py:305
  10.6 0.7 copy-start.16
  17.7 0.7 copy-start.26
  18.4 1.0 copy-start.22
  19.4 1.0 copy-start.23
  20.4 0.9 copy-start.27
  21.3 7.3 %copy-start.21 = (f32[224,512]{1,0:T(8,128)S(1)}, f32[224,512]{1,0:T(8,128)}, u32[]{:S(2)}) copy-start(f32[224,512]{1,0:T(8,128)} %refs_4_.3) | copy-start | bytes 1376260
  22.1 0.7 copy-start.24
  22.8 22.2 %collective-permute-start.4 = (f32[224,768]{1,0:T(8,128)S(1)}, f32[224,768]{1,0:T(8,128)S(1)}, u32[]{:S(2)}, u32[]{:S(2)}) collective-permute-start(f32[224,768]{1,0:T(8,128)S(1)} %shard_map.89.refs_0_.refs_2_.refs_1_), channel_id=1, source_target_pairs={{0,8},{1,9},{2,10},{3,11},{4,12},{5,13},{6,14},{7,15},{8,16},{9,17... | collective-permute-start | bytes 2064392 | tf_op jit(solution)/shard_map/ppermute | solution.py:349
  24.7 20.3 %collective-permute-start.5 = (f32[224,768]{1,0:T(8,128)S(1)}, f32[224,768]{1,0:T(8,128)}, u32[]{:S(2)}, u32[]{:S(2)}) collective-permute-start(f32[224,768]{1,0:T(8,128)S(1)} %shard_map.89.refs_0_.refs_2_.refs_1_), channel_id=1, source_target_pairs={{8,0},{9,1},{10,2},{11,3},{12,4},{13,5},{14,6},{15,7},{16,8},{17,9... | collective-permute-start | bytes 2064392 | tf_op jit(solution)/shard_map/ppermute | solution.py:349
  28.6 0.9 copy-start.25
  30.3 17.1 %copy-start.10 = (f32[224,768]{1,0:T(8,128)}, f32[224,768]{1,0:T(8,128)S(1)}, u32[]{:S(2)}) copy-start(f32[224,768]{1,0:T(8,128)S(1)} %shard_map.90.refs_1_.refs_3_) | copy-start | bytes 2064388
  30.4 29.5 %collective-permute-start.6 = (f32[224,768]{1,0:T(8,128)S(1)}, f32[224,768]{1,0:T(8,128)}, u32[]{:S(2)}, u32[]{:S(2)}) collective-permute-start(f32[224,768]{1,0:T(8,128)S(1)} %shard_map.90.refs_1_.refs_3_), channel_id=1, source_target_pairs={{0,8},{1,9},{2,10},{3,11},{4,12},{5,13},{6,14},{7,15},{8,16},{9,17... | collective-permute-start | bytes 2064392 | tf_op jit(solution)/shard_map/ppermute | solution.py:349
  30.4 29.4 %collective-permute-start.7 = (f32[224,768]{1,0:T(8,128)S(1)}, f32[224,768]{1,0:T(8,128)}, u32[]{:S(2)}, u32[]{:S(2)}) collective-permute-start(f32[224,768]{1,0:T(8,128)S(1)} %shard_map.90.refs_1_.refs_3_), channel_id=1, source_target_pairs={{8,0},{9,1},{10,2},{11,3},{12,4},{13,5},{14,6},{15,7},{16,8},{17,9... | collective-permute-start | bytes 2064392 | tf_op jit(solution)/shard_map/ppermute | solution.py:349
  33.7 13.7 %all-to-all-start = ((s32[8,8,128]{2,1,0:T(8,128)}), s32[8,8,128]{2,1,0:T(8,128)S(1)}, u32[]{:S(2)}, u32[]{:S(2)}) async-start(s32[8,8,128]{2,1,0:T(8,128)} %get-tuple-element.21.refs_8_), calls=%async_computation | async-start | bytes 65536 | tf_op jit(solution)/shard_map/all_to_all | solution.py:280
  45.0 2.4 %copy-start.15 = (f32[224,768]{1,0:T(8,128)}, f32[224,768]{1,0:T(8,128)S(1)}, u32[]{:S(2)}) copy-start(f32[224,768]{1,0:T(8,128)S(1)} %collective-permute-done.4.refs_2_.refs_4_.refs_0_) | copy-start | bytes 2064388
  50.2 25.7 %all-to-all-start.1 = ((f32[8,56,768]{2,1,0:T(8,128)}), f32[8,56,768]{2,1,0:T(8,128)S(1)}, u32[]{:S(2)}, u32[]{:S(2)}) async-start(f32[8,56,768]{2,1,0:T(8,128)} %shard_map.92.refs_2_), calls=%async_computation.1 | async-start | bytes 2752512 | tf_op jit(solution)/shard_map/all_to_all | solution.py:344
  56.1 19.8 %collective-permute-start.8 = (f32[224,768]{1,0:T(8,128)}, f32[224,768]{1,0:T(8,128)S(1)}, u32[]{:S(2)}, u32[]{:S(2)}) collective-permute-start(f32[224,768]{1,0:T(8,128)} %get-tuple-element.24), channel_id=1, source_target_pairs={{0,8},{1,9},{2,10},{3,11},{4,12},{5,13},{6,14},{7,15},{8,16},{9,17... | collective-permute-start | bytes 2064392 | tf_op jit(solution)/shard_map/ppermute | solution.py:349
  56.1 19.8 %collective-permute-start.9 = (f32[224,768]{1,0:T(8,128)}, f32[224,768]{1,0:T(8,128)}, u32[]{:S(2)}, u32[]{:S(2)}) collective-permute-start(f32[224,768]{1,0:T(8,128)} %get-tuple-element.25), channel_id=1, source_target_pairs={{8,0},{9,1},{10,2},{11,3},{12,4},{13,5},{14,6},{15,7},{16,8},{17,9... | collective-permute-start | bytes 2064392 | tf_op jit(solution)/shard_map/ppermute | solution.py:349
  59.8 31.1 %collective-permute-start.10 = (f32[224,768]{1,0:T(8,128)}, f32[224,768]{1,0:T(8,128)}, u32[]{:S(2)}, u32[]{:S(2)}) collective-permute-start(f32[224,768]{1,0:T(8,128)} %get-tuple-element.22.refs_0_.refs_2_), channel_id=1, source_target_pairs={{0,8},{1,9},{2,10},{3,11},{4,12},{5,13},{6,14},{7,15},{8,16},{9,17... | collective-permute-start | bytes 2064392 | tf_op jit(solution)/shard_map/ppermute | solution.py:349
  59.8 31.1 %collective-permute-start.11 = (f32[224,768]{1,0:T(8,128)}, f32[224,768]{1,0:T(8,128)}, u32[]{:S(2)}, u32[]{:S(2)}) collective-permute-start(f32[224,768]{1,0:T(8,128)} %get-tuple-element.23.refs_1_.refs_3_), channel_id=1, source_target_pairs={{8,0},{9,1},{10,2},{11,3},{12,4},{13,5},{14,6},{15,7},{16,8},{17,9... | collective-permute-start | bytes 2064392 | tf_op jit(solution)/shard_map/ppermute | solution.py:349
  75.9 0.8 copy-start.14
  76.7 3.7 %copy-start.4 = (f32[8,56,768]{2,1,0:T(8,128)}, f32[8,56,768]{2,1,0:T(8,128)S(1)}, u32[]{:S(2)}) copy-start(f32[8,56,768]{2,1,0:T(8,128)S(1)} %all-to-all-done.1.refs_6_.refs_2_) | copy-start | bytes 4128772
  80.5 27.1 %all-to-all-start.2 = ((f32[8,56,768]{2,1,0:T(8,128)}), f32[8,56,768]{2,1,0:T(8,128)S(1)}, u32[]{:S(2)}, u32[]{:S(2)}) async-start(f32[8,56,768]{2,1,0:T(8,128)} %shard_map.96.refs_2_), calls=%async_computation.2 | async-start | bytes 2752512 | tf_op jit(solution)/shard_map/all_to_all | solution.py:344
  87.7 19.8 %collective-permute-start.12 = (f32[224,768]{1,0:T(8,128)}, f32[224,768]{1,0:T(8,128)S(1)}, u32[]{:S(2)}, u32[]{:S(2)}) collective-permute-start(f32[224,768]{1,0:T(8,128)} %get-tuple-element.28), channel_id=1, source_target_pairs={{0,8},{1,9},{2,10},{3,11},{4,12},{5,13},{6,14},{7,15},{8,16},{9,17... | collective-permute-start | bytes 2064392 | tf_op jit(solution)/shard_map/ppermute | solution.py:349
  89.3 18.3 %collective-permute-start.13 = (f32[224,768]{1,0:T(8,128)}, f32[224,768]{1,0:T(8,128)S(1)}, u32[]{:S(2)}, u32[]{:S(2)}) collective-permute-start(f32[224,768]{1,0:T(8,128)} %get-tuple-element.29), channel_id=1, source_target_pairs={{8,0},{9,1},{10,2},{11,3},{12,4},{13,5},{14,6},{15,7},{16,8},{17,9... | collective-permute-start | bytes 2064392 | tf_op jit(solution)/shard_map/ppermute | solution.py:349
  90.9 28.6 %collective-permute-start.14 = (f32[224,768]{1,0:T(8,128)}, f32[224,768]{1,0:T(8,128)}, u32[]{:S(2)}, u32[]{:S(2)}) collective-permute-start(f32[224,768]{1,0:T(8,128)} %get-tuple-element.26.refs_0_.refs_2_), channel_id=1, source_target_pairs={{0,8},{1,9},{2,10},{3,11},{4,12},{5,13},{6,14},{7,15},{8,16},{9,17... | collective-permute-start | bytes 2064392 | tf_op jit(solution)/shard_map/ppermute | solution.py:349
  91.4 28.1 %collective-permute-start.15 = (f32[224,768]{1,0:T(8,128)}, f32[224,768]{1,0:T(8,128)}, u32[]{:S(2)}, u32[]{:S(2)}) collective-permute-start(f32[224,768]{1,0:T(8,128)} %get-tuple-element.27.refs_1_.refs_3_), channel_id=1, source_target_pairs={{8,0},{9,1},{10,2},{11,3},{12,4},{13,5},{14,6},{15,7},{16,8},{17,9... | collective-permute-start | bytes 2064392 | tf_op jit(solution)/shard_map/ppermute | solution.py:349
  107.5 0.9 copy-start.12
  107.6 1.0 copy-start.13
  108.6 3.5 %copy-start.6 = (f32[8,56,768]{2,1,0:T(8,128)}, f32[8,56,768]{2,1,0:T(8,128)S(1)}, u32[]{:S(2)}) copy-start(f32[8,56,768]{2,1,0:T(8,128)S(1)} %all-to-all-done.2.refs_6_.refs_3_) | copy-start | bytes 4128772
  112.1 22.7 %all-to-all-start.3 = ((f32[8,56,768]{2,1,0:T(8,128)}), f32[8,56,768]{2,1,0:T(8,128)S(1)}, u32[]{:S(2)}, u32[]{:S(2)}) async-start(f32[8,56,768]{2,1,0:T(8,128)} %shard_map.100.refs_2_), calls=%async_computation.3 | async-start | bytes 2752512 | tf_op jit(solution)/shard_map/all_to_all | solution.py:344
  119.5 11.9 %collective-permute-start.17 = (f32[224,768]{1,0:T(8,128)}, f32[224,768]{1,0:T(8,128)S(1)}, u32[]{:S(2)}, u32[]{:S(2)}) collective-permute-start(f32[224,768]{1,0:T(8,128)} %get-tuple-element.31.refs_1_.refs_3_), channel_id=1, source_target_pairs={{8,0},{9,1},{10,2},{11,3},{12,4},{13,5},{14,6},{15,7},{16,8},{17,9... | collective-permute-start | bytes 2064392 | tf_op jit(solution)/shard_map/ppermute | solution.py:365
  122.4 12.4 %collective-permute-start.16 = (f32[224,768]{1,0:T(8,128)}, f32[224,768]{1,0:T(8,128)S(1)}, u32[]{:S(2)}, u32[]{:S(2)}) collective-permute-start(f32[224,768]{1,0:T(8,128)} %get-tuple-element.32), channel_id=1, source_target_pairs={{0,8},{1,9},{2,10},{3,11},{4,12},{5,13},{6,14},{7,15},{8,16},{9,17... | collective-permute-start | bytes 2064392 | tf_op jit(solution)/shard_map/ppermute | solution.py:364
  134.8 3.6 %copy-start.8 = (f32[8,56,768]{2,1,0:T(8,128)}, f32[8,56,768]{2,1,0:T(8,128)S(1)}, u32[]{:S(2)}) copy-start(f32[8,56,768]{2,1,0:T(8,128)S(1)} %all-to-all-done.3.refs_4_.refs_6_) | copy-start | bytes 4128772
  138.4 20.4 %all-to-all-start.4 = ((f32[8,56,768]{2,1,0:T(8,128)}), f32[8,56,768]{2,1,0:T(8,128)S(1)}, u32[]{:S(2)}, u32[]{:S(2)}) async-start(f32[8,56,768]{2,1,0:T(8,128)} %shard_map.106), calls=%async_computation.4 | async-start | bytes 2752512 | tf_op jit(solution)/shard_map/all_to_all | solution.py:344
  145.6 1.3 copy-start.5
  146.9 1.3 copy-start.7
  148.2 1.3 copy-start.9
  149.6 1.1 copy-start.11
  150.7 0.9 copy-start.17
  151.6 2.8 %copy-start.18 = (s32[448,128]{1,0:T(8,128)S(1)}, s32[448,128]{1,0:T(8,128)}, u32[]{:S(2)}) copy-start(s32[448,128]{1,0:T(8,128)} %copy-done.16) | copy-start | bytes 688132
  157.6 1.1 copy-start.2
  158.7 1.3 copy-start.3
  160.1 0.9 copy-start.19

commit v9 on v8

--- a/solution.py
+++ b/solution.py
@@ -32,7 +32,7 @@
 VMEM = pltpu.CompilerParams(vmem_limit_bytes=12 * 1024 * 1024)
 
 
-def call(kernel, out, *, grid=None, in_specs=None, out_specs=None, flops=0, moved=0, aliases=None):
+def call(kernel, out, *, grid=None, in_specs=None, out_specs=None, flops=0, moved=0, aliases=None, scratch=()):
     extra = {}
     if grid is not None:
         extra = dict(grid=grid, in_specs=in_specs, out_specs=out_specs)
@@ -43,6 +43,7 @@
         out_shape=out,
         compiler_params=VMEM,
         input_output_aliases=aliases or {},
+        scratch_shapes=scratch,
         cost_estimate=pl.CostEstimate(flops=flops, bytes_accessed=moved, transcendentals=0),
         **extra,
     )
@@ -54,6 +55,10 @@
 
 def whole():
     return pl.BlockSpec(memory_space=pltpu.VMEM)
+
+
+def far_away():
+    return pl.BlockSpec(memory_space=pltpu.HBM)
 
 
 def scalar():
@@ -90,10 +95,26 @@
 
 
 def update_kernel(half, place, grad, got, got_y, weight, first, second, *refs):
-    out = refs[-1]
-    dp = place[1]
-    at = pl.multiple_of(dp * FEATS + half * HALF, HALF)
-    total = grad[:, pl.ds(at, HALF)].astype(F32) + got[...] + got_y[...]
+    out, mine, held, done = refs[-4:]
+    at = pl.multiple_of(place[1] * FEATS + half * HALF, HALF)
+    here = pl.ds(half * HALF, HALF)
+    copies = [pltpu.make_async_copy(grad.at[:, pl.ds(at, HALF)], mine, done.at[0])]
+    for k, source in enumerate(
+        (
+            got.at[:, pl.ds(HALF, HALF)],
+            got_y,
+            first.at[:, here],
+            second.at[:, here],
+            weight.at[:, here],
+        )
+    ):
+        copies.append(pltpu.make_async_copy(source, held.at[k], done.at[k + 1]))
+    for copy in copies:
+        copy.start()
+    for copy in copies:
+        copy.wait()
+    got, got_y, first, second, weight = (held.at[k] for k in range(5))
+    total = mine[...].astype(F32) + got[...] + got_y[...]
     new_first = first_decay * first[...] + (1.0 - first_decay) * total
     new_second = second_decay * second[...] + (1.0 - second_decay) * total * total
     first_hat = new_first / (1.0 - first_decay**STEP)
@@ -116,7 +137,11 @@
         I32, (FINE, FINE), 0
     )
     slot = jnp.sum(jnp.where(earlier & (d == r), 1, 0), axis=1, keepdims=True)
-    source_xy, source_z = d & (PLANE - 1), d >> 3
+    later = lax.broadcasted_iota(I32, (FINE, FINE), 0) < lax.broadcasted_iota(
+        I32, (FINE, FINE), 1
+    )
+    slot_row = jnp.sum(jnp.where(later & (d == r), 1, 0), axis=0, keepdims=True)
+    source_xy, source_z = r & (PLANE - 1), r >> 3
     row_of = ((r & (PLANE - 1)) << 3) + (r >> 3)
     left = jnp.where(lax.broadcasted_iota(I32, (64, FINE), 0) == row_of, 1.0, 0.0).astype(BF16)
     right = jnp.where(
@@ -128,9 +153,9 @@
     none = -1
 
     def place_in(offsets):
-        at = jnp.full((FINE, 1), none, I32)
+        at = jnp.full((1, FINE), none, I32)
         for k, offset in offsets:
-            at = jnp.where(away == k, source_xy * 128 + offset + slot, at)
+            at = jnp.where(away == k, source_xy * 128 + offset + slot_row, at)
         return at
 
     groups = (
@@ -143,11 +168,7 @@
         place_in(((6, 0), (2, 14))),
         place_in(((5, 0), (3, 14), (4, 42))),
     )
-    lane = lax.broadcasted_iota(I32, (FINE, 128), 1)
-    out = jnp.full((FINE, 128), none, I32)
-    for g, at in enumerate(groups):
-        out = jnp.where(lane == g, at, out)
-    codes[...] = out
+    codes[...] = jnp.concatenate(groups, axis=0)
 
 
 def asked_rows(asked, plane):
@@ -164,10 +185,16 @@
 
 
 def pick_kernel(planes, place, asked, *refs):
-    out = refs[-1]
+    out, held, done = refs[-3:]
     plane = lax.div(place[0], PLANE)
+    copies = [
+        pltpu.make_async_copy(refs[n], held.at[n], done.at[n]) for n in range(len(planes))
+    ]
+    for copy in copies:
+        copy.start()
     for n, away in enumerate(planes):
-        got = pick_from(asked, (plane + away + RING) & (RING - 1), refs[n][...])
+        copies[n].wait()
+        got = pick_from(asked, (plane + away + RING) & (RING - 1), held[n])
         for d in range(PLANE):
             out[d, n * USED : (n + 1) * USED, :] = got[d * SLOTS : d * SLOTS + USED]
 
@@ -204,13 +231,13 @@
 def far_dot(at, far):
     rows = far.shape[0] * far.shape[1]
     chosen = jnp.where(
-        lax.broadcasted_iota(I32, (FINE, rows), 1) == at, 1.0 - own_share, 0.0
+        lax.broadcasted_iota(I32, (rows, FINE), 0) == at, 1.0 - own_share, 0.0
     ).astype(BF16)
-    return split_dot(chosen, far.reshape(rows, far.shape[2]))
+    return split_dot(chosen, far.reshape(rows, far.shape[2]), ((0,), (0,)))
 
 
 def far_part(codes, lane, far, low, high):
-    at = codes[:, lane : lane + 1]
+    at = codes[lane : lane + 1, :]
     xy, row = at >> 7, at & 127
     here = (at >= 0) & (row >= low) & (row < high)
     at = jnp.where(here, xy * (high - low) + row - low, -1)
@@ -234,17 +261,22 @@
 
 def final_kernel(codes, *refs):
     first_half = pl.program_id(0) < 2
-    at = jnp.where(first_half, codes[:, 3:4], codes[:, 7:8])
+    at = jnp.where(first_half, codes[3:4, :], codes[7:8, :])
     at = jnp.where(at >= 0, (at >> 7) * SENT + (at & 127), -1)
     rows = PLANE * SENT
     chosen = jnp.where(
-        lax.broadcasted_iota(I32, (FINE, rows), 1) == at, 1.0 - own_share, 0.0
+        lax.broadcasted_iota(I32, (rows, FINE), 0) == at, 1.0 - own_share, 0.0
     ).astype(BF16)
     row = lax.broadcasted_iota(I32, (256, 256), 0) & 127
     lane = lax.broadcasted_iota(I32, (256, 256), 1) >> 1
     twice = jnp.where(row == lane, 1.0, 0.0).astype(BF16)
     far = [piece for k in range(3) for piece in halves(refs[6 + k][...].reshape(rows, 128))]
-    far = jnp.dot(chosen, jnp.concatenate(far, axis=1), preferred_element_type=F32)
+    far = lax.dot_general(
+        chosen,
+        jnp.concatenate(far, axis=1),
+        (((0,), (0,)), ((), ())),
+        preferred_element_type=F32,
+    )
     for state in range(3):
         acc0, acc1, out = (refs[3 * k + state] for k in (0, 1, 3))
         at = state * 256
@@ -268,7 +300,7 @@
 
     wanted, codes = call(
         index_kernel,
-        (shape(PLANE, RING, 128, dtype=I32), shape(FINE, 128, dtype=I32)),
+        (shape(PLANE, RING, 128, dtype=I32), shape(8, FINE, dtype=I32)),
         in_specs=[scalar(), whole(), whole(), whole()],
         moved=1 << 20,
     )(
@@ -305,24 +337,19 @@
     got_y = [lax.ppermute(p, "dp", NEXT_Y) for p in passed]
     state = []
     for half in range(2):
-        block = pl.BlockSpec((ROWS, HALF), lambda i, half=half: (0, half))
         after = (got_y[1], wanted) if half == 0 else ()
         state.append(
             call(
                 lambda *refs, half=half: update_kernel(half, *refs),
                 shape(ROWS, WIDE),
-                grid=(1,),
-                in_specs=[
-                    scalar(),
-                    pl.BlockSpec((ROWS, 4 * FEATS), lambda i: (0, 0)),
-                    pl.BlockSpec((ROWS, HALF), lambda i: (0, 1)),
-                    pl.BlockSpec((ROWS, HALF), lambda i: (0, 0)),
-                    block,
-                    block,
-                    block,
-                ]
+                in_specs=[scalar()]
+                + [far_away()] * 6
                 + [pl.BlockSpec(memory_space=pl.ANY)] * len(after),
-                out_specs=pl.BlockSpec((ROWS, WIDE), lambda i: (0, 0)),
+                scratch=(
+                    pltpu.VMEM((ROWS, HALF), BF16),
+                    pltpu.VMEM((5, ROWS, HALF), F32),
+                    pltpu.SemaphoreType.DMA((6,)),
+                ),
                 moved=2 << 20,
             )(place, grad, got_core[half], got_y[half], weight, first, second, *after)
         )
@@ -333,9 +360,13 @@
         return call(
             lambda *refs: pick_kernel(planes, *refs),
             shape(PLANE, SENT, WIDE),
-            in_specs=[scalar()]
-            + [whole()] * (1 + len(sources))
+            in_specs=[scalar(), whole()]
+            + [far_away()] * len(sources)
             + [pl.BlockSpec(memory_space=pl.ANY)] * len(after),
+            scratch=(
+                pltpu.VMEM((len(sources), ROWS, WIDE), F32),
+                pltpu.SemaphoreType.DMA((len(sources),)),
+            ),
             flops=4 * SLOTS * PLANE * ROWS * WIDE * 4,
             moved=5 << 20,
         )(place, asked, *sources, *after)
@@ -351,15 +382,15 @@
     one = [around((x, x)) for x in state]
     rows = pick((0, 0, -1, 1), (*state, *one[0]), 4)
     far1 = to_plane(rows)
-    one = [hold(one[0], rows), hold(one[1], wait=10)]
+    one[1] = hold(one[1], wait=10)
     two = [around(pair) for pair in one]
     rows = pick((-1, 1, -2, 2), (*one[1], *two[0]), 5, (far1,))
     far2 = to_plane(rows)
-    two = [hold(two[0], rows), hold(two[1], wait=10)]
+    two[1] = hold(two[1], wait=10)
     three = [around(pair) for pair in two]
     rows = pick((-2, 2, -3, 3), (*two[1], *three[0]), 5, (far2,))
     far3 = to_plane(rows)
-    three = [hold(three[0], rows), hold(three[1], wait=10)]
+    three[1] = hold(three[1], wait=10)
     four = (
         lax.ppermute(three[0][0], "shard", UP),
         lax.ppermute(three[1][1], "shard", DOWN),
@@ -379,7 +410,7 @@
                 shape(FINE, WIDE),
                 grid=(3,),
                 in_specs=[
-                    pl.BlockSpec((FINE, 128), lambda i: (0, 0)),
+                    pl.BlockSpec((8, FINE), lambda i: (0, 0)),
                     pl.BlockSpec((ROWS, HALF), lambda i: (0, i)),
                 ]
                 + [pl.BlockSpec((PLANE, SENT, HALF), lambda i: (0, 0, i))] * 3,
@@ -403,7 +434,7 @@
         final_kernel,
         (shape(FINE, 2 * FEATS),) * 3,
         grid=(4,),
-        in_specs=[pl.BlockSpec((FINE, 128), lambda j: (0, 0))]
+        in_specs=[pl.BlockSpec((8, FINE), lambda j: (0, 0))]
         + [acc_block(half, s) for half in range(2) for s in range(3)]
         + [far_block(s) for s in range(3)],
         out_specs=(pl.BlockSpec((FINE, 256), lambda j: (0, j)),) * 3,

time: 167 us -> 166 us (level)
  local copies, waits for them, and re-layouts: 18.7 us -> 11 us
  waiting for transfers between devices: 53.1 us -> 57.3 us
  Pallas kernels: 30.8 us -> 33.1 us
    ppermute x1, waiting for transfers between devices: 8.96 us -> 0.02 us  [on_device(): lax.ppermute(three[1][1], 'shard', DOWN)]
    unnamed x61 -> x39, local copies, waits for them, and re-layouts: 18.5 us -> 10.9 us
    ppermute x1, waiting for transfers between devices: 3.39 us -> 9.36 us  [on_device(): lax.ppermute(three[0][0], 'shard', UP)]
    all_to_all x4, waiting for transfers between devices: 0.01 us -> 4.43 us  [to_plane(): lax.all_to_all(rows, 'shard', split_axis=0, concat_axis=0, axis_index_gro...]
    ppermute x6, waiting for transfers between devices: 30.5 us -> 32.7 us  [around(): lax.ppermute(pair[0], 'shard', UP)]
  transfers between devices with their start and end apart: 23 -> 23, of which waited for: 11 -> 11; matrix products, arithmetic and copies ran while one was open for 0% -> 0% of each run, Pallas kernels for 12% -> 13%
where the time goes in v9:
time: 166 us; the launch traced here: 164 us
  starting transfers between devices  62.1 us (37%)
  waiting for transfers between devices  57.3 us (35%)
  Pallas kernels  33.1 us (20%)
  local copies, waits for them, and re-layouts  11 us (7%)
    ppermute x6, waiting for transfers between devices, around(): lax.ppermute(pair[0], 'shard', UP)  32.7 us
    all_to_all x4, starting transfers between devices, to_plane(): lax.all_to_all(rows, 'shard', split_axis=0, concat_axis=0, axis_index_gro...  27.7 us
    ppermute x6, starting transfers between devices, around(): lax.ppermute(pair[1], 'shard', DOWN)  17.3 us
    pallas_call x4, Pallas kernels, pick(): call(lambda *refs: pick_kernel(planes, *refs), shape(PLANE, SENT, WIDE),...  15.3 us
    unnamed x39, local copies, waits for them, and re-layouts  10.9 us
    ppermute x1, waiting for transfers between devices, on_device(): lax.ppermute(three[0][0], 'shard', UP)  9.36 us
    ppermute x2, waiting for transfers between devices, on_device(): got_y = [lax.ppermute(p, 'dp', NEXT_Y) for p in passed]  7.52 us
    all_to_all x1, starting transfers between devices, on_device(): lax.all_to_all(wanted, 'shard', split_axis=0, concat_axis=0, axis_index_g...  7.46 us
  transfers between devices with their start and end apart: 23, of which 11 were waited for; matrix products, arithmetic and copies ran while one was open for 0% of the time, Pallas kernels for 13%

profile of v9, /device:TPU:2, one launch (start us, length us, event | category | flops | bytes accessed | tf_op | source)
XLA Modules:
  0.0 164.5 jit_solution(5716021160952374953)
XLA Ops:
  0.6 0.1 pad_add_fusion.place.refs_0_
  0.7 1.2 copy-done
  1.9 0.6 shard_map.86
  2.5 0.1 collective-permute-start
  2.6 0.0 copy-start.17
  2.6 0.0 copy-start.18
  2.6 0.5 collective-permute-start.2
  3.1 1.3 collective-permute-done.refs_2_
  4.4 1.3 shard_map.87
  5.7 1.6 collective-permute-start.1
  7.3 0.0 collective-permute-done.2.refs_2_
  7.3 1.3 shard_map.88
  8.5 0.4 collective-permute-start.3
  9.0 0.1 copy.16.dev
  9.1 0.1 copy.17.col
  9.3 1.7 %shard_map.85 = (s32[8,8,128]{2,1,0:T(8,128)}, s32[8,448]{1,0:T(8,128)S(1)}) custom-call(s32[2]{0:T(128)S(1)} %pad_add_fusion.place.refs_0_, s32[448,1]{1,0:T(8,128)S(1)} %copy.16.dev, s32[1,448]{1,0:T(1,128)S(1)} %bitcast.10, s32[448,1]{1,0:T(8,128)S(1)} %copy.17.col), custom_call_target="tpu_custom_call" | custom-call | bytes 1048576 | tf_op jit(solution)/shard_map/pallas_call | solution.py:301
  10.9 3.4 %collective-permute-done.1.refs_3_ = f32[224,256]{1,0:T(8,128)S(1)} collective-permute-done((f32[224,256]{1,0:T(8,128)}, f32[224,256]{1,0:T(8,128)S(1)}, u32[]{:S(2)}, u32[]{:S(2)}) %collective-permute-start.1) | collective-permute-done | bytes 229408 | tf_op jit(solution)/shard_map/ppermute | solution.py:337
  14.3 4.1 %collective-permute-done.3.refs_7_.refs_3_ = f32[224,256]{1,0:T(8,128)S(1)} collective-permute-done((f32[224,256]{1,0:T(8,128)}, f32[224,256]{1,0:T(8,128)S(1)}, u32[]{:S(2)}, u32[]{:S(2)}) %collective-permute-start.3) | collective-permute-done | bytes 229408 | tf_op jit(solution)/shard_map/ppermute | solution.py:337
  18.5 1.0 copy-done.15
  19.5 1.0 copy-done.16
  20.5 1.3 shard_map.89.refs_0_.refs_2_.refs_1_
  21.8 2.0 %collective-permute-start.4 = (f32[224,768]{1,0:T(8,128)S(1)}, f32[224,768]{1,0:T(8,128)}, u32[]{:S(2)}, u32[]{:S(2)}) collective-permute-start(f32[224,768]{1,0:T(8,128)S(1)} %shard_map.89.refs_0_.refs_2_.refs_1_), channel_id=1, source_target_pairs={{0,8},{1,9},{2,10},{3,11},{4,12},{5,13},{6,14},{7,15},{8,16},{9,17... | collective-permute-start | bytes 2064392 | tf_op jit(solution)/shard_map/ppermute | solution.py:380
  23.7 4.0 %collective-permute-start.5 = (f32[224,768]{1,0:T(8,128)S(1)}, f32[224,768]{1,0:T(8,128)}, u32[]{:S(2)}, u32[]{:S(2)}) collective-permute-start(f32[224,768]{1,0:T(8,128)S(1)} %shard_map.89.refs_0_.refs_2_.refs_1_), channel_id=1, source_target_pairs={{8,0},{9,1},{10,2},{11,3},{12,4},{13,5},{14,6},{15,7},{16,8},{17,9... | collective-permute-start | bytes 2064392 | tf_op jit(solution)/shard_map/ppermute | solution.py:380
  27.8 1.3 shard_map.90.refs_1_.refs_3_
  29.1 0.1 collective-permute-start.6
  29.1 3.2 %collective-permute-start.7 = (f32[224,768]{1,0:T(8,128)S(1)}, f32[224,768]{1,0:T(8,128)}, u32[]{:S(2)}, u32[]{:S(2)}) collective-permute-start(f32[224,768]{1,0:T(8,128)S(1)} %shard_map.90.refs_1_.refs_3_), channel_id=1, source_target_pairs={{8,0},{9,1},{10,2},{11,3},{12,4},{13,5},{14,6},{15,7},{16,8},{17,9... | collective-permute-start | bytes 2064392 | tf_op jit(solution)/shard_map/ppermute | solution.py:380
  32.4 7.5 %all-to-all-start = ((s32[8,8,128]{2,1,0:T(8,128)}), s32[8,8,128]{2,1,0:T(8,128)S(1)}, u32[]{:S(2)}, u32[]{:S(2)}) async-start(s32[8,8,128]{2,1,0:T(8,128)} %get-tuple-element.16.refs_8_), calls=%async_computation | async-start | bytes 65536 | tf_op jit(solution)/shard_map/all_to_all | solution.py:312
  39.8 4.3 %collective-permute-done.4.refs_2_.refs_4_ = f32[224,768]{1,0:T(8,128)} collective-permute-done((f32[224,768]{1,0:T(8,128)S(1)}, f32[224,768]{1,0:T(8,128)}, u32[]{:S(2)}, u32[]{:S(2)}) %collective-permute-start.4) | collective-permute-done | bytes 688160 | tf_op jit(solution)/shard_map/ppermute | solution.py:380
  44.1 0.0 collective-permute-done.5.refs_3_.refs_5_
  44.1 2.0 %all-to-all-done.refs_1_ = s32[8,8,128]{2,1,0:T(8,128)S(1)} async-done(((s32[8,8,128]{2,1,0:T(8,128)}), s32[8,8,128]{2,1,0:T(8,128)S(1)}, u32[]{:S(2)}, u32[]{:S(2)}) %all-to-all-start) | async-done | bytes 32800 | tf_op jit(solution)/shard_map/all_to_all | solution.py:312
  46.1 2.9 %shard_map.92 = f32[8,56,768]{2,1,0:T(8,128)S(1)} custom-call(s32[2]{0:T(128)S(1)} %pad_add_fusion.place.refs_0_, s32[8,8,128]{2,1,0:T(8,128)S(1)} %all-to-all-done.refs_1_, f32[224,768]{1,0:T(8,128)S(1)} %shard_map.89.refs_0_.refs_2_.refs_1_, f32[224,768]{1,0:T(8,128)S(1)} %shard_map.90.refs_1_.refs_3_, f32[224,768]{1,0:T(8,128)} %collective-permute-done.4.refs_2_.refs_4_, ...), custom_call_target="tpu_custom_call" | custom-call | flops 352321536 | bytes 5242880 | tf_op jit(solution)/shard_map/pallas_call | solution.py:360
  49.0 0.0 copy-start.12
  49.0 1.1 copy-done.12
  50.0 5.5 %all-to-all-start.1 = ((f32[8,56,768]{2,1,0:T(8,128)}), f32[8,56,768]{2,1,0:T(8,128)S(1)}, u32[]{:S(2)}, u32[]{:S(2)}) async-start(f32[8,56,768]{2,1,0:T(8,128)} %copy-done.12), calls=%async_computation.1 | async-start | bytes 2752512 | tf_op jit(solution)/shard_map/all_to_all | solution.py:375
  55.6 0.0 collective-permute-start.8
  55.6 3.3 %collective-permute-start.9 = (f32[224,768]{1,0:T(8,128)}, f32[224,768]{1,0:T(8,128)S(1)}, u32[]{:S(2)}, u32[]{:S(2)}) collective-permute-start(f32[224,768]{1,0:T(8,128)} %collective-permute-done.5.refs_3_.refs_5_), channel_id=1, source_target_pairs={{8,0},{9,1},{10,2},{11,3},{12,4},{13,5},{14,6},{15,7},{16,8},{17,9... | collective-permute-start | bytes 2064392 | tf_op jit(solution)/shard_map/ppermute | solution.py:380
  58.9 3.2 %collective-permute-start.11 = (f32[224,768]{1,0:T(8,128)}, f32[224,768]{1,0:T(8,128)}, u32[]{:S(2)}, u32[]{:S(2)}) collective-permute-start(f32[224,768]{1,0:T(8,128)} %get-tuple-element.18.refs_1_.refs_3_), channel_id=1, source_target_pairs={{8,0},{9,1},{10,2},{11,3},{12,4},{13,5},{14,6},{15,7},{16,8},{17,9... | collective-permute-start | bytes 2064392 | tf_op jit(solution)/shard_map/ppermute | solution.py:380
  62.1 13.4 %collective-permute-done.8.refs_2_.refs_4_ = f32[224,768]{1,0:T(8,128)} collective-permute-done((f32[224,768]{1,0:T(8,128)}, f32[224,768]{1,0:T(8,128)}, u32[]{:S(2)}, u32[]{:S(2)}) %collective-permute-start.8) | collective-permute-done | bytes 688160 | tf_op jit(solution)/shard_map/ppermute | solution.py:380
  75.6 3.2 %collective-permute-start.13 = (f32[224,768]{1,0:T(8,128)S(1)}, f32[224,768]{1,0:T(8,128)}, u32[]{:S(2)}, u32[]{:S(2)}) collective-permute-start(f32[224,768]{1,0:T(8,128)S(1)} %collective-permute-done.9.refs_3_.refs_5_), channel_id=1, source_target_pairs={{8,0},{9,1},{10,2},{11,3},{12,4},{13,5},{14,6},{15,7},{16,8},{17,9... | collective-permute-start | bytes 2064392 | tf_op jit(solution)/shard_map/ppermute | solution.py:380
  78.8 4.1 %shard_map.95 = f32[8,56,768]{2,1,0:T(8,128)} custom-call(s32[2]{0:T(128)S(1)} %pad_add_fusion.place.refs_0_, s32[8,8,128]{2,1,0:T(8,128)S(1)} %all-to-all-done.refs_1_, f32[224,768]{1,0:T(8,128)} %get-tuple-element.17.refs_0_.refs_2_, f32[224,768]{1,0:T(8,128)} %get-tuple-element.18.refs_1_.refs_3_, f32[224,768]{1,0:T(8,128)} %collective-permute-done.8.refs_2_.refs_4_, ...), custom_call_target="tpu_custom_call" | custom-call | flops 352321536 | bytes 5242880 | tf_op jit(solution)/shard_map/pallas_call | solution.py:360
  82.9 7.2 %all-to-all-start.2 = ((f32[8,56,768]{2,1,0:T(8,128)}), f32[8,56,768]{2,1,0:T(8,128)S(1)}, u32[]{:S(2)}, u32[]{:S(2)}) async-start(f32[8,56,768]{2,1,0:T(8,128)} %shard_map.95), calls=%async_computation.2 | async-start | bytes 2752512 | tf_op jit(solution)/shard_map/all_to_all | solution.py:375
  90.2 0.1 collective-permute-done.10.refs_0_
  90.3 2.9 %collective-permute-start.14 = (f32[224,768]{1,0:T(8,128)}, f32[224,768]{1,0:T(8,128)}, u32[]{:S(2)}, u32[]{:S(2)}) collective-permute-start(f32[224,768]{1,0:T(8,128)} %get-tuple-element.19.refs_0_.refs_2_), channel_id=1, source_target_pairs={{0,8},{1,9},{2,10},{3,11},{4,12},{5,13},{6,14},{7,15},{8,16},{9,17... | collective-permute-start | bytes 2064392 | tf_op jit(solution)/shard_map/ppermute | solution.py:380
  93.2 0.3 collective-permute-start.15
  93.5 11.4 %collective-permute-done.12.refs_2_.refs_4_ = f32[224,768]{1,0:T(8,128)S(1)} collective-permute-done((f32[224,768]{1,0:T(8,128)}, f32[224,768]{1,0:T(8,128)S(1)}, u32[]{:S(2)}, u32[]{:S(2)}) %collective-permute-start.12) | collective-permute-done | bytes 688160 | tf_op jit(solution)/shard_map/ppermute | solution.py:380
  105.0 0.0 copy-start.6
  105.0 4.1 %shard_map.98 = f32[8,56,768]{2,1,0:T(8,128)} custom-call(s32[2]{0:T(128)S(1)} %pad_add_fusion.place.refs_0_, s32[8,8,128]{2,1,0:T(8,128)S(1)} %all-to-all-done.refs_1_, f32[224,768]{1,0:T(8,128)} %get-tuple-element.19.refs_0_.refs_2_, f32[224,768]{1,0:T(8,128)} %get-tuple-element.20.refs_1_.refs_3_, f32[224,768]{1,0:T(8,128)S(1)} %collective-permute-done.12.refs_2_.refs_4_, ...), custom_call_target="tpu_custom_call" | custom-call | flops 352321536 | bytes 5242880 | tf_op jit(solution)/shard_map/pallas_call | solution.py:360
  109.1 7.2 %all-to-all-start.3 = ((f32[8,56,768]{2,1,0:T(8,128)}), f32[8,56,768]{2,1,0:T(8,128)S(1)}, u32[]{:S(2)}, u32[]{:S(2)}) async-start(f32[8,56,768]{2,1,0:T(8,128)} %shard_map.98), calls=%async_computation.3 | async-start | bytes 2752512 | tf_op jit(solution)/shard_map/all_to_all | solution.py:375
  116.3 3.5 %collective-permute-done.14.refs_0_ = f32[224,768]{1,0:T(8,128)} collective-permute-done((f32[224,768]{1,0:T(8,128)}, f32[224,768]{1,0:T(8,128)}, u32[]{:S(2)}, u32[]{:S(2)}) %collective-permute-start.14) | collective-permute-done | bytes 688160 | tf_op jit(solution)/shard_map/ppermute | solution.py:380
  119.8 2.0 %collective-permute-start.17 = (f32[224,768]{1,0:T(8,128)}, f32[224,768]{1,0:T(8,128)S(1)}, u32[]{:S(2)}, u32[]{:S(2)}) collective-permute-start(f32[224,768]{1,0:T(8,128)} %get-tuple-element.22.refs_1_.refs_3_), channel_id=1, source_target_pairs={{8,0},{9,1},{10,2},{11,3},{12,4},{13,5},{14,6},{15,7},{16,8},{17,9... | collective-permute-start | bytes 2064392 | tf_op jit(solution)/shard_map/ppermute | solution.py:396
  121.8 9.4 %collective-permute-done.16.refs_2_.refs_4_ = f32[224,768]{1,0:T(8,128)} collective-permute-done((f32[224,768]{1,0:T(8,128)S(1)}, f32[224,768]{1,0:T(8,128)}, u32[]{:S(2)}, u32[]{:S(2)}) %collective-permute-start.16) | collective-permute-done | bytes 688160 | tf_op jit(solution)/shard_map/ppermute | solution.py:395
  131.2 0.0 collective-permute-done.17.refs_3_.refs_5_
  131.2 4.2 %shard_map.103 = f32[8,56,768]{2,1,0:T(8,128)} custom-call(s32[2]{0:T(128)S(1)} %pad_add_fusion.place.refs_0_, s32[8,8,128]{2,1,0:T(8,128)S(1)} %all-to-all-done.refs_1_, f32[224,768]{1,0:T(8,128)} %get-tuple-element.21.refs_0_.refs_2_, f32[224,768]{1,0:T(8,128)} %get-tuple-element.22.refs_1_.refs_3_, f32[224,768]{1,0:T(8,128)} %collective-permute-done.16.refs_2_.refs_4_, ...), custom_call_target="tpu_custom_call" | custom-call | flops 352321536 | bytes 5242880 | tf_op jit(solution)/shard_map/pallas_call | solution.py:360
  135.4 7.7 %all-to-all-start.4 = ((f32[8,56,768]{2,1,0:T(8,128)}), f32[8,56,768]{2,1,0:T(8,128)S(1)}, u32[]{:S(2)}, u32[]{:S(2)}) async-start(f32[8,56,768]{2,1,0:T(8,128)} %shard_map.103), calls=%async_computation.4 | async-start | bytes 2752512 | tf_op jit(solution)/shard_map/all_to_all | solution.py:375
  143.1 1.3 copy-done.5
  144.5 1.3 copy-done.7
  145.8 1.3 copy-done.9
  147.2 2.9 %shard_map.99.refs_0_.refs_1_.refs_2_ = f32[448,768]{1,0:T(8,128)S(1)} custom-call(s32[8,448]{1,0:T(8,128)S(1)} %get-tuple-element.13.refs_0_.codes, f32[224,768]{1,0:T(8,128)S(1)} %shard_map.89.refs_0_.refs_2_.refs_1_, f32[8,56,768]{2,1,0:T(8,128)S(1)} %copy-done.5, f32[8,56,768]{2,1,0:T(8,128)S(1)} %copy-done.7, f32[8,56,768]{2,1,0:T(8,128)S(1)} %copy-done.9), custom_call_target="tpu_custom_call" | custom-call | flops 1541406720 | bytes 8388608 | tf_op jit(solution)/shard_map/pallas_call | solution.py:408
  150.1 2.6 %shard_map.100.refs_3_.refs_4_.refs_5_ = f32[448,768]{1,0:T(8,128)S(1)} custom-call(s32[8,448]{1,0:T(8,128)S(1)} %get-tuple-element.13.refs_0_.codes, f32[224,768]{1,0:T(8,128)S(1)} %copy-done.11, f32[8,56,768]{2,1,0:T(8,128)S(1)} %copy-done.5, f32[8,56,768]{2,1,0:T(8,128)S(1)} %copy-done.7, f32[8,56,768]{2,1,0:T(8,128)S(1)} %copy-done.9), custom_call_target="tpu_custom_call" | custom-call | flops 1541406720 | bytes 8388608 | tf_op jit(solution)/shard_map/pallas_call | solution.py:408
  152.7 0.0 copy-start.2
  152.7 1.1 copy-done.2
  153.8 4.4 %all-to-all-done.4.refs_6_.refs_7_.refs_8_ = f32[8,56,768]{2,1,0:T(8,128)S(1)} async-done(((f32[8,56,768]{2,1,0:T(8,128)}), f32[8,56,768]{2,1,0:T(8,128)S(1)}, u32[]{:S(2)}, u32[]{:S(2)}) %all-to-all-start.4) | async-done | bytes 1376288 | tf_op jit(solution)/shard_map/all_to_all | solution.py:375
  158.2 1.3 copy-done.3
  159.5 5.0 %shard_map.104 = (f32[448,1024]{1,0:T(8,128)}, f32[448,1024]{1,0:T(8,128)}, f32[448,1024]{1,0:T(8,128)}) custom-call(s32[8,448]{1,0:T(8,128)S(1)} %get-tuple-element.13.refs_0_.codes, f32[448,768]{1,0:T(8,128)S(1)} %shard_map.99.refs_0_.refs_1_.refs_2_, f32[448,768]{1,0:T(8,128)S(1)} %shard_map.99.refs_0_.refs_1_.refs_2_, ...), custom_call_target="tpu_custom_call" | custom-call | flops 1409286144 | bytes 12582912 | tf_op jit(solution)/shard_map/pallas_call | solution.py:433
  (43 shorter events, 0.1 us)
Async XLA Ops:
  0.7 1.2 copy-start
  2.5 1.9 %collective-permute-start = (f32[224,512]{1,0:T(8,128)S(1)}, f32[224,512]{1,0:T(8,128)S(1)}, u32[]{:S(2)}, u32[]{:S(2)}) collective-permute-start(f32[224,512]{1,0:T(8,128)S(1)} %get-tuple-element.14), channel_id=1, source_target_pairs={{0,64},{64,0},{128,192},{192,128},{1,65},{65,1},{129,193},{193,129... | collective-permute-start | bytes 1376264 | tf_op jit(solution)/shard_map/ppermute | solution.py:321
  2.6 6.4 %copy-start.17 = (s32[448,1]{0,1:T(1,128)S(1)}, s32[448,1]{0,1:T(1,128)}, u32[]{:S(2)}) copy-start(s32[448,1]{0,1:T(1,128)} %param.10) | copy-start | bytes 5380
  2.6 6.5 %copy-start.18 = (s32[448]{0:T(512)S(1)}, s32[448]{0:T(512)}, u32[]{:S(2)}) copy-start(s32[448]{0:T(512)} %param.11) | copy-start | bytes 5380
  2.6 4.6 %collective-permute-start.2 = (f32[224,512]{1,0:T(8,128)S(1)}, f32[224,512]{1,0:T(8,128)S(1)}, u32[]{:S(2)}, u32[]{:S(2)}) collective-permute-start(f32[224,512]{1,0:T(8,128)S(1)} %get-tuple-element.15), channel_id=1, source_target_pairs={{0,64},{64,0},{128,192},{192,128},{1,65},{65,1},{129,193},{193,129... | collective-permute-start | bytes 1376264 | tf_op jit(solution)/shard_map/ppermute | solution.py:321
  5.7 12.8 %copy-start.1 = (bf16[1,224,2048]{2,1,0:T(8,128)(2,1)S(1)}, bf16[1,224,2048]{2,1,0:T(8,128)(2,1)}, u32[]{:S(2)}) copy-start(bf16[1,224,2048]{2,1,0:T(8,128)(2,1)} %param.6) | copy-start | bytes 2752516
  5.7 12.8 %copy-start.13 = (f32[224,512]{1,0:T(8,128)S(1)}, f32[224,512]{1,0:T(8,128)}, u32[]{:S(2)}) copy-start(f32[224,512]{1,0:T(8,128)} %refs_4_.3) | copy-start | bytes 1376260
  5.7 8.7 %collective-permute-start.1 = (f32[224,256]{1,0:T(8,128)}, f32[224,256]{1,0:T(8,128)S(1)}, u32[]{:S(2)}, u32[]{:S(2)}) collective-permute-start(f32[224,256]{1,0:T(8,128)} %shard_map.87), channel_id=1, source_target_pairs={{0,128},{128,0},{64,192},{192,64},{1,129},{129,1},{65,193},{193,65... | collective-permute-start | bytes 688136 | tf_op jit(solution)/shard_map/ppermute | solution.py:337
  8.5 9.9 %collective-permute-start.3 = (f32[224,256]{1,0:T(8,128)}, f32[224,256]{1,0:T(8,128)S(1)}, u32[]{:S(2)}, u32[]{:S(2)}) collective-permute-start(f32[224,256]{1,0:T(8,128)} %shard_map.88), channel_id=1, source_target_pairs={{0,128},{128,0},{64,192},{192,64},{1,129},{129,1},{65,193},{193,65... | collective-permute-start | bytes 688136 | tf_op jit(solution)/shard_map/ppermute | solution.py:337
  18.5 1.0 copy-start.15
  19.5 1.0 copy-start.16
  20.5 7.3 %copy-start.14 = (f32[224,512]{1,0:T(8,128)S(1)}, f32[224,512]{1,0:T(8,128)}, u32[]{:S(2)}) copy-start(f32[224,512]{1,0:T(8,128)} %refs_4_.3) | copy-start | bytes 1376260
  21.8 22.4 %collective-permute-start.4 = (f32[224,768]{1,0:T(8,128)S(1)}, f32[224,768]{1,0:T(8,128)}, u32[]{:S(2)}, u32[]{:S(2)}) collective-permute-start(f32[224,768]{1,0:T(8,128)S(1)} %shard_map.89.refs_0_.refs_2_.refs_1_), channel_id=1, source_target_pairs={{0,8},{1,9},{2,10},{3,11},{4,12},{5,13},{6,14},{7,15},{8,16},{9,17... | collective-permute-start | bytes 2064392 | tf_op jit(solution)/shard_map/ppermute | solution.py:380
  23.7 20.4 %collective-permute-start.5 = (f32[224,768]{1,0:T(8,128)S(1)}, f32[224,768]{1,0:T(8,128)}, u32[]{:S(2)}, u32[]{:S(2)}) collective-permute-start(f32[224,768]{1,0:T(8,128)S(1)} %shard_map.89.refs_0_.refs_2_.refs_1_), channel_id=1, source_target_pairs={{8,0},{9,1},{10,2},{11,3},{12,4},{13,5},{14,6},{15,7},{16,8},{17,9... | collective-permute-start | bytes 2064392 | tf_op jit(solution)/shard_map/ppermute | solution.py:380
  29.0 17.1 %copy-start.10 = (f32[224,768]{1,0:T(8,128)}, f32[224,768]{1,0:T(8,128)S(1)}, u32[]{:S(2)}) copy-start(f32[224,768]{1,0:T(8,128)S(1)} %shard_map.90.refs_1_.refs_3_) | copy-start | bytes 2064388
  29.1 29.8 %collective-permute-start.6 = (f32[224,768]{1,0:T(8,128)S(1)}, f32[224,768]{1,0:T(8,128)}, u32[]{:S(2)}, u32[]{:S(2)}) collective-permute-start(f32[224,768]{1,0:T(8,128)S(1)} %shard_map.90.refs_1_.refs_3_), channel_id=1, source_target_pairs={{0,8},{1,9},{2,10},{3,11},{4,12},{5,13},{6,14},{7,15},{8,16},{9,17... | collective-permute-start | bytes 2064392 | tf_op jit(solution)/shard_map/ppermute | solution.py:380
  29.1 29.7 %collective-permute-start.7 = (f32[224,768]{1,0:T(8,128)S(1)}, f32[224,768]{1,0:T(8,128)}, u32[]{:S(2)}, u32[]{:S(2)}) collective-permute-start(f32[224,768]{1,0:T(8,128)S(1)} %shard_map.90.refs_1_.refs_3_), channel_id=1, source_target_pairs={{8,0},{9,1},{10,2},{11,3},{12,4},{13,5},{14,6},{15,7},{16,8},{17,9... | collective-permute-start | bytes 2064392 | tf_op jit(solution)/shard_map/ppermute | solution.py:380
  32.4 13.7 %all-to-all-start = ((s32[8,8,128]{2,1,0:T(8,128)}), s32[8,8,128]{2,1,0:T(8,128)S(1)}, u32[]{:S(2)}, u32[]{:S(2)}) async-start(s32[8,8,128]{2,1,0:T(8,128)} %get-tuple-element.16.refs_8_), calls=%async_computation | async-start | bytes 65536 | tf_op jit(solution)/shard_map/all_to_all | solution.py:312
  49.0 1.1 copy-start.12
  50.0 28.8 %all-to-all-start.1 = ((f32[8,56,768]{2,1,0:T(8,128)}), f32[8,56,768]{2,1,0:T(8,128)S(1)}, u32[]{:S(2)}, u32[]{:S(2)}) async-start(f32[8,56,768]{2,1,0:T(8,128)} %copy-done.12), calls=%async_computation.1 | async-start | bytes 2752512 | tf_op jit(solution)/shard_map/all_to_all | solution.py:375
  55.6 20.0 %collective-permute-start.8 = (f32[224,768]{1,0:T(8,128)}, f32[224,768]{1,0:T(8,128)}, u32[]{:S(2)}, u32[]{:S(2)}) collective-permute-start(f32[224,768]{1,0:T(8,128)} %collective-permute-done.4.refs_2_.refs_4_), channel_id=1, source_target_pairs={{0,8},{1,9},{2,10},{3,11},{4,12},{5,13},{6,14},{7,15},{8,16},{9,17... | collective-permute-start | bytes 2064392 | tf_op jit(solution)/shard_map/ppermute | solution.py:380
  55.6 20.0 %collective-permute-start.9 = (f32[224,768]{1,0:T(8,128)}, f32[224,768]{1,0:T(8,128)S(1)}, u32[]{:S(2)}, u32[]{:S(2)}) collective-permute-start(f32[224,768]{1,0:T(8,128)} %collective-permute-done.5.refs_3_.refs_5_), channel_id=1, source_target_pairs={{8,0},{9,1},{10,2},{11,3},{12,4},{13,5},{14,6},{15,7},{16,8},{17,9... | collective-permute-start | bytes 2064392 | tf_op jit(solution)/shard_map/ppermute | solution.py:380
  58.9 31.4 %collective-permute-start.10 = (f32[224,768]{1,0:T(8,128)}, f32[224,768]{1,0:T(8,128)}, u32[]{:S(2)}, u32[]{:S(2)}) collective-permute-start(f32[224,768]{1,0:T(8,128)} %get-tuple-element.17.refs_0_.refs_2_), channel_id=1, source_target_pairs={{0,8},{1,9},{2,10},{3,11},{4,12},{5,13},{6,14},{7,15},{8,16},{9,17... | collective-permute-start | bytes 2064392 | tf_op jit(solution)/shard_map/ppermute | solution.py:380
  58.9 31.4 %collective-permute-start.11 = (f32[224,768]{1,0:T(8,128)}, f32[224,768]{1,0:T(8,128)}, u32[]{:S(2)}, u32[]{:S(2)}) collective-permute-start(f32[224,768]{1,0:T(8,128)} %get-tuple-element.18.refs_1_.refs_3_), channel_id=1, source_target_pairs={{8,0},{9,1},{10,2},{11,3},{12,4},{13,5},{14,6},{15,7},{16,8},{17,9... | collective-permute-start | bytes 2064392 | tf_op jit(solution)/shard_map/ppermute | solution.py:380
  75.6 29.4 %collective-permute-start.12 = (f32[224,768]{1,0:T(8,128)}, f32[224,768]{1,0:T(8,128)S(1)}, u32[]{:S(2)}, u32[]{:S(2)}) collective-permute-start(f32[224,768]{1,0:T(8,128)} %collective-permute-done.8.refs_2_.refs_4_), channel_id=1, source_target_pairs={{0,8},{1,9},{2,10},{3,11},{4,12},{5,13},{6,14},{7,15},{8,16},{9,17... | collective-permute-start | bytes 2064392 | tf_op jit(solution)/shard_map/ppermute | solution.py:380
  75.6 29.4 %collective-permute-start.13 = (f32[224,768]{1,0:T(8,128)S(1)}, f32[224,768]{1,0:T(8,128)}, u32[]{:S(2)}, u32[]{:S(2)}) collective-permute-start(f32[224,768]{1,0:T(8,128)S(1)} %collective-permute-done.9.refs_3_.refs_5_), channel_id=1, source_target_pairs={{8,0},{9,1},{10,2},{11,3},{12,4},{13,5},{14,6},{15,7},{16,8},{17,9... | collective-permute-start | bytes 2064392 | tf_op jit(solution)/shard_map/ppermute | solution.py:380
  78.8 4.1 %copy-start.4 = (f32[8,56,768]{2,1,0:T(8,128)}, f32[8,56,768]{2,1,0:T(8,128)S(1)}, u32[]{:S(2)}) copy-start(f32[8,56,768]{2,1,0:T(8,128)S(1)} %all-to-all-done.1.refs_6_.refs_2_) | copy-start | bytes 4128772
  82.9 22.0 %all-to-all-start.2 = ((f32[8,56,768]{2,1,0:T(8,128)}), f32[8,56,768]{2,1,0:T(8,128)S(1)}, u32[]{:S(2)}, u32[]{:S(2)}) async-start(f32[8,56,768]{2,1,0:T(8,128)} %shard_map.95), calls=%async_computation.2 | async-start | bytes 2752512 | tf_op jit(solution)/shard_map/all_to_all | solution.py:375
  90.3 29.5 %collective-permute-start.14 = (f32[224,768]{1,0:T(8,128)}, f32[224,768]{1,0:T(8,128)}, u32[]{:S(2)}, u32[]{:S(2)}) collective-permute-start(f32[224,768]{1,0:T(8,128)} %get-tuple-element.19.refs_0_.refs_2_), channel_id=1, source_target_pairs={{0,8},{1,9},{2,10},{3,11},{4,12},{5,13},{6,14},{7,15},{8,16},{9,17... | collective-permute-start | bytes 2064392 | tf_op jit(solution)/shard_map/ppermute | solution.py:380
  93.2 26.6 %collective-permute-start.15 = (f32[224,768]{1,0:T(8,128)}, f32[224,768]{1,0:T(8,128)}, u32[]{:S(2)}, u32[]{:S(2)}) collective-permute-start(f32[224,768]{1,0:T(8,128)} %get-tuple-element.20.refs_1_.refs_3_), channel_id=1, source_target_pairs={{8,0},{9,1},{10,2},{11,3},{12,4},{13,5},{14,6},{15,7},{16,8},{17,9... | collective-permute-start | bytes 2064392 | tf_op jit(solution)/shard_map/ppermute | solution.py:380
  104.9 26.2 %collective-permute-start.16 = (f32[224,768]{1,0:T(8,128)S(1)}, f32[224,768]{1,0:T(8,128)}, u32[]{:S(2)}, u32[]{:S(2)}) collective-permute-start(f32[224,768]{1,0:T(8,128)S(1)} %collective-permute-done.12.refs_2_.refs_4_), channel_id=1, source_target_pairs={{0,8},{1,9},{2,10},{3,11},{4,12},{5,13},{6,14},{7,15},{8,16},{9,17... | collective-permute-start | bytes 2064392 | tf_op jit(solution)/shard_map/ppermute | solution.py:395
  105.0 4.2 %copy-start.6 = (f32[8,56,768]{2,1,0:T(8,128)}, f32[8,56,768]{2,1,0:T(8,128)S(1)}, u32[]{:S(2)}) copy-start(f32[8,56,768]{2,1,0:T(8,128)S(1)} %all-to-all-done.2.refs_6_.refs_3_) | copy-start | bytes 4128772
  109.1 22.1 %all-to-all-start.3 = ((f32[8,56,768]{2,1,0:T(8,128)}), f32[8,56,768]{2,1,0:T(8,128)S(1)}, u32[]{:S(2)}, u32[]{:S(2)}) async-start(f32[8,56,768]{2,1,0:T(8,128)} %shard_map.98), calls=%async_computation.3 | async-start | bytes 2752512 | tf_op jit(solution)/shard_map/all_to_all | solution.py:375
  119.8 11.4 %collective-permute-start.17 = (f32[224,768]{1,0:T(8,128)}, f32[224,768]{1,0:T(8,128)S(1)}, u32[]{:S(2)}, u32[]{:S(2)}) collective-permute-start(f32[224,768]{1,0:T(8,128)} %get-tuple-element.22.refs_1_.refs_3_), channel_id=1, source_target_pairs={{8,0},{9,1},{10,2},{11,3},{12,4},{13,5},{14,6},{15,7},{16,8},{17,9... | collective-permute-start | bytes 2064392 | tf_op jit(solution)/shard_map/ppermute | solution.py:396
  131.2 4.2 %copy-start.8 = (f32[8,56,768]{2,1,0:T(8,128)}, f32[8,56,768]{2,1,0:T(8,128)S(1)}, u32[]{:S(2)}) copy-start(f32[8,56,768]{2,1,0:T(8,128)S(1)} %all-to-all-done.3.refs_4_.refs_6_) | copy-start | bytes 4128772
  135.4 22.8 %all-to-all-start.4 = ((f32[8,56,768]{2,1,0:T(8,128)}), f32[8,56,768]{2,1,0:T(8,128)S(1)}, u32[]{:S(2)}, u32[]{:S(2)}) async-start(f32[8,56,768]{2,1,0:T(8,128)} %shard_map.103), calls=%async_computation.4 | async-start | bytes 2752512 | tf_op jit(solution)/shard_map/all_to_all | solution.py:375
  143.1 1.3 copy-start.5
  144.5 1.3 copy-start.7
  145.8 1.3 copy-start.9
  147.2 2.9 %copy-start.11 = (f32[224,768]{1,0:T(8,128)S(1)}, f32[224,768]{1,0:T(8,128)}, u32[]{:S(2)}) copy-start(f32[224,768]{1,0:T(8,128)} %copy-done.10) | copy-start | bytes 2064388
  152.7 1.1 copy-start.2
  158.2 1.3 copy-start.3

commit v10 on v9

--- a/solution.py
+++ b/solution.py
@@ -337,7 +337,7 @@
     got_y = [lax.ppermute(p, "dp", NEXT_Y) for p in passed]
     state = []
     for half in range(2):
-        after = (got_y[1], wanted) if half == 0 else ()
+        after = (passed[1], wanted) if half == 0 else (token((state[0],), 10),)
         state.append(
             call(
                 lambda *refs, half=half: update_kernel(half, *refs),

time: 166 us -> 162 us (0.976)
  waiting for transfers between devices: 57.3 us -> 53.5 us
    ppermute x2, waiting for transfers between devices: 7.52 us -> 3.99 us  [on_device(): got_y = [lax.ppermute(p, 'dp', NEXT_Y) for p in passed]]
    unnamed x39 -> x45, local copies, waits for them, and re-layouts: 10.9 us -> 10.7 us
  transfers between devices with their start and end apart: 23 -> 23, of which waited for: 11 -> 11; matrix products, arithmetic and copies ran while one was open for 0% -> 0% of each run, Pallas kernels for 13% -> 14%
where the time goes in v10:
time: 162 us; the launch traced here: 160 us
  starting transfers between devices  61.6 us (38%)
  waiting for transfers between devices  53.5 us (33%)
  Pallas kernels  33.1 us (20%)
  local copies, waits for them, and re-layouts  10.8 us (7%)
    ppermute x6, waiting for transfers between devices, around(): lax.ppermute(pair[0], 'shard', UP)  32.7 us
    all_to_all x4, starting transfers between devices, to_plane(): lax.all_to_all(rows, 'shard', split_axis=0, concat_axis=0, axis_index_gro...  27.2 us
    ppermute x6, starting transfers between devices, around(): lax.ppermute(pair[1], 'shard', DOWN)  17.3 us
    pallas_call x4, Pallas kernels, pick(): call(lambda *refs: pick_kernel(planes, *refs), shape(PLANE, SENT, WIDE),...  15.3 us
    unnamed x45, local copies, waits for them, and re-layouts  10.7 us
    ppermute x1, waiting for transfers between devices, on_device(): lax.ppermute(three[0][0], 'shard', UP)  8.56 us
    all_to_all x1, starting transfers between devices, on_device(): lax.all_to_all(wanted, 'shard', split_axis=0, concat_axis=0, axis_index_g...  7.46 us
    pallas_call x2, Pallas kernels, on_device(): call(lambda *refs, parts=parts: gather_kernel(parts, *refs), shape(FINE,...  5.49 us
  transfers between devices with their start and end apart: 23, of which 11 were waited for; matrix products, arithmetic and copies ran while one was open for 0% of the time, Pallas kernels for 14%

profile of v10, /device:TPU:2, one launch (start us, length us, event | category | flops | bytes accessed | tf_op | source)
XLA Modules:
  0.0 160.0 jit_solution(13933849615774883857)
XLA Ops:
  0.6 0.1 pad_add_fusion.place.refs_0_
  0.7 1.2 copy-done
  1.9 1.4 shard_map.86
  3.3 0.5 collective-permute-start.2
  3.8 1.9 %collective-permute-done.refs_2_ = f32[224,512]{1,0:T(8,128)S(1)} collective-permute-done((f32[224,512]{1,0:T(8,128)S(1)}, f32[224,512]{1,0:T(8,128)S(1)}, u32[]{:S(2)}, u32[]{:S(2)}) %collective-permute-start) | collective-permute-done | bytes 458784 | tf_op jit(solution)/shard_map/ppermute | solution.py:321
  5.7 1.3 shard_map.87
  7.0 0.8 copy-done.18
  7.7 1.6 collective-permute-start.1
  9.3 0.1 copy.16.dev
  9.5 0.1 copy.17.col
  9.6 0.0 copy-start.19
  9.6 1.7 %shard_map.85 = (s32[8,8,128]{2,1,0:T(8,128)}, s32[8,448]{1,0:T(8,128)S(1)}) custom-call(s32[2]{0:T(128)S(1)} %pad_add_fusion.place.refs_0_, s32[448,1]{1,0:T(8,128)S(1)} %copy.16.dev, s32[1,448]{1,0:T(1,128)S(1)} %bitcast.10, s32[448,1]{1,0:T(8,128)S(1)} %copy.17.col), custom_call_target="tpu_custom_call" | custom-call | bytes 1048576 | tf_op jit(solution)/shard_map/pallas_call | solution.py:301
  11.3 0.6 shard_map.88.refs_7_
  11.9 0.5 collective-permute-start.3
  12.4 4.0 %collective-permute-done.1.refs_3_ = f32[224,256]{1,0:T(8,128)S(1)} collective-permute-done((f32[224,256]{1,0:T(8,128)}, f32[224,256]{1,0:T(8,128)S(1)}, u32[]{:S(2)}, u32[]{:S(2)}) %collective-permute-start.1) | collective-permute-done | bytes 229408 | tf_op jit(solution)/shard_map/ppermute | solution.py:337
  16.4 0.0 copy-start.16
  16.4 1.0 copy-done.16
  17.4 1.3 shard_map.89.refs_0_.refs_2_.refs_1_
  18.7 0.0 copy-start.15
  18.7 0.0 copy-start.17
  18.7 2.0 %collective-permute-start.4 = (f32[224,768]{1,0:T(8,128)S(1)}, f32[224,768]{1,0:T(8,128)}, u32[]{:S(2)}, u32[]{:S(2)}) collective-permute-start(f32[224,768]{1,0:T(8,128)S(1)} %shard_map.89.refs_0_.refs_2_.refs_1_), channel_id=1, source_target_pairs={{0,8},{1,9},{2,10},{3,11},{4,12},{5,13},{6,14},{7,15},{8,16},{9,17... | collective-permute-start | bytes 2064392 | tf_op jit(solution)/shard_map/ppermute | solution.py:380
  20.7 4.0 %collective-permute-start.5 = (f32[224,768]{1,0:T(8,128)S(1)}, f32[224,768]{1,0:T(8,128)}, u32[]{:S(2)}, u32[]{:S(2)}) collective-permute-start(f32[224,768]{1,0:T(8,128)S(1)} %shard_map.89.refs_0_.refs_2_.refs_1_), channel_id=1, source_target_pairs={{8,0},{9,1},{10,2},{11,3},{12,4},{13,5},{14,6},{15,7},{16,8},{17,9... | collective-permute-start | bytes 2064392 | tf_op jit(solution)/shard_map/ppermute | solution.py:380
  24.7 0.0 collective-permute-done.3.refs_3_
  24.7 1.3 shard_map.91.refs_1_.refs_3_
  26.0 0.1 collective-permute-start.6
  26.1 3.2 %collective-permute-start.7 = (f32[224,768]{1,0:T(8,128)S(1)}, f32[224,768]{1,0:T(8,128)}, u32[]{:S(2)}, u32[]{:S(2)}) collective-permute-start(f32[224,768]{1,0:T(8,128)S(1)} %shard_map.91.refs_1_.refs_3_), channel_id=1, source_target_pairs={{8,0},{9,1},{10,2},{11,3},{12,4},{13,5},{14,6},{15,7},{16,8},{17,9... | collective-permute-start | bytes 2064392 | tf_op jit(solution)/shard_map/ppermute | solution.py:380
  29.3 7.5 %all-to-all-start = ((s32[8,8,128]{2,1,0:T(8,128)}), s32[8,8,128]{2,1,0:T(8,128)S(1)}, u32[]{:S(2)}, u32[]{:S(2)}) async-start(s32[8,8,128]{2,1,0:T(8,128)} %get-tuple-element.16.refs_8_), calls=%async_computation | async-start | bytes 65536 | tf_op jit(solution)/shard_map/all_to_all | solution.py:312
  36.8 4.3 %collective-permute-done.4.refs_2_.refs_4_ = f32[224,768]{1,0:T(8,128)} collective-permute-done((f32[224,768]{1,0:T(8,128)S(1)}, f32[224,768]{1,0:T(8,128)}, u32[]{:S(2)}, u32[]{:S(2)}) %collective-permute-start.4) | collective-permute-done | bytes 688160 | tf_op jit(solution)/shard_map/ppermute | solution.py:380
  41.1 0.0 collective-permute-done.5.refs_3_.refs_5_
  41.1 2.0 %all-to-all-done.refs_1_ = s32[8,8,128]{2,1,0:T(8,128)S(1)} async-done(((s32[8,8,128]{2,1,0:T(8,128)}), s32[8,8,128]{2,1,0:T(8,128)S(1)}, u32[]{:S(2)}, u32[]{:S(2)}) %all-to-all-start) | async-done | bytes 32800 | tf_op jit(solution)/shard_map/all_to_all | solution.py:312
  43.1 2.9 %shard_map.93 = f32[8,56,768]{2,1,0:T(8,128)S(1)} custom-call(s32[2]{0:T(128)S(1)} %pad_add_fusion.place.refs_0_, s32[8,8,128]{2,1,0:T(8,128)S(1)} %all-to-all-done.refs_1_, f32[224,768]{1,0:T(8,128)S(1)} %shard_map.89.refs_0_.refs_2_.refs_1_, f32[224,768]{1,0:T(8,128)S(1)} %shard_map.91.refs_1_.refs_3_, f32[224,768]{1,0:T(8,128)} %collective-permute-done.4.refs_2_.refs_4_, ...), custom_call_target="tpu_custom_call" | custom-call | flops 352321536 | bytes 5242880 | tf_op jit(solution)/shard_map/pallas_call | solution.py:360
  45.9 0.0 copy-start.12
  45.9 1.1 copy-done.12
  47.0 5.5 %all-to-all-start.1 = ((f32[8,56,768]{2,1,0:T(8,128)}), f32[8,56,768]{2,1,0:T(8,128)S(1)}, u32[]{:S(2)}, u32[]{:S(2)}) async-start(f32[8,56,768]{2,1,0:T(8,128)} %copy-done.12), calls=%async_computation.1 | async-start | bytes 2752512 | tf_op jit(solution)/shard_map/all_to_all | solution.py:375
  52.5 0.0 collective-permute-start.8
  52.5 3.3 %collective-permute-start.9 = (f32[224,768]{1,0:T(8,128)}, f32[224,768]{1,0:T(8,128)S(1)}, u32[]{:S(2)}, u32[]{:S(2)}) collective-permute-start(f32[224,768]{1,0:T(8,128)} %collective-permute-done.5.refs_3_.refs_5_), channel_id=1, source_target_pairs={{8,0},{9,1},{10,2},{11,3},{12,4},{13,5},{14,6},{15,7},{16,8},{17,9... | collective-permute-start | bytes 2064392 | tf_op jit(solution)/shard_map/ppermute | solution.py:380
  55.9 3.2 %collective-permute-start.11 = (f32[224,768]{1,0:T(8,128)}, f32[224,768]{1,0:T(8,128)}, u32[]{:S(2)}, u32[]{:S(2)}) collective-permute-start(f32[224,768]{1,0:T(8,128)} %get-tuple-element.18.refs_1_.refs_3_), channel_id=1, source_target_pairs={{8,0},{9,1},{10,2},{11,3},{12,4},{13,5},{14,6},{15,7},{16,8},{17,9... | collective-permute-start | bytes 2064392 | tf_op jit(solution)/shard_map/ppermute | solution.py:380
  59.1 13.4 %collective-permute-done.8.refs_2_.refs_4_ = f32[224,768]{1,0:T(8,128)} collective-permute-done((f32[224,768]{1,0:T(8,128)}, f32[224,768]{1,0:T(8,128)}, u32[]{:S(2)}, u32[]{:S(2)}) %collective-permute-start.8) | collective-permute-done | bytes 688160 | tf_op jit(solution)/shard_map/ppermute | solution.py:380
  72.5 3.2 %collective-permute-start.13 = (f32[224,768]{1,0:T(8,128)S(1)}, f32[224,768]{1,0:T(8,128)}, u32[]{:S(2)}, u32[]{:S(2)}) collective-permute-start(f32[224,768]{1,0:T(8,128)S(1)} %collective-permute-done.9.refs_3_.refs_5_), channel_id=1, source_target_pairs={{8,0},{9,1},{10,2},{11,3},{12,4},{13,5},{14,6},{15,7},{16,8},{17,9... | collective-permute-start | bytes 2064392 | tf_op jit(solution)/shard_map/ppermute | solution.py:380
  75.8 4.1 %shard_map.96 = f32[8,56,768]{2,1,0:T(8,128)} custom-call(s32[2]{0:T(128)S(1)} %pad_add_fusion.place.refs_0_, s32[8,8,128]{2,1,0:T(8,128)S(1)} %all-to-all-done.refs_1_, f32[224,768]{1,0:T(8,128)} %get-tuple-element.17.refs_0_.refs_2_, f32[224,768]{1,0:T(8,128)} %get-tuple-element.18.refs_1_.refs_3_, f32[224,768]{1,0:T(8,128)} %collective-permute-done.8.refs_2_.refs_4_, ...), custom_call_target="tpu_custom_call" | custom-call | flops 352321536 | bytes 5242880 | tf_op jit(solution)/shard_map/pallas_call | solution.py:360
  79.9 7.2 %all-to-all-start.2 = ((f32[8,56,768]{2,1,0:T(8,128)}), f32[8,56,768]{2,1,0:T(8,128)S(1)}, u32[]{:S(2)}, u32[]{:S(2)}) async-start(f32[8,56,768]{2,1,0:T(8,128)} %shard_map.96), calls=%async_computation.2 | async-start | bytes 2752512 | tf_op jit(solution)/shard_map/all_to_all | solution.py:375
  87.1 0.1 collective-permute-done.10.refs_0_
  87.3 2.9 %collective-permute-start.14 = (f32[224,768]{1,0:T(8,128)}, f32[224,768]{1,0:T(8,128)}, u32[]{:S(2)}, u32[]{:S(2)}) collective-permute-start(f32[224,768]{1,0:T(8,128)} %get-tuple-element.19.refs_0_.refs_2_), channel_id=1, source_target_pairs={{0,8},{1,9},{2,10},{3,11},{4,12},{5,13},{6,14},{7,15},{8,16},{9,17... | collective-permute-start | bytes 2064392 | tf_op jit(solution)/shard_map/ppermute | solution.py:380
  90.2 0.3 collective-permute-start.15
  90.5 11.4 %collective-permute-done.12.refs_2_.refs_4_ = f32[224,768]{1,0:T(8,128)S(1)} collective-permute-done((f32[224,768]{1,0:T(8,128)}, f32[224,768]{1,0:T(8,128)S(1)}, u32[]{:S(2)}, u32[]{:S(2)}) %collective-permute-start.12) | collective-permute-done | bytes 688160 | tf_op jit(solution)/shard_map/ppermute | solution.py:380
  101.9 0.0 copy-start.6
  101.9 4.1 %shard_map.99 = f32[8,56,768]{2,1,0:T(8,128)} custom-call(s32[2]{0:T(128)S(1)} %pad_add_fusion.place.refs_0_, s32[8,8,128]{2,1,0:T(8,128)S(1)} %all-to-all-done.refs_1_, f32[224,768]{1,0:T(8,128)} %get-tuple-element.19.refs_0_.refs_2_, f32[224,768]{1,0:T(8,128)} %get-tuple-element.20.refs_1_.refs_3_, f32[224,768]{1,0:T(8,128)S(1)} %collective-permute-done.12.refs_2_.refs_4_, ...), custom_call_target="tpu_custom_call" | custom-call | flops 352321536 | bytes 5242880 | tf_op jit(solution)/shard_map/pallas_call | solution.py:360
  106.1 7.2 %all-to-all-start.3 = ((f32[8,56,768]{2,1,0:T(8,128)}), f32[8,56,768]{2,1,0:T(8,128)S(1)}, u32[]{:S(2)}, u32[]{:S(2)}) async-start(f32[8,56,768]{2,1,0:T(8,128)} %shard_map.99), calls=%async_computation.3 | async-start | bytes 2752512 | tf_op jit(solution)/shard_map/all_to_all | solution.py:375
  113.3 3.5 %collective-permute-done.14.refs_0_ = f32[224,768]{1,0:T(8,128)} collective-permute-done((f32[224,768]{1,0:T(8,128)}, f32[224,768]{1,0:T(8,128)}, u32[]{:S(2)}, u32[]{:S(2)}) %collective-permute-start.14) | collective-permute-done | bytes 688160 | tf_op jit(solution)/shard_map/ppermute | solution.py:380
  116.7 2.0 %collective-permute-start.17 = (f32[224,768]{1,0:T(8,128)}, f32[224,768]{1,0:T(8,128)S(1)}, u32[]{:S(2)}, u32[]{:S(2)}) collective-permute-start(f32[224,768]{1,0:T(8,128)} %get-tuple-element.22.refs_1_.refs_3_), channel_id=1, source_target_pairs={{8,0},{9,1},{10,2},{11,3},{12,4},{13,5},{14,6},{15,7},{16,8},{17,9... | collective-permute-start | bytes 2064392 | tf_op jit(solution)/shard_map/ppermute | solution.py:396
  118.8 8.6 %collective-permute-done.16.refs_2_.refs_4_ = f32[224,768]{1,0:T(8,128)} collective-permute-done((f32[224,768]{1,0:T(8,128)S(1)}, f32[224,768]{1,0:T(8,128)}, u32[]{:S(2)}, u32[]{:S(2)}) %collective-permute-start.16) | collective-permute-done | bytes 688160 | tf_op jit(solution)/shard_map/ppermute | solution.py:395
  127.3 0.6 collective-permute-done.17.refs_3_.refs_5_
  127.9 4.2 %shard_map.104 = f32[8,56,768]{2,1,0:T(8,128)} custom-call(s32[2]{0:T(128)S(1)} %pad_add_fusion.place.refs_0_, s32[8,8,128]{2,1,0:T(8,128)S(1)} %all-to-all-done.refs_1_, f32[224,768]{1,0:T(8,128)} %get-tuple-element.21.refs_0_.refs_2_, f32[224,768]{1,0:T(8,128)} %get-tuple-element.22.refs_1_.refs_3_, f32[224,768]{1,0:T(8,128)} %collective-permute-done.16.refs_2_.refs_4_, ...), custom_call_target="tpu_custom_call" | custom-call | flops 352321536 | bytes 5242880 | tf_op jit(solution)/shard_map/pallas_call | solution.py:360
  132.1 7.2 %all-to-all-start.4 = ((f32[8,56,768]{2,1,0:T(8,128)}), f32[8,56,768]{2,1,0:T(8,128)S(1)}, u32[]{:S(2)}, u32[]{:S(2)}) async-start(f32[8,56,768]{2,1,0:T(8,128)} %shard_map.104), calls=%async_computation.4 | async-start | bytes 2752512 | tf_op jit(solution)/shard_map/all_to_all | solution.py:375
  139.3 1.3 copy-done.5
  140.6 1.3 copy-done.7
  142.0 1.3 copy-done.9
  143.3 2.9 %shard_map.100.refs_0_.refs_1_.refs_2_ = f32[448,768]{1,0:T(8,128)S(1)} custom-call(s32[8,448]{1,0:T(8,128)S(1)} %get-tuple-element.13.refs_0_.codes, f32[224,768]{1,0:T(8,128)S(1)} %shard_map.89.refs_0_.refs_2_.refs_1_, f32[8,56,768]{2,1,0:T(8,128)S(1)} %copy-done.5, f32[8,56,768]{2,1,0:T(8,128)S(1)} %copy-done.7, f32[8,56,768]{2,1,0:T(8,128)S(1)} %copy-done.9), custom_call_target="tpu_custom_call" | custom-call | flops 1541406720 | bytes 8388608 | tf_op jit(solution)/shard_map/pallas_call | solution.py:408
  146.3 2.6 %shard_map.101.refs_3_.refs_4_.refs_5_ = f32[448,768]{1,0:T(8,128)S(1)} custom-call(s32[8,448]{1,0:T(8,128)S(1)} %get-tuple-element.13.refs_0_.codes, f32[224,768]{1,0:T(8,128)S(1)} %copy-done.11, f32[8,56,768]{2,1,0:T(8,128)S(1)} %copy-done.5, f32[8,56,768]{2,1,0:T(8,128)S(1)} %copy-done.7, f32[8,56,768]{2,1,0:T(8,128)S(1)} %copy-done.9), custom_call_target="tpu_custom_call" | custom-call | flops 1541406720 | bytes 8388608 | tf_op jit(solution)/shard_map/pallas_call | solution.py:408
  148.8 0.0 copy-start.2
  148.9 1.1 copy-done.2
  149.9 3.7 %all-to-all-done.4.refs_6_.refs_7_.refs_8_ = f32[8,56,768]{2,1,0:T(8,128)S(1)} async-done(((f32[8,56,768]{2,1,0:T(8,128)}), f32[8,56,768]{2,1,0:T(8,128)S(1)}, u32[]{:S(2)}, u32[]{:S(2)}) %all-to-all-start.4) | async-done | bytes 1376288 | tf_op jit(solution)/shard_map/all_to_all | solution.py:375
  153.7 1.3 copy-done.3
  155.0 5.0 %shard_map.105 = (f32[448,1024]{1,0:T(8,128)}, f32[448,1024]{1,0:T(8,128)}, f32[448,1024]{1,0:T(8,128)}) custom-call(s32[8,448]{1,0:T(8,128)S(1)} %get-tuple-element.13.refs_0_.codes, f32[448,768]{1,0:T(8,128)S(1)} %shard_map.100.refs_0_.refs_1_.refs_2_, f32[448,768]{1,0:T(8,128)S(1)} %shard_map.100.refs_0_.refs_1_.refs_2_, ...), custom_call_target="tpu_custom_call" | custom-call | flops 1409286144 | bytes 12582912 | tf_op jit(solution)/shard_map/pallas_call | solution.py:433
  (50 shorter events, 0.1 us)
Async XLA Ops:
  0.6 8.7 %copy-start.20 = (s32[448,1]{0,1:T(1,128)S(1)}, s32[448,1]{0,1:T(1,128)}, u32[]{:S(2)}) copy-start(s32[448,1]{0,1:T(1,128)} %param.10) | copy-start | bytes 5380
  0.7 1.2 copy-start
  1.9 7.6 %copy-start.21 = (s32[448]{0:T(512)S(1)}, s32[448]{0:T(512)}, u32[]{:S(2)}) copy-start(s32[448]{0:T(512)} %param.11) | copy-start | bytes 5380
  3.3 8.0 %copy-start.1 = (bf16[1,224,2048]{2,1,0:T(8,128)(2,1)S(1)}, bf16[1,224,2048]{2,1,0:T(8,128)(2,1)}, u32[]{:S(2)}) copy-start(bf16[1,224,2048]{2,1,0:T(8,128)(2,1)} %param.6) | copy-start | bytes 2752516
  3.3 2.4 %collective-permute-start = (f32[224,512]{1,0:T(8,128)S(1)}, f32[224,512]{1,0:T(8,128)S(1)}, u32[]{:S(2)}, u32[]{:S(2)}) collective-permute-start(f32[224,512]{1,0:T(8,128)S(1)} %get-tuple-element.14), channel_id=1, source_target_pairs={{0,64},{64,0},{128,192},{192,128},{1,65},{65,1},{129,193},{193,129... | collective-permute-start | bytes 1376264 | tf_op jit(solution)/shard_map/ppermute | solution.py:321
  3.3 8.0 %collective-permute-start.2 = (f32[224,512]{1,0:T(8,128)}, f32[224,512]{1,0:T(8,128)S(1)}, u32[]{:S(2)}, u32[]{:S(2)}) collective-permute-start(f32[224,512]{1,0:T(8,128)} %get-tuple-element.15), channel_id=1, source_target_pairs={{0,64},{64,0},{128,192},{192,128},{1,65},{65,1},{129,193},{193,129... | collective-permute-start | bytes 1376264 | tf_op jit(solution)/shard_map/ppermute | solution.py:321
  7.0 0.8 copy-start.18
  7.7 8.7 %copy-start.13 = (f32[224,512]{1,0:T(8,128)S(1)}, f32[224,512]{1,0:T(8,128)}, u32[]{:S(2)}) copy-start(f32[224,512]{1,0:T(8,128)} %refs_4_.3) | copy-start | bytes 1376260
  7.7 8.7 %copy-start.14 = (f32[224,512]{1,0:T(8,128)S(1)}, f32[224,512]{1,0:T(8,128)}, u32[]{:S(2)}) copy-start(f32[224,512]{1,0:T(8,128)} %refs_5_.3) | copy-start | bytes 1376260
  7.7 8.7 %collective-permute-start.1 = (f32[224,256]{1,0:T(8,128)}, f32[224,256]{1,0:T(8,128)S(1)}, u32[]{:S(2)}, u32[]{:S(2)}) collective-permute-start(f32[224,256]{1,0:T(8,128)} %shard_map.87), channel_id=1, source_target_pairs={{0,128},{128,0},{64,192},{192,64},{1,129},{129,1},{65,193},{193,65... | collective-permute-start | bytes 688136 | tf_op jit(solution)/shard_map/ppermute | solution.py:337
  9.6 6.8 %copy-start.19 = (f32[224,512]{1,0:T(8,128)S(1)}, f32[224,512]{1,0:T(8,128)}, u32[]{:S(2)}) copy-start(f32[224,512]{1,0:T(8,128)} %copy-done.18) | copy-start | bytes 1376260
  11.9 12.9 %collective-permute-start.3 = (f32[224,256]{1,0:T(8,128)S(1)}, f32[224,256]{1,0:T(8,128)S(1)}, u32[]{:S(2)}, u32[]{:S(2)}) collective-permute-start(f32[224,256]{1,0:T(8,128)S(1)} %shard_map.88.refs_7_), channel_id=1, source_target_pairs={{0,128},{128,0},{64,192},{192,64},{1,129},{129,1},{65,193},{193,65... | collective-permute-start | bytes 688136 | tf_op jit(solution)/shard_map/ppermute | solution.py:337
  16.4 1.0 copy-start.16
  18.7 6.1 %copy-start.15 = (f32[224,512]{1,0:T(8,128)S(1)}, f32[224,512]{1,0:T(8,128)}, u32[]{:S(2)}) copy-start(f32[224,512]{1,0:T(8,128)} %refs_5_.3) | copy-start | bytes 1376260
  18.7 6.0 %copy-start.17 = (f32[224,512]{1,0:T(8,128)S(1)}, f32[224,512]{1,0:T(8,128)}, u32[]{:S(2)}) copy-start(f32[224,512]{1,0:T(8,128)} %refs_6_.3) | copy-start | bytes 1376260
  18.7 22.4 %collective-permute-start.4 = (f32[224,768]{1,0:T(8,128)S(1)}, f32[224,768]{1,0:T(8,128)}, u32[]{:S(2)}, u32[]{:S(2)}) collective-permute-start(f32[224,768]{1,0:T(8,128)S(1)} %shard_map.89.refs_0_.refs_2_.refs_1_), channel_id=1, source_target_pairs={{0,8},{1,9},{2,10},{3,11},{4,12},{5,13},{6,14},{7,15},{8,16},{9,17... | collective-permute-start | bytes 2064392 | tf_op jit(solution)/shard_map/ppermute | solution.py:380
  20.7 20.4 %collective-permute-start.5 = (f32[224,768]{1,0:T(8,128)S(1)}, f32[224,768]{1,0:T(8,128)}, u32[]{:S(2)}, u32[]{:S(2)}) collective-permute-start(f32[224,768]{1,0:T(8,128)S(1)} %shard_map.89.refs_0_.refs_2_.refs_1_), channel_id=1, source_target_pairs={{8,0},{9,1},{10,2},{11,3},{12,4},{13,5},{14,6},{15,7},{16,8},{17,9... | collective-permute-start | bytes 2064392 | tf_op jit(solution)/shard_map/ppermute | solution.py:380
  26.0 17.1 %copy-start.10 = (f32[224,768]{1,0:T(8,128)}, f32[224,768]{1,0:T(8,128)S(1)}, u32[]{:S(2)}) copy-start(f32[224,768]{1,0:T(8,128)S(1)} %shard_map.91.refs_1_.refs_3_) | copy-start | bytes 2064388
  26.0 29.8 %collective-permute-start.6 = (f32[224,768]{1,0:T(8,128)S(1)}, f32[224,768]{1,0:T(8,128)}, u32[]{:S(2)}, u32[]{:S(2)}) collective-permute-start(f32[224,768]{1,0:T(8,128)S(1)} %shard_map.91.refs_1_.refs_3_), channel_id=1, source_target_pairs={{0,8},{1,9},{2,10},{3,11},{4,12},{5,13},{6,14},{7,15},{8,16},{9,17... | collective-permute-start | bytes 2064392 | tf_op jit(solution)/shard_map/ppermute | solution.py:380
  26.1 29.7 %collective-permute-start.7 = (f32[224,768]{1,0:T(8,128)S(1)}, f32[224,768]{1,0:T(8,128)}, u32[]{:S(2)}, u32[]{:S(2)}) collective-permute-start(f32[224,768]{1,0:T(8,128)S(1)} %shard_map.91.refs_1_.refs_3_), channel_id=1, source_target_pairs={{8,0},{9,1},{10,2},{11,3},{12,4},{13,5},{14,6},{15,7},{16,8},{17,9... | collective-permute-start | bytes 2064392 | tf_op jit(solution)/shard_map/ppermute | solution.py:380
  29.3 13.7 %all-to-all-start = ((s32[8,8,128]{2,1,0:T(8,128)}), s32[8,8,128]{2,1,0:T(8,128)S(1)}, u32[]{:S(2)}, u32[]{:S(2)}) async-start(s32[8,8,128]{2,1,0:T(8,128)} %get-tuple-element.16.refs_8_), calls=%async_computation | async-start | bytes 65536 | tf_op jit(solution)/shard_map/all_to_all | solution.py:312
  45.9 1.1 copy-start.12
  47.0 28.7 %all-to-all-start.1 = ((f32[8,56,768]{2,1,0:T(8,128)}), f32[8,56,768]{2,1,0:T(8,128)S(1)}, u32[]{:S(2)}, u32[]{:S(2)}) async-start(f32[8,56,768]{2,1,0:T(8,128)} %copy-done.12), calls=%async_computation.1 | async-start | bytes 2752512 | tf_op jit(solution)/shard_map/all_to_all | solution.py:375
  52.5 20.0 %collective-permute-start.8 = (f32[224,768]{1,0:T(8,128)}, f32[224,768]{1,0:T(8,128)}, u32[]{:S(2)}, u32[]{:S(2)}) collective-permute-start(f32[224,768]{1,0:T(8,128)} %collective-permute-done.4.refs_2_.refs_4_), channel_id=1, source_target_pairs={{0,8},{1,9},{2,10},{3,11},{4,12},{5,13},{6,14},{7,15},{8,16},{9,17... | collective-permute-start | bytes 2064392 | tf_op jit(solution)/shard_map/ppermute | solution.py:380
  52.5 20.0 %collective-permute-start.9 = (f32[224,768]{1,0:T(8,128)}, f32[224,768]{1,0:T(8,128)S(1)}, u32[]{:S(2)}, u32[]{:S(2)}) collective-permute-start(f32[224,768]{1,0:T(8,128)} %collective-permute-done.5.refs_3_.refs_5_), channel_id=1, source_target_pairs={{8,0},{9,1},{10,2},{11,3},{12,4},{13,5},{14,6},{15,7},{16,8},{17,9... | collective-permute-start | bytes 2064392 | tf_op jit(solution)/shard_map/ppermute | solution.py:380
  55.8 31.4 %collective-permute-start.10 = (f32[224,768]{1,0:T(8,128)}, f32[224,768]{1,0:T(8,128)}, u32[]{:S(2)}, u32[]{:S(2)}) collective-permute-start(f32[224,768]{1,0:T(8,128)} %get-tuple-element.17.refs_0_.refs_2_), channel_id=1, source_target_pairs={{0,8},{1,9},{2,10},{3,11},{4,12},{5,13},{6,14},{7,15},{8,16},{9,17... | collective-permute-start | bytes 2064392 | tf_op jit(solution)/shard_map/ppermute | solution.py:380
  55.9 31.4 %collective-permute-start.11 = (f32[224,768]{1,0:T(8,128)}, f32[224,768]{1,0:T(8,128)}, u32[]{:S(2)}, u32[]{:S(2)}) collective-permute-start(f32[224,768]{1,0:T(8,128)} %get-tuple-element.18.refs_1_.refs_3_), channel_id=1, source_target_pairs={{8,0},{9,1},{10,2},{11,3},{12,4},{13,5},{14,6},{15,7},{16,8},{17,9... | collective-permute-start | bytes 2064392 | tf_op jit(solution)/shard_map/ppermute | solution.py:380
  72.5 29.4 %collective-permute-start.12 = (f32[224,768]{1,0:T(8,128)}, f32[224,768]{1,0:T(8,128)S(1)}, u32[]{:S(2)}, u32[]{:S(2)}) collective-permute-start(f32[224,768]{1,0:T(8,128)} %collective-permute-done.8.refs_2_.refs_4_), channel_id=1, source_target_pairs={{0,8},{1,9},{2,10},{3,11},{4,12},{5,13},{6,14},{7,15},{8,16},{9,17... | collective-permute-start | bytes 2064392 | tf_op jit(solution)/shard_map/ppermute | solution.py:380
  72.5 29.4 %collective-permute-start.13 = (f32[224,768]{1,0:T(8,128)S(1)}, f32[224,768]{1,0:T(8,128)}, u32[]{:S(2)}, u32[]{:S(2)}) collective-permute-start(f32[224,768]{1,0:T(8,128)S(1)} %collective-permute-done.9.refs_3_.refs_5_), channel_id=1, source_target_pairs={{8,0},{9,1},{10,2},{11,3},{12,4},{13,5},{14,6},{15,7},{16,8},{17,9... | collective-permute-start | bytes 2064392 | tf_op jit(solution)/shard_map/ppermute | solution.py:380
  75.7 4.1 %copy-start.4 = (f32[8,56,768]{2,1,0:T(8,128)}, f32[8,56,768]{2,1,0:T(8,128)S(1)}, u32[]{:S(2)}) copy-start(f32[8,56,768]{2,1,0:T(8,128)S(1)} %all-to-all-done.1.refs_6_.refs_2_) | copy-start | bytes 4128772
  79.9 22.0 %all-to-all-start.2 = ((f32[8,56,768]{2,1,0:T(8,128)}), f32[8,56,768]{2,1,0:T(8,128)S(1)}, u32[]{:S(2)}, u32[]{:S(2)}) async-start(f32[8,56,768]{2,1,0:T(8,128)} %shard_map.96), calls=%async_computation.2 | async-start | bytes 2752512 | tf_op jit(solution)/shard_map/all_to_all | solution.py:375
  87.3 29.5 %collective-permute-start.14 = (f32[224,768]{1,0:T(8,128)}, f32[224,768]{1,0:T(8,128)}, u32[]{:S(2)}, u32[]{:S(2)}) collective-permute-start(f32[224,768]{1,0:T(8,128)} %get-tuple-element.19.refs_0_.refs_2_), channel_id=1, source_target_pairs={{0,8},{1,9},{2,10},{3,11},{4,12},{5,13},{6,14},{7,15},{8,16},{9,17... | collective-permute-start | bytes 2064392 | tf_op jit(solution)/shard_map/ppermute | solution.py:380
  90.2 26.6 %collective-permute-start.15 = (f32[224,768]{1,0:T(8,128)}, f32[224,768]{1,0:T(8,128)}, u32[]{:S(2)}, u32[]{:S(2)}) collective-permute-start(f32[224,768]{1,0:T(8,128)} %get-tuple-element.20.refs_1_.refs_3_), channel_id=1, source_target_pairs={{8,0},{9,1},{10,2},{11,3},{12,4},{13,5},{14,6},{15,7},{16,8},{17,9... | collective-permute-start | bytes 2064392 | tf_op jit(solution)/shard_map/ppermute | solution.py:380
  101.9 25.4 %collective-permute-start.16 = (f32[224,768]{1,0:T(8,128)S(1)}, f32[224,768]{1,0:T(8,128)}, u32[]{:S(2)}, u32[]{:S(2)}) collective-permute-start(f32[224,768]{1,0:T(8,128)S(1)} %collective-permute-done.12.refs_2_.refs_4_), channel_id=1, source_target_pairs={{0,8},{1,9},{2,10},{3,11},{4,12},{5,13},{6,14},{7,15},{8,16},{9,17... | collective-permute-start | bytes 2064392 | tf_op jit(solution)/shard_map/ppermute | solution.py:395
  101.9 4.1 %copy-start.6 = (f32[8,56,768]{2,1,0:T(8,128)}, f32[8,56,768]{2,1,0:T(8,128)S(1)}, u32[]{:S(2)}) copy-start(f32[8,56,768]{2,1,0:T(8,128)S(1)} %all-to-all-done.2.refs_6_.refs_3_) | copy-start | bytes 4128772
  106.1 21.8 %all-to-all-start.3 = ((f32[8,56,768]{2,1,0:T(8,128)}), f32[8,56,768]{2,1,0:T(8,128)S(1)}, u32[]{:S(2)}, u32[]{:S(2)}) async-start(f32[8,56,768]{2,1,0:T(8,128)} %shard_map.99), calls=%async_computation.3 | async-start | bytes 2752512 | tf_op jit(solution)/shard_map/all_to_all | solution.py:375
  116.7 11.1 %collective-permute-start.17 = (f32[224,768]{1,0:T(8,128)}, f32[224,768]{1,0:T(8,128)S(1)}, u32[]{:S(2)}, u32[]{:S(2)}) collective-permute-start(f32[224,768]{1,0:T(8,128)} %get-tuple-element.22.refs_1_.refs_3_), channel_id=1, source_target_pairs={{8,0},{9,1},{10,2},{11,3},{12,4},{13,5},{14,6},{15,7},{16,8},{17,9... | collective-permute-start | bytes 2064392 | tf_op jit(solution)/shard_map/ppermute | solution.py:396
  127.9 4.2 %copy-start.8 = (f32[8,56,768]{2,1,0:T(8,128)}, f32[8,56,768]{2,1,0:T(8,128)S(1)}, u32[]{:S(2)}) copy-start(f32[8,56,768]{2,1,0:T(8,128)S(1)} %all-to-all-done.3.refs_4_.refs_6_) | copy-start | bytes 4128772
  132.1 21.6 %all-to-all-start.4 = ((f32[8,56,768]{2,1,0:T(8,128)}), f32[8,56,768]{2,1,0:T(8,128)S(1)}, u32[]{:S(2)}, u32[]{:S(2)}) async-start(f32[8,56,768]{2,1,0:T(8,128)} %shard_map.104), calls=%async_computation.4 | async-start | bytes 2752512 | tf_op jit(solution)/shard_map/all_to_all | solution.py:375
  139.3 1.3 copy-start.5
  140.6 1.3 copy-start.7
  142.0 1.3 copy-start.9
  143.3 2.9 %copy-start.11 = (f32[224,768]{1,0:T(8,128)S(1)}, f32[224,768]{1,0:T(8,128)}, u32[]{:S(2)}) copy-start(f32[224,768]{1,0:T(8,128)} %copy-done.10) | copy-start | bytes 2064388
  148.8 1.1 copy-start.2
  153.7 1.3 copy-start.3

commit v11 on v10

--- a/solution.py
+++ b/solution.py
@@ -380,7 +380,7 @@
         return lax.ppermute(pair[0], "shard", UP), lax.ppermute(pair[1], "shard", DOWN)
 
     one = [around((x, x)) for x in state]
-    rows = pick((0, 0, -1, 1), (*state, *one[0]), 4)
+    rows = pick((0, 0, -1, 1), (*state, *one[0]), 8)
     far1 = to_plane(rows)
     one[1] = hold(one[1], wait=10)
     two = [around(pair) for pair in one]

time: 162 us -> 164 us (1.012)
  starting transfers between devices: 61.6 us -> 64.8 us
  waiting for transfers between devices: 53.5 us -> 51.3 us
  local copies, waits for them, and re-layouts: 10.8 us -> 12.9 us
    ppermute x6, waiting for transfers between devices: 32.7 us -> 38.4 us  [around(): lax.ppermute(pair[0], 'shard', UP)]
    ppermute x2, waiting for transfers between devices: 3.99 us -> 0.01 us  [on_device(): got_y = [lax.ppermute(p, 'dp', NEXT_Y) for p in passed]]
    all_to_all x4, starting transfers between devices: 27.2 us -> 29.4 us  [to_plane(): lax.all_to_all(rows, 'shard', split_axis=0, concat_axis=0, axis_index_gro...]
    unnamed x45 -> x51, local copies, waits for them, and re-layouts: 10.7 us -> 12.8 us
    all_to_all x1, waiting for transfers between devices: 1.96 us -> 0.01 us  [on_device(): lax.all_to_all(wanted, 'shard', split_axis=0, concat_axis=0, axis_index_g...]
    all_to_all x4, waiting for transfers between devices: 3.76 us -> 1.85 us  [to_plane(): lax.all_to_all(rows, 'shard', split_axis=0, concat_axis=0, axis_index_gro...]
  transfers between devices with their start and end apart: 23 -> 23, of which waited for: 11 -> 8; matrix products, arithmetic and copies ran while one was open for 0% -> 0% of each run, Pallas kernels for 14% -> 13%
where the time goes in v11:
time: 164 us; the launch traced here: 162 us
  starting transfers between devices  64.8 us (40%)
  waiting for transfers between devices  51.3 us (31%)
  Pallas kernels  32.3 us (20%)
  local copies, waits for them, and re-layouts  12.9 us (8%)
    ppermute x6, waiting for transfers between devices, around(): lax.ppermute(pair[0], 'shard', UP)  38.4 us
    all_to_all x4, starting transfers between devices, to_plane(): lax.all_to_all(rows, 'shard', split_axis=0, concat_axis=0, axis_index_gro...  29.4 us
    ppermute x6, starting transfers between devices, around(): lax.ppermute(pair[1], 'shard', DOWN)  18.6 us
    pallas_call x4, Pallas kernels, pick(): call(lambda *refs: pick_kernel(planes, *refs), shape(PLANE, SENT, WIDE),...  15.2 us
    unnamed x51, local copies, waits for them, and re-layouts  12.8 us
    ppermute x1, waiting for transfers between devices, on_device(): lax.ppermute(three[0][0], 'shard', UP)  7.58 us
    all_to_all x1, starting transfers between devices, on_device(): lax.all_to_all(wanted, 'shard', split_axis=0, concat_axis=0, axis_index_g...  7.17 us
    pallas_call x2, Pallas kernels, on_device(): call(lambda *refs, parts=parts: gather_kernel(parts, *refs), shape(FINE,...  5.49 us
  transfers between devices with their start and end apart: 23, of which 8 were waited for; matrix products, arithmetic and copies ran while one was open for 0% of the time, Pallas kernels for 13%

profile of v11, /device:TPU:2, one launch (start us, length us, event | category | flops | bytes accessed | tf_op | source)
XLA Modules:
  0.0 162.4 jit_solution(6787591691289819353)
XLA Ops:
  0.6 0.1 pad_add_fusion.place.refs_0_
  0.7 1.2 copy-done
  1.9 1.4 shard_map.86
  3.3 0.0 collective-permute-start
  3.3 0.5 collective-permute-start.2
  3.8 1.9 %collective-permute-done.refs_2_ = f32[224,512]{1,0:T(8,128)S(1)} collective-permute-done((f32[224,512]{1,0:T(8,128)S(1)}, f32[224,512]{1,0:T(8,128)S(1)}, u32[]{:S(2)}, u32[]{:S(2)}) %collective-permute-start) | collective-permute-done | bytes 458784 | tf_op jit(solution)/shard_map/ppermute | solution.py:321
  5.7 0.6 shard_map.87
  6.3 0.0 copy-start.18
  6.3 0.8 copy-done.18
  7.0 1.6 collective-permute-start.1
  8.6 0.1 copy.16.dev
  8.8 0.1 copy.17.col
  8.9 1.7 %shard_map.85 = (s32[8,8,128]{2,1,0:T(8,128)}, s32[8,448]{1,0:T(8,128)S(1)}) custom-call(s32[2]{0:T(128)S(1)} %pad_add_fusion.place.refs_0_, s32[448,1]{1,0:T(8,128)S(1)} %copy.16.dev, s32[1,448]{1,0:T(1,128)S(1)} %bitcast.10, s32[448,1]{1,0:T(8,128)S(1)} %copy.17.col), custom_call_target="tpu_custom_call" | custom-call | bytes 1048576 | tf_op jit(solution)/shard_map/pallas_call | solution.py:301
  10.6 7.2 %all-to-all-start = ((s32[8,8,128]{2,1,0:T(8,128)}), s32[8,8,128]{2,1,0:T(8,128)S(1)}, u32[]{:S(2)}, u32[]{:S(2)}) async-start(s32[8,8,128]{2,1,0:T(8,128)} %get-tuple-element.16.refs_8_), calls=%async_computation | async-start | bytes 65536 | tf_op jit(solution)/shard_map/all_to_all | solution.py:312
  17.8 0.0 collective-permute-done.2.refs_2_
  17.8 0.6 shard_map.88.refs_7_
  18.4 0.2 collective-permute-start.3
  18.6 0.0 collective-permute-done.1.refs_3_
  18.6 0.2 copy-done.19
  18.8 1.0 copy-done.16
  19.8 1.3 shard_map.89.refs_0_.refs_2_.refs_1_
  21.1 0.0 copy-start.15
  21.1 0.0 copy-start.17
  21.1 2.0 %collective-permute-start.4 = (f32[224,768]{1,0:T(8,128)S(1)}, f32[224,768]{1,0:T(8,128)S(1)}, u32[]{:S(2)}, u32[]{:S(2)}) collective-permute-start(f32[224,768]{1,0:T(8,128)S(1)} %shard_map.89.refs_0_.refs_2_.refs_1_), channel_id=1, source_target_pairs={{0,8},{1,9},{2,10},{3,11},{4,12},{5,13},{6,14},{7,15},{8,16},{9,17... | collective-permute-start | bytes 2064392 | tf_op jit(solution)/shard_map/ppermute | solution.py:380
  23.1 4.0 %collective-permute-start.5 = (f32[224,768]{1,0:T(8,128)S(1)}, f32[224,768]{1,0:T(8,128)}, u32[]{:S(2)}, u32[]{:S(2)}) collective-permute-start(f32[224,768]{1,0:T(8,128)S(1)} %shard_map.89.refs_0_.refs_2_.refs_1_), channel_id=1, source_target_pairs={{8,0},{9,1},{10,2},{11,3},{12,4},{13,5},{14,6},{15,7},{16,8},{17,9... | collective-permute-start | bytes 2064392 | tf_op jit(solution)/shard_map/ppermute | solution.py:380
  27.1 1.3 shard_map.91.refs_1_.refs_3_
  28.4 0.2 collective-permute-start.6
  28.6 4.0 %collective-permute-start.7 = (f32[224,768]{1,0:T(8,128)S(1)}, f32[224,768]{1,0:T(8,128)}, u32[]{:S(2)}, u32[]{:S(2)}) collective-permute-start(f32[224,768]{1,0:T(8,128)S(1)} %shard_map.91.refs_1_.refs_3_), channel_id=1, source_target_pairs={{8,0},{9,1},{10,2},{11,3},{12,4},{13,5},{14,6},{15,7},{16,8},{17,9... | collective-permute-start | bytes 2064392 | tf_op jit(solution)/shard_map/ppermute | solution.py:380
  32.6 10.7 %collective-permute-done.4.refs_2_.refs_4_ = f32[224,768]{1,0:T(8,128)S(1)} collective-permute-done((f32[224,768]{1,0:T(8,128)S(1)}, f32[224,768]{1,0:T(8,128)S(1)}, u32[]{:S(2)}, u32[]{:S(2)}) %collective-permute-start.4) | collective-permute-done | bytes 688160 | tf_op jit(solution)/shard_map/ppermute | solution.py:380
  43.4 0.8 copy-done.20
  44.2 1.1 copy-done.21
  45.3 2.8 %shard_map.93 = f32[8,56,768]{2,1,0:T(8,128)S(1)} custom-call(s32[2]{0:T(128)S(1)} %pad_add_fusion.place.refs_0_, s32[8,8,128]{2,1,0:T(8,128)S(1)} %all-to-all-done.refs_1_, f32[224,768]{1,0:T(8,128)S(1)} %shard_map.89.refs_0_.refs_2_.refs_1_, f32[224,768]{1,0:T(8,128)S(1)} %shard_map.91.refs_1_.refs_3_, f32[224,768]{1,0:T(8,128)S(1)} %copy-done.21, ...), custom_call_target="tpu_custom_call" | custom-call | flops 352321536 | bytes 5242880 | tf_op jit(solution)/shard_map/pallas_call | solution.py:360
  48.1 0.0 copy-start.12
  48.1 1.1 copy-done.12
  49.2 7.8 %all-to-all-start.1 = ((f32[8,56,768]{2,1,0:T(8,128)}), f32[8,56,768]{2,1,0:T(8,128)S(1)}, u32[]{:S(2)}, u32[]{:S(2)}) async-start(f32[8,56,768]{2,1,0:T(8,128)} %copy-done.12), calls=%async_computation.1 | async-start | bytes 2752512 | tf_op jit(solution)/shard_map/all_to_all | solution.py:375
  57.0 0.1 collective-permute-start.8
  57.1 3.4 %collective-permute-start.9 = (f32[224,768]{1,0:T(8,128)}, f32[224,768]{1,0:T(8,128)}, u32[]{:S(2)}, u32[]{:S(2)}) collective-permute-start(f32[224,768]{1,0:T(8,128)} %collective-permute-done.5.refs_3_.refs_5_), channel_id=1, source_target_pairs={{8,0},{9,1},{10,2},{11,3},{12,4},{13,5},{14,6},{15,7},{16,8},{17,9... | collective-permute-start | bytes 2064392 | tf_op jit(solution)/shard_map/ppermute | solution.py:380
  60.5 3.2 %collective-permute-start.11 = (f32[224,768]{1,0:T(8,128)}, f32[224,768]{1,0:T(8,128)}, u32[]{:S(2)}, u32[]{:S(2)}) collective-permute-start(f32[224,768]{1,0:T(8,128)} %get-tuple-element.18.refs_1_.refs_3_), channel_id=1, source_target_pairs={{8,0},{9,1},{10,2},{11,3},{12,4},{13,5},{14,6},{15,7},{16,8},{17,9... | collective-permute-start | bytes 2064392 | tf_op jit(solution)/shard_map/ppermute | solution.py:380
  63.7 13.1 %collective-permute-done.8.refs_2_.refs_4_ = f32[224,768]{1,0:T(8,128)} collective-permute-done((f32[224,768]{1,0:T(8,128)S(1)}, f32[224,768]{1,0:T(8,128)}, u32[]{:S(2)}, u32[]{:S(2)}) %collective-permute-start.8) | collective-permute-done | bytes 688160 | tf_op jit(solution)/shard_map/ppermute | solution.py:380
  76.8 3.5 %collective-permute-start.13 = (f32[224,768]{1,0:T(8,128)}, f32[224,768]{1,0:T(8,128)S(1)}, u32[]{:S(2)}, u32[]{:S(2)}) collective-permute-start(f32[224,768]{1,0:T(8,128)} %collective-permute-done.9.refs_3_.refs_5_), channel_id=1, source_target_pairs={{8,0},{9,1},{10,2},{11,3},{12,4},{13,5},{14,6},{15,7},{16,8},{17,9... | collective-permute-start | bytes 2064392 | tf_op jit(solution)/shard_map/ppermute | solution.py:380
  80.4 4.1 %shard_map.96 = f32[8,56,768]{2,1,0:T(8,128)} custom-call(s32[2]{0:T(128)S(1)} %pad_add_fusion.place.refs_0_, s32[8,8,128]{2,1,0:T(8,128)S(1)} %all-to-all-done.refs_1_, f32[224,768]{1,0:T(8,128)} %get-tuple-element.17.refs_0_.refs_2_, f32[224,768]{1,0:T(8,128)} %get-tuple-element.18.refs_1_.refs_3_, f32[224,768]{1,0:T(8,128)} %collective-permute-done.8.refs_2_.refs_4_, ...), custom_call_target="tpu_custom_call" | custom-call | flops 352321536 | bytes 5242880 | tf_op jit(solution)/shard_map/pallas_call | solution.py:360
  84.5 7.2 %all-to-all-start.2 = ((f32[8,56,768]{2,1,0:T(8,128)}), f32[8,56,768]{2,1,0:T(8,128)S(1)}, u32[]{:S(2)}, u32[]{:S(2)}) async-start(f32[8,56,768]{2,1,0:T(8,128)} %shard_map.96), calls=%async_computation.2 | async-start | bytes 2752512 | tf_op jit(solution)/shard_map/all_to_all | solution.py:375
  91.8 3.0 %collective-permute-start.14 = (f32[224,768]{1,0:T(8,128)}, f32[224,768]{1,0:T(8,128)}, u32[]{:S(2)}, u32[]{:S(2)}) collective-permute-start(f32[224,768]{1,0:T(8,128)} %get-tuple-element.19.refs_0_.refs_2_), channel_id=1, source_target_pairs={{0,8},{1,9},{2,10},{3,11},{4,12},{5,13},{6,14},{7,15},{8,16},{9,17... | collective-permute-start | bytes 2064392 | tf_op jit(solution)/shard_map/ppermute | solution.py:380
  94.7 0.4 collective-permute-start.15
  95.1 11.1 %collective-permute-done.12.refs_2_.refs_4_ = f32[224,768]{1,0:T(8,128)S(1)} collective-permute-done((f32[224,768]{1,0:T(8,128)}, f32[224,768]{1,0:T(8,128)S(1)}, u32[]{:S(2)}, u32[]{:S(2)}) %collective-permute-start.12) | collective-permute-done | bytes 688160 | tf_op jit(solution)/shard_map/ppermute | solution.py:380
  106.2 0.0 copy-start.6
  106.3 4.1 %shard_map.99 = f32[8,56,768]{2,1,0:T(8,128)} custom-call(s32[2]{0:T(128)S(1)} %pad_add_fusion.place.refs_0_, s32[8,8,128]{2,1,0:T(8,128)S(1)} %all-to-all-done.refs_1_, f32[224,768]{1,0:T(8,128)} %get-tuple-element.19.refs_0_.refs_2_, f32[224,768]{1,0:T(8,128)} %get-tuple-element.20.refs_1_.refs_3_, f32[224,768]{1,0:T(8,128)S(1)} %collective-permute-done.12.refs_2_.refs_4_, ...), custom_call_target="tpu_custom_call" | custom-call | flops 352321536 | bytes 5242880 | tf_op jit(solution)/shard_map/pallas_call | solution.py:360
  110.4 7.2 %all-to-all-start.3 = ((f32[8,56,768]{2,1,0:T(8,128)}), f32[8,56,768]{2,1,0:T(8,128)S(1)}, u32[]{:S(2)}, u32[]{:S(2)}) async-start(f32[8,56,768]{2,1,0:T(8,128)} %shard_map.99), calls=%async_computation.3 | async-start | bytes 2752512 | tf_op jit(solution)/shard_map/all_to_all | solution.py:375
  117.6 3.5 %collective-permute-done.14.refs_0_ = f32[224,768]{1,0:T(8,128)} collective-permute-done((f32[224,768]{1,0:T(8,128)}, f32[224,768]{1,0:T(8,128)}, u32[]{:S(2)}, u32[]{:S(2)}) %collective-permute-start.14) | collective-permute-done | bytes 688160 | tf_op jit(solution)/shard_map/ppermute | solution.py:380
  121.1 2.0 %collective-permute-start.17 = (f32[224,768]{1,0:T(8,128)}, f32[224,768]{1,0:T(8,128)S(1)}, u32[]{:S(2)}, u32[]{:S(2)}) collective-permute-start(f32[224,768]{1,0:T(8,128)} %get-tuple-element.22.refs_1_.refs_3_), channel_id=1, source_target_pairs={{8,0},{9,1},{10,2},{11,3},{12,4},{13,5},{14,6},{15,7},{16,8},{17,9... | collective-permute-start | bytes 2064392 | tf_op jit(solution)/shard_map/ppermute | solution.py:396
  123.1 7.6 %collective-permute-done.16.refs_2_.refs_4_ = f32[224,768]{1,0:T(8,128)} collective-permute-done((f32[224,768]{1,0:T(8,128)S(1)}, f32[224,768]{1,0:T(8,128)}, u32[]{:S(2)}, u32[]{:S(2)}) %collective-permute-start.16) | collective-permute-done | bytes 688160 | tf_op jit(solution)/shard_map/ppermute | solution.py:395
  130.7 1.6 collective-permute-done.17.refs_3_.refs_5_
  132.2 4.2 %shard_map.104 = f32[8,56,768]{2,1,0:T(8,128)} custom-call(s32[2]{0:T(128)S(1)} %pad_add_fusion.place.refs_0_, s32[8,8,128]{2,1,0:T(8,128)S(1)} %all-to-all-done.refs_1_, f32[224,768]{1,0:T(8,128)} %get-tuple-element.21.refs_0_.refs_2_, f32[224,768]{1,0:T(8,128)} %get-tuple-element.22.refs_1_.refs_3_, f32[224,768]{1,0:T(8,128)} %collective-permute-done.16.refs_2_.refs_4_, ...), custom_call_target="tpu_custom_call" | custom-call | flops 352321536 | bytes 5242880 | tf_op jit(solution)/shard_map/pallas_call | solution.py:360
  136.4 7.2 %all-to-all-start.4 = ((f32[8,56,768]{2,1,0:T(8,128)}), f32[8,56,768]{2,1,0:T(8,128)S(1)}, u32[]{:S(2)}, u32[]{:S(2)}) async-start(f32[8,56,768]{2,1,0:T(8,128)} %shard_map.104), calls=%async_computation.4 | async-start | bytes 2752512 | tf_op jit(solution)/shard_map/all_to_all | solution.py:375
  143.6 1.3 copy-done.5
  145.0 1.3 copy-done.7
  146.3 1.3 copy-done.9
  147.6 2.9 %shard_map.100.refs_0_.refs_1_.refs_2_ = f32[448,768]{1,0:T(8,128)S(1)} custom-call(s32[8,448]{1,0:T(8,128)S(1)} %get-tuple-element.13.refs_0_.codes, f32[224,768]{1,0:T(8,128)S(1)} %shard_map.89.refs_0_.refs_2_.refs_1_, f32[8,56,768]{2,1,0:T(8,128)S(1)} %copy-done.5, f32[8,56,768]{2,1,0:T(8,128)S(1)} %copy-done.7, f32[8,56,768]{2,1,0:T(8,128)S(1)} %copy-done.9), custom_call_target="tpu_custom_call" | custom-call | flops 1541406720 | bytes 8388608 | tf_op jit(solution)/shard_map/pallas_call | solution.py:408
  150.6 2.6 %shard_map.101.refs_3_.refs_4_.refs_5_ = f32[448,768]{1,0:T(8,128)S(1)} custom-call(s32[8,448]{1,0:T(8,128)S(1)} %get-tuple-element.13.refs_0_.codes, f32[224,768]{1,0:T(8,128)S(1)} %copy-done.11, f32[8,56,768]{2,1,0:T(8,128)S(1)} %copy-done.5, f32[8,56,768]{2,1,0:T(8,128)S(1)} %copy-done.7, f32[8,56,768]{2,1,0:T(8,128)S(1)} %copy-done.9), custom_call_target="tpu_custom_call" | custom-call | flops 1541406720 | bytes 8388608 | tf_op jit(solution)/shard_map/pallas_call | solution.py:408
  153.2 0.0 copy-start.2
  153.2 1.1 copy-done.2
  154.2 1.8 %all-to-all-done.4.refs_6_.refs_7_.refs_8_ = f32[8,56,768]{2,1,0:T(8,128)S(1)} async-done(((f32[8,56,768]{2,1,0:T(8,128)}), f32[8,56,768]{2,1,0:T(8,128)S(1)}, u32[]{:S(2)}, u32[]{:S(2)}) %all-to-all-start.4) | async-done | bytes 1376288 | tf_op jit(solution)/shard_map/all_to_all | solution.py:375
  156.1 1.3 copy-done.3
  157.4 5.0 %shard_map.105 = (f32[448,1024]{1,0:T(8,128)}, f32[448,1024]{1,0:T(8,128)}, f32[448,1024]{1,0:T(8,128)}) custom-call(s32[8,448]{1,0:T(8,128)S(1)} %get-tuple-element.13.refs_0_.codes, f32[448,768]{1,0:T(8,128)S(1)} %shard_map.100.refs_0_.refs_1_.refs_2_, f32[448,768]{1,0:T(8,128)S(1)} %shard_map.100.refs_0_.refs_1_.refs_2_, ...), custom_call_target="tpu_custom_call" | custom-call | flops 1409286144 | bytes 12582912 | tf_op jit(solution)/shard_map/pallas_call | solution.py:433
  (56 shorter events, 0.1 us)
Async XLA Ops:
  0.6 8.0 %copy-start.23 = (s32[448,1]{0,1:T(1,128)S(1)}, s32[448,1]{0,1:T(1,128)}, u32[]{:S(2)}) copy-start(s32[448,1]{0,1:T(1,128)} %param.10) | copy-start | bytes 5380
  0.7 1.2 copy-start
  1.9 6.9 %copy-start.24 = (s32[448]{0:T(512)S(1)}, s32[448]{0:T(512)}, u32[]{:S(2)}) copy-start(s32[448]{0:T(512)} %param.11) | copy-start | bytes 5380
  3.3 14.5 %copy-start.1 = (bf16[1,224,2048]{2,1,0:T(8,128)(2,1)S(1)}, bf16[1,224,2048]{2,1,0:T(8,128)(2,1)}, u32[]{:S(2)}) copy-start(bf16[1,224,2048]{2,1,0:T(8,128)(2,1)} %param.6) | copy-start | bytes 2752516
  3.3 2.4 %collective-permute-start = (f32[224,512]{1,0:T(8,128)S(1)}, f32[224,512]{1,0:T(8,128)S(1)}, u32[]{:S(2)}, u32[]{:S(2)}) collective-permute-start(f32[224,512]{1,0:T(8,128)S(1)} %get-tuple-element.14), channel_id=1, source_target_pairs={{0,64},{64,0},{128,192},{192,128},{1,65},{65,1},{129,193},{193,129... | collective-permute-start | bytes 1376264 | tf_op jit(solution)/shard_map/ppermute | solution.py:321
  3.3 14.5 %collective-permute-start.2 = (f32[224,512]{1,0:T(8,128)}, f32[224,512]{1,0:T(8,128)S(1)}, u32[]{:S(2)}, u32[]{:S(2)}) collective-permute-start(f32[224,512]{1,0:T(8,128)} %get-tuple-element.15), channel_id=1, source_target_pairs={{0,64},{64,0},{128,192},{192,128},{1,65},{65,1},{129,193},{193,129... | collective-permute-start | bytes 1376264 | tf_op jit(solution)/shard_map/ppermute | solution.py:321
  6.3 0.8 copy-start.18
  7.0 11.5 %copy-start.13 = (f32[224,512]{1,0:T(8,128)S(1)}, f32[224,512]{1,0:T(8,128)}, u32[]{:S(2)}) copy-start(f32[224,512]{1,0:T(8,128)} %refs_4_.3) | copy-start | bytes 1376260
  7.0 11.5 %copy-start.14 = (f32[224,512]{1,0:T(8,128)S(1)}, f32[224,512]{1,0:T(8,128)}, u32[]{:S(2)}) copy-start(f32[224,512]{1,0:T(8,128)} %refs_5_.3) | copy-start | bytes 1376260
  7.0 11.5 %collective-permute-start.1 = (f32[224,256]{1,0:T(8,128)S(1)}, f32[224,256]{1,0:T(8,128)S(1)}, u32[]{:S(2)}, u32[]{:S(2)}) collective-permute-start(f32[224,256]{1,0:T(8,128)S(1)} %shard_map.87), channel_id=1, source_target_pairs={{0,128},{128,0},{64,192},{192,64},{1,129},{129,1},{65,193},{193,65... | collective-permute-start | bytes 688136 | tf_op jit(solution)/shard_map/ppermute | solution.py:337
  10.6 33.6 %all-to-all-start = ((s32[8,8,128]{2,1,0:T(8,128)}), s32[8,8,128]{2,1,0:T(8,128)S(1)}, u32[]{:S(2)}, u32[]{:S(2)}) async-start(s32[8,8,128]{2,1,0:T(8,128)} %get-tuple-element.16.refs_8_), calls=%async_computation | async-start | bytes 65536 | tf_op jit(solution)/shard_map/all_to_all | solution.py:312
  17.8 1.0 copy-start.19
  18.4 8.8 %collective-permute-start.3 = (f32[224,256]{1,0:T(8,128)S(1)}, f32[224,256]{1,0:T(8,128)S(1)}, u32[]{:S(2)}, u32[]{:S(2)}) collective-permute-start(f32[224,256]{1,0:T(8,128)S(1)} %shard_map.88.refs_7_), channel_id=1, source_target_pairs={{0,128},{128,0},{64,192},{192,64},{1,129},{129,1},{65,193},{193,65... | collective-permute-start | bytes 688136 | tf_op jit(solution)/shard_map/ppermute | solution.py:337
  18.8 1.0 copy-start.16
  21.1 6.1 %copy-start.15 = (f32[224,512]{1,0:T(8,128)S(1)}, f32[224,512]{1,0:T(8,128)}, u32[]{:S(2)}) copy-start(f32[224,512]{1,0:T(8,128)} %refs_5_.3) | copy-start | bytes 1376260
  21.1 6.0 %copy-start.17 = (f32[224,512]{1,0:T(8,128)S(1)}, f32[224,512]{1,0:T(8,128)}, u32[]{:S(2)}) copy-start(f32[224,512]{1,0:T(8,128)} %refs_6_.3) | copy-start | bytes 1376260
  21.1 22.3 %collective-permute-start.4 = (f32[224,768]{1,0:T(8,128)S(1)}, f32[224,768]{1,0:T(8,128)S(1)}, u32[]{:S(2)}, u32[]{:S(2)}) collective-permute-start(f32[224,768]{1,0:T(8,128)S(1)} %shard_map.89.refs_0_.refs_2_.refs_1_), channel_id=1, source_target_pairs={{0,8},{1,9},{2,10},{3,11},{4,12},{5,13},{6,14},{7,15},{8,16},{9,17... | collective-permute-start | bytes 2064392 | tf_op jit(solution)/shard_map/ppermute | solution.py:380
  23.1 20.3 %collective-permute-start.5 = (f32[224,768]{1,0:T(8,128)S(1)}, f32[224,768]{1,0:T(8,128)}, u32[]{:S(2)}, u32[]{:S(2)}) collective-permute-start(f32[224,768]{1,0:T(8,128)S(1)} %shard_map.89.refs_0_.refs_2_.refs_1_), channel_id=1, source_target_pairs={{8,0},{9,1},{10,2},{11,3},{12,4},{13,5},{14,6},{15,7},{16,8},{17,9... | collective-permute-start | bytes 2064392 | tf_op jit(solution)/shard_map/ppermute | solution.py:380
  28.4 15.8 %copy-start.10 = (f32[224,768]{1,0:T(8,128)}, f32[224,768]{1,0:T(8,128)S(1)}, u32[]{:S(2)}) copy-start(f32[224,768]{1,0:T(8,128)S(1)} %shard_map.91.refs_1_.refs_3_) | copy-start | bytes 2064388
  28.4 32.1 %collective-permute-start.6 = (f32[224,768]{1,0:T(8,128)S(1)}, f32[224,768]{1,0:T(8,128)}, u32[]{:S(2)}, u32[]{:S(2)}) collective-permute-start(f32[224,768]{1,0:T(8,128)S(1)} %shard_map.91.refs_1_.refs_3_), channel_id=1, source_target_pairs={{0,8},{1,9},{2,10},{3,11},{4,12},{5,13},{6,14},{7,15},{8,16},{9,17... | collective-permute-start | bytes 2064392 | tf_op jit(solution)/shard_map/ppermute | solution.py:380
  28.6 31.8 %collective-permute-start.7 = (f32[224,768]{1,0:T(8,128)S(1)}, f32[224,768]{1,0:T(8,128)}, u32[]{:S(2)}, u32[]{:S(2)}) collective-permute-start(f32[224,768]{1,0:T(8,128)S(1)} %shard_map.91.refs_1_.refs_3_), channel_id=1, source_target_pairs={{8,0},{9,1},{10,2},{11,3},{12,4},{13,5},{14,6},{15,7},{16,8},{17,9... | collective-permute-start | bytes 2064392 | tf_op jit(solution)/shard_map/ppermute | solution.py:380
  43.4 0.8 copy-start.20
  44.2 1.1 copy-start.21
  48.1 1.1 copy-start.12
  49.2 7.8 %copy-start.22 = (f32[224,768]{1,0:T(8,128)S(1)}, f32[224,768]{1,0:T(8,128)}, u32[]{:S(2)}) copy-start(f32[224,768]{1,0:T(8,128)} %copy-done.20) | copy-start | bytes 2064388
  49.2 31.2 %all-to-all-start.1 = ((f32[8,56,768]{2,1,0:T(8,128)}), f32[8,56,768]{2,1,0:T(8,128)S(1)}, u32[]{:S(2)}, u32[]{:S(2)}) async-start(f32[8,56,768]{2,1,0:T(8,128)} %copy-done.12), calls=%async_computation.1 | async-start | bytes 2752512 | tf_op jit(solution)/shard_map/all_to_all | solution.py:375
  57.0 19.9 %collective-permute-start.8 = (f32[224,768]{1,0:T(8,128)S(1)}, f32[224,768]{1,0:T(8,128)}, u32[]{:S(2)}, u32[]{:S(2)}) collective-permute-start(f32[224,768]{1,0:T(8,128)S(1)} %copy-done.22), channel_id=1, source_target_pairs={{0,8},{1,9},{2,10},{3,11},{4,12},{5,13},{6,14},{7,15},{8,16},{9,17... | collective-permute-start | bytes 2064392 | tf_op jit(solution)/shard_map/ppermute | solution.py:380
  57.1 19.8 %collective-permute-start.9 = (f32[224,768]{1,0:T(8,128)}, f32[224,768]{1,0:T(8,128)}, u32[]{:S(2)}, u32[]{:S(2)}) collective-permute-start(f32[224,768]{1,0:T(8,128)} %collective-permute-done.5.refs_3_.refs_5_), channel_id=1, source_target_pairs={{8,0},{9,1},{10,2},{11,3},{12,4},{13,5},{14,6},{15,7},{16,8},{17,9... | collective-permute-start | bytes 2064392 | tf_op jit(solution)/shard_map/ppermute | solution.py:380
  60.5 31.3 %collective-permute-start.10 = (f32[224,768]{1,0:T(8,128)}, f32[224,768]{1,0:T(8,128)}, u32[]{:S(2)}, u32[]{:S(2)}) collective-permute-start(f32[224,768]{1,0:T(8,128)} %get-tuple-element.17.refs_0_.refs_2_), channel_id=1, source_target_pairs={{0,8},{1,9},{2,10},{3,11},{4,12},{5,13},{6,14},{7,15},{8,16},{9,17... | collective-permute-start | bytes 2064392 | tf_op jit(solution)/shard_map/ppermute | solution.py:380
  60.5 31.3 %collective-permute-start.11 = (f32[224,768]{1,0:T(8,128)}, f32[224,768]{1,0:T(8,128)}, u32[]{:S(2)}, u32[]{:S(2)}) collective-permute-start(f32[224,768]{1,0:T(8,128)} %get-tuple-element.18.refs_1_.refs_3_), channel_id=1, source_target_pairs={{8,0},{9,1},{10,2},{11,3},{12,4},{13,5},{14,6},{15,7},{16,8},{17,9... | collective-permute-start | bytes 2064392 | tf_op jit(solution)/shard_map/ppermute | solution.py:380
  76.8 29.4 %collective-permute-start.12 = (f32[224,768]{1,0:T(8,128)}, f32[224,768]{1,0:T(8,128)S(1)}, u32[]{:S(2)}, u32[]{:S(2)}) collective-permute-start(f32[224,768]{1,0:T(8,128)} %collective-permute-done.8.refs_2_.refs_4_), channel_id=1, source_target_pairs={{0,8},{1,9},{2,10},{3,11},{4,12},{5,13},{6,14},{7,15},{8,16},{9,17... | collective-permute-start | bytes 2064392 | tf_op jit(solution)/shard_map/ppermute | solution.py:380
  76.8 29.4 %collective-permute-start.13 = (f32[224,768]{1,0:T(8,128)}, f32[224,768]{1,0:T(8,128)S(1)}, u32[]{:S(2)}, u32[]{:S(2)}) collective-permute-start(f32[224,768]{1,0:T(8,128)} %collective-permute-done.9.refs_3_.refs_5_), channel_id=1, source_target_pairs={{8,0},{9,1},{10,2},{11,3},{12,4},{13,5},{14,6},{15,7},{16,8},{17,9... | collective-permute-start | bytes 2064392 | tf_op jit(solution)/shard_map/ppermute | solution.py:380
  80.4 4.1 %copy-start.4 = (f32[8,56,768]{2,1,0:T(8,128)}, f32[8,56,768]{2,1,0:T(8,128)S(1)}, u32[]{:S(2)}) copy-start(f32[8,56,768]{2,1,0:T(8,128)S(1)} %all-to-all-done.1.refs_6_.refs_2_) | copy-start | bytes 4128772
  84.5 21.7 %all-to-all-start.2 = ((f32[8,56,768]{2,1,0:T(8,128)}), f32[8,56,768]{2,1,0:T(8,128)S(1)}, u32[]{:S(2)}, u32[]{:S(2)}) async-start(f32[8,56,768]{2,1,0:T(8,128)} %shard_map.96), calls=%async_computation.2 | async-start | bytes 2752512 | tf_op jit(solution)/shard_map/all_to_all | solution.py:375
  91.8 29.3 %collective-permute-start.14 = (f32[224,768]{1,0:T(8,128)}, f32[224,768]{1,0:T(8,128)}, u32[]{:S(2)}, u32[]{:S(2)}) collective-permute-start(f32[224,768]{1,0:T(8,128)} %get-tuple-element.19.refs_0_.refs_2_), channel_id=1, source_target_pairs={{0,8},{1,9},{2,10},{3,11},{4,12},{5,13},{6,14},{7,15},{8,16},{9,17... | collective-permute-start | bytes 2064392 | tf_op jit(solution)/shard_map/ppermute | solution.py:380
  94.7 26.3 %collective-permute-start.15 = (f32[224,768]{1,0:T(8,128)}, f32[224,768]{1,0:T(8,128)}, u32[]{:S(2)}, u32[]{:S(2)}) collective-permute-start(f32[224,768]{1,0:T(8,128)} %get-tuple-element.20.refs_1_.refs_3_), channel_id=1, source_target_pairs={{8,0},{9,1},{10,2},{11,3},{12,4},{13,5},{14,6},{15,7},{16,8},{17,9... | collective-permute-start | bytes 2064392 | tf_op jit(solution)/shard_map/ppermute | solution.py:380
  106.2 24.5 %collective-permute-start.16 = (f32[224,768]{1,0:T(8,128)S(1)}, f32[224,768]{1,0:T(8,128)}, u32[]{:S(2)}, u32[]{:S(2)}) collective-permute-start(f32[224,768]{1,0:T(8,128)S(1)} %collective-permute-done.12.refs_2_.refs_4_), channel_id=1, source_target_pairs={{0,8},{1,9},{2,10},{3,11},{4,12},{5,13},{6,14},{7,15},{8,16},{9,17... | collective-permute-start | bytes 2064392 | tf_op jit(solution)/shard_map/ppermute | solution.py:395
  106.2 4.1 %copy-start.6 = (f32[8,56,768]{2,1,0:T(8,128)}, f32[8,56,768]{2,1,0:T(8,128)S(1)}, u32[]{:S(2)}) copy-start(f32[8,56,768]{2,1,0:T(8,128)S(1)} %all-to-all-done.2.refs_6_.refs_3_) | copy-start | bytes 4128772
  110.4 21.8 %all-to-all-start.3 = ((f32[8,56,768]{2,1,0:T(8,128)}), f32[8,56,768]{2,1,0:T(8,128)S(1)}, u32[]{:S(2)}, u32[]{:S(2)}) async-start(f32[8,56,768]{2,1,0:T(8,128)} %shard_map.99), calls=%async_computation.3 | async-start | bytes 2752512 | tf_op jit(solution)/shard_map/all_to_all | solution.py:375
  121.1 11.1 %collective-permute-start.17 = (f32[224,768]{1,0:T(8,128)}, f32[224,768]{1,0:T(8,128)S(1)}, u32[]{:S(2)}, u32[]{:S(2)}) collective-permute-start(f32[224,768]{1,0:T(8,128)} %get-tuple-element.22.refs_1_.refs_3_), channel_id=1, source_target_pairs={{8,0},{9,1},{10,2},{11,3},{12,4},{13,5},{14,6},{15,7},{16,8},{17,9... | collective-permute-start | bytes 2064392 | tf_op jit(solution)/shard_map/ppermute | solution.py:396
  132.2 4.2 %copy-start.8 = (f32[8,56,768]{2,1,0:T(8,128)}, f32[8,56,768]{2,1,0:T(8,128)S(1)}, u32[]{:S(2)}) copy-start(f32[8,56,768]{2,1,0:T(8,128)S(1)} %all-to-all-done.3.refs_4_.refs_6_) | copy-start | bytes 4128772
  136.4 19.7 %all-to-all-start.4 = ((f32[8,56,768]{2,1,0:T(8,128)}), f32[8,56,768]{2,1,0:T(8,128)S(1)}, u32[]{:S(2)}, u32[]{:S(2)}) async-start(f32[8,56,768]{2,1,0:T(8,128)} %shard_map.104), calls=%async_computation.4 | async-start | bytes 2752512 | tf_op jit(solution)/shard_map/all_to_all | solution.py:375
  143.6 1.3 copy-start.5
  145.0 1.3 copy-start.7
  146.3 1.3 copy-start.9
  147.6 2.9 %copy-start.11 = (f32[224,768]{1,0:T(8,128)S(1)}, f32[224,768]{1,0:T(8,128)}, u32[]{:S(2)}) copy-start(f32[224,768]{1,0:T(8,128)} %copy-done.10) | copy-start | bytes 2064388
  153.2 1.1 copy-start.2
  156.1 1.3 copy-start.3
